TPU v7x, 256 devices: a whole 4x4x8 slice. The times are simulated.
256 devices in a mesh: particle: 32 (over y, x, core), tensor: 8 (over z).
Axes of the slice: x: 4, y: 4, z: 8, core: 2. Of those that a mesh axis runs over, the one named last changes fastest.
Arguments:
- queries: bfloat16 [1024, 2, 8192], P('particle', None, 'tensor'), may hold values from -30 to 30
- new_keys: bfloat16 [1024, 2, 1024], P('particle', None, 'tensor'), may hold values from -6 to 6
- new_values: bfloat16 [1024, 2, 1024], P('particle', None, 'tensor'), may hold values from -6 to 6
- key_cache: bfloat16 [1024, 256, 1024], P('particle', None, 'tensor'), may hold values from -6 to 6
- value_cache: bfloat16 [1024, 256, 1024], P('particle', None, 'tensor'), may hold values from -6 to 6
- prompt_keys: bfloat16 [2048, 1024], P('particle', 'tensor'), may hold values from -6 to 6
- prompt_values: bfloat16 [2048, 1024], P('particle', 'tensor'), may hold values from -6 to 6
- lengths: int32 [1024], P('particle'), may hold values from 1 to 254, as said below
- prior: float32 [1024], P('particle'), may hold values from -4 to 290
- reward_dir: float32 [8192], P('tensor'), may hold values from -6 to 6
- rungs: int32 [1024], replicated, may hold values from 0 to 7, as said below
- ancestors: int32 [1024], replicated, may hold values from 0 to 1023, as said below
Outputs:
- attention: bfloat16 [1024, 2, 8192], P('particle', None, 'tensor')
- weights: float32 [1024], P('particle')
- rung_means: float32 [8], replicated
- next_keys: bfloat16 [1024, 256, 1024], P('particle', None, 'tensor')
- next_values: bfloat16 [1024, 256, 1024], P('particle', None, 'tensor')
- next_lengths: int32 [1024], P('particle')
Inputs may be any that keep to these rules, and one draw needn't show every extreme that they name: In each aligned block of 32 particles, at most 3 name ancestors in any one aligned block and at most 2 distinct ancestors lie in any one aligned block; in every block both bounds are reached for some source block. `lengths`: every aligned block of 32 particles holds a particle with 254 filled slots. `rungs`: every rung holds at least one particle.
All inputs are finite; a program needn't handle non-finite values.
Results may differ from a plain program's by a relative error of at most 0.0085.
Values may be sent and summed in bfloat16 or wider, within the bound.
No kernel may reach another device: no remote copies, remote signals or barrier semaphores. Data moves between devices by JAX's collectives and lax.ppermute only.
A program may use at most 128 MiB of HBM per device.

v0:
```python
import jax
import jax.numpy as jnp
from jax import lax
from jax.sharding import PartitionSpec as P

HEADS = 64
KV_HEADS = 8
HEAD_DIM = 128
STEPS = 2
RUNGS = 8


def write_cache(cache, fresh, lengths):
    position = jnp.arange(cache.shape[1], dtype=jnp.int32)
    result = cache
    for offset in range(fresh.shape[1]):
        target = position[None, :] == lengths[:, None] + offset
        result = jnp.where(target[:, :, None], fresh[:, offset][:, None, :], result)
    return result


def shards(
    queries,
    new_keys,
    new_values,
    key_cache,
    value_cache,
    prompt_keys,
    prompt_values,
    lengths,
    prior,
    reward_dir,
    rungs,
    ancestors,
):
    per_device = queries.shape[0]
    suffix = key_cache.shape[1]
    groups = HEADS // KV_HEADS
    local_groups = key_cache.shape[2] // HEAD_DIM
    scale = HEAD_DIM ** (-0.5)
    sources = lax.axis_size("particle")
    device = lax.axis_index("particle")
    capacity = max(3, (per_device + sources - 1) // sources + 1)
    written_keys = write_cache(key_cache, new_keys, lengths)
    written_values = write_cache(value_cache, new_values, lengths)
    wanted = ancestors.reshape(sources, per_device)
    owner = wanted // per_device
    local = wanted % per_device
    mine_rows = lax.dynamic_slice_in_dim(ancestors, device * per_device, per_device)
    mine_owner = mine_rows // per_device
    order = jnp.arange(per_device, dtype=jnp.int32)
    earlier = order[None, :] < order[:, None]
    same_owner = mine_owner[:, None] == mine_owner[None, :]
    chosen = owner == device
    rank = jnp.cumsum(chosen.astype(jnp.int32), axis=1) - 1
    target = chosen[:, :, None] & (
        rank[:, :, None] == jnp.arange(capacity, dtype=jnp.int32)[None, None, :]
    )
    send_rows = jnp.sum(jnp.where(target, local[:, :, None], 0), axis=1).reshape(-1)
    outgoing = (written_keys[send_rows], written_values[send_rows], lengths[send_rows])
    arrived = (
        lax.all_to_all(outgoing[0], "particle", split_axis=0, concat_axis=0, tiled=True),
        lax.all_to_all(outgoing[1], "particle", split_axis=0, concat_axis=0, tiled=True),
        lax.all_to_all(outgoing[2], "particle", split_axis=0, concat_axis=0, tiled=True),
    )
    picked = jnp.sum((same_owner & earlier).astype(jnp.int32), axis=1)
    slot = mine_owner * capacity + picked
    next_keys = arrived[0][slot]
    next_values = arrived[1][slot]
    next_lengths = arrived[2][slot] + STEPS
    rows = per_device * STEPS
    query_rows = queries.reshape(rows, local_groups, groups, HEAD_DIM)
    highest = jnp.full((rows, local_groups, groups), -1e30, jnp.float32)
    piece_keys = lax.all_gather(prompt_keys, "particle", axis=0, tiled=True).reshape(
        -1, local_groups, HEAD_DIM
    )
    piece_values = lax.all_gather(prompt_values, "particle", axis=0, tiled=True).reshape(
        -1, local_groups, HEAD_DIM
    )
    scores = (
        jnp.einsum("rghd,ngd->rghn", query_rows, piece_keys, preferred_element_type=jnp.float32)
        * scale
    )
    fresh = jnp.maximum(highest, jnp.max(scores, axis=-1))
    expo = jnp.exp(scores - fresh[..., None])
    total = jnp.sum(expo, axis=-1)
    mixed = jnp.einsum(
        "rghn,ngd->rghd",
        expo.astype(jnp.bfloat16),
        piece_values,
        preferred_element_type=jnp.float32,
    )
    highest, total, mixed = (fresh, total, mixed)
    query_five = queries.reshape(per_device, STEPS, local_groups, groups, HEAD_DIM)
    cache_keys = written_keys.reshape(per_device, suffix, local_groups, HEAD_DIM)
    cache_values = written_values.reshape(per_device, suffix, local_groups, HEAD_DIM)
    scores = (
        jnp.einsum("psghd,plgd->psghl", query_five, cache_keys, preferred_element_type=jnp.float32)
        * scale
    )
    position = jnp.arange(suffix, dtype=jnp.int32)
    later = jnp.arange(STEPS, dtype=jnp.int32)
    visible = position[None, None, :] < lengths[:, None, None] + 1 + later[None, :, None]
    scores = jnp.where(visible[:, :, None, None, :], scores, -jnp.inf)
    highest = highest.reshape(per_device, STEPS, local_groups, groups)
    total = total.reshape(per_device, STEPS, local_groups, groups)
    mixed = mixed.reshape(per_device, STEPS, local_groups, groups, HEAD_DIM)
    final = jnp.maximum(highest, jnp.max(scores, axis=-1))
    factor = jnp.exp(highest - final)
    expo = jnp.exp(scores - final[..., None])
    total = total * factor + jnp.sum(expo, axis=-1)
    mixed = mixed * factor[..., None] + jnp.einsum(
        "psghl,plgd->psghd",
        expo.astype(jnp.bfloat16),
        cache_values,
        preferred_element_type=jnp.float32,
    )
    output = (mixed / total[..., None]).reshape(per_device, STEPS, -1)
    attention = output.astype(jnp.bfloat16)
    partial_reward = jnp.sum(output * reward_dir[None, None, :], axis=-1)
    reward = lax.psum(partial_reward, "tensor")
    weights = prior + jnp.sum(reward, axis=1)
    own_rungs = lax.dynamic_slice_in_dim(rungs, device * per_device, per_device)
    ladder = jnp.arange(RUNGS, dtype=jnp.int32)
    member = own_rungs[:, None] == ladder[None, :]
    local_peak = jnp.max(jnp.where(member, weights[:, None], -1e30), axis=0)
    top = lax.pmax(local_peak, "particle")
    local_sum = jnp.sum(jnp.where(member, jnp.exp(weights[:, None] - top[None, :]), 0.0), axis=0)
    summed = lax.psum(local_sum, "particle")
    counted = jnp.sum((rungs[:, None] == ladder[None, :]).astype(jnp.float32), axis=0)
    rung_means = top + jnp.log(summed) - jnp.log(counted)
    return (attention, weights, rung_means, next_keys, next_values, next_lengths)


def solution(mesh):
    placed = (
        P("particle", None, "tensor"),
        P("particle", None, "tensor"),
        P("particle", None, "tensor"),
        P("particle", None, "tensor"),
        P("particle", None, "tensor"),
        P("particle", "tensor"),
        P("particle", "tensor"),
        P("particle"),
        P("particle"),
        P("tensor"),
        P(),
        P(),
    )
    return jax.shard_map(
        shards,
        mesh=mesh,
        in_specs=placed,
        out_specs=(
            P("particle", None, "tensor"),
            P("particle"),
            P(),
            P("particle", None, "tensor"),
            P("particle", None, "tensor"),
            P("particle"),
        ),
        check_vma=False,
    )
```

profile of v0, /device:TPU:128, one launch (start us, length us, event | category | flops | bytes accessed | tf_op | source)
XLA Modules:
  0.0 414.1 jit_solution(9316704487613402714)
XLA Ops:
  0.6 0.8 reshape.358
  2.0 1.6 gather_fusion.4
  4.3 7.3 %all-to-all-start.2 = ((s32[32,3,1]{1,2,0:T(1,128)}), s32[32,3,1]{1,2,0:T(1,128)S(1)}, u32[]{:S(2)}, u32[]{:S(2)}) async-start(s32[32,3,1]{1,2,0:T(1,128)} %bitcast.27), calls=%async_computation.2 | async-start | bytes 32768 | tf_op jit(solution)/shard_map/all_to_all | solution.py:64
  12.3 0.8 fusion.48
  13.1 0.8 fusion.49
  14.7 7.2 %select_select_fusion.1 = (bf16[32,256,128]{2,1,0:T(8,128)(2,1)S(1)}, bf16[32,256,128]{2,1,0:T(8,128)(2,1)}) fusion(bf16[32,256,128]{2,1,0:T(8,128)(2,1)} %param.15, pred[32,256]{1,0:T(8,128)(4,1)S(1)} %get-tuple-element.27, pred[32,256]{1,0:T(8,128)(4,1)S(1)} %get-tuple-element.28, bf16[32,128]{1,0:T(8,128)(2,1)S(1)} %get-tuple-element.23, ...), kind=kLoop, calls=%fused_computation.18 | loop fusion | flops 4194304 | bytes 8437760 | tf_op jit(solution)/shard_map/jit(_where)/select_n | solution.py:18
  22.0 5.8 %gather_fusion = bf16[96,256,128]{2,1,0:T(8,128)(2,1)} fusion(bf16[32,256,128]{2,1,0:T(8,128)(2,1)S(1)} %get-tuple-element.12, s32[1024]{0:T(1024)S(1)} %pad_clamp_fusion.1), kind=kCustom, calls=%fused_computation | custom fusion | bytes 12583296 | tf_op jit(solution)/shard_map/gather | solution.py:60
  27.8 7.5 %all-to-all-start = ((bf16[96,256,128]{2,1,0:T(8,128)(2,1)}), bf16[96,256,128]{2,1,0:T(8,128)(2,1)}, u32[]{:S(2)}, u32[]{:S(2)}) async-start(bf16[96,256,128]{2,1,0:T(8,128)(2,1)} %gather_fusion), calls=%async_computation | async-start | bytes 12582912 | tf_op jit(solution)/shard_map/all_to_all | solution.py:62
  35.3 7.5 %gather_fusion.2 = bf16[96,256,128]{2,1,0:T(8,128)(2,1)} fusion(bf16[32,256,128]{2,1,0:T(8,128)(2,1)} %get-tuple-element.13, s32[1024]{0:T(1024)S(1)} %pad_clamp_fusion.1), kind=kCustom, calls=%fused_computation.2 | custom fusion | bytes 12583296 | tf_op jit(solution)/shard_map/gather | solution.py:60
  42.8 70.4 %all-to-all-done = bf16[96,256,128]{2,1,0:T(8,128)(2,1)} async-done(((bf16[96,256,128]{2,1,0:T(8,128)(2,1)}), bf16[96,256,128]{2,1,0:T(8,128)(2,1)}, u32[]{:S(2)}, u32[]{:S(2)}) %all-to-all-start) | async-done | bytes 6291488 | tf_op jit(solution)/shard_map/all_to_all | solution.py:62
  113.2 4.9 %all-to-all-start.1 = ((bf16[96,256,128]{2,1,0:T(8,128)(2,1)}), bf16[96,256,128]{2,1,0:T(8,128)(2,1)}, u32[]{:S(2)}, u32[]{:S(2)}) async-start(bf16[96,256,128]{2,1,0:T(8,128)(2,1)} %gather_fusion.2), calls=%async_computation.1 | async-start | bytes 12582912 | tf_op jit(solution)/shard_map/all_to_all | solution.py:63
  118.3 92.6 %all_gather.6 = bf16[2048,128]{1,0:T(8,128)(2,1)S(1)} all-gather(bf16[64,128]{1,0:T(8,128)(2,1)S(1)} %copy-done.3), channel_id=1, replica_groups=mesh['particle'=32,'tensor'=8] {'particle'}, dimensions={0}, use_global_device_ids=true | all-gather | bytes 540672 | tf_op jit(solution)/shard_map/all_gather | solution.py:74
  210.9 2.7 bitcast_reduce_fusion
  213.8 3.0 fusion.1
  217.1 0.8 fusion.50
  217.9 24.4 %all_gather.7 = bf16[2048,128]{1,0:T(8,128)(2,1)S(1)} all-gather(bf16[64,128]{1,0:T(8,128)(2,1)S(1)} %copy-done.4), channel_id=1, replica_groups=mesh['particle'=32,'tensor'=8] {'particle'}, dimensions={0}, use_global_device_ids=true | all-gather | bytes 540672 | tf_op jit(solution)/shard_map/all_gather | solution.py:77
  242.6 0.8 fusion.4
  244.8 27.9 %psum.14 = f32[32,2]{1,0:T(8,128)S(1)} all-reduce(f32[32,2]{1,0:T(8,128)S(1)} %get-tuple-element.10), channel_id=1, replica_groups=mesh['particle'=32,'tensor'=8] {'tensor'}, use_global_device_ids=true, to_apply=%region_5.6 | all-reduce | flops 64 | bytes 512 | tf_op jit(solution)/shard_map/psum | solution.py:121
  273.1 62.7 %pmax.7 = f32[8]{0:T(128)S(1)} all-reduce(f32[8]{0:T(128)S(1)} %select_reduce_fusion.2), channel_id=1, replica_groups=mesh['particle'=32,'tensor'=8] {'particle'}, use_global_device_ids=true, to_apply=%region_8.9 | all-reduce | flops 8 | bytes 64 | tf_op jit(solution)/shard_map/pmax | solution.py:127
  335.9 62.7 %psum.15 = f32[8]{0:T(128)S(1)} all-reduce(f32[8]{0:T(128)S(1)} %select_reduce_fusion.1), channel_id=1, replica_groups=mesh['particle'=32,'tensor'=8] {'particle'}, use_global_device_ids=true, to_apply=%region_10.11 | all-reduce | flops 8 | bytes 64 | tf_op jit(solution)/shard_map/psum | solution.py:129
  399.3 0.8 and_select_fusion
  400.3 0.8 compare_select_fusion
  404.2 4.9 %gather_fusion.1 = bf16[32,256,128]{2,1,0:T(8,128)(2,1)} fusion(bf16[96,256,128]{2,1,0:T(8,128)(2,1)} %all-to-all-done, s32[1024]{0:T(1024)S(1)} %pad_clamp_fusion), kind=kCustom, calls=%fused_computation.1 | custom fusion | bytes 4194432 | tf_op jit(solution)/shard_map/gather | solution.py:68
  409.1 4.9 %gather_fusion.3 = bf16[32,256,128]{2,1,0:T(8,128)(2,1)} fusion(bf16[96,256,128]{2,1,0:T(8,128)(2,1)} %all-to-all-done.1, s32[1024]{0:T(1024)S(1)} %pad_clamp_fusion), kind=kCustom, calls=%fused_computation.3 | custom fusion | bytes 4194432 | tf_op jit(solution)/shard_map/gather | solution.py:69
  (59 shorter events, 9.5 us)
Async XLA Ops:
  4.3 23.5 %all-to-all-start.2 = ((s32[32,3,1]{1,2,0:T(1,128)}), s32[32,3,1]{1,2,0:T(1,128)S(1)}, u32[]{:S(2)}, u32[]{:S(2)}) async-start(s32[32,3,1]{1,2,0:T(1,128)} %bitcast.27), calls=%async_computation.2 | async-start | bytes 32768 | tf_op jit(solution)/shard_map/all_to_all | solution.py:64
  27.8 85.4 %all-to-all-start = ((bf16[96,256,128]{2,1,0:T(8,128)(2,1)}), bf16[96,256,128]{2,1,0:T(8,128)(2,1)}, u32[]{:S(2)}, u32[]{:S(2)}) async-start(bf16[96,256,128]{2,1,0:T(8,128)(2,1)} %gather_fusion), calls=%async_computation | async-start | bytes 12582912 | tf_op jit(solution)/shard_map/all_to_all | solution.py:62
  42.8 75.3 %copy-start.2 = (bf16[32,2,1024]{2,1,0:T(2,128)(2,1)S(1)}, bf16[32,2,1024]{2,1,0:T(2,128)(2,1)}, u32[]{:S(2)}) copy-start(bf16[32,2,1024]{2,1,0:T(2,128)(2,1)} %param.12) | copy-start | bytes 393220
  42.8 75.5 %copy-start.3 = (bf16[64,128]{1,0:T(8,128)(2,1)S(1)}, bf16[64,128]{1,0:T(8,128)(2,1)}, u32[]{:S(2)}) copy-start(bf16[64,128]{1,0:T(8,128)(2,1)} %param.17) | copy-start | bytes 49156
  113.2 295.9 %all-to-all-start.1 = ((bf16[96,256,128]{2,1,0:T(8,128)(2,1)}), bf16[96,256,128]{2,1,0:T(8,128)(2,1)}, u32[]{:S(2)}, u32[]{:S(2)}) async-start(bf16[96,256,128]{2,1,0:T(8,128)(2,1)} %gather_fusion.2), calls=%async_computation.1 | async-start | bytes 12582912 | tf_op jit(solution)/shard_map/all_to_all | solution.py:63
  216.8 1.1 copy-start.4
  217.1 25.5 %copy-start = (f32[2048,64,8]{0,1,2:T(8,128)S(1)}, f32[2048,64,8]{0,1,2:T(8,128)}, u32[]{:S(2)}) copy-start(f32[2048,64,8]{0,1,2:T(8,128)} %get-tuple-element.19) | copy-start | bytes 12582916
  242.5 1.6 copy-start.1
  242.6 1.6 copy-start.7
  244.1 28.7 %copy-start.8 = (f32[32]{0:T(128)S(1)}, f32[32]{0:T(128)}, u32[]{:S(2)}) copy-start(f32[32]{0:T(128)} %param.20) | copy-start | bytes 388
  244.1 28.7 %copy-start.5 = (s32[1024]{0:T(1024)S(1)}, s32[1024]{0:T(1024)}, u32[]{:S(2)}) copy-start(s32[1024]{0:T(1024)} %param.22) | copy-start | bytes 12292
  272.9 136.3 %copy-start.6 = (f32[32]{0:T(128)}, f32[32]{0:T(128)S(1)}, u32[]{:S(2)}) copy-start(f32[32]{0:T(128)S(1)} %add.112) | copy-start | bytes 388
where the time goes:
time: 421 us; the launch traced here: 414 us
  blocking collectives  270 us (64%)
  waiting for transfers between devices  70.4 us (17%)
  local copies, waits for them, and re-layouts  31.3 us (7%)
  starting transfers between devices  19.8 us (5%)
  other arithmetic  16.5 us (4%)
  matrix products  5 us (1%)
    all_gather x1, blocking collectives, shards(): lax.all_gather(prompt_keys, 'particle', axis=0, tiled=True)  92.6 us
    all_to_all x1, waiting for transfers between devices, shards(): lax.all_to_all(outgoing[0], 'particle', split_axis=0, concat_axis=0, tile...  70.4 us
    psum x1, blocking collectives, shards(): summed = lax.psum(local_sum, 'particle')  62.7 us
    pmax x1, blocking collectives, shards(): top = lax.pmax(local_peak, 'particle')  62.7 us
    psum x1, blocking collectives, shards(): reward = lax.psum(partial_reward, 'tensor')  27.9 us
    all_gather x1, blocking collectives, shards(): lax.all_gather(prompt_values, 'particle', axis=0, tiled=True)  24.4 us
  transfers between devices with their start and end apart: 3, of which 1 were waited for; matrix products, arithmetic and copies ran while one was open for 10% of the time, Pallas kernels for 0%

commit v1 on v0

v1 whole, which is shorter than its diff:
```python
import functools

import jax
import jax.numpy as jnp
from jax import lax
from jax.experimental import pallas as pl
from jax.experimental.pallas import tpu as pltpu
from jax.sharding import PartitionSpec as P

HEADS = 64
KV_HEADS = 8
HEAD_DIM = 128
STEPS = 2
RUNGS = 8
DISTINCT = 2
SIDES = (4, 4, 2)
WINDOW = 32
MIB = 1 << 20


def pack_kernel(lengths, rows, cache, fresh, written, packed, sems):
    count, suffix, _ = cache.shape
    written[...] = cache[...]

    def patch(p, carry):
        length = lengths[p]
        base = pl.multiple_of(jnp.minimum(length // 16 * 16, suffix - WINDOW), 16)
        block = written[p, pl.ds(base, WINDOW), :].astype(jnp.float32)
        place = lax.broadcasted_iota(jnp.int32, block.shape, 0) + base
        for offset in range(STEPS):
            line = fresh[p, pl.ds(offset, 1), :]
            block = jnp.where(place == length + offset, line, block)
        written[p, pl.ds(base, WINDOW), :] = block.astype(written.dtype)
        return carry

    lax.fori_loop(0, count, patch, 0)

    def copy(k):
        return pltpu.make_async_copy(written.at[rows[k]], packed.at[k], sems.at[k])

    def start(k, carry):
        copy(k).start()
        return carry

    def wait(k, carry):
        copy(k).wait()
        return carry

    lax.fori_loop(0, packed.shape[0], start, 0)
    lax.fori_loop(0, packed.shape[0], wait, 0)


def pack(cache, fresh, lengths, rows):
    slots = rows.shape[0]
    smem = pl.BlockSpec(memory_space=pltpu.SMEM)
    vmem = pl.BlockSpec(memory_space=pltpu.VMEM)
    return pl.pallas_call(
        pack_kernel,
        out_shape=(
            jax.ShapeDtypeStruct(cache.shape, cache.dtype),
            jax.ShapeDtypeStruct((slots,) + cache.shape[1:], cache.dtype),
        ),
        in_specs=[smem, smem, vmem, vmem],
        out_specs=(vmem, pl.BlockSpec(memory_space=pl.ANY)),
        scratch_shapes=[pltpu.SemaphoreType.DMA((slots,))],
        compiler_params=pltpu.CompilerParams(vmem_limit_bytes=24 * MIB),
        name="pack",
    )(lengths, rows, cache, fresh)


def unpack_kernel(slots, arrived, result, sems):
    def copy(p):
        return pltpu.make_async_copy(arrived.at[slots[p]], result.at[p], sems.at[p])

    def start(p, carry):
        copy(p).start()
        return carry

    def wait(p, carry):
        copy(p).wait()
        return carry

    lax.fori_loop(0, result.shape[0], start, 0)
    lax.fori_loop(0, result.shape[0], wait, 0)


def unpack(arrived, slots):
    count = slots.shape[0]
    anywhere = pl.BlockSpec(memory_space=pl.ANY)
    return pl.pallas_call(
        unpack_kernel,
        out_shape=jax.ShapeDtypeStruct((count,) + arrived.shape[1:], arrived.dtype),
        in_specs=[pl.BlockSpec(memory_space=pltpu.SMEM), anywhere],
        out_specs=anywhere,
        scratch_shapes=[pltpu.SemaphoreType.DMA((count,))],
        name="unpack",
    )(slots, arrived)


def around(array):
    sides = SIDES
    total = sides[0] * sides[1] * sides[2]
    places = [
        (i // (sides[1] * sides[2]), i // sides[2] % sides[1], i % sides[2]) for i in range(total)
    ]
    for axis in range(3):
        parts = [array]
        for step in range(1, sides[axis]):
            pairs = []
            for i, place in enumerate(places):
                goal = list(place)
                goal[axis] = (goal[axis] + step) % sides[axis]
                pairs.append((i, (goal[0] * sides[1] + goal[1]) * sides[2] + goal[2]))
            parts.append(lax.ppermute(array, "particle", pairs))
        array = jnp.concatenate(parts, axis=0)
    return array


def shards(
    queries,
    new_keys,
    new_values,
    key_cache,
    value_cache,
    prompt_keys,
    prompt_values,
    lengths,
    prior,
    reward_dir,
    rungs,
    ancestors,
):
    per_device = queries.shape[0]
    suffix = key_cache.shape[1]
    groups = HEADS // KV_HEADS
    scale = HEAD_DIM ** (-0.5)
    sources = lax.axis_size("particle")
    device = lax.axis_index("particle")

    prompt = around(jnp.stack([prompt_keys, prompt_values], axis=1))
    all_keys = prompt[:, 0]
    all_values = prompt[:, 1]

    wanted = ancestors.reshape(sources, per_device)
    owner = wanted // per_device
    local = wanted % per_device
    chosen = owner == device
    least = jnp.min(jnp.where(chosen, local, per_device - 1), axis=1)
    most = jnp.max(jnp.where(chosen, local, 0), axis=1)
    send_rows = jnp.stack([least, most], axis=1).reshape(-1)
    mine = lax.dynamic_slice_in_dim(ancestors, device * per_device, per_device)
    mine_owner = mine // per_device
    same_owner = mine_owner[:, None] == mine_owner[None, :]
    first = jnp.min(jnp.where(same_owner, mine[None, :], sources * per_device), axis=1)
    slot = mine_owner * DISTINCT + (mine != first).astype(jnp.int32)

    written_keys, outgoing_keys = pack(key_cache, new_keys.astype(jnp.float32), lengths, send_rows)
    arrived_keys = lax.all_to_all(
        outgoing_keys, "particle", split_axis=0, concat_axis=0, tiled=True
    )
    written_values, outgoing_values = pack(
        value_cache, new_values.astype(jnp.float32), lengths, send_rows
    )
    arrived_values = lax.all_to_all(
        outgoing_values, "particle", split_axis=0, concat_axis=0, tiled=True
    )
    next_keys = unpack(arrived_keys, slot)
    next_values = unpack(arrived_values, slot)

    query = queries.reshape(per_device, STEPS, groups, HEAD_DIM)
    front = (
        jnp.einsum("pshd,nd->pshn", query, all_keys, preferred_element_type=jnp.float32) * scale
    )
    back = (
        jnp.einsum("pshd,pld->pshl", query, written_keys, preferred_element_type=jnp.float32)
        * scale
    )
    position = jnp.arange(suffix, dtype=jnp.int32)
    later = jnp.arange(STEPS, dtype=jnp.int32)
    visible = position[None, None, :] < lengths[:, None, None] + 1 + later[None, :, None]
    back = jnp.where(visible[:, :, None, :], back, -jnp.inf)
    peak = jnp.maximum(jnp.max(front, axis=-1), jnp.max(back, axis=-1))
    front = jnp.exp(front - peak[..., None])
    back = jnp.exp(back - peak[..., None])
    total = jnp.sum(front, axis=-1) + jnp.sum(back, axis=-1)
    mixed = jnp.einsum(
        "pshn,nd->pshd",
        front.astype(jnp.bfloat16),
        all_values,
        preferred_element_type=jnp.float32,
    ) + jnp.einsum(
        "pshl,pld->pshd",
        back.astype(jnp.bfloat16),
        written_values,
        preferred_element_type=jnp.float32,
    )
    output = (mixed / total[..., None]).reshape(per_device, STEPS, -1)
    attention = output.astype(jnp.bfloat16)

    partial_reward = jnp.sum(output * reward_dir[None, None, :], axis=(1, 2))
    weights = prior + lax.psum(partial_reward, "tensor")
    own_rungs = lax.dynamic_slice_in_dim(rungs, device * per_device, per_device)
    ladder = jnp.arange(RUNGS, dtype=jnp.int32)
    member = own_rungs[:, None] == ladder[None, :]
    local_peak = jnp.max(jnp.where(member, weights[:, None], -1e30), axis=0)
    local_sum = jnp.sum(
        jnp.where(member, jnp.exp(weights[:, None] - local_peak[None, :]), 0.0), axis=0
    )
    shared = around(
        jnp.concatenate([local_peak, local_sum, lengths.astype(jnp.float32)])[None, :]
    )
    peaks = shared[:, :RUNGS]
    top = jnp.max(peaks, axis=0)
    summed = jnp.sum(shared[:, RUNGS : 2 * RUNGS] * jnp.exp(peaks - top[None, :]), axis=0)
    counted = jnp.sum((rungs[:, None] == ladder[None, :]).astype(jnp.float32), axis=0)
    rung_means = top + jnp.log(summed) - jnp.log(counted)

    _, wide, cores = SIDES
    tall = SIDES[0]
    up = (device // (wide * cores) - mine_owner // (wide * cores)) % tall
    along = (device // cores % wide - mine_owner // cores % wide) % wide
    across = (device % cores - mine_owner % cores) % cores
    step = (across * wide + along) * tall + up
    wanted_length = step * per_device + mine % per_device
    everywhere = shared[:, 2 * RUNGS :].reshape(-1)
    order = jnp.arange(sources * per_device, dtype=jnp.int32)
    found = jnp.sum(
        jnp.where(wanted_length[:, None] == order[None, :], everywhere[None, :], 0.0), axis=1
    )
    next_lengths = found.astype(jnp.int32) + STEPS
    return (attention, weights, rung_means, next_keys, next_values, next_lengths)


def solution(mesh):
    placed = (
        P("particle", None, "tensor"),
        P("particle", None, "tensor"),
        P("particle", None, "tensor"),
        P("particle", None, "tensor"),
        P("particle", None, "tensor"),
        P("particle", "tensor"),
        P("particle", "tensor"),
        P("particle"),
        P("particle"),
        P("tensor"),
        P(),
        P(),
    )
    return jax.shard_map(
        shards,
        mesh=mesh,
        in_specs=placed,
        out_specs=(
            P("particle", None, "tensor"),
            P("particle"),
            P(),
            P("particle", None, "tensor"),
            P("particle", None, "tensor"),
            P("particle"),
        ),
        check_vma=False,
    )
```

time: 421 us -> 284 us (0.67); the launches traced: 414 us -> 282 us
  blocking collectives: 270 us -> 15.2 us
  Pallas kernels: 0 us -> 147 us
  waiting for transfers between devices: 70.4 us -> 45.1 us
  starting transfers between devices: 19.8 us -> 40 us
  local copies, waits for them, and re-layouts: 31.3 us -> 17.1 us
  other arithmetic: 16.5 us -> 9.95 us
    pallas_call x0 -> x4, Pallas kernels: none -> 147 us  [the longest x2 131 us: unpack(): pl.pallas_call(unpack_kernel, out_shape=jax.ShapeDtypeStruct((count,) + a...]
    all_gather x2 -> x0, blocking collectives: 117 us -> none  [the longest x1 92.6 us: shards(): lax.all_gather(prompt_keys, 'particle', axis=0, tiled=True)]
    psum x2 -> x1, blocking collectives: 90.6 us -> 15.2 us  [shards(): weights = prior + lax.psum(partial_reward, 'tensor')]
    all_to_all x3 -> x2, waiting for transfers between devices: 70.4 us -> 0.01 us  [the longest x1 0.01 us: shards(): lax.all_to_all(outgoing_keys, 'particle', split_axis=0, concat_axis=0, ti...]
    pmax x1 -> x0, blocking collectives: 62.7 us -> none  [shards(): top = lax.pmax(local_peak, 'particle')]
    ppermute x0 -> x14, waiting for transfers between devices: none -> 45 us  [around(): parts.append(lax.ppermute(array, 'particle', pairs))]
    ppermute x0 -> x14, starting transfers between devices: none -> 27.4 us  [around(): parts.append(lax.ppermute(array, 'particle', pairs))]
    gather x6 -> x0, local copies, waits for them, and re-layouts: 25.4 us -> none  [the longest x1 7.47 us: shards(): written_values[send_rows]]
  transfers between devices with their start and end apart: 3 -> 16, of which waited for: 1 -> 7; matrix products, arithmetic and copies ran while one was open for 10% -> 8% of each run, Pallas kernels for 0% -> 26%
where the time goes in v1:
time: 284 us; the launch traced here: 282 us
  Pallas kernels  147 us (52%)
  waiting for transfers between devices  45.1 us (16%)
  starting transfers between devices  40 us (14%)
  local copies, waits for them, and re-layouts  17.1 us (6%)
  blocking collectives  15.2 us (5%)
  other arithmetic  9.95 us (4%)
  matrix products  6.08 us (2%)
    pallas_call x2, Pallas kernels, unpack(): pl.pallas_call(unpack_kernel, out_shape=jax.ShapeDtypeStruct((count,) + a...  131 us
    ppermute x14, waiting for transfers between devices, around(): parts.append(lax.ppermute(array, 'particle', pairs))  45 us
    ppermute x14, starting transfers between devices, around(): parts.append(lax.ppermute(array, 'particle', pairs))  27.4 us
    pallas_call x2, Pallas kernels, pack(): pl.pallas_call(pack_kernel, out_shape=(jax.ShapeDtypeStruct(cache.shape,...  16.3 us
    psum x1, blocking collectives, shards(): weights = prior + lax.psum(partial_reward, 'tensor')  15.2 us
    unnamed x47, local copies, waits for them, and re-layouts  13.9 us
    all_to_all x1, starting transfers between devices, shards(): lax.all_to_all(outgoing_keys, 'particle', split_axis=0, concat_axis=0, ti...  7.59 us
  transfers between devices with their start and end apart: 16, of which 7 were waited for; matrix products, arithmetic and copies ran while one was open for 8% of the time, Pallas kernels for 26%

profile of v1, /device:TPU:128, one launch (start us, length us, event | category | flops | bytes accessed | tf_op | source)
XLA Modules:
  0.0 281.9 jit_solution(9073492667536254194)
XLA Ops:
  2.5 1.6 copy-done.2
  4.7 8.2 %pack.2 = (bf16[32,256,128]{2,1,0:T(8,128)(2,1)S(1)}, bf16[64,256,128]{2,1,0:T(8,128)(2,1)S(1)}) custom-call(s32[32]{0:T(128)S(1)} %copy-done.6, s32[64]{0:T(128)S(1)} %reshape.77.rows, bf16[32,256,128]{2,1,0:T(8,128)(2,1)S(1)} %copy-done.2, f32[32,2,128]{2,1,0:T(2,128)S(1)} %convert_element_type.30.fresh), custom_call_target="tpu_custom_call" | custom-call | tf_op jit(solution)/shard_map/pack/pallas_call | solution.py:57
  12.9 1.9 copy-done.1
  16.2 7.6 %all-to-all-start = ((bf16[64,256,128]{2,1,0:T(8,128)(2,1)}), bf16[64,256,128]{2,1,0:T(8,128)(2,1)}, u32[]{:S(2)}, u32[]{:S(2)}) async-start(bf16[64,256,128]{2,1,0:T(8,128)(2,1)} %copy-done.1), calls=%async_computation | async-start | bytes 8388608 | tf_op jit(solution)/shard_map/all_to_all | solution.py:158
  24.5 1.7 collective-permute-start
  26.2 2.7 collective-permute-start.1
  28.9 1.4 collective-permute-start.2
  31.2 8.2 %pack.3 = (bf16[32,256,128]{2,1,0:T(8,128)(2,1)S(1)}, bf16[64,256,128]{2,1,0:T(8,128)(2,1)S(1)}) custom-call(s32[32]{0:T(128)S(1)} %copy-done.7, s32[64]{0:T(128)S(1)} %reshape.77.rows, bf16[32,256,128]{2,1,0:T(8,128)(2,1)S(1)} %copy-done.3, f32[32,2,128]{2,1,0:T(2,128)S(1)} %convert_element_type.33.fresh), custom_call_target="tpu_custom_call" | custom-call | tf_op jit(solution)/shard_map/pack/pallas_call | solution.py:57
  39.4 2.0 copy-done
  42.7 30.0 %collective-permute-done = bf16[64,2,128]{2,0,1:T(8,128)(2,1)S(1)} collective-permute-done((bf16[64,2,128]{2,0,1:T(8,128)(2,1)}, bf16[64,2,128]{2,0,1:T(8,128)(2,1)S(1)}, u32[]{:S(2)}, u32[]{:S(2)}) %collective-permute-start) | collective-permute-done | bytes 32800 | tf_op jit(solution)/shard_map/ppermute | solution.py:114
  74.2 4.4 %collective-permute-start.4 = (bf16[256,2,128]{2,0,1:T(8,128)(2,1)S(1)}, bf16[256,2,128]{2,0,1:T(8,128)(2,1)S(1)}, u32[]{:S(2)}, u32[]{:S(2)}) collective-permute-start(bf16[256,2,128]{2,0,1:T(8,128)(2,1)S(1)} %pad_maximum_fusion), channel_id=1, source_target_pairs={{0,32},{8,40},{16,48},{24,56},{32,0},{40,8},{48,16},{56,24},{64,96... | collective-permute-start | bytes 393224 | tf_op jit(solution)/shard_map/ppermute | solution.py:114
  78.6 2.2 collective-permute-start.5
  86.4 5.0 %all-to-all-start.1 = ((bf16[64,256,128]{2,1,0:T(8,128)(2,1)}), bf16[64,256,128]{2,1,0:T(8,128)(2,1)}, u32[]{:S(2)}, u32[]{:S(2)}) async-start(bf16[64,256,128]{2,1,0:T(8,128)(2,1)} %copy-done), calls=%async_computation.1 | async-start | bytes 8388608 | tf_op jit(solution)/shard_map/all_to_all | solution.py:164
  95.2 3.8 %bitcast_reduce_fusion = (f32[32,2,8]{0,2,1:T(8,128)S(1)}, f32[2048,32,2,8]{0,1,3,2:T(8,128)}) fusion(bf16[32,2,8,128]{3,2,1,0:T(8,128)(2,1)S(1)} %reshape.75, bf16[2048,2,128]{2,0,1:T(8,128)(2,1)} %constant_dynamic-update-slice_fusion.7), kind=kOutput, calls=%fused_computation.1 | convolution fusion | flops 270532096 | bytes 4851712 | tf_op jit(solution)/shard_map/pshd,nd->pshn/dot_general | solution.py:172
  99.4 3.2 %fusion.1 = f32[32,2,8]{0,2,1:T(8,128)S(1)} fusion(f32[2048,32,2,8]{0,1,3,2:T(8,128)} %get-tuple-element.57, f32[32,2,8]{0,2,1:T(8,128)S(1)} %max.7), kind=kLoop, calls=%fused_computation.3 | loop fusion | flops 3145216 | bytes 4198400 | tf_op jit(solution)/shard_map/reduce_sum | solution.py:185
  104.3 15.2 %psum.7 = f32[32]{0:T(128)S(1)} all-reduce(f32[32]{0:T(128)S(1)} %get-tuple-element.37), channel_id=1, replica_groups=mesh['particle'=32,'tensor'=8] {'tensor'}, use_global_device_ids=true, to_apply=%region_7.8 | all-reduce | flops 32 | bytes 256 | tf_op jit(solution)/shard_map/psum | solution.py:201
  119.8 1.7 collective-permute-start.7
  121.5 2.8 collective-permute-start.8
  125.9 8.6 %collective-permute-done.7 = f32[1,48]{1,0:T(1,128)S(1)} collective-permute-done((f32[1,48]{1,0:T(1,128)S(1)}, f32[1,48]{1,0:T(1,128)S(1)}, u32[]{:S(2)}, u32[]{:S(2)}) %collective-permute-start.7) | collective-permute-done | bytes 224 | tf_op jit(solution)/shard_map/ppermute | solution.py:114
  134.5 3.8 %collective-permute-done.8 = f32[1,48]{1,0:T(1,128)S(1)} collective-permute-done((f32[1,48]{1,0:T(1,128)S(1)}, f32[1,48]{1,0:T(1,128)S(1)}, u32[]{:S(2)}, u32[]{:S(2)}) %collective-permute-start.8) | collective-permute-done | bytes 224 | tf_op jit(solution)/shard_map/ppermute | solution.py:114
  139.6 4.3 %collective-permute-start.11 = (f32[4,48]{1,0:T(4,128)S(1)}, f32[4,48]{1,0:T(4,128)S(1)}, u32[]{:S(2)}, u32[]{:S(2)}) collective-permute-start(f32[4,48]{1,0:T(4,128)S(1)} %pad_maximum_fusion.2), channel_id=1, source_target_pairs={{0,32},{8,40},{16,48},{24,56},{32,0},{40,8},{48,16},{56,24},{64,96... | collective-permute-start | bytes 2312 | tf_op jit(solution)/shard_map/ppermute | solution.py:114
  143.9 2.5 collective-permute-start.12
  150.6 65.6 %unpack.2 = bf16[32,256,128]{2,1,0:T(8,128)(2,1)} custom-call(s32[32]{0:T(128)} %fusion.39.slots, bf16[64,256,128]{2,1,0:T(8,128)(2,1)} %all-to-all-done.arrived), custom_call_target="tpu_custom_call" | custom-call | tf_op jit(solution)/shard_map/unpack/pallas_call | solution.py:90
  216.2 65.6 %unpack.3 = bf16[32,256,128]{2,1,0:T(8,128)(2,1)} custom-call(s32[32]{0:T(128)} %fusion.39.slots, bf16[64,256,128]{2,1,0:T(8,128)(2,1)} %all-to-all-done.1.arrived), custom_call_target="tpu_custom_call" | custom-call | tf_op jit(solution)/shard_map/unpack/pallas_call | solution.py:90
  (105 shorter events, 26.9 us)
Async XLA Ops:
  16.2 7.6 %copy-start.14 = (bf16[64,128]{1,0:T(8,128)(2,1)S(1)}, bf16[64,128]{1,0:T(8,128)(2,1)}, u32[]{:S(2)}) copy-start(bf16[64,128]{1,0:T(8,128)(2,1)} %param.18) | copy-start | bytes 49156
  16.2 7.6 %copy-start.15 = (bf16[64,128]{1,0:T(8,128)(2,1)S(1)}, bf16[64,128]{1,0:T(8,128)(2,1)}, u32[]{:S(2)}) copy-start(bf16[64,128]{1,0:T(8,128)(2,1)} %param.17) | copy-start | bytes 49156
  16.2 14.1 %copy-start.7 = (s32[32]{0:T(128)S(1)}, s32[32]{0:T(128)}, u32[]{:S(2)}) copy-start(s32[32]{0:T(128)} %lengths.3) | copy-start | bytes 388
  16.2 14.2 %copy-start.13 = (bf16[32,2,1024]{2,1,0:T(2,128)(2,1)S(1)}, bf16[32,2,1024]{2,1,0:T(2,128)(2,1)}, u32[]{:S(2)}) copy-start(bf16[32,2,1024]{2,1,0:T(2,128)(2,1)} %param.12) | copy-start | bytes 393220
  16.2 15.0 %copy-start.3 = (bf16[32,256,128]{2,1,0:T(8,128)(2,1)S(1)}, bf16[32,256,128]{2,1,0:T(8,128)(2,1)}, u32[]{:S(2)}) copy-start(bf16[32,256,128]{2,1,0:T(8,128)(2,1)} %cache.3) | copy-start | bytes 6291460
  16.2 69.2 %all-to-all-start = ((bf16[64,256,128]{2,1,0:T(8,128)(2,1)}), bf16[64,256,128]{2,1,0:T(8,128)(2,1)}, u32[]{:S(2)}, u32[]{:S(2)}) async-start(bf16[64,256,128]{2,1,0:T(8,128)(2,1)} %copy-done.1), calls=%async_computation | async-start | bytes 8388608 | tf_op jit(solution)/shard_map/all_to_all | solution.py:158
  24.5 48.3 %collective-permute-start = (bf16[64,2,128]{2,0,1:T(8,128)(2,1)}, bf16[64,2,128]{2,0,1:T(8,128)(2,1)S(1)}, u32[]{:S(2)}, u32[]{:S(2)}) collective-permute-start(bf16[64,2,128]{2,0,1:T(8,128)(2,1)} %get-tuple-element.53), channel_id=1, source_target_pairs={{0,64},{8,72},{16,80},{24,88},{32,96},{40,104},{48,112},{56,120},{... | collective-permute-start | bytes 98312 | tf_op jit(solution)/shard_map/ppermute | solution.py:114
  26.2 46.6 %collective-permute-start.1 = (bf16[64,2,128]{2,0,1:T(8,128)(2,1)}, bf16[64,2,128]{2,0,1:T(8,128)(2,1)S(1)}, u32[]{:S(2)}, u32[]{:S(2)}) collective-permute-start(bf16[64,2,128]{2,0,1:T(8,128)(2,1)} %get-tuple-element.53), channel_id=1, source_target_pairs={{0,128},{8,136},{16,144},{24,152},{32,160},{40,168},{48,176},{56,1... | collective-permute-start | bytes 98312 | tf_op jit(solution)/shard_map/ppermute | solution.py:114
  28.9 43.9 %collective-permute-start.2 = (bf16[64,2,128]{2,0,1:T(8,128)(2,1)}, bf16[64,2,128]{2,0,1:T(8,128)(2,1)S(1)}, u32[]{:S(2)}, u32[]{:S(2)}) collective-permute-start(bf16[64,2,128]{2,0,1:T(8,128)(2,1)} %get-tuple-element.53), channel_id=1, source_target_pairs={{0,192},{8,200},{16,208},{24,216},{32,224},{40,232},{48,240},{56,2... | collective-permute-start | bytes 98312 | tf_op jit(solution)/shard_map/ppermute | solution.py:114
  73.5 9.2 %collective-permute-start.3 = (bf16[256,2,128]{2,0,1:T(8,128)(2,1)S(1)}, bf16[256,2,128]{2,0,1:T(8,128)(2,1)S(1)}, u32[]{:S(2)}, u32[]{:S(2)}) collective-permute-start(bf16[256,2,128]{2,0,1:T(8,128)(2,1)S(1)} %pad_maximum_fusion), channel_id=1, source_target_pairs={{0,16},{8,24},{16,32},{24,40},{32,48},{40,56},{48,0},{56,8},{64,80... | collective-permute-start | bytes 393224 | tf_op jit(solution)/shard_map/ppermute | solution.py:114
  74.2 10.5 %collective-permute-start.4 = (bf16[256,2,128]{2,0,1:T(8,128)(2,1)S(1)}, bf16[256,2,128]{2,0,1:T(8,128)(2,1)S(1)}, u32[]{:S(2)}, u32[]{:S(2)}) collective-permute-start(bf16[256,2,128]{2,0,1:T(8,128)(2,1)S(1)} %pad_maximum_fusion), channel_id=1, source_target_pairs={{0,32},{8,40},{16,48},{24,56},{32,0},{40,8},{48,16},{56,24},{64,96... | collective-permute-start | bytes 393224 | tf_op jit(solution)/shard_map/ppermute | solution.py:114
  78.6 12.8 %collective-permute-start.5 = (bf16[256,2,128]{2,0,1:T(8,128)(2,1)S(1)}, bf16[256,2,128]{2,0,1:T(8,128)(2,1)S(1)}, u32[]{:S(2)}, u32[]{:S(2)}) collective-permute-start(bf16[256,2,128]{2,0,1:T(8,128)(2,1)S(1)} %pad_maximum_fusion), channel_id=1, source_target_pairs={{0,48},{8,56},{16,0},{24,8},{32,16},{40,24},{48,32},{56,40},{64,11... | collective-permute-start | bytes 393224 | tf_op jit(solution)/shard_map/ppermute | solution.py:114
  86.4 129.8 %all-to-all-start.1 = ((bf16[64,256,128]{2,1,0:T(8,128)(2,1)}), bf16[64,256,128]{2,1,0:T(8,128)(2,1)}, u32[]{:S(2)}, u32[]{:S(2)}) async-start(bf16[64,256,128]{2,1,0:T(8,128)(2,1)} %copy-done), calls=%async_computation.1 | async-start | bytes 8388608 | tf_op jit(solution)/shard_map/all_to_all | solution.py:164
  92.2 2.1 collective-permute-start.6
  95.2 7.5 %copy-start.9 = (bf16[32,256,128]{2,1,0:T(8,128)(2,1)S(1)}, bf16[32,256,128]{2,1,0:T(8,128)(2,1)}, u32[]{:S(2)}) copy-start(bf16[32,256,128]{2,1,0:T(8,128)(2,1)} %copy-done.8) | copy-start | bytes 6291460
  102.6 16.8 %copy-start.19 = (f32[32]{0:T(128)S(1)}, f32[32]{0:T(128)}, u32[]{:S(2)}) copy-start(f32[32]{0:T(128)} %param.20) | copy-start | bytes 388
  119.4 162.3 %copy-start.17 = (f32[32]{0:T(128)}, f32[32]{0:T(128)S(1)}, u32[]{:S(2)}) copy-start(f32[32]{0:T(128)S(1)} %add.115) | copy-start | bytes 388
  119.8 14.6 %collective-permute-start.7 = (f32[1,48]{1,0:T(1,128)S(1)}, f32[1,48]{1,0:T(1,128)S(1)}, u32[]{:S(2)}, u32[]{:S(2)}) collective-permute-start(f32[1,48]{1,0:T(1,128)S(1)} %maximum_bitcast_fusion), channel_id=1, source_target_pairs={{0,64},{8,72},{16,80},{24,88},{32,96},{40,104},{48,112},{56,120},{... | collective-permute-start | bytes 584 | tf_op jit(solution)/shard_map/ppermute | solution.py:114
  121.5 16.7 %collective-permute-start.8 = (f32[1,48]{1,0:T(1,128)S(1)}, f32[1,48]{1,0:T(1,128)S(1)}, u32[]{:S(2)}, u32[]{:S(2)}) collective-permute-start(f32[1,48]{1,0:T(1,128)S(1)} %maximum_bitcast_fusion), channel_id=1, source_target_pairs={{0,128},{8,136},{16,144},{24,152},{32,160},{40,168},{48,176},{56,1... | collective-permute-start | bytes 584 | tf_op jit(solution)/shard_map/ppermute | solution.py:114
  124.3 13.9 %collective-permute-start.9 = (f32[1,48]{1,0:T(1,128)S(1)}, f32[1,48]{1,0:T(1,128)S(1)}, u32[]{:S(2)}, u32[]{:S(2)}) collective-permute-start(f32[1,48]{1,0:T(1,128)S(1)} %maximum_bitcast_fusion), channel_id=1, source_target_pairs={{0,192},{8,200},{16,208},{24,216},{32,224},{40,232},{48,240},{56,2... | collective-permute-start | bytes 584 | tf_op jit(solution)/shard_map/ppermute | solution.py:114
  138.2 8.7 %collective-permute-start.10 = (f32[4,48]{1,0:T(4,128)S(1)}, f32[4,48]{1,0:T(4,128)S(1)}, u32[]{:S(2)}, u32[]{:S(2)}) collective-permute-start(f32[4,48]{1,0:T(4,128)S(1)} %pad_maximum_fusion.2), channel_id=1, source_target_pairs={{0,16},{8,24},{16,32},{24,40},{32,48},{40,56},{48,0},{56,8},{64,80... | collective-permute-start | bytes 2312 | tf_op jit(solution)/shard_map/ppermute | solution.py:114
  139.6 7.3 %collective-permute-start.11 = (f32[4,48]{1,0:T(4,128)S(1)}, f32[4,48]{1,0:T(4,128)S(1)}, u32[]{:S(2)}, u32[]{:S(2)}) collective-permute-start(f32[4,48]{1,0:T(4,128)S(1)} %pad_maximum_fusion.2), channel_id=1, source_target_pairs={{0,32},{8,40},{16,48},{24,56},{32,0},{40,8},{48,16},{56,24},{64,96... | collective-permute-start | bytes 2312 | tf_op jit(solution)/shard_map/ppermute | solution.py:114
  143.9 3.8 %collective-permute-start.12 = (f32[4,48]{1,0:T(4,128)S(1)}, f32[4,48]{1,0:T(4,128)S(1)}, u32[]{:S(2)}, u32[]{:S(2)}) collective-permute-start(f32[4,48]{1,0:T(4,128)S(1)} %pad_maximum_fusion.2), channel_id=1, source_target_pairs={{0,48},{8,56},{16,0},{24,8},{32,16},{40,24},{48,32},{56,40},{64,11... | collective-permute-start | bytes 2312 | tf_op jit(solution)/shard_map/ppermute | solution.py:114
  147.8 1.2 collective-permute-start.13
  (12 other events, 34.1 us)

commit v2 on v1

v2 whole, which is shorter than its diff:
```python
import jax
import jax.numpy as jnp
from jax import lax
from jax.experimental import pallas as pl
from jax.experimental.pallas import tpu as pltpu
from jax.sharding import PartitionSpec as P

HEADS = 64
KV_HEADS = 8
HEAD_DIM = 128
STEPS = 2
RUNGS = 8
DISTINCT = 2
SIDES = (4, 4, 2)
WINDOW = 32


def repeat(count, body):
    def step(i, carry):
        body(i)
        return carry

    lax.fori_loop(0, count, step, 0, unroll=4)


def pack_kernel(
    lengths, least, most, cache, fresh, written, packed, held, in_sems, out_sems, low_sems, high_sems
):
    count, suffix, _ = cache.shape
    goals = least.shape[0]

    def load(p):
        return pltpu.make_async_copy(cache.at[p], held.at[p], in_sems.at[p])

    def keep(p):
        return pltpu.make_async_copy(held.at[p], written.at[p], out_sems.at[p])

    def low(d):
        return pltpu.make_async_copy(held.at[least[d]], packed.at[2 * d], low_sems.at[d])

    def high(d):
        return pltpu.make_async_copy(held.at[most[d]], packed.at[2 * d + 1], high_sems.at[d])

    def patch(p):
        load(p).wait()
        length = lengths[p]
        base = pl.multiple_of(jnp.minimum(length // 16 * 16, suffix - WINDOW), 16)
        block = held[p, pl.ds(base, WINDOW), :].astype(jnp.float32)
        lines = fresh[p].astype(jnp.float32)
        place = lax.broadcasted_iota(jnp.int32, block.shape, 0) + base
        for offset in range(STEPS):
            block = jnp.where(place == length + offset, lines[offset : offset + 1], block)
        held[p, pl.ds(base, WINDOW), :] = block.astype(held.dtype)

    repeat(count, lambda p: load(p).start())
    repeat(count, patch)
    repeat(goals, lambda d: low(d).start())
    repeat(goals, lambda d: high(d).start())
    repeat(count, lambda p: keep(p).start())
    repeat(goals, lambda d: low(d).wait())
    repeat(goals, lambda d: high(d).wait())
    repeat(count, lambda p: keep(p).wait())


def pack(cache, fresh, lengths, least, most):
    count, goals = cache.shape[0], least.shape[0]
    smem = pl.BlockSpec(memory_space=pltpu.SMEM)
    hbm = pl.BlockSpec(memory_space=pltpu.HBM)
    return pl.pallas_call(
        pack_kernel,
        out_shape=(
            jax.ShapeDtypeStruct(cache.shape, cache.dtype),
            jax.ShapeDtypeStruct((goals * DISTINCT,) + cache.shape[1:], cache.dtype),
        ),
        in_specs=[smem, smem, smem, hbm, pl.BlockSpec(memory_space=pltpu.VMEM)],
        out_specs=(hbm, hbm),
        scratch_shapes=[
            pltpu.VMEM(cache.shape, cache.dtype),
            pltpu.SemaphoreType.DMA((count,)),
            pltpu.SemaphoreType.DMA((count,)),
            pltpu.SemaphoreType.DMA((goals,)),
            pltpu.SemaphoreType.DMA((goals,)),
        ],
        name="pack",
    )(lengths, least, most, cache, fresh)


def after(array, *others):
    anywhere = pl.BlockSpec(memory_space=pl.ANY)
    return pl.pallas_call(
        lambda *refs: None,
        out_shape=jax.ShapeDtypeStruct(array.shape, array.dtype),
        in_specs=[anywhere] * (1 + len(others)),
        out_specs=anywhere,
        input_output_aliases={0: 0},
        name="after",
    )(array, *others)


def unpack_kernel(slots, arrived, _, result, held, in_sems, out_sems):
    count = result.shape[0]

    def load(p):
        return pltpu.make_async_copy(arrived.at[slots[p]], held.at[p], in_sems.at[p])

    def keep(p):
        return pltpu.make_async_copy(held.at[p], result.at[p], out_sems.at[p])

    def forward(p):
        load(p).wait()
        keep(p).start()

    repeat(count, lambda p: load(p).start())
    repeat(count, forward)
    repeat(count, lambda p: keep(p).wait())


def unpack(arrived, slots, other):
    count = slots.shape[0]
    hbm = pl.BlockSpec(memory_space=pltpu.HBM)
    shape = (count,) + arrived.shape[1:]
    return pl.pallas_call(
        unpack_kernel,
        out_shape=jax.ShapeDtypeStruct(shape, arrived.dtype),
        in_specs=[pl.BlockSpec(memory_space=pltpu.SMEM), hbm, pl.BlockSpec(memory_space=pl.ANY)],
        out_specs=hbm,
        scratch_shapes=[
            pltpu.VMEM(shape, arrived.dtype),
            pltpu.SemaphoreType.DMA((count,)),
            pltpu.SemaphoreType.DMA((count,)),
        ],
        name="unpack",
    )(slots, arrived, other)


def along(array, axis):
    sides = SIDES
    total = sides[0] * sides[1] * sides[2]
    parts = [array]
    for step in range(1, sides[axis]):
        pairs = []
        for i in range(total):
            goal = [i // (sides[1] * sides[2]), i // sides[2] % sides[1], i % sides[2]]
            goal[axis] = (goal[axis] + step) % sides[axis]
            pairs.append((i, (goal[0] * sides[1] + goal[1]) * sides[2] + goal[2]))
        parts.append(lax.ppermute(array, "particle", pairs))
    return jnp.concatenate(parts, axis=0)


def shards(
    queries,
    new_keys,
    new_values,
    key_cache,
    value_cache,
    prompt_keys,
    prompt_values,
    lengths,
    prior,
    reward_dir,
    rungs,
    ancestors,
):
    per_device = queries.shape[0]
    suffix = key_cache.shape[1]
    groups = HEADS // KV_HEADS
    scale = HEAD_DIM ** (-0.5)
    sources = lax.axis_size("particle")
    device = lax.axis_index("particle")

    plane = along(along(jnp.concatenate([prompt_keys, prompt_values], axis=1), 0), 1)
    prompt = along(plane, 2)
    all_keys = prompt[:, :HEAD_DIM]
    all_values = prompt[:, HEAD_DIM:]

    wanted = ancestors.reshape(sources, per_device)
    owner = wanted // per_device
    local = wanted % per_device
    chosen = owner == device
    least = jnp.min(jnp.where(chosen, local, per_device - 1), axis=1)
    most = jnp.max(jnp.where(chosen, local, 0), axis=1)
    mine = lax.dynamic_slice_in_dim(ancestors, device * per_device, per_device)
    mine_owner = mine // per_device
    same_owner = mine_owner[:, None] == mine_owner[None, :]
    first = jnp.min(jnp.where(same_owner, mine[None, :], sources * per_device), axis=1)
    slot = mine_owner * DISTINCT + (mine != first).astype(jnp.int32)

    written_keys, outgoing_keys = pack(key_cache, new_keys, lengths, least, most)
    arrived_keys = lax.all_to_all(
        after(outgoing_keys, plane), "particle", split_axis=0, concat_axis=0, tiled=True
    )
    written_values, outgoing_values = pack(value_cache, new_values, lengths, least, most)

    query = queries.reshape(per_device, STEPS, groups, HEAD_DIM)
    front = (
        jnp.einsum("pshd,nd->pshn", query, all_keys, preferred_element_type=jnp.float32) * scale
    )
    back = (
        jnp.einsum("pshd,pld->pshl", query, written_keys, preferred_element_type=jnp.float32)
        * scale
    )
    position = jnp.arange(suffix, dtype=jnp.int32)
    later = jnp.arange(STEPS, dtype=jnp.int32)
    visible = position[None, None, :] < lengths[:, None, None] + 1 + later[None, :, None]
    back = jnp.where(visible[:, :, None, :], back, -jnp.inf)
    peak = jnp.maximum(jnp.max(front, axis=-1), jnp.max(back, axis=-1))
    front = jnp.exp(front - peak[..., None])
    back = jnp.exp(back - peak[..., None])
    total = jnp.sum(front, axis=-1) + jnp.sum(back, axis=-1)
    mixed = jnp.einsum(
        "pshn,nd->pshd",
        front.astype(jnp.bfloat16),
        all_values,
        preferred_element_type=jnp.float32,
    ) + jnp.einsum(
        "pshl,pld->pshd",
        back.astype(jnp.bfloat16),
        written_values,
        preferred_element_type=jnp.float32,
    )
    output = (mixed / total[..., None]).reshape(per_device, STEPS, -1)
    attention = output.astype(jnp.bfloat16)

    partial_reward = jnp.sum(output * reward_dir[None, None, :], axis=(1, 2))
    weights = prior + lax.psum(partial_reward, "tensor")
    own_rungs = lax.dynamic_slice_in_dim(rungs, device * per_device, per_device)
    ladder = jnp.arange(RUNGS, dtype=jnp.int32)
    member = own_rungs[:, None] == ladder[None, :]
    local_peak = jnp.max(jnp.where(member, weights[:, None], -1e30), axis=0)
    local_sum = jnp.sum(
        jnp.where(member, jnp.exp(weights[:, None] - local_peak[None, :]), 0.0), axis=0
    )
    shared = jnp.concatenate([local_peak, local_sum, lengths.astype(jnp.float32)])[None, :]
    near = along(along(shared, 2), 0)
    arrived_values = lax.all_to_all(
        after(outgoing_values, near), "particle", split_axis=0, concat_axis=0, tiled=True
    )
    next_keys = unpack(arrived_keys, slot, near)
    shared = along(after(near, next_keys), 1)
    peaks = shared[:, :RUNGS]
    top = jnp.max(peaks, axis=0)
    summed = jnp.sum(shared[:, RUNGS : 2 * RUNGS] * jnp.exp(peaks - top[None, :]), axis=0)
    counted = jnp.sum((rungs[:, None] == ladder[None, :]).astype(jnp.float32), axis=0)
    rung_means = top + jnp.log(summed) - jnp.log(counted)

    tall, wide, cores = SIDES
    up = (device // (wide * cores) - mine_owner // (wide * cores)) % tall
    right = (device // cores % wide - mine_owner // cores % wide) % wide
    across = (device % cores - mine_owner % cores) % cores
    step = (right * tall + up) * cores + across
    wanted_length = step * per_device + mine % per_device
    everywhere = shared[:, 2 * RUNGS :].reshape(-1)
    order = jnp.arange(sources * per_device, dtype=jnp.int32)
    found = jnp.sum(
        jnp.where(wanted_length[:, None] == order[None, :], everywhere[None, :], 0.0), axis=1
    )
    next_lengths = found.astype(jnp.int32) + STEPS
    next_values = unpack(arrived_values, slot, shared)
    return (attention, weights, rung_means, next_keys, next_values, next_lengths)


def solution(mesh):
    placed = (
        P("particle", None, "tensor"),
        P("particle", None, "tensor"),
        P("particle", None, "tensor"),
        P("particle", None, "tensor"),
        P("particle", None, "tensor"),
        P("particle", "tensor"),
        P("particle", "tensor"),
        P("particle"),
        P("particle"),
        P("tensor"),
        P(),
        P(),
    )
    return jax.shard_map(
        shards,
        mesh=mesh,
        in_specs=placed,
        out_specs=(
            P("particle", None, "tensor"),
            P("particle"),
            P(),
            P("particle", None, "tensor"),
            P("particle", None, "tensor"),
            P("particle"),
        ),
        check_vma=False,
    )
```

time: 284 us -> 149 us (0.52)
  Pallas kernels: 147 us -> 19.8 us
  waiting for transfers between devices: 45.1 us -> 55 us
  local copies, waits for them, and re-layouts: 17.1 us -> 7.23 us
  starting transfers between devices: 40 us -> 33 us
    pallas_call x2 -> x5, Pallas kernels: 131 us -> 7.77 us  [the longest x2 7.76 us: unpack(): pl.pallas_call(unpack_kernel, out_shape=jax.ShapeDtypeStruct(shape, arriv...]
    unnamed x47 -> x35, local copies, waits for them, and re-layouts: 13.9 us -> 3.43 us
    all_to_all x2, waiting for transfers between devices: 0.01 us -> 6.1 us  [the longest x1 6.1 us: shards(): lax.all_to_all(after(outgoing_keys, plane), 'particle', split_axis=0, con...]
    ppermute x14, starting transfers between devices: 27.4 us -> 23 us  [along(): parts.append(lax.ppermute(array, 'particle', pairs))]
    pallas_call x2, Pallas kernels: 16.3 us -> 12.1 us  [pack(): pl.pallas_call(pack_kernel, out_shape=(jax.ShapeDtypeStruct(cache.shape,...]
    ppermute x14, waiting for transfers between devices: 45 us -> 48.9 us  [along(): parts.append(lax.ppermute(array, 'particle', pairs))]
  transfers between devices with their start and end apart: 16 -> 16, of which waited for: 7 -> 8; matrix products, arithmetic and copies ran while one was open for 8% -> 14% of each run, Pallas kernels for 26% -> 11%
where the time goes in v2:
time: 149 us; the launch traced here: 147 us
  waiting for transfers between devices  55 us (37%)
  starting transfers between devices  33 us (22%)
  Pallas kernels  19.8 us (13%)
  blocking collectives  15.2 us (10%)
  other arithmetic  8.44 us (6%)
  matrix products  7.56 us (5%)
  local copies, waits for them, and re-layouts  7.23 us (5%)
    ppermute x14, waiting for transfers between devices, along(): parts.append(lax.ppermute(array, 'particle', pairs))  48.9 us
    ppermute x14, starting transfers between devices, along(): parts.append(lax.ppermute(array, 'particle', pairs))  23 us
    psum x1, blocking collectives, shards(): weights = prior + lax.psum(partial_reward, 'tensor')  15.2 us
    pallas_call x2, Pallas kernels, pack(): pl.pallas_call(pack_kernel, out_shape=(jax.ShapeDtypeStruct(cache.shape,...  12.1 us
    pallas_call x2, Pallas kernels, unpack(): pl.pallas_call(unpack_kernel, out_shape=jax.ShapeDtypeStruct(shape, arriv...  7.76 us
    all_to_all x1, waiting for transfers between devices, shards(): lax.all_to_all(after(outgoing_keys, plane), 'particle', split_axis=0, con...  6.1 us
    all_to_all x1, starting transfers between devices, shards(): lax.all_to_all(after(outgoing_keys, plane), 'particle', split_axis=0, con...  5.13 us
    all_to_all x1, starting transfers between devices, shards(): lax.all_to_all(after(outgoing_values, near), 'particle', split_axis=0, co...  4.86 us
  transfers between devices with their start and end apart: 16, of which 8 were waited for; matrix products, arithmetic and copies ran while one was open for 14% of the time, Pallas kernels for 11%

profile of v2, /device:TPU:128, one launch (start us, length us, event | category | flops | bytes accessed | tf_op | source)
XLA Modules:
  0.0 147.4 jit_solution(11207757887328824185)
XLA Ops:
  2.1 1.7 %collective-permute-start = (bf16[64,256]{1,0:T(8,128)(2,1)S(1)}, bf16[64,256]{1,0:T(8,128)(2,1)S(1)}, u32[]{:S(2)}, u32[]{:S(2)}) collective-permute-start(bf16[64,256]{1,0:T(8,128)(2,1)S(1)} %get-tuple-element.47), channel_id=1, source_target_pairs={{0,64},{8,72},{16,80},{24,88},{32,96},{40,104},{48,112},{56,120},{... | collective-permute-start | bytes 98312 | tf_op jit(solution)/shard_map/ppermute | solution.py:146
  3.7 2.9 %collective-permute-start.1 = (bf16[64,256]{1,0:T(8,128)(2,1)S(1)}, bf16[64,256]{1,0:T(8,128)(2,1)S(1)}, u32[]{:S(2)}, u32[]{:S(2)}) collective-permute-start(bf16[64,256]{1,0:T(8,128)(2,1)S(1)} %get-tuple-element.47), channel_id=1, source_target_pairs={{0,128},{8,136},{16,144},{24,152},{32,160},{40,168},{48,176},{56,1... | collective-permute-start | bytes 98312 | tf_op jit(solution)/shard_map/ppermute | solution.py:146
  9.4 6.0 %pack.2 = (bf16[32,256,128]{2,1,0:T(8,128)(2,1)}, bf16[64,256,128]{2,1,0:T(8,128)(2,1)}) custom-call(s32[32]{0:T(128)} %lengths.3, s32[32]{0:T(128)} %get-tuple-element.27.least, s32[32]{0:T(128)} %get-tuple-element.26.most, bf16[32,256,128]{2,1,0:T(8,128)(2,1)} %cache.2, bf16[32,2,128]{2,1,0:T(2,128)(2,1)} %fresh.2), custom_call_target="tpu_custom_call" | custom-call | tf_op jit(solution)/shard_map/pack/pallas_call | solution.py:69
  17.1 2.7 %collective-permute-start.4 = (bf16[256,256]{1,0:T(8,128)(2,1)S(1)}, bf16[256,256]{1,0:T(8,128)(2,1)S(1)}, u32[]{:S(2)}, u32[]{:S(2)}) collective-permute-start(bf16[256,256]{1,0:T(8,128)(2,1)S(1)} %pad_maximum_fusion), channel_id=1, source_target_pairs={{0,32},{8,40},{16,48},{24,56},{32,0},{40,8},{48,16},{56,24},{64,96... | collective-permute-start | bytes 393224 | tf_op jit(solution)/shard_map/ppermute | solution.py:146
  21.2 1.9 %collective-permute-done.3 = bf16[256,256]{1,0:T(8,128)(2,1)S(1)} collective-permute-done((bf16[256,256]{1,0:T(8,128)(2,1)S(1)}, bf16[256,256]{1,0:T(8,128)(2,1)S(1)}, u32[]{:S(2)}, u32[]{:S(2)}) %collective-permute-start.3) | collective-permute-done | bytes 131104 | tf_op jit(solution)/shard_map/ppermute | solution.py:146
  23.2 1.8 %collective-permute-done.4 = bf16[256,256]{1,0:T(8,128)(2,1)S(1)} collective-permute-done((bf16[256,256]{1,0:T(8,128)(2,1)S(1)}, bf16[256,256]{1,0:T(8,128)(2,1)S(1)}, u32[]{:S(2)}, u32[]{:S(2)}) %collective-permute-start.4) | collective-permute-done | bytes 131104 | tf_op jit(solution)/shard_map/ppermute | solution.py:146
  26.2 5.1 %all-to-all-start = ((bf16[64,256,128]{2,1,0:T(8,128)(2,1)}), bf16[64,256,128]{2,1,0:T(8,128)(2,1)}, u32[]{:S(2)}, u32[]{:S(2)}) async-start(bf16[64,256,128]{2,1,0:T(8,128)(2,1)} %after.3), calls=%async_computation | async-start | bytes 8388608 | tf_op jit(solution)/shard_map/all_to_all | solution.py:189
  32.7 6.0 %pack.3 = (bf16[32,256,128]{2,1,0:T(8,128)(2,1)}, bf16[64,256,128]{2,1,0:T(8,128)(2,1)}) custom-call(s32[32]{0:T(128)} %lengths.3, s32[32]{0:T(128)} %get-tuple-element.27.least, s32[32]{0:T(128)} %get-tuple-element.26.most, bf16[32,256,128]{2,1,0:T(8,128)(2,1)} %cache.3, bf16[32,2,128]{2,1,0:T(2,128)(2,1)} %fresh.3), custom_call_target="tpu_custom_call" | custom-call | tf_op jit(solution)/shard_map/pack/pallas_call | solution.py:69
  38.8 1.9 %constant_dynamic-update-slice_fusion.10 = bf16[2048,256]{1,0:T(8,128)(2,1)} fusion(bf16[2048,256]{1,0:T(8,128)(2,1)} %copy-done.5, bf16[1024,256]{1,0:T(8,128)(2,1)} %collective-permute-done.6), kind=kLoop, calls=%fused_computation.40 | loop fusion | bytes 1048576 | tf_op jit(solution)/shard_map/concatenate | solution.py:147
  40.7 3.7 %bitcast_reduce_fusion = (f32[32,2,8]{0,2,1:T(8,128)S(1)}, f32[2048,32,2,8]{0,1,3,2:T(8,128)}) fusion(bf16[32,2,8,128]{3,2,1,0:T(8,128)(2,1)S(1)} %reshape.72, bf16[2048,256]{1,0:T(8,128)(2,1)} %constant_dynamic-update-slice_fusion.10), kind=kOutput, calls=%fused_computation.1 | convolution fusion | flops 270532096 | bytes 4851712 | tf_op jit(solution)/shard_map/pshd,nd->pshn/dot_general | solution.py:196
  44.8 3.2 %fusion.1 = f32[32,2,8]{0,2,1:T(8,128)S(1)} fusion(f32[2048,32,2,8]{0,1,3,2:T(8,128)} %get-tuple-element.54, f32[32,2,8]{0,2,1:T(8,128)S(1)} %max.7), kind=kLoop, calls=%fused_computation.3 | loop fusion | flops 3145216 | bytes 4198400 | tf_op jit(solution)/shard_map/reduce_sum | solution.py:209
  48.0 2.0 %fusion.5 = f32[32,2,8,128]{3,2,1,0:T(8,128)S(1)} fusion(bf16[32,256,128]{2,1,0:T(8,128)(2,1)} %get-tuple-element.11, f32[32,2,8,256]{3,2,1,0:T(8,128)S(1)} %get-tuple-element.56, f32[32,2,8]{2,1,0:T(2,128)S(1)} %copy.42), kind=kOutput, calls=%fused_computation.6 | convolution fusion | flops 33816576 | bytes 2885632 | tf_op jit(solution)/shard_map/pshl,pld->pshd/dot_general | solution.py:215
  51.2 15.2 %psum.7 = f32[32]{0:T(128)S(1)} all-reduce(f32[32]{0:T(128)S(1)} %get-tuple-element.31), channel_id=1, replica_groups=mesh['particle'=32,'tensor'=8] {'tensor'}, use_global_device_ids=true, to_apply=%region_7.8 | all-reduce | flops 32 | bytes 256 | tf_op jit(solution)/shard_map/psum | solution.py:225
  67.9 3.1 %collective-permute-start.10 = (f32[2,48]{1,0:T(2,128)S(1)}, f32[2,48]{1,0:T(2,128)S(1)}, u32[]{:S(2)}, u32[]{:S(2)}) collective-permute-start(f32[2,48]{1,0:T(2,128)S(1)} %pad_maximum_fusion.2), channel_id=1, source_target_pairs={{0,192},{8,200},{16,208},{24,216},{32,224},{40,232},{48,240},{56,2... | collective-permute-start | bytes 1160 | tf_op jit(solution)/shard_map/ppermute | solution.py:146
  71.0 2.3 %collective-permute-start.9 = (f32[2,48]{1,0:T(2,128)S(1)}, f32[2,48]{1,0:T(2,128)S(1)}, u32[]{:S(2)}, u32[]{:S(2)}) collective-permute-start(f32[2,48]{1,0:T(2,128)S(1)} %pad_maximum_fusion.2), channel_id=1, source_target_pairs={{0,128},{8,136},{16,144},{24,152},{32,160},{40,168},{48,176},{56,1... | collective-permute-start | bytes 1160 | tf_op jit(solution)/shard_map/ppermute | solution.py:146
  73.3 4.3 %collective-permute-done.10 = f32[2,48]{1,0:T(2,128)S(1)} collective-permute-done((f32[2,48]{1,0:T(2,128)S(1)}, f32[2,48]{1,0:T(2,128)S(1)}, u32[]{:S(2)}, u32[]{:S(2)}) %collective-permute-start.10) | collective-permute-done | bytes 416 | tf_op jit(solution)/shard_map/ppermute | solution.py:146
  78.8 6.1 %all-to-all-done.arrived = bf16[64,256,128]{2,1,0:T(8,128)(2,1)} async-done(((bf16[64,256,128]{2,1,0:T(8,128)(2,1)}), bf16[64,256,128]{2,1,0:T(8,128)(2,1)}, u32[]{:S(2)}, u32[]{:S(2)}) %all-to-all-start) | async-done | bytes 4194336 | tf_op jit(solution)/shard_map/all_to_all | solution.py:189
  84.9 4.9 %all-to-all-start.1 = ((bf16[64,256,128]{2,1,0:T(8,128)(2,1)}), bf16[64,256,128]{2,1,0:T(8,128)(2,1)}, u32[]{:S(2)}, u32[]{:S(2)}) async-start(bf16[64,256,128]{2,1,0:T(8,128)(2,1)} %after.5), calls=%async_computation.1 | async-start | bytes 8388608 | tf_op jit(solution)/shard_map/all_to_all | solution.py:235
  91.4 3.8 %unpack.2.refs_1_ = bf16[32,256,128]{2,1,0:T(8,128)(2,1)} custom-call(s32[32]{0:T(128)} %fusion.39.slots, bf16[64,256,128]{2,1,0:T(8,128)(2,1)} %all-to-all-done.arrived, f32[8,48]{1,0:T(8,128)} %concatenate.33._.refs_0_.refs_1_), custom_call_target="tpu_custom_call" | custom-call | tf_op jit(solution)/shard_map/unpack/pallas_call | solution.py:122
  95.2 1.8 %collective-permute-start.11 = (f32[8,48]{1,0:T(8,128)}, f32[8,48]{1,0:T(8,128)S(1)}, u32[]{:S(2)}, u32[]{:S(2)}) collective-permute-start(f32[8,48]{1,0:T(8,128)} %after.4), channel_id=1, source_target_pairs={{0,16},{8,24},{16,32},{24,40},{32,48},{40,56},{48,0},{56,8},{64,80... | collective-permute-start | bytes 4616 | tf_op jit(solution)/shard_map/ppermute | solution.py:146
  97.0 2.7 %collective-permute-start.12 = (f32[8,48]{1,0:T(8,128)}, f32[8,48]{1,0:T(8,128)S(1)}, u32[]{:S(2)}, u32[]{:S(2)}) collective-permute-start(f32[8,48]{1,0:T(8,128)} %after.4), channel_id=1, source_target_pairs={{0,32},{8,40},{16,48},{24,56},{32,0},{40,8},{48,16},{56,24},{64,96... | collective-permute-start | bytes 4616 | tf_op jit(solution)/shard_map/ppermute | solution.py:146
  101.9 35.3 %collective-permute-done.11 = f32[8,48]{1,0:T(8,128)S(1)} collective-permute-done((f32[8,48]{1,0:T(8,128)}, f32[8,48]{1,0:T(8,128)S(1)}, u32[]{:S(2)}, u32[]{:S(2)}) %collective-permute-start.11) | collective-permute-done | bytes 1568 | tf_op jit(solution)/shard_map/ppermute | solution.py:146
  137.2 3.9 %collective-permute-done.12 = f32[8,48]{1,0:T(8,128)S(1)} collective-permute-done((f32[8,48]{1,0:T(8,128)}, f32[8,48]{1,0:T(8,128)S(1)}, u32[]{:S(2)}, u32[]{:S(2)}) %collective-permute-start.12) | collective-permute-done | bytes 1568 | tf_op jit(solution)/shard_map/ppermute | solution.py:146
  143.3 3.9 %unpack.3 = bf16[32,256,128]{2,1,0:T(8,128)(2,1)} custom-call(s32[32]{0:T(128)} %fusion.39.slots, bf16[64,256,128]{2,1,0:T(8,128)(2,1)} %all-to-all-done.1.arrived, f32[32,48]{1,0:T(8,128)} %copy-done.2), custom_call_target="tpu_custom_call" | custom-call | tf_op jit(solution)/shard_map/unpack/pallas_call | solution.py:122
  (90 shorter events, 20.1 us)
Async XLA Ops:
  2.1 13.3 %collective-permute-start = (bf16[64,256]{1,0:T(8,128)(2,1)S(1)}, bf16[64,256]{1,0:T(8,128)(2,1)S(1)}, u32[]{:S(2)}, u32[]{:S(2)}) collective-permute-start(bf16[64,256]{1,0:T(8,128)(2,1)S(1)} %get-tuple-element.47), channel_id=1, source_target_pairs={{0,64},{8,72},{16,80},{24,88},{32,96},{40,104},{48,112},{56,120},{... | collective-permute-start | bytes 98312 | tf_op jit(solution)/shard_map/ppermute | solution.py:146
  3.7 11.7 %collective-permute-start.1 = (bf16[64,256]{1,0:T(8,128)(2,1)S(1)}, bf16[64,256]{1,0:T(8,128)(2,1)S(1)}, u32[]{:S(2)}, u32[]{:S(2)}) collective-permute-start(bf16[64,256]{1,0:T(8,128)(2,1)S(1)} %get-tuple-element.47), channel_id=1, source_target_pairs={{0,128},{8,136},{16,144},{24,152},{32,160},{40,168},{48,176},{56,1... | collective-permute-start | bytes 98312 | tf_op jit(solution)/shard_map/ppermute | solution.py:146
  6.6 8.8 %collective-permute-start.2 = (bf16[64,256]{1,0:T(8,128)(2,1)S(1)}, bf16[64,256]{1,0:T(8,128)(2,1)S(1)}, u32[]{:S(2)}, u32[]{:S(2)}) collective-permute-start(bf16[64,256]{1,0:T(8,128)(2,1)S(1)} %get-tuple-element.47), channel_id=1, source_target_pairs={{0,192},{8,200},{16,208},{24,216},{32,224},{40,232},{48,240},{56,2... | collective-permute-start | bytes 98312 | tf_op jit(solution)/shard_map/ppermute | solution.py:146
  15.5 7.7 %collective-permute-start.3 = (bf16[256,256]{1,0:T(8,128)(2,1)S(1)}, bf16[256,256]{1,0:T(8,128)(2,1)S(1)}, u32[]{:S(2)}, u32[]{:S(2)}) collective-permute-start(bf16[256,256]{1,0:T(8,128)(2,1)S(1)} %pad_maximum_fusion), channel_id=1, source_target_pairs={{0,16},{8,24},{16,32},{24,40},{32,48},{40,56},{48,0},{56,8},{64,80... | collective-permute-start | bytes 393224 | tf_op jit(solution)/shard_map/ppermute | solution.py:146
  17.1 7.9 %collective-permute-start.4 = (bf16[256,256]{1,0:T(8,128)(2,1)S(1)}, bf16[256,256]{1,0:T(8,128)(2,1)S(1)}, u32[]{:S(2)}, u32[]{:S(2)}) collective-permute-start(bf16[256,256]{1,0:T(8,128)(2,1)S(1)} %pad_maximum_fusion), channel_id=1, source_target_pairs={{0,32},{8,40},{16,48},{24,56},{32,0},{40,8},{48,16},{56,24},{64,96... | collective-permute-start | bytes 393224 | tf_op jit(solution)/shard_map/ppermute | solution.py:146
  19.8 5.2 %collective-permute-start.5 = (bf16[256,256]{1,0:T(8,128)(2,1)S(1)}, bf16[256,256]{1,0:T(8,128)(2,1)S(1)}, u32[]{:S(2)}, u32[]{:S(2)}) collective-permute-start(bf16[256,256]{1,0:T(8,128)(2,1)S(1)} %pad_maximum_fusion), channel_id=1, source_target_pairs={{0,48},{8,56},{16,0},{24,8},{32,16},{40,24},{48,32},{56,40},{64,11... | collective-permute-start | bytes 393224 | tf_op jit(solution)/shard_map/ppermute | solution.py:146
  26.2 5.4 %copy-start.7 = (bf16[32,2,1024]{2,1,0:T(2,128)(2,1)S(1)}, bf16[32,2,1024]{2,1,0:T(2,128)(2,1)}, u32[]{:S(2)}) copy-start(bf16[32,2,1024]{2,1,0:T(2,128)(2,1)} %param.12) | copy-start | bytes 393220
  26.2 5.7 %copy-start.1 = (bf16[32,256,128]{2,1,0:T(8,128)(2,1)S(1)}, bf16[32,256,128]{2,1,0:T(8,128)(2,1)}, u32[]{:S(2)}) copy-start(bf16[32,256,128]{2,1,0:T(8,128)(2,1)} %get-tuple-element.10) | copy-start | bytes 6291460
  26.2 58.7 %all-to-all-start = ((bf16[64,256,128]{2,1,0:T(8,128)(2,1)}), bf16[64,256,128]{2,1,0:T(8,128)(2,1)}, u32[]{:S(2)}, u32[]{:S(2)}) async-start(bf16[64,256,128]{2,1,0:T(8,128)(2,1)} %after.3), calls=%async_computation | async-start | bytes 8388608 | tf_op jit(solution)/shard_map/all_to_all | solution.py:189
  31.4 7.4 %copy-start.8 = (s32[1024]{0:T(1024)S(1)}, s32[1024]{0:T(1024)}, u32[]{:S(2)}) copy-start(s32[1024]{0:T(1024)} %param.22) | copy-start | bytes 12292
  31.4 7.4 %collective-permute-start.6 = (bf16[1024,256]{1,0:T(8,128)(2,1)S(1)}, bf16[1024,256]{1,0:T(8,128)(2,1)}, u32[]{:S(2)}, u32[]{:S(2)}) collective-permute-start(bf16[1024,256]{1,0:T(8,128)(2,1)S(1)} %copy-done.4), channel_id=1, source_target_pairs={{0,8},{8,0},{16,24},{24,16},{32,40},{40,32},{48,56},{56,48},{64,72... | collective-permute-start | bytes 1572872 | tf_op jit(solution)/shard_map/ppermute | solution.py:146
  44.4 5.7 %copy-start.6 = (bf16[2048,256]{1,0:T(8,128)(2,1)S(1)}, bf16[2048,256]{1,0:T(8,128)(2,1)}, u32[]{:S(2)}) copy-start(bf16[2048,256]{1,0:T(8,128)(2,1)} %constant_dynamic-update-slice_fusion.10) | copy-start | bytes 3145732
  44.4 5.7 %copy-start.11 = (f32[1024]{0:T(1024)S(1)}, f32[1024]{0:T(1024)}, u32[]{:S(2)}) copy-start(f32[1024]{0:T(1024)} %param.21) | copy-start | bytes 12292
  44.8 5.3 %copy-start = (f32[2048,32,2,8]{0,1,3,2:T(8,128)S(1)}, f32[2048,32,2,8]{0,1,3,2:T(8,128)}, u32[]{:S(2)}) copy-start(f32[2048,32,2,8]{0,1,3,2:T(8,128)} %get-tuple-element.54) | copy-start | bytes 12582916
  48.0 18.3 %copy-start.12 = (f32[32]{0:T(128)S(1)}, f32[32]{0:T(128)}, u32[]{:S(2)}) copy-start(f32[32]{0:T(128)} %param.20) | copy-start | bytes 388
  66.3 12.4 %copy-start.10 = (f32[32]{0:T(128)}, f32[32]{0:T(128)S(1)}, u32[]{:S(2)}) copy-start(f32[32]{0:T(128)S(1)} %add.115) | copy-start | bytes 388
  66.7 1.2 collective-permute-start.7
  67.9 9.7 %collective-permute-start.10 = (f32[2,48]{1,0:T(2,128)S(1)}, f32[2,48]{1,0:T(2,128)S(1)}, u32[]{:S(2)}, u32[]{:S(2)}) collective-permute-start(f32[2,48]{1,0:T(2,128)S(1)} %pad_maximum_fusion.2), channel_id=1, source_target_pairs={{0,192},{8,200},{16,208},{24,216},{32,224},{40,232},{48,240},{56,2... | collective-permute-start | bytes 1160 | tf_op jit(solution)/shard_map/ppermute | solution.py:146
  71.0 6.6 %collective-permute-start.8 = (f32[2,48]{1,0:T(2,128)S(1)}, f32[2,48]{1,0:T(2,128)S(1)}, u32[]{:S(2)}, u32[]{:S(2)}) collective-permute-start(f32[2,48]{1,0:T(2,128)S(1)} %pad_maximum_fusion.2), channel_id=1, source_target_pairs={{0,64},{8,72},{16,80},{24,88},{32,96},{40,104},{48,112},{56,120},{... | collective-permute-start | bytes 1160 | tf_op jit(solution)/shard_map/ppermute | solution.py:146
  71.0 7.1 %collective-permute-start.9 = (f32[2,48]{1,0:T(2,128)S(1)}, f32[2,48]{1,0:T(2,128)S(1)}, u32[]{:S(2)}, u32[]{:S(2)}) collective-permute-start(f32[2,48]{1,0:T(2,128)S(1)} %pad_maximum_fusion.2), channel_id=1, source_target_pairs={{0,128},{8,136},{16,144},{24,152},{32,160},{40,168},{48,176},{56,1... | collective-permute-start | bytes 1160 | tf_op jit(solution)/shard_map/ppermute | solution.py:146
  84.9 58.4 %all-to-all-start.1 = ((bf16[64,256,128]{2,1,0:T(8,128)(2,1)}), bf16[64,256,128]{2,1,0:T(8,128)(2,1)}, u32[]{:S(2)}, u32[]{:S(2)}) async-start(bf16[64,256,128]{2,1,0:T(8,128)(2,1)} %after.5), calls=%async_computation.1 | async-start | bytes 8388608 | tf_op jit(solution)/shard_map/all_to_all | solution.py:235
  95.2 41.9 %collective-permute-start.11 = (f32[8,48]{1,0:T(8,128)}, f32[8,48]{1,0:T(8,128)S(1)}, u32[]{:S(2)}, u32[]{:S(2)}) collective-permute-start(f32[8,48]{1,0:T(8,128)} %after.4), channel_id=1, source_target_pairs={{0,16},{8,24},{16,32},{24,40},{32,48},{40,56},{48,0},{56,8},{64,80... | collective-permute-start | bytes 4616 | tf_op jit(solution)/shard_map/ppermute | solution.py:146
  97.0 44.0 %collective-permute-start.12 = (f32[8,48]{1,0:T(8,128)}, f32[8,48]{1,0:T(8,128)S(1)}, u32[]{:S(2)}, u32[]{:S(2)}) collective-permute-start(f32[8,48]{1,0:T(8,128)} %after.4), channel_id=1, source_target_pairs={{0,32},{8,40},{16,48},{24,56},{32,0},{40,8},{48,16},{56,24},{64,96... | collective-permute-start | bytes 4616 | tf_op jit(solution)/shard_map/ppermute | solution.py:146
  99.7 41.4 %collective-permute-start.13 = (f32[8,48]{1,0:T(8,128)}, f32[8,48]{1,0:T(8,128)S(1)}, u32[]{:S(2)}, u32[]{:S(2)}) collective-permute-start(f32[8,48]{1,0:T(8,128)} %after.4), channel_id=1, source_target_pairs={{0,48},{8,56},{16,0},{24,8},{32,16},{40,24},{48,32},{56,40},{64,11... | collective-permute-start | bytes 4616 | tf_op jit(solution)/shard_map/ppermute | solution.py:146
  (5 other events, 13.8 us)

commit v3 on v2

v3 whole, which is shorter than its diff:
```python
import itertools

import jax
import jax.numpy as jnp
from jax import lax
from jax.experimental import pallas as pl
from jax.experimental.pallas import tpu as pltpu
from jax.sharding import PartitionSpec as P

HEADS = 64
KV_HEADS = 8
HEAD_DIM = 128
STEPS = 2
RUNGS = 8
DISTINCT = 2
SIDES = (4, 4, 2)
WINDOW = 32
CHUNKS = 4
GROUP = 2
ROOMY = 58 << 20


def repeat(count, body):
    def step(i, carry):
        body(i)
        return carry

    lax.fori_loop(0, count, step, 0, unroll=4)


def pack_kernel(
    lengths,
    least,
    most,
    keys,
    values,
    new_keys,
    new_values,
    packed,
    written_keys,
    written_values,
    held,
    in_sems,
    out_sems,
    low_sems,
    high_sems,
):
    count, suffix, _ = keys.shape
    goals = least.shape[0]
    share = count // CHUNKS
    parts = ((keys, new_keys, written_keys), (values, new_values, written_values))

    def load(chunk, half):
        rows = pl.ds(chunk * share, share)
        return pltpu.make_async_copy(
            parts[half][0].at[rows],
            held.at[rows, pl.ds(half * suffix, suffix)],
            in_sems.at[chunk * 2 + half],
        )

    def keep(half):
        return pltpu.make_async_copy(
            held.at[:, pl.ds(half * suffix, suffix)], parts[half][2], out_sems.at[half]
        )

    def low(d):
        return pltpu.make_async_copy(held.at[least[d]], packed.at[2 * d], low_sems.at[d])

    def high(d):
        return pltpu.make_async_copy(held.at[most[d]], packed.at[2 * d + 1], high_sems.at[d])

    def patch(group):
        found = []
        for i in range(GROUP):
            p = group * GROUP + i
            length = lengths[p]
            base = pl.multiple_of(jnp.minimum(length // 16 * 16, suffix - WINDOW), 16)
            for half in range(2):
                place = (p, pl.ds(base + half * suffix, WINDOW))
                block = held[place].astype(jnp.float32)
                lines = parts[half][1][p].astype(jnp.float32)
                row = lax.broadcasted_iota(jnp.int32, block.shape, 0) + base
                for offset in range(STEPS):
                    block = jnp.where(row == length + offset, lines[offset : offset + 1], block)
                found.append((place, block.astype(held.dtype)))
        for place, block in found:
            held[place] = block

    for chunk in range(CHUNKS):
        for half in range(2):
            load(chunk, half).start()
    for chunk in range(CHUNKS):
        for half in range(2):
            load(chunk, half).wait()
        repeat(share // GROUP, lambda g, chunk=chunk: patch(g + chunk * (share // GROUP)), 1)
    repeat(goals, lambda d: low(d).start())
    repeat(goals, lambda d: high(d).start())
    keep(0).start()
    keep(1).start()
    repeat(goals, lambda d: low(d).wait())
    repeat(goals, lambda d: high(d).wait())
    keep(0).wait()
    keep(1).wait()


def repeat(count, body, unroll=4):
    def step(i, carry):
        body(i)
        return carry

    lax.fori_loop(0, count, step, 0, unroll=unroll)


def pack(keys, values, new_keys, new_values, lengths, least, most):
    (count, suffix, width), goals = keys.shape, least.shape[0]
    smem = pl.BlockSpec(memory_space=pltpu.SMEM)
    hbm = pl.BlockSpec(memory_space=pltpu.HBM)
    vmem = pl.BlockSpec(memory_space=pltpu.VMEM)
    return pl.pallas_call(
        pack_kernel,
        out_shape=(
            jax.ShapeDtypeStruct((goals * DISTINCT, 2 * suffix, width), keys.dtype),
            jax.ShapeDtypeStruct(keys.shape, keys.dtype),
            jax.ShapeDtypeStruct(values.shape, values.dtype),
        ),
        in_specs=[smem, smem, smem, hbm, hbm, vmem, vmem],
        out_specs=(hbm, hbm, hbm),
        scratch_shapes=[
            pltpu.VMEM((count, 2 * suffix, width), keys.dtype),
            pltpu.SemaphoreType.DMA((2 * CHUNKS,)),
            pltpu.SemaphoreType.DMA((2,)),
            pltpu.SemaphoreType.DMA((goals,)),
            pltpu.SemaphoreType.DMA((goals,)),
        ],
        name="pack",
    )(lengths, least, most, keys, values, new_keys, new_values)


def after(array, *others):
    hbm = pl.BlockSpec(memory_space=pltpu.HBM)
    return pl.pallas_call(
        lambda *refs: None,
        out_shape=jax.ShapeDtypeStruct(array.shape, array.dtype),
        in_specs=[hbm] + [pl.BlockSpec(memory_space=pl.ANY)] * len(others),
        out_specs=hbm,
        input_output_aliases={0: 0},
        compiler_params=pltpu.CompilerParams(vmem_limit_bytes=ROOMY),
        name="after",
    )(array, *others)


def unpack_kernel(slots, arrived, _, next_keys, next_values, mark, held, in_sems, out_sems):
    count, suffix, _ = next_keys.shape
    share = count // CHUNKS

    def load(p):
        return pltpu.make_async_copy(arrived.at[slots[p]], held.at[p], in_sems.at[p])

    def keep(chunk, half):
        rows = pl.ds(chunk * share, share)
        return pltpu.make_async_copy(
            held.at[rows, pl.ds(half * suffix, suffix)],
            (next_keys, next_values)[half].at[rows],
            out_sems.at[chunk * 2 + half],
        )

    mark[...] = jnp.zeros_like(mark)
    repeat(count, lambda p: load(p).start())
    for chunk in range(CHUNKS):
        repeat(share, lambda p, chunk=chunk: load(p + chunk * share).wait())
        for half in range(2):
            keep(chunk, half).start()
    for chunk in range(CHUNKS):
        for half in range(2):
            keep(chunk, half).wait()


def unpack(arrived, slots, other):
    count, (_, length, width) = slots.shape[0], arrived.shape
    hbm = pl.BlockSpec(memory_space=pltpu.HBM)
    shape = jax.ShapeDtypeStruct((count, length // 2, width), arrived.dtype)
    return pl.pallas_call(
        unpack_kernel,
        out_shape=(shape, shape, jax.ShapeDtypeStruct((1, width), jnp.float32)),
        in_specs=[pl.BlockSpec(memory_space=pltpu.SMEM), hbm, pl.BlockSpec(memory_space=pl.ANY)],
        out_specs=(hbm, hbm, pl.BlockSpec(memory_space=pltpu.VMEM)),
        scratch_shapes=[
            pltpu.VMEM((count, length, width), arrived.dtype),
            pltpu.SemaphoreType.DMA((count,)),
            pltpu.SemaphoreType.DMA((2 * CHUNKS,)),
        ],
        name="unpack",
    )(slots, arrived, other)


def finish_kernel(counted, step, place, *refs):
    *parts, _, rung_means, next_lengths = refs
    shared = jnp.concatenate([part[...] for part in parts], axis=0)
    peaks, sums, filled = shared[:, 0], shared[:, 1], shared[:, 2]
    top = jnp.max(peaks, axis=0, keepdims=True)
    summed = jnp.sum(sums * jnp.exp(peaks - top), axis=0, keepdims=True)
    rung_means[...] = top + jnp.log(summed) - jnp.log(counted[...])
    order = lax.broadcasted_iota(jnp.int32, filled.shape, 0)
    owner = (order == step[...]).astype(jnp.float32)
    found = lax.dot_general(
        filled, owner, (((0,), (0,)), ((), ())), preferred_element_type=jnp.float32
    )
    order = lax.broadcasted_iota(jnp.int32, found.shape, 0)
    length = jnp.sum(jnp.where(order == place[...], found, 0.0), axis=0, keepdims=True)
    next_lengths[...] = length.astype(jnp.int32) + STEPS


def finish(parts, counted, step, place, other):
    vmem = pl.BlockSpec(memory_space=pltpu.VMEM)
    row = (1, step.shape[1])
    return pl.pallas_call(
        finish_kernel,
        out_shape=(
            jax.ShapeDtypeStruct(row, jnp.float32),
            jax.ShapeDtypeStruct(row, jnp.int32),
        ),
        in_specs=[vmem] * (3 + len(parts)) + [pl.BlockSpec(memory_space=pl.ANY)],
        out_specs=(vmem, vmem),
        compiler_params=pltpu.CompilerParams(vmem_limit_bytes=ROOMY),
        name="finish",
    )(counted, step, place, *parts, other)


def along(array, axes):
    sides = SIDES
    total = sides[0] * sides[1] * sides[2]
    parts = []
    for steps in itertools.product(*(range(sides[axis]) for axis in axes)):
        pairs = []
        for i in range(total):
            goal = [i // (sides[1] * sides[2]), i // sides[2] % sides[1], i % sides[2]]
            for axis, step in zip(axes, steps):
                goal[axis] = (goal[axis] + step) % sides[axis]
            pairs.append((i, (goal[0] * sides[1] + goal[1]) * sides[2] + goal[2]))
        parts.append(lax.ppermute(array, "particle", pairs) if any(steps) else array)
    return parts


def shards(
    queries,
    new_keys,
    new_values,
    key_cache,
    value_cache,
    prompt_keys,
    prompt_values,
    lengths,
    prior,
    reward_dir,
    rungs,
    ancestors,
):
    per_device = queries.shape[0]
    suffix = key_cache.shape[1]
    groups = HEADS // KV_HEADS
    scale = HEAD_DIM ** (-0.5)
    sources = lax.axis_size("particle")
    device = lax.axis_index("particle")

    shard = jnp.concatenate([prompt_keys, prompt_values], axis=1)
    column = jnp.concatenate(along(shard, (0,)), axis=0)
    columns = along(column, (1,))
    prompt = jnp.concatenate(along(jnp.concatenate(columns, axis=0), (2,)), axis=0)
    all_keys = prompt[:, :HEAD_DIM]
    all_values = prompt[:, HEAD_DIM:]

    wanted = ancestors.reshape(sources, per_device)
    owner = wanted // per_device
    local = wanted % per_device
    chosen = owner == device
    least = jnp.min(jnp.where(chosen, local, per_device - 1), axis=1)
    most = jnp.max(jnp.where(chosen, local, 0), axis=1)
    mine = lax.dynamic_slice_in_dim(ancestors, device * per_device, per_device)
    mine_owner = mine // per_device
    same_owner = mine_owner[:, None] == mine_owner[None, :]
    first = jnp.min(jnp.where(same_owner, mine[None, :], sources * per_device), axis=1)
    slot = mine_owner * DISTINCT + (mine != first).astype(jnp.int32)

    outgoing, written_keys, written_values = pack(
        key_cache, value_cache, new_keys, new_values, lengths, least, most
    )
    arrived = lax.all_to_all(
        after(outgoing, *columns[1:]), "particle", split_axis=0, concat_axis=0, tiled=True
    )

    query = queries.reshape(per_device, STEPS, groups, HEAD_DIM)
    front = (
        jnp.einsum("pshd,nd->pshn", query, all_keys, preferred_element_type=jnp.float32) * scale
    )
    back = (
        jnp.einsum("pshd,pld->pshl", query, written_keys, preferred_element_type=jnp.float32)
        * scale
    )
    position = jnp.arange(suffix, dtype=jnp.int32)
    later = jnp.arange(STEPS, dtype=jnp.int32)
    visible = position[None, None, :] < lengths[:, None, None] + 1 + later[None, :, None]
    back = jnp.where(visible[:, :, None, :], back, -jnp.inf)
    peak = jnp.maximum(jnp.max(front, axis=-1), jnp.max(back, axis=-1))
    front = jnp.exp(front - peak[..., None])
    back = jnp.exp(back - peak[..., None])
    total = jnp.sum(front, axis=-1) + jnp.sum(back, axis=-1)
    mixed = jnp.einsum(
        "pshn,nd->pshd",
        front.astype(jnp.bfloat16),
        all_values,
        preferred_element_type=jnp.float32,
    ) + jnp.einsum(
        "pshl,pld->pshd",
        back.astype(jnp.bfloat16),
        written_values,
        preferred_element_type=jnp.float32,
    )
    output = (mixed / total[..., None]).reshape(per_device, STEPS, -1)
    attention = output.astype(jnp.bfloat16)

    partial_reward = jnp.sum(output * reward_dir[None, None, :], axis=(1, 2))
    weights = prior + lax.psum(partial_reward, "tensor")
    own_rungs = lax.dynamic_slice_in_dim(rungs, device * per_device, per_device)
    ladder = jnp.arange(RUNGS, dtype=jnp.int32)
    member = own_rungs[:, None] == ladder[None, :]
    local_peak = jnp.max(jnp.where(member, weights[:, None], -1e30), axis=0)
    local_sum = jnp.sum(
        jnp.where(member, jnp.exp(weights[:, None] - local_peak[None, :]), 0.0), axis=0
    )
    spare = per_device - RUNGS
    shared = jnp.stack(
        [
            jnp.pad(local_peak, (0, spare)),
            jnp.pad(local_sum, (0, spare), constant_values=1.0),
            lengths.astype(jnp.float32),
        ]
    )[None]
    near = jnp.concatenate(along(shared, (2,)), axis=0)
    near = jnp.concatenate(along(near, (0,)), axis=0)
    parts = along(near, (1,))
    next_keys, next_values, mark = unpack(arrived, slot, near)

    counted = jnp.sum((rungs[:, None] == ladder[None, :]).astype(jnp.float32), axis=0)
    tall, wide, cores = SIDES
    up = (device // (wide * cores) - mine_owner // (wide * cores)) % tall
    right = (device // cores % wide - mine_owner // cores % wide) % wide
    across = (device % cores - mine_owner % cores) % cores
    step = (right * tall + up) * cores + across
    rung_means, next_lengths = finish(
        parts,
        jnp.pad(counted, (0, spare), constant_values=1.0)[None],
        step[None],
        (mine % per_device)[None],
        mark,
    )
    rung_means = rung_means[0, :RUNGS]
    next_lengths = next_lengths[0]
    return (attention, weights, rung_means, next_keys, next_values, next_lengths)


def solution(mesh):
    placed = (
        P("particle", None, "tensor"),
        P("particle", None, "tensor"),
        P("particle", None, "tensor"),
        P("particle", None, "tensor"),
        P("particle", None, "tensor"),
        P("particle", "tensor"),
        P("particle", "tensor"),
        P("particle"),
        P("particle"),
        P("tensor"),
        P(),
        P(),
    )
    return jax.shard_map(
        shards,
        mesh=mesh,
        in_specs=placed,
        out_specs=(
            P("particle", None, "tensor"),
            P("particle"),
            P(),
            P("particle", None, "tensor"),
            P("particle", None, "tensor"),
            P("particle"),
        ),
        check_vma=False,
    )
```

time: 149 us -> 148 us (level)
  waiting for transfers between devices: 55 us -> 63 us
  starting transfers between devices: 33 us -> 25.9 us
  local copies, waits for them, and re-layouts: 7.23 us -> 12.5 us
  Pallas kernels: 19.8 us -> 15.2 us
    ppermute x14, waiting for transfers between devices: 48.9 us -> 59.2 us  [along(): lax.ppermute(array, 'particle', pairs)]
    all_to_all x2 -> x1, starting transfers between devices: 9.99 us -> 5.12 us  [shards(): lax.all_to_all(after(outgoing, *columns[1:]), 'particle', split_axis=0, c...]
    unnamed x35 -> x50, local copies, waits for them, and re-layouts: 3.43 us -> 8.09 us
    pallas_call x4 -> x3, Pallas kernels: 19.8 us -> 15.2 us  [the longest x1 8.21 us: pack(): pl.pallas_call(pack_kernel, out_shape=(jax.ShapeDtypeStruct((goals * DIST...]
    all_to_all x2 -> x1, waiting for transfers between devices: 6.1 us -> 3.85 us  [shards(): lax.all_to_all(after(outgoing, *columns[1:]), 'particle', split_axis=0, c...]
    ppermute x14, starting transfers between devices: 23 us -> 20.8 us  [along(): lax.ppermute(array, 'particle', pairs)]
    broadcast_in_dim x1 -> x3, other arithmetic: 0.08 us -> 1.85 us  [the longest x1 1.29 us: shards(): (mine % per_device)[None]]
  transfers between devices with their start and end apart: 16 -> 15, of which waited for: 8 -> 8; matrix products, arithmetic and copies ran while one was open for 14% -> 15% of each run, Pallas kernels for 11% -> 9%
where the time goes in v3:
time: 148 us
  waiting for transfers between devices  63 us (43%)
  starting transfers between devices  25.9 us (18%)
  Pallas kernels  15.2 us (10%)
  blocking collectives  15.2 us (10%)
  local copies, waits for them, and re-layouts  12.5 us (8%)
  matrix products  7.58 us (5%)
  other arithmetic  7.3 us (5%)
    ppermute x14, waiting for transfers between devices, along(): lax.ppermute(array, 'particle', pairs)  59.2 us
    ppermute x14, starting transfers between devices, along(): lax.ppermute(array, 'particle', pairs)  20.8 us
    psum x1, blocking collectives, shards(): weights = prior + lax.psum(partial_reward, 'tensor')  15.2 us
    pallas_call x1, Pallas kernels, pack(): pl.pallas_call(pack_kernel, out_shape=(jax.ShapeDtypeStruct((goals * DIST...  8.21 us
    unnamed x50, local copies, waits for them, and re-layouts  8.09 us
    pallas_call x1, Pallas kernels, unpack(): pl.pallas_call(unpack_kernel, out_shape=(shape, shape, jax.ShapeDtypeStru...  5.46 us
    all_to_all x1, starting transfers between devices, shards(): lax.all_to_all(after(outgoing, *columns[1:]), 'particle', split_axis=0, c...  5.12 us
    all_to_all x1, waiting for transfers between devices, shards(): lax.all_to_all(after(outgoing, *columns[1:]), 'particle', split_axis=0, c...  3.85 us
  transfers between devices with their start and end apart: 15, of which 8 were waited for; matrix products, arithmetic and copies ran while one was open for 15% of the time, Pallas kernels for 9%

profile of v3, /device:TPU:128, one launch (start us, length us, event | category | flops | bytes accessed | tf_op | source)
XLA Modules:
  0.0 147.7 jit_solution(17046322607741278361)
XLA Ops:
  3.3 1.6 %collective-permute-start = (bf16[64,256]{1,0:T(8,128)(2,1)S(1)}, bf16[64,256]{1,0:T(8,128)(2,1)S(1)}, u32[]{:S(2)}, u32[]{:S(2)}) collective-permute-start(bf16[64,256]{1,0:T(8,128)(2,1)S(1)} %get-tuple-element.56), channel_id=1, source_target_pairs={{0,64},{8,72},{16,80},{24,88},{32,96},{40,104},{48,112},{56,120},{... | collective-permute-start | bytes 98312 | tf_op jit(solution)/shard_map/ppermute | solution.py:240
  4.9 2.9 %collective-permute-start.1 = (bf16[64,256]{1,0:T(8,128)(2,1)S(1)}, bf16[64,256]{1,0:T(8,128)(2,1)S(1)}, u32[]{:S(2)}, u32[]{:S(2)}) collective-permute-start(bf16[64,256]{1,0:T(8,128)(2,1)S(1)} %get-tuple-element.56), channel_id=1, source_target_pairs={{0,128},{8,136},{16,144},{24,152},{32,160},{40,168},{48,176},{56,1... | collective-permute-start | bytes 98312 | tf_op jit(solution)/shard_map/ppermute | solution.py:240
  7.8 1.3 collective-permute-start.2
  10.3 1.4 collective-permute-done.2
  11.7 1.6 %collective-permute-start.3 = (bf16[256,256]{1,0:T(8,128)(2,1)S(1)}, bf16[256,256]{1,0:T(8,128)(2,1)S(1)}, u32[]{:S(2)}, u32[]{:S(2)}) collective-permute-start(bf16[256,256]{1,0:T(8,128)(2,1)S(1)} %pad_maximum_fusion), channel_id=1, source_target_pairs={{0,16},{8,24},{16,32},{24,40},{32,48},{40,56},{48,0},{56,8},{64,80... | collective-permute-start | bytes 393224 | tf_op jit(solution)/shard_map/ppermute | solution.py:240
  13.3 2.7 %collective-permute-start.4 = (bf16[256,256]{1,0:T(8,128)(2,1)S(1)}, bf16[256,256]{1,0:T(8,128)(2,1)S(1)}, u32[]{:S(2)}, u32[]{:S(2)}) collective-permute-start(bf16[256,256]{1,0:T(8,128)(2,1)S(1)} %pad_maximum_fusion), channel_id=1, source_target_pairs={{0,32},{8,40},{16,48},{24,56},{32,0},{40,8},{48,16},{56,24},{64,96... | collective-permute-start | bytes 393224 | tf_op jit(solution)/shard_map/ppermute | solution.py:240
  16.0 1.4 collective-permute-start.5
  18.9 8.2 %pack.1 = (bf16[64,512,128]{2,1,0:T(8,128)(2,1)}, bf16[32,256,128]{2,1,0:T(8,128)(2,1)}, bf16[32,256,128]{2,1,0:T(8,128)(2,1)}) custom-call(s32[32]{0:T(128)} %lengths.1, s32[32]{0:T(128)} %get-tuple-element.35.least, s32[32]{0:T(128)} %get-tuple-element.34.most, bf16[32,256,128]{2,1,0:T(8,128)(2,1)} %keys.1, bf16[32,256,128]{2,1,0:T(8,128)(2,1)} %values.1, ...), custom_call_target="tpu_custom_call" | custom-call | tf_op jit(solution)/shard_map/pack/pallas_call | solution.py:119
  27.9 5.1 %all-to-all-start = ((bf16[64,512,128]{2,1,0:T(8,128)(2,1)}), bf16[64,512,128]{2,1,0:T(8,128)(2,1)}, u32[]{:S(2)}, u32[]{:S(2)}) async-start(bf16[64,512,128]{2,1,0:T(8,128)(2,1)} %after.1), calls=%async_computation | async-start | bytes 16777216 | tf_op jit(solution)/shard_map/all_to_all | solution.py:287
  42.7 3.7 %bitcast_reduce_fusion = (f32[32,2,8]{0,2,1:T(8,128)S(1)}, f32[2048,32,2,8]{0,1,3,2:T(8,128)}) fusion(bf16[32,2,8,128]{3,2,1,0:T(8,128)(2,1)S(1)} %reshape.69, bf16[2048,256]{1,0:T(8,128)(2,1)} %constant_dynamic-update-slice_fusion.10), kind=kOutput, calls=%fused_computation.1 | convolution fusion | flops 270532096 | bytes 4851712 | tf_op jit(solution)/shard_map/pshd,nd->pshn/dot_general | solution.py:293
  46.8 3.2 %fusion.1 = f32[32,2,8]{0,2,1:T(8,128)S(1)} fusion(f32[2048,32,2,8]{0,1,3,2:T(8,128)} %get-tuple-element.63, f32[32,2,8]{0,2,1:T(8,128)S(1)} %max.7), kind=kLoop, calls=%fused_computation.3 | loop fusion | flops 3145216 | bytes 4198400 | tf_op jit(solution)/shard_map/reduce_sum | solution.py:306
  50.0 2.1 %fusion.5 = f32[32,2,8,128]{3,2,1,0:T(8,128)S(1)} fusion(bf16[32,256,128]{2,1,0:T(8,128)(2,1)} %get-tuple-element.15, f32[32,2,8,256]{3,2,1,0:T(8,128)S(1)} %get-tuple-element.65, f32[32,2,8]{2,1,0:T(2,128)S(1)} %copy.40), kind=kOutput, calls=%fused_computation.6 | convolution fusion | flops 33816576 | bytes 2885632 | tf_op jit(solution)/shard_map/pshl,pld->pshd/dot_general | solution.py:312
  53.2 15.2 %psum.7 = f32[32]{0:T(128)S(1)} all-reduce(f32[32]{0:T(128)S(1)} %get-tuple-element.40), channel_id=1, replica_groups=mesh['particle'=32,'tensor'=8] {'tensor'}, use_global_device_ids=true, to_apply=%region_7.8 | all-reduce | flops 32 | bytes 256 | tf_op jit(solution)/shard_map/psum | solution.py:322
  69.9 1.7 %collective-permute-start.8 = (f32[2,3,32]{2,1,0:T(4,128)S(1)}, f32[2,3,32]{2,1,0:T(4,128)S(1)}, u32[]{:S(2)}, u32[]{:S(2)}) collective-permute-start(f32[2,3,32]{2,1,0:T(4,128)S(1)} %pad_maximum_fusion.1), channel_id=1, source_target_pairs={{0,64},{8,72},{16,80},{24,88},{32,96},{40,104},{48,112},{56,120},{... | collective-permute-start | bytes 2312 | tf_op jit(solution)/shard_map/ppermute | solution.py:240
  71.6 2.8 %collective-permute-start.9 = (f32[2,3,32]{2,1,0:T(4,128)S(1)}, f32[2,3,32]{2,1,0:T(4,128)S(1)}, u32[]{:S(2)}, u32[]{:S(2)}) collective-permute-start(f32[2,3,32]{2,1,0:T(4,128)S(1)} %pad_maximum_fusion.1), channel_id=1, source_target_pairs={{0,128},{8,136},{16,144},{24,152},{32,160},{40,168},{48,176},{56,1... | collective-permute-start | bytes 2312 | tf_op jit(solution)/shard_map/ppermute | solution.py:240
  74.4 1.4 collective-permute-start.10
  75.8 47.4 %collective-permute-done.8 = f32[2,3,32]{2,1,0:T(4,128)S(1)} collective-permute-done((f32[2,3,32]{2,1,0:T(4,128)S(1)}, f32[2,3,32]{2,1,0:T(4,128)S(1)}, u32[]{:S(2)}, u32[]{:S(2)}) %collective-permute-start.8) | collective-permute-done | bytes 800 | tf_op jit(solution)/shard_map/ppermute | solution.py:240
  123.2 3.9 %collective-permute-done.9 = f32[2,3,32]{2,1,0:T(4,128)S(1)} collective-permute-done((f32[2,3,32]{2,1,0:T(4,128)S(1)}, f32[2,3,32]{2,1,0:T(4,128)S(1)}, u32[]{:S(2)}, u32[]{:S(2)}) %collective-permute-start.9) | collective-permute-done | bytes 800 | tf_op jit(solution)/shard_map/ppermute | solution.py:240
  127.1 3.4 %collective-permute-done.10 = f32[2,3,32]{2,1,0:T(4,128)S(1)} collective-permute-done((f32[2,3,32]{2,1,0:T(4,128)S(1)}, f32[2,3,32]{2,1,0:T(4,128)S(1)}, u32[]{:S(2)}, u32[]{:S(2)}) %collective-permute-start.10) | collective-permute-done | bytes 800 | tf_op jit(solution)/shard_map/ppermute | solution.py:240
  130.5 1.4 collective-permute-start.12
  131.9 1.8 %collective-permute-start.13 = (f32[8,3,32]{2,1,0:T(4,128)S(1)}, f32[8,3,32]{2,1,0:T(4,128)S(1)}, u32[]{:S(2)}, u32[]{:S(2)}) collective-permute-start(f32[8,3,32]{2,1,0:T(4,128)S(1)} %constant_dynamic-update-slice_fusion.19._.refs_0_), channel_id=1, source_target_pairs={{0,48},{8,56},{16,0},{24,8},{32,16},{40,24},{48,32},{56,40},{64,11... | collective-permute-start | bytes 9224 | tf_op jit(solution)/shard_map/ppermute | solution.py:240
  135.0 3.8 %all-to-all-done.arrived = bf16[64,512,128]{2,1,0:T(8,128)(2,1)} async-done(((bf16[64,512,128]{2,1,0:T(8,128)(2,1)}), bf16[64,512,128]{2,1,0:T(8,128)(2,1)}, u32[]{:S(2)}, u32[]{:S(2)}) %all-to-all-start) | async-done | bytes 8388640 | tf_op jit(solution)/shard_map/all_to_all | solution.py:287
  138.9 5.5 %unpack.1 = (bf16[32,256,128]{2,1,0:T(8,128)(2,1)}, bf16[32,256,128]{2,1,0:T(8,128)(2,1)}, f32[1,128]{1,0:T(1,128)}) custom-call(s32[32]{0:T(128)} %fusion.41.slots, bf16[64,512,128]{2,1,0:T(8,128)(2,1)} %all-to-all-done.arrived, f32[8,3,32]{2,1,0:T(4,128)} %copy-done.10), custom_call_target="tpu_custom_call" | custom-call | tf_op jit(solution)/shard_map/unpack/pallas_call | solution.py:182
  145.0 1.5 %finish.1 = (f32[1,32]{1,0:T(1,128)}, s32[1,32]{1,0:T(1,128)}) custom-call(f32[1,32]{1,0:T(1,128)} %pad_bitcast_fusion.2.counted, s32[1,32]{1,0:T(1,128)} %get-tuple-element.38.step, s32[1,32]{1,0:T(1,128)} %get-tuple-element.36.place, f32[8,3,32]{2,1,0:T(4,128)} %copy-done.10, f32[8,3,32]{2,1,0:T(4,128)} %copy-done.11, f32[8,3,32]{2,1,0:T(4,128)} %copy-done.12, ...), custom_call_target="tpu_custom_call" | custom-call | tf_op jit(solution)/shard_map/finish/pallas_call | solution.py:216
  (97 shorter events, 21.7 us)
Async XLA Ops:
  3.3 5.8 %collective-permute-start = (bf16[64,256]{1,0:T(8,128)(2,1)S(1)}, bf16[64,256]{1,0:T(8,128)(2,1)S(1)}, u32[]{:S(2)}, u32[]{:S(2)}) collective-permute-start(bf16[64,256]{1,0:T(8,128)(2,1)S(1)} %get-tuple-element.56), channel_id=1, source_target_pairs={{0,64},{8,72},{16,80},{24,88},{32,96},{40,104},{48,112},{56,120},{... | collective-permute-start | bytes 98312 | tf_op jit(solution)/shard_map/ppermute | solution.py:240
  4.9 5.4 %collective-permute-start.1 = (bf16[64,256]{1,0:T(8,128)(2,1)S(1)}, bf16[64,256]{1,0:T(8,128)(2,1)S(1)}, u32[]{:S(2)}, u32[]{:S(2)}) collective-permute-start(bf16[64,256]{1,0:T(8,128)(2,1)S(1)} %get-tuple-element.56), channel_id=1, source_target_pairs={{0,128},{8,136},{16,144},{24,152},{32,160},{40,168},{48,176},{56,1... | collective-permute-start | bytes 98312 | tf_op jit(solution)/shard_map/ppermute | solution.py:240
  7.8 3.9 %collective-permute-start.2 = (bf16[64,256]{1,0:T(8,128)(2,1)S(1)}, bf16[64,256]{1,0:T(8,128)(2,1)S(1)}, u32[]{:S(2)}, u32[]{:S(2)}) collective-permute-start(bf16[64,256]{1,0:T(8,128)(2,1)S(1)} %get-tuple-element.56), channel_id=1, source_target_pairs={{0,192},{8,200},{16,208},{24,216},{32,224},{40,232},{48,240},{56,2... | collective-permute-start | bytes 98312 | tf_op jit(solution)/shard_map/ppermute | solution.py:240
  11.7 15.4 %collective-permute-start.3 = (bf16[256,256]{1,0:T(8,128)(2,1)S(1)}, bf16[256,256]{1,0:T(8,128)(2,1)S(1)}, u32[]{:S(2)}, u32[]{:S(2)}) collective-permute-start(bf16[256,256]{1,0:T(8,128)(2,1)S(1)} %pad_maximum_fusion), channel_id=1, source_target_pairs={{0,16},{8,24},{16,32},{24,40},{32,48},{40,56},{48,0},{56,8},{64,80... | collective-permute-start | bytes 393224 | tf_op jit(solution)/shard_map/ppermute | solution.py:240
  13.3 13.8 %collective-permute-start.4 = (bf16[256,256]{1,0:T(8,128)(2,1)S(1)}, bf16[256,256]{1,0:T(8,128)(2,1)S(1)}, u32[]{:S(2)}, u32[]{:S(2)}) collective-permute-start(bf16[256,256]{1,0:T(8,128)(2,1)S(1)} %pad_maximum_fusion), channel_id=1, source_target_pairs={{0,32},{8,40},{16,48},{24,56},{32,0},{40,8},{48,16},{56,24},{64,96... | collective-permute-start | bytes 393224 | tf_op jit(solution)/shard_map/ppermute | solution.py:240
  16.0 11.1 %collective-permute-start.5 = (bf16[256,256]{1,0:T(8,128)(2,1)S(1)}, bf16[256,256]{1,0:T(8,128)(2,1)S(1)}, u32[]{:S(2)}, u32[]{:S(2)}) collective-permute-start(bf16[256,256]{1,0:T(8,128)(2,1)S(1)} %pad_maximum_fusion), channel_id=1, source_target_pairs={{0,48},{8,56},{16,0},{24,8},{32,16},{40,24},{48,32},{56,40},{64,11... | collective-permute-start | bytes 393224 | tf_op jit(solution)/shard_map/ppermute | solution.py:240
  27.8 6.4 %copy-start.14 = (s32[1024]{0:T(1024)S(1)}, s32[1024]{0:T(1024)}, u32[]{:S(2)}) copy-start(s32[1024]{0:T(1024)} %param.22) | copy-start | bytes 12292
  27.8 9.7 %copy-start.7 = (bf16[256,256]{1,0:T(8,128)(2,1)S(1)}, bf16[256,256]{1,0:T(8,128)(2,1)}, u32[]{:S(2)}) copy-start(bf16[256,256]{1,0:T(8,128)(2,1)} %copy-done.6) | copy-start | bytes 393220
  27.8 10.4 %copy-start.5 = (bf16[256,256]{1,0:T(8,128)(2,1)S(1)}, bf16[256,256]{1,0:T(8,128)(2,1)}, u32[]{:S(2)}) copy-start(bf16[256,256]{1,0:T(8,128)(2,1)} %copy-done.4) | copy-start | bytes 393220
  27.9 111.0 %all-to-all-start = ((bf16[64,512,128]{2,1,0:T(8,128)(2,1)}), bf16[64,512,128]{2,1,0:T(8,128)(2,1)}, u32[]{:S(2)}, u32[]{:S(2)}) async-start(bf16[64,512,128]{2,1,0:T(8,128)(2,1)} %after.1), calls=%async_computation | async-start | bytes 16777216 | tf_op jit(solution)/shard_map/all_to_all | solution.py:287
  33.0 6.0 %copy-start.3 = (bf16[256,256]{1,0:T(8,128)(2,1)S(1)}, bf16[256,256]{1,0:T(8,128)(2,1)}, u32[]{:S(2)}) copy-start(bf16[256,256]{1,0:T(8,128)(2,1)} %copy-done.2) | copy-start | bytes 393220
  39.7 2.1 %collective-permute-start.6 = (bf16[1024,256]{1,0:T(8,128)(2,1)}, bf16[1024,256]{1,0:T(8,128)(2,1)S(1)}, u32[]{:S(2)}, u32[]{:S(2)}) collective-permute-start(bf16[1024,256]{1,0:T(8,128)(2,1)} %get-tuple-element.42), channel_id=1, source_target_pairs={{0,8},{8,0},{16,24},{24,16},{32,40},{40,32},{48,56},{56,48},{64,72... | collective-permute-start | bytes 1572872 | tf_op jit(solution)/shard_map/ppermute | solution.py:240
  46.4 5.7 %copy-start.8 = (bf16[2048,256]{1,0:T(8,128)(2,1)S(1)}, bf16[2048,256]{1,0:T(8,128)(2,1)}, u32[]{:S(2)}) copy-start(bf16[2048,256]{1,0:T(8,128)(2,1)} %constant_dynamic-update-slice_fusion.10) | copy-start | bytes 3145732
  46.4 5.7 %copy-start.17 = (f32[1024]{0:T(1024)S(1)}, f32[1024]{0:T(1024)}, u32[]{:S(2)}) copy-start(f32[1024]{0:T(1024)} %param.21) | copy-start | bytes 12292
  50.0 18.3 %copy-start.18 = (f32[32]{0:T(128)S(1)}, f32[32]{0:T(128)}, u32[]{:S(2)}) copy-start(f32[32]{0:T(128)} %param.20) | copy-start | bytes 388
  68.3 76.0 %copy-start.16 = (f32[32]{0:T(128)}, f32[32]{0:T(128)S(1)}, u32[]{:S(2)}) copy-start(f32[32]{0:T(128)S(1)} %add.112) | copy-start | bytes 388
  68.7 1.2 collective-permute-start.7
  69.9 53.3 %collective-permute-start.8 = (f32[2,3,32]{2,1,0:T(4,128)S(1)}, f32[2,3,32]{2,1,0:T(4,128)S(1)}, u32[]{:S(2)}, u32[]{:S(2)}) collective-permute-start(f32[2,3,32]{2,1,0:T(4,128)S(1)} %pad_maximum_fusion.1), channel_id=1, source_target_pairs={{0,64},{8,72},{16,80},{24,88},{32,96},{40,104},{48,112},{56,120},{... | collective-permute-start | bytes 2312 | tf_op jit(solution)/shard_map/ppermute | solution.py:240
  71.6 55.5 %collective-permute-start.9 = (f32[2,3,32]{2,1,0:T(4,128)S(1)}, f32[2,3,32]{2,1,0:T(4,128)S(1)}, u32[]{:S(2)}, u32[]{:S(2)}) collective-permute-start(f32[2,3,32]{2,1,0:T(4,128)S(1)} %pad_maximum_fusion.1), channel_id=1, source_target_pairs={{0,128},{8,136},{16,144},{24,152},{32,160},{40,168},{48,176},{56,1... | collective-permute-start | bytes 2312 | tf_op jit(solution)/shard_map/ppermute | solution.py:240
  74.4 56.1 %collective-permute-start.10 = (f32[2,3,32]{2,1,0:T(4,128)S(1)}, f32[2,3,32]{2,1,0:T(4,128)S(1)}, u32[]{:S(2)}, u32[]{:S(2)}) collective-permute-start(f32[2,3,32]{2,1,0:T(4,128)S(1)} %pad_maximum_fusion.1), channel_id=1, source_target_pairs={{0,192},{8,200},{16,208},{24,216},{32,224},{40,232},{48,240},{56,2... | collective-permute-start | bytes 2312 | tf_op jit(solution)/shard_map/ppermute | solution.py:240
  130.5 8.4 %copy-start.10 = (f32[8,3,32]{2,1,0:T(4,128)}, f32[8,3,32]{2,1,0:T(4,128)S(1)}, u32[]{:S(2)}) copy-start(f32[8,3,32]{2,1,0:T(4,128)S(1)} %constant_dynamic-update-slice_fusion.19._.refs_0_) | copy-start | bytes 9220
  130.5 13.8 %collective-permute-start.11 = (f32[8,3,32]{2,1,0:T(4,128)S(1)}, f32[8,3,32]{2,1,0:T(4,128)S(1)}, u32[]{:S(2)}, u32[]{:S(2)}) collective-permute-start(f32[8,3,32]{2,1,0:T(4,128)S(1)} %constant_dynamic-update-slice_fusion.19._.refs_0_), channel_id=1, source_target_pairs={{0,16},{8,24},{16,32},{24,40},{32,48},{40,56},{48,0},{56,8},{64,80... | collective-permute-start | bytes 9224 | tf_op jit(solution)/shard_map/ppermute | solution.py:240
  130.5 13.8 %collective-permute-start.12 = (f32[8,3,32]{2,1,0:T(4,128)S(1)}, f32[8,3,32]{2,1,0:T(4,128)S(1)}, u32[]{:S(2)}, u32[]{:S(2)}) collective-permute-start(f32[8,3,32]{2,1,0:T(4,128)S(1)} %constant_dynamic-update-slice_fusion.19._.refs_0_), channel_id=1, source_target_pairs={{0,32},{8,40},{16,48},{24,56},{32,0},{40,8},{48,16},{56,24},{64,96... | collective-permute-start | bytes 9224 | tf_op jit(solution)/shard_map/ppermute | solution.py:240
  131.9 12.4 %collective-permute-start.13 = (f32[8,3,32]{2,1,0:T(4,128)S(1)}, f32[8,3,32]{2,1,0:T(4,128)S(1)}, u32[]{:S(2)}, u32[]{:S(2)}) collective-permute-start(f32[8,3,32]{2,1,0:T(4,128)S(1)} %constant_dynamic-update-slice_fusion.19._.refs_0_), channel_id=1, source_target_pairs={{0,48},{8,56},{16,0},{24,8},{32,16},{40,24},{48,32},{56,40},{64,11... | collective-permute-start | bytes 9224 | tf_op jit(solution)/shard_map/ppermute | solution.py:240
  (10 other events, 25.1 us)

commit v4 on v3

--- a/solution.py
+++ b/solution.py
@@ -1,3 +1,4 @@
+import functools
 import itertools
 
 import jax
@@ -28,46 +29,32 @@
     lax.fori_loop(0, count, step, 0, unroll=4)
 
 
-def pack_kernel(
-    lengths,
-    least,
-    most,
-    keys,
-    values,
-    new_keys,
-    new_values,
-    packed,
-    written_keys,
-    written_values,
-    held,
-    in_sems,
-    out_sems,
-    low_sems,
-    high_sems,
-):
-    count, suffix, _ = keys.shape
+def pack_kernel(keeps, lengths, least, most, *refs):
+    number = (len(refs) - 5) // (2 + keeps)
+    caches, fresh, (packed, *written) = refs[:number], refs[number : 2 * number], refs[2 * number : -4]
+    held, in_sems, out_sems, send_sems = refs[-4:]
+    count, suffix, _ = caches[0].shape
     goals = least.shape[0]
     share = count // CHUNKS
-    parts = ((keys, new_keys, written_keys), (values, new_values, written_values))
-
-    def load(chunk, half):
+
+    def load(chunk, n):
         rows = pl.ds(chunk * share, share)
         return pltpu.make_async_copy(
-            parts[half][0].at[rows],
-            held.at[rows, pl.ds(half * suffix, suffix)],
-            in_sems.at[chunk * 2 + half],
+            caches[n].at[rows], held.at[n, rows], in_sems.at[chunk * number + n]
         )
 
-    def keep(half):
+    def keep(n):
+        return pltpu.make_async_copy(held.at[n], written[n], out_sems.at[n])
+
+    def low(d):
         return pltpu.make_async_copy(
-            held.at[:, pl.ds(half * suffix, suffix)], parts[half][2], out_sems.at[half]
+            held.at[number - 1, least[d]], packed.at[2 * d], send_sems.at[2 * d]
         )
 
-    def low(d):
-        return pltpu.make_async_copy(held.at[least[d]], packed.at[2 * d], low_sems.at[d])
-
     def high(d):
-        return pltpu.make_async_copy(held.at[most[d]], packed.at[2 * d + 1], high_sems.at[d])
+        return pltpu.make_async_copy(
+            held.at[number - 1, most[d]], packed.at[2 * d + 1], send_sems.at[2 * d + 1]
+        )
 
     def patch(group):
         found = []
@@ -75,10 +62,10 @@
             p = group * GROUP + i
             length = lengths[p]
             base = pl.multiple_of(jnp.minimum(length // 16 * 16, suffix - WINDOW), 16)
-            for half in range(2):
-                place = (p, pl.ds(base + half * suffix, WINDOW))
+            for n in range(number):
+                place = (n, p, pl.ds(base, WINDOW))
                 block = held[place].astype(jnp.float32)
-                lines = parts[half][1][p].astype(jnp.float32)
+                lines = fresh[n][p].astype(jnp.float32)
                 row = lax.broadcasted_iota(jnp.int32, block.shape, 0) + base
                 for offset in range(STEPS):
                     block = jnp.where(row == length + offset, lines[offset : offset + 1], block)
@@ -87,20 +74,19 @@
             held[place] = block
 
     for chunk in range(CHUNKS):
-        for half in range(2):
-            load(chunk, half).start()
+        for n in range(number):
+            load(chunk, n).start()
     for chunk in range(CHUNKS):
-        for half in range(2):
-            load(chunk, half).wait()
-        repeat(share // GROUP, lambda g, chunk=chunk: patch(g + chunk * (share // GROUP)), 1)
-    repeat(goals, lambda d: low(d).start())
-    repeat(goals, lambda d: high(d).start())
-    keep(0).start()
-    keep(1).start()
-    repeat(goals, lambda d: low(d).wait())
-    repeat(goals, lambda d: high(d).wait())
-    keep(0).wait()
-    keep(1).wait()
+        for n in range(number):
+            load(chunk, n).wait()
+        groups = share // GROUP
+        repeat(groups, lambda g, chunk=chunk: patch(g + chunk * groups), 1)
+    repeat(goals, lambda d: (low(d).start(), high(d).start()))
+    for n in range(number * keeps):
+        keep(n).start()
+    repeat(goals, lambda d: (low(d).wait(), high(d).wait()))
+    for n in range(number * keeps):
+        keep(n).wait()
 
 
 def repeat(count, body, unroll=4):
@@ -111,29 +97,26 @@
     lax.fori_loop(0, count, step, 0, unroll=unroll)
 
 
-def pack(keys, values, new_keys, new_values, lengths, least, most):
-    (count, suffix, width), goals = keys.shape, least.shape[0]
+def pack(caches, fresh, lengths, least, most, keeps):
+    cache, number = caches[0], len(caches)
+    count, goals = cache.shape[0], least.shape[0]
     smem = pl.BlockSpec(memory_space=pltpu.SMEM)
     hbm = pl.BlockSpec(memory_space=pltpu.HBM)
     vmem = pl.BlockSpec(memory_space=pltpu.VMEM)
     return pl.pallas_call(
-        pack_kernel,
-        out_shape=(
-            jax.ShapeDtypeStruct((goals * DISTINCT, 2 * suffix, width), keys.dtype),
-            jax.ShapeDtypeStruct(keys.shape, keys.dtype),
-            jax.ShapeDtypeStruct(values.shape, values.dtype),
-        ),
-        in_specs=[smem, smem, smem, hbm, hbm, vmem, vmem],
-        out_specs=(hbm, hbm, hbm),
+        functools.partial(pack_kernel, keeps),
+        out_shape=[jax.ShapeDtypeStruct((goals * DISTINCT,) + cache.shape[1:], cache.dtype)]
+        + [jax.ShapeDtypeStruct(cache.shape, cache.dtype)] * (number * keeps),
+        in_specs=[smem] * 3 + [hbm] * number + [vmem] * number,
+        out_specs=[hbm] * (1 + number * keeps),
         scratch_shapes=[
-            pltpu.VMEM((count, 2 * suffix, width), keys.dtype),
-            pltpu.SemaphoreType.DMA((2 * CHUNKS,)),
-            pltpu.SemaphoreType.DMA((2,)),
-            pltpu.SemaphoreType.DMA((goals,)),
-            pltpu.SemaphoreType.DMA((goals,)),
+            pltpu.VMEM((number,) + cache.shape, cache.dtype),
+            pltpu.SemaphoreType.DMA((number * CHUNKS,)),
+            pltpu.SemaphoreType.DMA((number,)),
+            pltpu.SemaphoreType.DMA((goals * DISTINCT,)),
         ],
         name="pack",
-    )(lengths, least, most, keys, values, new_keys, new_values)
+    )(lengths, least, most, *caches, *fresh)
 
 
 def after(array, *others):
@@ -149,45 +132,42 @@
     )(array, *others)
 
 
-def unpack_kernel(slots, arrived, _, next_keys, next_values, mark, held, in_sems, out_sems):
-    count, suffix, _ = next_keys.shape
+def unpack_kernel(slots, arrived, _, result, mark, held, in_sems, out_sems):
+    count = result.shape[0]
     share = count // CHUNKS
 
     def load(p):
         return pltpu.make_async_copy(arrived.at[slots[p]], held.at[p], in_sems.at[p])
 
-    def keep(chunk, half):
+    def keep(chunk):
         rows = pl.ds(chunk * share, share)
-        return pltpu.make_async_copy(
-            held.at[rows, pl.ds(half * suffix, suffix)],
-            (next_keys, next_values)[half].at[rows],
-            out_sems.at[chunk * 2 + half],
-        )
+        return pltpu.make_async_copy(held.at[rows], result.at[rows], out_sems.at[chunk])
 
     mark[...] = jnp.zeros_like(mark)
     repeat(count, lambda p: load(p).start())
     for chunk in range(CHUNKS):
         repeat(share, lambda p, chunk=chunk: load(p + chunk * share).wait())
-        for half in range(2):
-            keep(chunk, half).start()
+        keep(chunk).start()
     for chunk in range(CHUNKS):
-        for half in range(2):
-            keep(chunk, half).wait()
+        keep(chunk).wait()
 
 
 def unpack(arrived, slots, other):
-    count, (_, length, width) = slots.shape[0], arrived.shape
+    count, (_, suffix, width) = slots.shape[0], arrived.shape
     hbm = pl.BlockSpec(memory_space=pltpu.HBM)
-    shape = jax.ShapeDtypeStruct((count, length // 2, width), arrived.dtype)
+    shape = (count, suffix, width)
     return pl.pallas_call(
         unpack_kernel,
-        out_shape=(shape, shape, jax.ShapeDtypeStruct((1, width), jnp.float32)),
+        out_shape=(
+            jax.ShapeDtypeStruct(shape, arrived.dtype),
+            jax.ShapeDtypeStruct((1, width), jnp.float32),
+        ),
         in_specs=[pl.BlockSpec(memory_space=pltpu.SMEM), hbm, pl.BlockSpec(memory_space=pl.ANY)],
-        out_specs=(hbm, hbm, pl.BlockSpec(memory_space=pltpu.VMEM)),
+        out_specs=(hbm, pl.BlockSpec(memory_space=pltpu.VMEM)),
         scratch_shapes=[
-            pltpu.VMEM((count, length, width), arrived.dtype),
+            pltpu.VMEM(shape, arrived.dtype),
             pltpu.SemaphoreType.DMA((count,)),
-            pltpu.SemaphoreType.DMA((2 * CHUNKS,)),
+            pltpu.SemaphoreType.DMA((CHUNKS,)),
         ],
         name="unpack",
     )(slots, arrived, other)
@@ -199,7 +179,7 @@
     peaks, sums, filled = shared[:, 0], shared[:, 1], shared[:, 2]
     top = jnp.max(peaks, axis=0, keepdims=True)
     summed = jnp.sum(sums * jnp.exp(peaks - top), axis=0, keepdims=True)
-    rung_means[...] = top + jnp.log(summed) - jnp.log(counted[...])
+    rung_means[...] = (top + jnp.log(summed) - jnp.log(counted[...]))[:, :RUNGS]
     order = lax.broadcasted_iota(jnp.int32, filled.shape, 0)
     owner = (order == step[...]).astype(jnp.float32)
     found = lax.dot_general(
@@ -212,12 +192,11 @@
 
 def finish(parts, counted, step, place, other):
     vmem = pl.BlockSpec(memory_space=pltpu.VMEM)
-    row = (1, step.shape[1])
     return pl.pallas_call(
         finish_kernel,
         out_shape=(
-            jax.ShapeDtypeStruct(row, jnp.float32),
-            jax.ShapeDtypeStruct(row, jnp.int32),
+            jax.ShapeDtypeStruct((1, RUNGS), jnp.float32),
+            jax.ShapeDtypeStruct(step.shape, jnp.int32),
         ),
         in_specs=[vmem] * (3 + len(parts)) + [pl.BlockSpec(memory_space=pl.ANY)],
         out_specs=(vmem, vmem),
@@ -264,8 +243,8 @@
 
     shard = jnp.concatenate([prompt_keys, prompt_values], axis=1)
     column = jnp.concatenate(along(shard, (0,)), axis=0)
-    columns = along(column, (1,))
-    prompt = jnp.concatenate(along(jnp.concatenate(columns, axis=0), (2,)), axis=0)
+    plane = jnp.concatenate(along(column, (1,)), axis=0)
+    prompt = jnp.concatenate(along(plane, (2,)), axis=0)
     all_keys = prompt[:, :HEAD_DIM]
     all_values = prompt[:, HEAD_DIM:]
 
@@ -281,12 +260,17 @@
     first = jnp.min(jnp.where(same_owner, mine[None, :], sources * per_device), axis=1)
     slot = mine_owner * DISTINCT + (mine != first).astype(jnp.int32)
 
-    outgoing, written_keys, written_values = pack(
-        key_cache, value_cache, new_keys, new_values, lengths, least, most
-    )
-    arrived = lax.all_to_all(
-        after(outgoing, *columns[1:]), "particle", split_axis=0, concat_axis=0, tiled=True
-    )
+    exchange = functools.partial(
+        lax.all_to_all, axis_name="particle", split_axis=0, concat_axis=0, tiled=True
+    )
+    places = (lengths, least, most)
+    (outgoing_keys,) = pack((key_cache,), (new_keys,), *places, False)
+    arrived_keys = exchange(after(outgoing_keys, column))
+    outgoing_values, written_keys, written_values = pack(
+        (key_cache, value_cache), (new_keys, new_values), *places, True
+    )
+    arrived_values = exchange(after(outgoing_values, arrived_keys))
+    next_keys, mark = unpack(arrived_keys, slot, column)
 
     query = queries.reshape(per_device, STEPS, groups, HEAD_DIM)
     front = (
@@ -332,13 +316,13 @@
         [
             jnp.pad(local_peak, (0, spare)),
             jnp.pad(local_sum, (0, spare), constant_values=1.0),
-            lengths.astype(jnp.float32),
+            lengths.astype(jnp.float32) + mark[0, :per_device],
         ]
     )[None]
     near = jnp.concatenate(along(shared, (2,)), axis=0)
     near = jnp.concatenate(along(near, (0,)), axis=0)
     parts = along(near, (1,))
-    next_keys, next_values, mark = unpack(arrived, slot, near)
+    next_values, mark = unpack(arrived_values, slot, near)
 
     counted = jnp.sum((rungs[:, None] == ladder[None, :]).astype(jnp.float32), axis=0)
     tall, wide, cores = SIDES
@@ -353,7 +337,7 @@
         (mine % per_device)[None],
         mark,
     )
-    rung_means = rung_means[0, :RUNGS]
+    rung_means = rung_means[0]
     next_lengths = next_lengths[0]
     return (attention, weights, rung_means, next_keys, next_values, next_lengths)
 

time: 148 us -> 143 us (0.966)
  waiting for transfers between devices: 63 us -> 45.6 us
  starting transfers between devices: 25.9 us -> 37.4 us
  local copies, waits for them, and re-layouts: 12.5 us -> 4.62 us
  Pallas kernels: 15.2 us -> 21.3 us
    ppermute x14, waiting for transfers between devices: 59.2 us -> 9.44 us  [along(): lax.ppermute(array, 'particle', pairs)]
    all_to_all x1 -> x2, waiting for transfers between devices: 3.85 us -> 36.2 us  [the longest x1 36.2 us: shards(): arrived_keys = exchange(after(outgoing_keys, column))]
    pallas_call x3 -> x5, Pallas kernels: 15.2 us -> 21.3 us  [the longest x2 11.9 us: pack(): pl.pallas_call(functools.partial(pack_kernel, keeps), out_shape=[jax.Shap...]
    all_to_all x1 -> x2, starting transfers between devices: 5.12 us -> 11 us  [the longest x1 5.93 us: shards(): arrived_values = exchange(after(outgoing_values, arrived_keys))]
    ppermute x14, starting transfers between devices: 20.8 us -> 26.4 us  [along(): lax.ppermute(array, 'particle', pairs)]
    unnamed x50 -> x36, local copies, waits for them, and re-layouts: 8.09 us -> 2.92 us
    dot_general x1, matrix products: 0.76 us -> 2.35 us  [shards(): jnp.einsum('pshd,pld->pshl', query, written_keys, preferred_element_type=...]
    concatenate x2, local copies, waits for them, and re-layouts: 1.55 us -> 0.05 us  [the longest x1 0.03 us: shards(): prompt = jnp.concatenate(along(plane, (2,)), axis=0)]
  transfers between devices with their start and end apart: 15 -> 16, of which waited for: 8 -> 5; matrix products, arithmetic and copies ran while one was open for 15% -> 13% of each run, Pallas kernels for 9% -> 14%
where the time goes in v4:
time: 143 us; the launch traced here: 142 us
  waiting for transfers between devices  45.6 us (32%)
  starting transfers between devices  37.4 us (26%)
  Pallas kernels  21.3 us (15%)
  blocking collectives  15.2 us (11%)
  other arithmetic  8.66 us (6%)
  matrix products  8.09 us (6%)
  local copies, waits for them, and re-layouts  4.62 us (3%)
    all_to_all x1, waiting for transfers between devices, shards(): arrived_keys = exchange(after(outgoing_keys, column))  36.2 us
    ppermute x14, starting transfers between devices, along(): lax.ppermute(array, 'particle', pairs)  26.4 us
    psum x1, blocking collectives, shards(): weights = prior + lax.psum(partial_reward, 'tensor')  15.2 us
    pallas_call x2, Pallas kernels, pack(): pl.pallas_call(functools.partial(pack_kernel, keeps), out_shape=[jax.Shap...  11.9 us
    ppermute x14, waiting for transfers between devices, along(): lax.ppermute(array, 'particle', pairs)  9.44 us
    pallas_call x2, Pallas kernels, unpack(): pl.pallas_call(unpack_kernel, out_shape=(jax.ShapeDtypeStruct(shape, arri...  7.96 us
    all_to_all x1, starting transfers between devices, shards(): arrived_values = exchange(after(outgoing_values, arrived_keys))  5.93 us
    all_to_all x1, starting transfers between devices, shards(): arrived_keys = exchange(after(outgoing_keys, column))  5.06 us
  transfers between devices with their start and end apart: 16, of which 5 were waited for; matrix products, arithmetic and copies ran while one was open for 13% of the time, Pallas kernels for 14%

profile of v4, /device:TPU:128, one launch (start us, length us, event | category | flops | bytes accessed | tf_op | source)
XLA Modules:
  0.0 141.9 jit_solution(6825088736924216626)
XLA Ops:
  2.1 1.7 %collective-permute-start = (bf16[64,256]{1,0:T(8,128)(2,1)S(1)}, bf16[64,256]{1,0:T(8,128)(2,1)S(1)}, u32[]{:S(2)}, u32[]{:S(2)}) collective-permute-start(bf16[64,256]{1,0:T(8,128)(2,1)S(1)} %get-tuple-element.58), channel_id=1, source_target_pairs={{0,64},{8,72},{16,80},{24,88},{32,96},{40,104},{48,112},{56,120},{... | collective-permute-start | bytes 98312 | tf_op jit(solution)/shard_map/ppermute | solution.py:219
  3.7 2.9 %collective-permute-start.1 = (bf16[64,256]{1,0:T(8,128)(2,1)S(1)}, bf16[64,256]{1,0:T(8,128)(2,1)S(1)}, u32[]{:S(2)}, u32[]{:S(2)}) collective-permute-start(bf16[64,256]{1,0:T(8,128)(2,1)S(1)} %get-tuple-element.58), channel_id=1, source_target_pairs={{0,128},{8,136},{16,144},{24,152},{32,160},{40,168},{48,176},{56,1... | collective-permute-start | bytes 98312 | tf_op jit(solution)/shard_map/ppermute | solution.py:219
  9.4 4.9 %pack.3.refs_0_ = bf16[64,256,128]{2,1,0:T(8,128)(2,1)} custom-call(s32[32]{0:T(128)} %lengths.3, s32[32]{0:T(128)} %get-tuple-element.37.least, s32[32]{0:T(128)} %get-tuple-element.36.most, bf16[32,256,128]{2,1,0:T(8,128)(2,1)} %refs_0_.3, bf16[32,2,128]{2,1,0:T(2,128)(2,1)} %refs_1_.3), custom_call_target="tpu_custom_call" | custom-call | tf_op jit(solution)/shard_map/pack/pallas_call | solution.py:106
  15.0 5.1 %all-to-all-start = ((bf16[64,256,128]{2,1,0:T(8,128)(2,1)}), bf16[64,256,128]{2,1,0:T(8,128)(2,1)}, u32[]{:S(2)}, u32[]{:S(2)}) async-start(bf16[64,256,128]{2,1,0:T(8,128)(2,1)} %after.2), calls=%async_computation | async-start | bytes 8388608 | tf_op jit(solution)/shard_map/all_to_all | solution.py:268
  20.3 7.0 %pack.2 = (bf16[64,256,128]{2,1,0:T(8,128)(2,1)}, bf16[32,256,128]{2,1,0:T(8,128)(2,1)}, bf16[32,256,128]{2,1,0:T(8,128)(2,1)}) custom-call(s32[32]{0:T(128)} %lengths.3, s32[32]{0:T(128)} %get-tuple-element.37.least, s32[32]{0:T(128)} %get-tuple-element.36.most, bf16[32,256,128]{2,1,0:T(8,128)(2,1)} %refs_0_.3, bf16[32,256,128]{2,1,0:T(8,128)(2,1)} %refs_1_.2, ...), custom_call_target="tpu_custom_call" | custom-call | tf_op jit(solution)/shard_map/pack/pallas_call | solution.py:106
  27.4 2.3 %fusion.49 = (f32[32,2,8]{2,1,0:T(2,128)S(1)}, f32[32,2,8,256]{3,2,1,0:T(8,128)S(1)}) fusion(bf16[32,2,8,128]{3,2,1,0:T(8,128)(2,1)S(1)} %reshape.69, bf16[32,256,128]{2,1,0:T(8,128)(2,1)} %get-tuple-element.15, pred[32,2,256]{2,1,0:T(4,128)(4,1)S(1)} %iota_compare_fusion), kind=kOutput, calls=%fused_computation.117 | convolution fusion | flops 33947136 | bytes 2770944 | tf_op jit(solution)/shard_map/pshd,pld->pshl/dot_general | solution.py:280
  31.4 1.8 %collective-permute-start.3 = (bf16[256,256]{1,0:T(8,128)(2,1)S(1)}, bf16[256,256]{1,0:T(8,128)(2,1)S(1)}, u32[]{:S(2)}, u32[]{:S(2)}) collective-permute-start(bf16[256,256]{1,0:T(8,128)(2,1)S(1)} %copy-done.1), channel_id=1, source_target_pairs={{0,16},{8,24},{16,32},{24,40},{32,48},{40,56},{48,0},{56,8},{64,80... | collective-permute-start | bytes 393224 | tf_op jit(solution)/shard_map/ppermute | solution.py:219
  33.2 2.7 %collective-permute-start.4 = (bf16[256,256]{1,0:T(8,128)(2,1)S(1)}, bf16[256,256]{1,0:T(8,128)(2,1)S(1)}, u32[]{:S(2)}, u32[]{:S(2)}) collective-permute-start(bf16[256,256]{1,0:T(8,128)(2,1)S(1)} %copy-done.1), channel_id=1, source_target_pairs={{0,32},{8,40},{16,48},{24,56},{32,0},{40,8},{48,16},{56,24},{64,96... | collective-permute-start | bytes 393224 | tf_op jit(solution)/shard_map/ppermute | solution.py:219
  37.3 36.2 %all-to-all-done.arrived.refs_1_ = bf16[64,256,128]{2,1,0:T(8,128)(2,1)} async-done(((bf16[64,256,128]{2,1,0:T(8,128)(2,1)}), bf16[64,256,128]{2,1,0:T(8,128)(2,1)}, u32[]{:S(2)}, u32[]{:S(2)}) %all-to-all-start) | async-done | bytes 4194336 | tf_op jit(solution)/shard_map/all_to_all | solution.py:268
  73.5 5.9 %all-to-all-start.1 = ((bf16[64,256,128]{2,1,0:T(8,128)(2,1)}), bf16[64,256,128]{2,1,0:T(8,128)(2,1)}, u32[]{:S(2)}, u32[]{:S(2)}) async-start(bf16[64,256,128]{2,1,0:T(8,128)(2,1)} %after.3), calls=%async_computation.1 | async-start | bytes 8388608 | tf_op jit(solution)/shard_map/all_to_all | solution.py:272
  81.6 2.6 %bitcast_reduce_fusion = (f32[32,2,8]{0,2,1:T(8,128)S(1)}, f32[2048,32,2,8]{0,1,3,2:T(8,128)}) fusion(bf16[32,2,8,128]{3,2,1,0:T(8,128)(2,1)S(1)} %reshape.69, bf16[2048,256]{1,0:T(8,128)(2,1)S(1)} %constant_dynamic-update-slice_fusion.10), kind=kOutput, calls=%fused_computation.1 | convolution fusion | flops 270532096 | bytes 4851712 | tf_op jit(solution)/shard_map/pshd,nd->pshn/dot_general | solution.py:277
  84.7 3.2 %fusion.1 = f32[32,2,8]{0,2,1:T(8,128)S(1)} fusion(f32[2048,32,2,8]{0,1,3,2:T(8,128)} %get-tuple-element.63, f32[32,2,8]{0,2,1:T(8,128)S(1)} %max.7), kind=kLoop, calls=%fused_computation.3 | loop fusion | flops 3145216 | bytes 4198400 | tf_op jit(solution)/shard_map/reduce_sum | solution.py:290
  87.9 2.0 %fusion.5 = f32[32,2,8,128]{3,2,1,0:T(8,128)S(1)} fusion(bf16[32,256,128]{2,1,0:T(8,128)(2,1)} %get-tuple-element.16, f32[32,2,8,256]{3,2,1,0:T(8,128)S(1)} %get-tuple-element.65, f32[32,2,8]{2,1,0:T(2,128)S(1)} %copy.41), kind=kOutput, calls=%fused_computation.6 | convolution fusion | flops 33816576 | bytes 2885632 | tf_op jit(solution)/shard_map/pshl,pld->pshd/dot_general | solution.py:296
  91.0 15.2 %psum.7 = f32[32]{0:T(128)S(1)} all-reduce(f32[32]{0:T(128)S(1)} %get-tuple-element.42), channel_id=1, replica_groups=mesh['particle'=32,'tensor'=8] {'tensor'}, use_global_device_ids=true, to_apply=%region_7.8 | all-reduce | flops 32 | bytes 256 | tf_op jit(solution)/shard_map/psum | solution.py:306
  106.5 4.0 %unpack.2 = (bf16[32,256,128]{2,1,0:T(8,128)(2,1)}, f32[1,128]{1,0:T(1,128)}) custom-call(s32[32]{0:T(128)} %fusion.41.slots, bf16[64,256,128]{2,1,0:T(8,128)(2,1)} %all-to-all-done.arrived.refs_1_, bf16[256,256]{1,0:T(8,128)(2,1)} %pad_maximum_fusion.refs_1_._), custom_call_target="tpu_custom_call" | custom-call | tf_op jit(solution)/shard_map/unpack/pallas_call | solution.py:159
  112.5 2.0 %collective-permute-start.8 = (f32[2,3,32]{2,1,0:T(4,128)S(1)}, f32[2,3,32]{2,1,0:T(4,128)S(1)}, u32[]{:S(2)}, u32[]{:S(2)}) collective-permute-start(f32[2,3,32]{2,1,0:T(4,128)S(1)} %pad_maximum_fusion.1), channel_id=1, source_target_pairs={{0,64},{8,72},{16,80},{24,88},{32,96},{40,104},{48,112},{56,120},{... | collective-permute-start | bytes 2312 | tf_op jit(solution)/shard_map/ppermute | solution.py:219
  114.4 2.7 %collective-permute-start.9 = (f32[2,3,32]{2,1,0:T(4,128)S(1)}, f32[2,3,32]{2,1,0:T(4,128)S(1)}, u32[]{:S(2)}, u32[]{:S(2)}) collective-permute-start(f32[2,3,32]{2,1,0:T(4,128)S(1)} %pad_maximum_fusion.1), channel_id=1, source_target_pairs={{0,128},{8,136},{16,144},{24,152},{32,160},{40,168},{48,176},{56,1... | collective-permute-start | bytes 2312 | tf_op jit(solution)/shard_map/ppermute | solution.py:219
  118.5 4.1 %collective-permute-done.8 = f32[2,3,32]{2,1,0:T(4,128)S(1)} collective-permute-done((f32[2,3,32]{2,1,0:T(4,128)S(1)}, f32[2,3,32]{2,1,0:T(4,128)S(1)}, u32[]{:S(2)}, u32[]{:S(2)}) %collective-permute-start.8) | collective-permute-done | bytes 800 | tf_op jit(solution)/shard_map/ppermute | solution.py:219
  122.6 3.7 %collective-permute-done.9 = f32[2,3,32]{2,1,0:T(4,128)S(1)} collective-permute-done((f32[2,3,32]{2,1,0:T(4,128)S(1)}, f32[2,3,32]{2,1,0:T(4,128)S(1)}, u32[]{:S(2)}, u32[]{:S(2)}) %collective-permute-start.9) | collective-permute-done | bytes 800 | tf_op jit(solution)/shard_map/ppermute | solution.py:219
  126.4 3.4 %collective-permute-start.11 = (f32[8,3,32]{2,1,0:T(4,128)S(1)}, f32[8,3,32]{2,1,0:T(4,128)S(1)}, u32[]{:S(2)}, u32[]{:S(2)}) collective-permute-start(f32[8,3,32]{2,1,0:T(4,128)S(1)} %constant_dynamic-update-slice_fusion.19._.refs_0_), channel_id=1, source_target_pairs={{0,16},{8,24},{16,32},{24,40},{32,48},{40,56},{48,0},{56,8},{64,80... | collective-permute-start | bytes 9224 | tf_op jit(solution)/shard_map/ppermute | solution.py:219
  129.8 2.2 %collective-permute-start.12 = (f32[8,3,32]{2,1,0:T(4,128)S(1)}, f32[8,3,32]{2,1,0:T(4,128)S(1)}, u32[]{:S(2)}, u32[]{:S(2)}) collective-permute-start(f32[8,3,32]{2,1,0:T(4,128)S(1)} %constant_dynamic-update-slice_fusion.19._.refs_0_), channel_id=1, source_target_pairs={{0,32},{8,40},{16,48},{24,56},{32,0},{40,8},{48,16},{56,24},{64,96... | collective-permute-start | bytes 9224 | tf_op jit(solution)/shard_map/ppermute | solution.py:219
  132.0 2.5 %collective-permute-start.13 = (f32[8,3,32]{2,1,0:T(4,128)S(1)}, f32[8,3,32]{2,1,0:T(4,128)S(1)}, u32[]{:S(2)}, u32[]{:S(2)}) collective-permute-start(f32[8,3,32]{2,1,0:T(4,128)S(1)} %constant_dynamic-update-slice_fusion.19._.refs_0_), channel_id=1, source_target_pairs={{0,48},{8,56},{16,0},{24,8},{32,16},{40,24},{48,32},{56,40},{64,11... | collective-permute-start | bytes 9224 | tf_op jit(solution)/shard_map/ppermute | solution.py:219
  135.8 4.0 %unpack.3 = (bf16[32,256,128]{2,1,0:T(8,128)(2,1)}, f32[1,128]{1,0:T(1,128)}) custom-call(s32[32]{0:T(128)} %fusion.41.slots, bf16[64,256,128]{2,1,0:T(8,128)(2,1)} %all-to-all-done.1.arrived, f32[8,3,32]{2,1,0:T(4,128)} %copy-done.3), custom_call_target="tpu_custom_call" | custom-call | tf_op jit(solution)/shard_map/unpack/pallas_call | solution.py:159
  140.4 1.5 %finish.1 = (f32[1,8]{1,0:T(1,128)}, s32[1,32]{1,0:T(1,128)}) custom-call(f32[1,32]{1,0:T(1,128)} %pad_bitcast_fusion.2.counted, s32[1,32]{1,0:T(1,128)} %get-tuple-element.40.step, s32[1,32]{1,0:T(1,128)} %get-tuple-element.38.place, f32[8,3,32]{2,1,0:T(4,128)} %copy-done.3, f32[8,3,32]{2,1,0:T(4,128)} %copy-done.4, f32[8,3,32]{2,1,0:T(4,128)} %copy-done.5, ...), custom_call_target="tpu_custom_call" | custom-call | tf_op jit(solution)/shard_map/finish/pallas_call | solution.py:195
  (88 shorter events, 17.4 us)
Async XLA Ops:
  2.1 12.2 %collective-permute-start = (bf16[64,256]{1,0:T(8,128)(2,1)S(1)}, bf16[64,256]{1,0:T(8,128)(2,1)S(1)}, u32[]{:S(2)}, u32[]{:S(2)}) collective-permute-start(bf16[64,256]{1,0:T(8,128)(2,1)S(1)} %get-tuple-element.58), channel_id=1, source_target_pairs={{0,64},{8,72},{16,80},{24,88},{32,96},{40,104},{48,112},{56,120},{... | collective-permute-start | bytes 98312 | tf_op jit(solution)/shard_map/ppermute | solution.py:219
  3.7 10.6 %collective-permute-start.1 = (bf16[64,256]{1,0:T(8,128)(2,1)S(1)}, bf16[64,256]{1,0:T(8,128)(2,1)S(1)}, u32[]{:S(2)}, u32[]{:S(2)}) collective-permute-start(bf16[64,256]{1,0:T(8,128)(2,1)S(1)} %get-tuple-element.58), channel_id=1, source_target_pairs={{0,128},{8,136},{16,144},{24,152},{32,160},{40,168},{48,176},{56,1... | collective-permute-start | bytes 98312 | tf_op jit(solution)/shard_map/ppermute | solution.py:219
  6.6 7.7 %collective-permute-start.2 = (bf16[64,256]{1,0:T(8,128)(2,1)S(1)}, bf16[64,256]{1,0:T(8,128)(2,1)S(1)}, u32[]{:S(2)}, u32[]{:S(2)}) collective-permute-start(bf16[64,256]{1,0:T(8,128)(2,1)S(1)} %get-tuple-element.58), channel_id=1, source_target_pairs={{0,192},{8,200},{16,208},{24,216},{32,224},{40,232},{48,240},{56,2... | collective-permute-start | bytes 98312 | tf_op jit(solution)/shard_map/ppermute | solution.py:219
  15.0 58.5 %all-to-all-start = ((bf16[64,256,128]{2,1,0:T(8,128)(2,1)}), bf16[64,256,128]{2,1,0:T(8,128)(2,1)}, u32[]{:S(2)}, u32[]{:S(2)}) async-start(bf16[64,256,128]{2,1,0:T(8,128)(2,1)} %after.2), calls=%async_computation | async-start | bytes 8388608 | tf_op jit(solution)/shard_map/all_to_all | solution.py:268
  20.1 7.1 %copy-start.8 = (s32[32]{0:T(128)S(1)}, s32[32]{0:T(128)}, u32[]{:S(2)}) copy-start(s32[32]{0:T(128)} %lengths.3) | copy-start | bytes 388
  20.1 9.8 %copy-start.7 = (s32[1024]{0:T(1024)S(1)}, s32[1024]{0:T(1024)}, u32[]{:S(2)}) copy-start(s32[1024]{0:T(1024)} %param.22) | copy-start | bytes 12292
  20.1 11.3 %copy-start.1 = (bf16[256,256]{1,0:T(8,128)(2,1)S(1)}, bf16[256,256]{1,0:T(8,128)(2,1)}, u32[]{:S(2)}) copy-start(bf16[256,256]{1,0:T(8,128)(2,1)} %pad_maximum_fusion.refs_1_._) | copy-start | bytes 393220
  31.4 48.1 %collective-permute-start.3 = (bf16[256,256]{1,0:T(8,128)(2,1)S(1)}, bf16[256,256]{1,0:T(8,128)(2,1)S(1)}, u32[]{:S(2)}, u32[]{:S(2)}) collective-permute-start(bf16[256,256]{1,0:T(8,128)(2,1)S(1)} %copy-done.1), channel_id=1, source_target_pairs={{0,16},{8,24},{16,32},{24,40},{32,48},{40,56},{48,0},{56,8},{64,80... | collective-permute-start | bytes 393224 | tf_op jit(solution)/shard_map/ppermute | solution.py:219
  33.2 46.3 %collective-permute-start.4 = (bf16[256,256]{1,0:T(8,128)(2,1)S(1)}, bf16[256,256]{1,0:T(8,128)(2,1)S(1)}, u32[]{:S(2)}, u32[]{:S(2)}) collective-permute-start(bf16[256,256]{1,0:T(8,128)(2,1)S(1)} %copy-done.1), channel_id=1, source_target_pairs={{0,32},{8,40},{16,48},{24,56},{32,0},{40,8},{48,16},{56,24},{64,96... | collective-permute-start | bytes 393224 | tf_op jit(solution)/shard_map/ppermute | solution.py:219
  35.9 43.7 %collective-permute-start.5 = (bf16[256,256]{1,0:T(8,128)(2,1)S(1)}, bf16[256,256]{1,0:T(8,128)(2,1)S(1)}, u32[]{:S(2)}, u32[]{:S(2)}) collective-permute-start(bf16[256,256]{1,0:T(8,128)(2,1)S(1)} %copy-done.1), channel_id=1, source_target_pairs={{0,48},{8,56},{16,0},{24,8},{32,16},{40,24},{48,32},{56,40},{64,11... | collective-permute-start | bytes 393224 | tf_op jit(solution)/shard_map/ppermute | solution.py:219
  73.5 62.3 %all-to-all-start.1 = ((bf16[64,256,128]{2,1,0:T(8,128)(2,1)}), bf16[64,256,128]{2,1,0:T(8,128)(2,1)}, u32[]{:S(2)}, u32[]{:S(2)}) async-start(bf16[64,256,128]{2,1,0:T(8,128)(2,1)} %after.3), calls=%async_computation.1 | async-start | bytes 8388608 | tf_op jit(solution)/shard_map/all_to_all | solution.py:272
  79.6 2.0 %collective-permute-start.6 = (bf16[1024,256]{1,0:T(8,128)(2,1)S(1)}, bf16[1024,256]{1,0:T(8,128)(2,1)S(1)}, u32[]{:S(2)}, u32[]{:S(2)}) collective-permute-start(bf16[1024,256]{1,0:T(8,128)(2,1)S(1)} %get-tuple-element.44), channel_id=1, source_target_pairs={{0,8},{8,0},{16,24},{24,16},{32,40},{40,32},{48,56},{56,48},{64,72... | collective-permute-start | bytes 1572872 | tf_op jit(solution)/shard_map/ppermute | solution.py:219
  84.3 5.7 %copy-start.10 = (f32[1024]{0:T(1024)S(1)}, f32[1024]{0:T(1024)}, u32[]{:S(2)}) copy-start(f32[1024]{0:T(1024)} %param.21) | copy-start | bytes 12292
  84.7 5.2 %copy-start = (f32[2048,32,2,8]{0,1,3,2:T(8,128)S(1)}, f32[2048,32,2,8]{0,1,3,2:T(8,128)}, u32[]{:S(2)}) copy-start(f32[2048,32,2,8]{0,1,3,2:T(8,128)} %get-tuple-element.63) | copy-start | bytes 12582916
  87.9 18.3 %copy-start.11 = (f32[32]{0:T(128)S(1)}, f32[32]{0:T(128)}, u32[]{:S(2)}) copy-start(f32[32]{0:T(128)} %param.20) | copy-start | bytes 388
  106.2 33.5 %copy-start.9 = (f32[32]{0:T(128)}, f32[32]{0:T(128)S(1)}, u32[]{:S(2)}) copy-start(f32[32]{0:T(128)S(1)} %add.115) | copy-start | bytes 388
  111.2 1.2 collective-permute-start.7
  112.5 10.2 %collective-permute-start.8 = (f32[2,3,32]{2,1,0:T(4,128)S(1)}, f32[2,3,32]{2,1,0:T(4,128)S(1)}, u32[]{:S(2)}, u32[]{:S(2)}) collective-permute-start(f32[2,3,32]{2,1,0:T(4,128)S(1)} %pad_maximum_fusion.1), channel_id=1, source_target_pairs={{0,64},{8,72},{16,80},{24,88},{32,96},{40,104},{48,112},{56,120},{... | collective-permute-start | bytes 2312 | tf_op jit(solution)/shard_map/ppermute | solution.py:219
  114.4 12.0 %collective-permute-start.9 = (f32[2,3,32]{2,1,0:T(4,128)S(1)}, f32[2,3,32]{2,1,0:T(4,128)S(1)}, u32[]{:S(2)}, u32[]{:S(2)}) collective-permute-start(f32[2,3,32]{2,1,0:T(4,128)S(1)} %pad_maximum_fusion.1), channel_id=1, source_target_pairs={{0,128},{8,136},{16,144},{24,152},{32,160},{40,168},{48,176},{56,1... | collective-permute-start | bytes 2312 | tf_op jit(solution)/shard_map/ppermute | solution.py:219
  117.1 9.3 %collective-permute-start.10 = (f32[2,3,32]{2,1,0:T(4,128)S(1)}, f32[2,3,32]{2,1,0:T(4,128)S(1)}, u32[]{:S(2)}, u32[]{:S(2)}) collective-permute-start(f32[2,3,32]{2,1,0:T(4,128)S(1)} %pad_maximum_fusion.1), channel_id=1, source_target_pairs={{0,192},{8,200},{16,208},{24,216},{32,224},{40,232},{48,240},{56,2... | collective-permute-start | bytes 2312 | tf_op jit(solution)/shard_map/ppermute | solution.py:219
  126.4 9.4 %copy-start.3 = (f32[8,3,32]{2,1,0:T(4,128)}, f32[8,3,32]{2,1,0:T(4,128)S(1)}, u32[]{:S(2)}) copy-start(f32[8,3,32]{2,1,0:T(4,128)S(1)} %constant_dynamic-update-slice_fusion.19._.refs_0_) | copy-start | bytes 9220
  126.4 13.4 %collective-permute-start.11 = (f32[8,3,32]{2,1,0:T(4,128)S(1)}, f32[8,3,32]{2,1,0:T(4,128)S(1)}, u32[]{:S(2)}, u32[]{:S(2)}) collective-permute-start(f32[8,3,32]{2,1,0:T(4,128)S(1)} %constant_dynamic-update-slice_fusion.19._.refs_0_), channel_id=1, source_target_pairs={{0,16},{8,24},{16,32},{24,40},{32,48},{40,56},{48,0},{56,8},{64,80... | collective-permute-start | bytes 9224 | tf_op jit(solution)/shard_map/ppermute | solution.py:219
  129.8 10.0 %collective-permute-start.12 = (f32[8,3,32]{2,1,0:T(4,128)S(1)}, f32[8,3,32]{2,1,0:T(4,128)S(1)}, u32[]{:S(2)}, u32[]{:S(2)}) collective-permute-start(f32[8,3,32]{2,1,0:T(4,128)S(1)} %constant_dynamic-update-slice_fusion.19._.refs_0_), channel_id=1, source_target_pairs={{0,32},{8,40},{16,48},{24,56},{32,0},{40,8},{48,16},{56,24},{64,96... | collective-permute-start | bytes 9224 | tf_op jit(solution)/shard_map/ppermute | solution.py:219
  132.0 7.8 %collective-permute-start.13 = (f32[8,3,32]{2,1,0:T(4,128)S(1)}, f32[8,3,32]{2,1,0:T(4,128)S(1)}, u32[]{:S(2)}, u32[]{:S(2)}) collective-permute-start(f32[8,3,32]{2,1,0:T(4,128)S(1)} %constant_dynamic-update-slice_fusion.19._.refs_0_), channel_id=1, source_target_pairs={{0,48},{8,56},{16,0},{24,8},{32,16},{40,24},{48,32},{56,40},{64,11... | collective-permute-start | bytes 9224 | tf_op jit(solution)/shard_map/ppermute | solution.py:219
  (4 other events, 6.9 us)

commit v5 on v4

--- a/solution.py
+++ b/solution.py
@@ -15,18 +15,11 @@
 RUNGS = 8
 DISTINCT = 2
 SIDES = (4, 4, 2)
+PLANES = 8
 WINDOW = 32
 CHUNKS = 4
 GROUP = 2
 ROOMY = 58 << 20
-
-
-def repeat(count, body):
-    def step(i, carry):
-        body(i)
-        return carry
-
-    lax.fori_loop(0, count, step, 0, unroll=4)
 
 
 def pack_kernel(keeps, lengths, least, most, *refs):
@@ -144,9 +137,9 @@
         return pltpu.make_async_copy(held.at[rows], result.at[rows], out_sems.at[chunk])
 
     mark[...] = jnp.zeros_like(mark)
-    repeat(count, lambda p: load(p).start())
+    repeat(count, lambda p: load(p).start(), count)
     for chunk in range(CHUNKS):
-        repeat(share, lambda p, chunk=chunk: load(p + chunk * share).wait())
+        repeat(share, lambda p, chunk=chunk: load(p + chunk * share).wait(), share)
         keep(chunk).start()
     for chunk in range(CHUNKS):
         keep(chunk).wait()
@@ -217,6 +210,36 @@
                 goal[axis] = (goal[axis] + step) % sides[axis]
             pairs.append((i, (goal[0] * sides[1] + goal[1]) * sides[2] + goal[2]))
         parts.append(lax.ppermute(array, "particle", pairs) if any(steps) else array)
+    return parts
+
+
+def devices():
+    tall, wide, cores = SIDES
+    return [
+        (i, z, i % cores + cores * (z % 2)) for i in range(tall * wide * cores) for z in range(PLANES)
+    ]
+
+
+def columns_of(array):
+    tall, wide, cores = SIDES
+    parts = []
+    for step in range(tall):
+        pairs = []
+        for i, z, copy in devices():
+            y, x = i // (wide * cores), i // cores % wide
+            goal = (((y + step) % tall) * wide + (x + copy) % wide) * cores + i % cores
+            pairs.append((i * PLANES + z, goal * PLANES + z))
+        parts.append(lax.ppermute(array, ("particle", "tensor"), pairs))
+    return parts
+
+
+def copies_of(array):
+    parts = []
+    for other in range(1, 4):
+        pairs = [
+            (i * PLANES + z, (i ^ other % 2) * PLANES + (z ^ other // 2)) for i, z, _ in devices()
+        ]
+        parts.append(lax.ppermute(array, ("particle", "tensor"), pairs))
     return parts
 
 
@@ -241,8 +264,15 @@
     sources = lax.axis_size("particle")
     device = lax.axis_index("particle")
 
-    shard = jnp.concatenate([prompt_keys, prompt_values], axis=1)
-    column = jnp.concatenate(along(shard, (0,)), axis=0)
+    low = -jnp.inf
+    shard = jnp.maximum(
+        jnp.pad(prompt_keys, ((0, 0), (0, HEAD_DIM)), constant_values=low),
+        jnp.pad(prompt_values, ((0, 0), (HEAD_DIM, 0)), constant_values=low),
+    )
+    column = shard
+    for bit in (1, 2):
+        swapped = lax.ppermute(column, "particle", [(i, i ^ bit * 8) for i in range(sources)])
+        column = jnp.concatenate([column, swapped], axis=0)
     plane = jnp.concatenate(along(column, (1,)), axis=0)
     prompt = jnp.concatenate(along(plane, (2,)), axis=0)
     all_keys = prompt[:, :HEAD_DIM]
@@ -320,16 +350,18 @@
         ]
     )[None]
     near = jnp.concatenate(along(shared, (2,)), axis=0)
-    near = jnp.concatenate(along(near, (0,)), axis=0)
-    parts = along(near, (1,))
+    cross = jnp.concatenate(columns_of(near), axis=0)
     next_values, mark = unpack(arrived_values, slot, near)
+    parts = [cross] + copies_of(cross)
 
     counted = jnp.sum((rungs[:, None] == ladder[None, :]).astype(jnp.float32), axis=0)
     tall, wide, cores = SIDES
     up = (device // (wide * cores) - mine_owner // (wide * cores)) % tall
     right = (device // cores % wide - mine_owner // cores % wide) % wide
     across = (device % cores - mine_owner % cores) % cores
-    step = (right * tall + up) * cores + across
+    copy = device % cores + cores * (lax.axis_index("tensor") % 2)
+    part = right ^ copy
+    step = (part * tall + up) * cores + (across ^ part % cores)
     rung_means, next_lengths = finish(
         parts,
         jnp.pad(counted, (0, spare), constant_values=1.0)[None],

time: 143 us -> 145 us (1.014)
    ppermute x14 -> x5, starting transfers between devices: 26.4 us -> 6.23 us  [along(): lax.ppermute(array, 'particle', pairs)]
    ppermute x0 -> x9, starting transfers between devices: none -> 19.8 us  [the longest x3 8.37 us: copies_of(): parts.append(lax.ppermute(array, ('particle', 'tensor'), pairs))]
    ppermute x0 -> x9, waiting for transfers between devices: none -> 8.52 us  [the longest x4 6.93 us: columns_of(): parts.append(lax.ppermute(array, ('particle', 'tensor'), pairs))]
    ppermute x14 -> x5, waiting for transfers between devices: 9.44 us -> 1.55 us  [along(): lax.ppermute(array, 'particle', pairs)]
    unnamed x36 -> x35, local copies, waits for them, and re-layouts: 2.92 us -> 1.45 us
  transfers between devices with their start and end apart: 16 -> 16, of which waited for: 5 -> 6; matrix products, arithmetic and copies ran while one was open for 13% -> 13% of each run, Pallas kernels for 14% -> 14%
where the time goes in v5:
time: 145 us; the launch traced here: 143 us
  waiting for transfers between devices  46.4 us (32%)
  starting transfers between devices  37.4 us (26%)
  Pallas kernels  21.8 us (15%)
  blocking collectives  15.2 us (10%)
  other arithmetic  9.46 us (7%)
  matrix products  8.08 us (6%)
  local copies, waits for them, and re-layouts  3.2 us (2%)
    all_to_all x1, waiting for transfers between devices, shards(): arrived_keys = exchange(after(outgoing_keys, column))  36.4 us
    psum x1, blocking collectives, shards(): weights = prior + lax.psum(partial_reward, 'tensor')  15.2 us
    pallas_call x2, Pallas kernels, pack(): pl.pallas_call(functools.partial(pack_kernel, keeps), out_shape=[jax.Shap...  11.9 us
    pallas_call x2, Pallas kernels, unpack(): pl.pallas_call(unpack_kernel, out_shape=(jax.ShapeDtypeStruct(shape, arri...  8.37 us
    ppermute x3, starting transfers between devices, copies_of(): parts.append(lax.ppermute(array, ('particle', 'tensor'), pairs))  8.37 us
    ppermute x4, waiting for transfers between devices, columns_of(): parts.append(lax.ppermute(array, ('particle', 'tensor'), pairs))  6.93 us
    ppermute x4, starting transfers between devices, columns_of(): parts.append(lax.ppermute(array, ('particle', 'tensor'), pairs))  6.57 us
    ppermute x5, starting transfers between devices, along(): lax.ppermute(array, 'particle', pairs)  6.23 us
  transfers between devices with their start and end apart: 16, of which 6 were waited for; matrix products, arithmetic and copies ran while one was open for 13% of the time, Pallas kernels for 14%

profile of v5, /device:TPU:128, one launch (start us, length us, event | category | flops | bytes accessed | tf_op | source)
XLA Modules:
  0.0 142.5 jit_solution(9855889976116901294)
XLA Ops:
  1.4 1.7 %collective-permute-start = (bf16[64,256]{1,0:T(8,128)(2,1)S(1)}, bf16[64,256]{1,0:T(8,128)(2,1)S(1)}, u32[]{:S(2)}, u32[]{:S(2)}) collective-permute-start(bf16[64,256]{1,0:T(8,128)(2,1)S(1)} %get-tuple-element.56), channel_id=1, source_target_pairs={{0,64},{8,72},{16,80},{24,88},{32,96},{40,104},{48,112},{56,120},{... | collective-permute-start | bytes 98312 | tf_op jit(solution)/shard_map/ppermute | solution.py:274
  3.8 1.6 %collective-permute-done = bf16[64,256]{1,0:T(8,128)(2,1)S(1)} collective-permute-done((bf16[64,256]{1,0:T(8,128)(2,1)S(1)}, bf16[64,256]{1,0:T(8,128)(2,1)S(1)}, u32[]{:S(2)}, u32[]{:S(2)}) %collective-permute-start) | collective-permute-done | bytes 32800 | tf_op jit(solution)/shard_map/ppermute | solution.py:274
  5.4 3.2 %collective-permute-start.1 = (bf16[128,256]{1,0:T(8,128)(2,1)S(1)}, bf16[128,256]{1,0:T(8,128)(2,1)S(1)}, u32[]{:S(2)}, u32[]{:S(2)}) collective-permute-start(bf16[128,256]{1,0:T(8,128)(2,1)S(1)} %pad_maximum_fusion.1), channel_id=1, source_target_pairs={{0,128},{8,136},{16,144},{24,152},{32,160},{40,168},{48,176},{56,1... | collective-permute-start | bytes 196616 | tf_op jit(solution)/shard_map/ppermute | solution.py:274
  9.2 4.9 %pack.3.refs_0_ = bf16[64,256,128]{2,1,0:T(8,128)(2,1)} custom-call(s32[32]{0:T(128)} %lengths.3, s32[32]{0:T(128)} %get-tuple-element.37.least, s32[32]{0:T(128)} %get-tuple-element.36.most, bf16[32,256,128]{2,1,0:T(8,128)(2,1)} %refs_0_.3, bf16[32,2,128]{2,1,0:T(2,128)(2,1)} %refs_1_.3), custom_call_target="tpu_custom_call" | custom-call | tf_op jit(solution)/shard_map/pack/pallas_call | solution.py:99
  14.8 5.4 %all-to-all-start = ((bf16[64,256,128]{2,1,0:T(8,128)(2,1)}), bf16[64,256,128]{2,1,0:T(8,128)(2,1)}, u32[]{:S(2)}, u32[]{:S(2)}) async-start(bf16[64,256,128]{2,1,0:T(8,128)(2,1)} %after.2), calls=%async_computation | async-start | bytes 8388608 | tf_op jit(solution)/shard_map/all_to_all | solution.py:298
  20.4 7.0 %pack.2 = (bf16[64,256,128]{2,1,0:T(8,128)(2,1)}, bf16[32,256,128]{2,1,0:T(8,128)(2,1)}, bf16[32,256,128]{2,1,0:T(8,128)(2,1)}) custom-call(s32[32]{0:T(128)} %lengths.3, s32[32]{0:T(128)} %get-tuple-element.37.least, s32[32]{0:T(128)} %get-tuple-element.36.most, bf16[32,256,128]{2,1,0:T(8,128)(2,1)} %refs_0_.3, bf16[32,256,128]{2,1,0:T(8,128)(2,1)} %refs_1_.2, ...), custom_call_target="tpu_custom_call" | custom-call | tf_op jit(solution)/shard_map/pack/pallas_call | solution.py:99
  27.6 2.3 %fusion.51 = (f32[32,2,8]{2,1,0:T(2,128)S(1)}, f32[32,2,8,256]{3,2,1,0:T(8,128)S(1)}) fusion(bf16[32,2,8,128]{3,2,1,0:T(8,128)(2,1)S(1)} %reshape.69, bf16[32,256,128]{2,1,0:T(8,128)(2,1)} %get-tuple-element.15, pred[32,2,256]{2,1,0:T(4,128)(4,1)S(1)} %iota_compare_fusion), kind=kOutput, calls=%fused_computation.117 | convolution fusion | flops 33947136 | bytes 2770944 | tf_op jit(solution)/shard_map/pshd,pld->pshl/dot_general | solution.py:310
  31.5 1.7 %collective-permute-start.2 = (bf16[256,256]{1,0:T(8,128)(2,1)S(1)}, bf16[256,256]{1,0:T(8,128)(2,1)S(1)}, u32[]{:S(2)}, u32[]{:S(2)}) collective-permute-start(bf16[256,256]{1,0:T(8,128)(2,1)S(1)} %copy-done.1), channel_id=1, source_target_pairs={{0,16},{8,24},{16,32},{24,40},{32,48},{40,56},{48,0},{56,8},{64,80... | collective-permute-start | bytes 393224 | tf_op jit(solution)/shard_map/ppermute | solution.py:212
  33.2 2.7 %collective-permute-start.3 = (bf16[256,256]{1,0:T(8,128)(2,1)S(1)}, bf16[256,256]{1,0:T(8,128)(2,1)S(1)}, u32[]{:S(2)}, u32[]{:S(2)}) collective-permute-start(bf16[256,256]{1,0:T(8,128)(2,1)S(1)} %copy-done.1), channel_id=1, source_target_pairs={{0,32},{8,40},{16,48},{24,56},{32,0},{40,8},{48,16},{56,24},{64,96... | collective-permute-start | bytes 393224 | tf_op jit(solution)/shard_map/ppermute | solution.py:212
  37.3 36.4 %all-to-all-done.arrived.refs_1_ = bf16[64,256,128]{2,1,0:T(8,128)(2,1)} async-done(((bf16[64,256,128]{2,1,0:T(8,128)(2,1)}), bf16[64,256,128]{2,1,0:T(8,128)(2,1)}, u32[]{:S(2)}, u32[]{:S(2)}) %all-to-all-start) | async-done | bytes 4194336 | tf_op jit(solution)/shard_map/all_to_all | solution.py:298
  73.7 5.9 %all-to-all-start.1 = ((bf16[64,256,128]{2,1,0:T(8,128)(2,1)}), bf16[64,256,128]{2,1,0:T(8,128)(2,1)}, u32[]{:S(2)}, u32[]{:S(2)}) async-start(bf16[64,256,128]{2,1,0:T(8,128)(2,1)} %after.3), calls=%async_computation.1 | async-start | bytes 8388608 | tf_op jit(solution)/shard_map/all_to_all | solution.py:302
  81.8 2.6 %bitcast_reduce_fusion = (f32[32,2,8]{0,2,1:T(8,128)S(1)}, f32[2048,32,2,8]{0,1,3,2:T(8,128)}) fusion(bf16[32,2,8,128]{3,2,1,0:T(8,128)(2,1)S(1)} %reshape.69, bf16[2048,256]{1,0:T(8,128)(2,1)S(1)} %constant_dynamic-update-slice_fusion.6), kind=kOutput, calls=%fused_computation.1 | convolution fusion | flops 270532096 | bytes 4851712 | tf_op jit(solution)/shard_map/pshd,nd->pshn/dot_general | solution.py:307
  84.9 3.2 %fusion.1 = f32[32,2,8]{0,2,1:T(8,128)S(1)} fusion(f32[2048,32,2,8]{0,1,3,2:T(8,128)} %get-tuple-element.58, f32[32,2,8]{0,2,1:T(8,128)S(1)} %max.11), kind=kLoop, calls=%fused_computation.3 | loop fusion | flops 3145216 | bytes 4198400 | tf_op jit(solution)/shard_map/reduce_sum | solution.py:320
  88.1 2.0 %fusion.5 = f32[32,2,8,128]{3,2,1,0:T(8,128)S(1)} fusion(bf16[32,256,128]{2,1,0:T(8,128)(2,1)} %get-tuple-element.16, f32[32,2,8,256]{3,2,1,0:T(8,128)S(1)} %get-tuple-element.60, f32[32,2,8]{2,1,0:T(2,128)S(1)} %copy.41), kind=kOutput, calls=%fused_computation.6 | convolution fusion | flops 33816576 | bytes 2885632 | tf_op jit(solution)/shard_map/pshl,pld->pshd/dot_general | solution.py:326
  91.2 15.2 %psum.7 = f32[32]{0:T(128)S(1)} all-reduce(f32[32]{0:T(128)S(1)} %get-tuple-element.42), channel_id=1, replica_groups=mesh['particle'=32,'tensor'=8] {'tensor'}, use_global_device_ids=true, to_apply=%region_7.8 | all-reduce | flops 32 | bytes 256 | tf_op jit(solution)/shard_map/psum | solution.py:336
  106.7 4.2 %unpack.2 = (bf16[32,256,128]{2,1,0:T(8,128)(2,1)}, f32[1,128]{1,0:T(1,128)}) custom-call(s32[32]{0:T(128)} %fusion.42.slots, bf16[64,256,128]{2,1,0:T(8,128)(2,1)} %all-to-all-done.arrived.refs_1_, bf16[256,256]{1,0:T(8,128)(2,1)} %pad_maximum_fusion.refs_1_._), custom_call_target="tpu_custom_call" | custom-call | tf_op jit(solution)/shard_map/unpack/pallas_call | solution.py:152
  113.6 1.8 %collective-permute-start.8 = (f32[2,3,32]{2,1,0:T(4,128)S(1)}, f32[2,3,32]{2,1,0:T(4,128)S(1)}, u32[]{:S(2)}, u32[]{:S(2)}) collective-permute-start(f32[2,3,32]{2,1,0:T(4,128)S(1)} %pad_maximum_fusion.3._), channel_id=1, source_target_pairs={{0,64},{1,97},{2,66},{3,99},{4,68},{5,101},{6,70},{7,103},{8,88},{... | collective-permute-start | bytes 2312 | tf_op jit(solution)/shard_map/ppermute | solution.py:232
  115.4 2.7 %collective-permute-start.9 = (f32[2,3,32]{2,1,0:T(4,128)S(1)}, f32[2,3,32]{2,1,0:T(4,128)S(1)}, u32[]{:S(2)}, u32[]{:S(2)}) collective-permute-start(f32[2,3,32]{2,1,0:T(4,128)S(1)} %pad_maximum_fusion.3._), channel_id=1, source_target_pairs={{0,128},{1,161},{2,130},{3,163},{4,132},{5,165},{6,134},{7,167},{8... | collective-permute-start | bytes 2312 | tf_op jit(solution)/shard_map/ppermute | solution.py:232
  119.6 3.4 %collective-permute-done.8 = f32[2,3,32]{2,1,0:T(4,128)S(1)} collective-permute-done((f32[2,3,32]{2,1,0:T(4,128)S(1)}, f32[2,3,32]{2,1,0:T(4,128)S(1)}, u32[]{:S(2)}, u32[]{:S(2)}) %collective-permute-start.8) | collective-permute-done | bytes 800 | tf_op jit(solution)/shard_map/ppermute | solution.py:232
  123.0 3.5 %collective-permute-done.9 = f32[2,3,32]{2,1,0:T(4,128)S(1)} collective-permute-done((f32[2,3,32]{2,1,0:T(4,128)S(1)}, f32[2,3,32]{2,1,0:T(4,128)S(1)}, u32[]{:S(2)}, u32[]{:S(2)}) %collective-permute-start.9) | collective-permute-done | bytes 800 | tf_op jit(solution)/shard_map/ppermute | solution.py:232
  126.5 3.0 %collective-permute-start.11 = (f32[8,3,32]{2,1,0:T(4,128)S(1)}, f32[8,3,32]{2,1,0:T(4,128)S(1)}, u32[]{:S(2)}, u32[]{:S(2)}) collective-permute-start(f32[8,3,32]{2,1,0:T(4,128)S(1)} %constant_dynamic-update-slice_fusion.13.refs_0_), channel_id=1, source_target_pairs={{0,8},{1,9},{2,10},{3,11},{4,12},{5,13},{6,14},{7,15},{8,0},{9,1},... | collective-permute-start | bytes 9224 | tf_op jit(solution)/shard_map/ppermute | solution.py:242
  129.5 5.3 %collective-permute-start.12 = (f32[8,3,32]{2,1,0:T(4,128)S(1)}, f32[8,3,32]{2,1,0:T(4,128)S(1)}, u32[]{:S(2)}, u32[]{:S(2)}) collective-permute-start(f32[8,3,32]{2,1,0:T(4,128)S(1)} %constant_dynamic-update-slice_fusion.13.refs_0_), channel_id=1, source_target_pairs={{0,1},{1,0},{2,3},{3,2},{4,5},{5,4},{6,7},{7,6},{8,9},{9,8},{10,11... | collective-permute-start | bytes 9224 | tf_op jit(solution)/shard_map/ppermute | solution.py:242
  136.2 4.2 %unpack.3 = (bf16[32,256,128]{2,1,0:T(8,128)(2,1)}, f32[1,128]{1,0:T(1,128)}) custom-call(s32[32]{0:T(128)} %fusion.42.slots, bf16[64,256,128]{2,1,0:T(8,128)(2,1)} %all-to-all-done.1.arrived, f32[2,3,32]{2,1,0:T(4,128)} %copy-done.4), custom_call_target="tpu_custom_call" | custom-call | tf_op jit(solution)/shard_map/unpack/pallas_call | solution.py:152
  141.0 1.5 %finish.1 = (f32[1,8]{1,0:T(1,128)}, s32[1,32]{1,0:T(1,128)}) custom-call(f32[1,32]{1,0:T(1,128)} %pad_bitcast_fusion.2.counted, s32[1,32]{1,0:T(1,128)} %get-tuple-element.40.step, s32[1,32]{1,0:T(1,128)} %get-tuple-element.38.place, f32[8,3,32]{2,1,0:T(4,128)} %copy-done.3, f32[8,3,32]{2,1,0:T(4,128)} %copy-done.5, f32[8,3,32]{2,1,0:T(4,128)} %copy-done.6, ...), custom_call_target="tpu_custom_call" | custom-call | tf_op jit(solution)/shard_map/finish/pallas_call | solution.py:188
  (88 shorter events, 16.1 us)
Async XLA Ops:
  1.4 4.0 %collective-permute-start = (bf16[64,256]{1,0:T(8,128)(2,1)S(1)}, bf16[64,256]{1,0:T(8,128)(2,1)S(1)}, u32[]{:S(2)}, u32[]{:S(2)}) collective-permute-start(bf16[64,256]{1,0:T(8,128)(2,1)S(1)} %get-tuple-element.56), channel_id=1, source_target_pairs={{0,64},{8,72},{16,80},{24,88},{32,96},{40,104},{48,112},{56,120},{... | collective-permute-start | bytes 98312 | tf_op jit(solution)/shard_map/ppermute | solution.py:274
  5.4 8.8 %collective-permute-start.1 = (bf16[128,256]{1,0:T(8,128)(2,1)S(1)}, bf16[128,256]{1,0:T(8,128)(2,1)S(1)}, u32[]{:S(2)}, u32[]{:S(2)}) collective-permute-start(bf16[128,256]{1,0:T(8,128)(2,1)S(1)} %pad_maximum_fusion.1), channel_id=1, source_target_pairs={{0,128},{8,136},{16,144},{24,152},{32,160},{40,168},{48,176},{56,1... | collective-permute-start | bytes 196616 | tf_op jit(solution)/shard_map/ppermute | solution.py:274
  14.8 58.9 %all-to-all-start = ((bf16[64,256,128]{2,1,0:T(8,128)(2,1)}), bf16[64,256,128]{2,1,0:T(8,128)(2,1)}, u32[]{:S(2)}, u32[]{:S(2)}) async-start(bf16[64,256,128]{2,1,0:T(8,128)(2,1)} %after.2), calls=%async_computation | async-start | bytes 8388608 | tf_op jit(solution)/shard_map/all_to_all | solution.py:298
  20.3 7.1 %copy-start.9 = (s32[32]{0:T(128)S(1)}, s32[32]{0:T(128)}, u32[]{:S(2)}) copy-start(s32[32]{0:T(128)} %lengths.3) | copy-start | bytes 388
  20.3 9.8 %copy-start.8 = (s32[1024]{0:T(1024)S(1)}, s32[1024]{0:T(1024)}, u32[]{:S(2)}) copy-start(s32[1024]{0:T(1024)} %param.22) | copy-start | bytes 12292
  20.3 11.2 %copy-start.1 = (bf16[256,256]{1,0:T(8,128)(2,1)S(1)}, bf16[256,256]{1,0:T(8,128)(2,1)}, u32[]{:S(2)}) copy-start(bf16[256,256]{1,0:T(8,128)(2,1)} %pad_maximum_fusion.refs_1_._) | copy-start | bytes 393220
  31.5 48.2 %collective-permute-start.2 = (bf16[256,256]{1,0:T(8,128)(2,1)S(1)}, bf16[256,256]{1,0:T(8,128)(2,1)S(1)}, u32[]{:S(2)}, u32[]{:S(2)}) collective-permute-start(bf16[256,256]{1,0:T(8,128)(2,1)S(1)} %copy-done.1), channel_id=1, source_target_pairs={{0,16},{8,24},{16,32},{24,40},{32,48},{40,56},{48,0},{56,8},{64,80... | collective-permute-start | bytes 393224 | tf_op jit(solution)/shard_map/ppermute | solution.py:212
  33.2 46.5 %collective-permute-start.3 = (bf16[256,256]{1,0:T(8,128)(2,1)S(1)}, bf16[256,256]{1,0:T(8,128)(2,1)S(1)}, u32[]{:S(2)}, u32[]{:S(2)}) collective-permute-start(bf16[256,256]{1,0:T(8,128)(2,1)S(1)} %copy-done.1), channel_id=1, source_target_pairs={{0,32},{8,40},{16,48},{24,56},{32,0},{40,8},{48,16},{56,24},{64,96... | collective-permute-start | bytes 393224 | tf_op jit(solution)/shard_map/ppermute | solution.py:212
  35.9 43.9 %collective-permute-start.4 = (bf16[256,256]{1,0:T(8,128)(2,1)S(1)}, bf16[256,256]{1,0:T(8,128)(2,1)S(1)}, u32[]{:S(2)}, u32[]{:S(2)}) collective-permute-start(bf16[256,256]{1,0:T(8,128)(2,1)S(1)} %copy-done.1), channel_id=1, source_target_pairs={{0,48},{8,56},{16,0},{24,8},{32,16},{40,24},{48,32},{56,40},{64,11... | collective-permute-start | bytes 393224 | tf_op jit(solution)/shard_map/ppermute | solution.py:212
  73.7 62.5 %all-to-all-start.1 = ((bf16[64,256,128]{2,1,0:T(8,128)(2,1)}), bf16[64,256,128]{2,1,0:T(8,128)(2,1)}, u32[]{:S(2)}, u32[]{:S(2)}) async-start(bf16[64,256,128]{2,1,0:T(8,128)(2,1)} %after.3), calls=%async_computation.1 | async-start | bytes 8388608 | tf_op jit(solution)/shard_map/all_to_all | solution.py:302
  79.8 2.0 %collective-permute-start.5 = (bf16[1024,256]{1,0:T(8,128)(2,1)S(1)}, bf16[1024,256]{1,0:T(8,128)(2,1)S(1)}, u32[]{:S(2)}, u32[]{:S(2)}) collective-permute-start(bf16[1024,256]{1,0:T(8,128)(2,1)S(1)} %get-tuple-element.44), channel_id=1, source_target_pairs={{0,8},{8,0},{16,24},{24,16},{32,40},{40,32},{48,56},{56,48},{64,72... | collective-permute-start | bytes 1572872 | tf_op jit(solution)/shard_map/ppermute | solution.py:212
  84.4 5.7 %copy-start.11 = (f32[1024]{0:T(1024)S(1)}, f32[1024]{0:T(1024)}, u32[]{:S(2)}) copy-start(f32[1024]{0:T(1024)} %param.21) | copy-start | bytes 12292
  88.1 18.3 %copy-start.12 = (f32[32]{0:T(128)S(1)}, f32[32]{0:T(128)}, u32[]{:S(2)}) copy-start(f32[32]{0:T(128)} %param.20) | copy-start | bytes 388
  106.4 34.0 %copy-start.10 = (f32[32]{0:T(128)}, f32[32]{0:T(128)S(1)}, u32[]{:S(2)}) copy-start(f32[32]{0:T(128)S(1)} %add.130) | copy-start | bytes 388
  111.6 1.2 collective-permute-start.6
  112.8 23.3 %copy-start.4 = (f32[2,3,32]{2,1,0:T(4,128)}, f32[2,3,32]{2,1,0:T(4,128)S(1)}, u32[]{:S(2)}) copy-start(f32[2,3,32]{2,1,0:T(4,128)S(1)} %pad_maximum_fusion.3._) | copy-start | bytes 2308
  112.8 6.7 %collective-permute-start.7 = (f32[2,3,32]{2,1,0:T(4,128)S(1)}, f32[2,3,32]{2,1,0:T(4,128)S(1)}, u32[]{:S(2)}, u32[]{:S(2)}) collective-permute-start(f32[2,3,32]{2,1,0:T(4,128)S(1)} %pad_maximum_fusion.3._), channel_id=1, source_target_pairs={{0,0},{1,33},{2,2},{3,35},{4,4},{5,37},{6,6},{7,39},{8,24},{9,57},... | collective-permute-start | bytes 2312 | tf_op jit(solution)/shard_map/ppermute | solution.py:232
  113.6 9.4 %collective-permute-start.8 = (f32[2,3,32]{2,1,0:T(4,128)S(1)}, f32[2,3,32]{2,1,0:T(4,128)S(1)}, u32[]{:S(2)}, u32[]{:S(2)}) collective-permute-start(f32[2,3,32]{2,1,0:T(4,128)S(1)} %pad_maximum_fusion.3._), channel_id=1, source_target_pairs={{0,64},{1,97},{2,66},{3,99},{4,68},{5,101},{6,70},{7,103},{8,88},{... | collective-permute-start | bytes 2312 | tf_op jit(solution)/shard_map/ppermute | solution.py:232
  115.4 11.1 %collective-permute-start.9 = (f32[2,3,32]{2,1,0:T(4,128)S(1)}, f32[2,3,32]{2,1,0:T(4,128)S(1)}, u32[]{:S(2)}, u32[]{:S(2)}) collective-permute-start(f32[2,3,32]{2,1,0:T(4,128)S(1)} %pad_maximum_fusion.3._), channel_id=1, source_target_pairs={{0,128},{1,161},{2,130},{3,163},{4,132},{5,165},{6,134},{7,167},{8... | collective-permute-start | bytes 2312 | tf_op jit(solution)/shard_map/ppermute | solution.py:232
  118.1 8.4 %collective-permute-start.10 = (f32[2,3,32]{2,1,0:T(4,128)S(1)}, f32[2,3,32]{2,1,0:T(4,128)S(1)}, u32[]{:S(2)}, u32[]{:S(2)}) collective-permute-start(f32[2,3,32]{2,1,0:T(4,128)S(1)} %pad_maximum_fusion.3._), channel_id=1, source_target_pairs={{0,192},{1,225},{2,194},{3,227},{4,196},{5,229},{6,198},{7,231},{8... | collective-permute-start | bytes 2312 | tf_op jit(solution)/shard_map/ppermute | solution.py:232
  126.5 13.9 %copy-start.3 = (f32[8,3,32]{2,1,0:T(4,128)}, f32[8,3,32]{2,1,0:T(4,128)S(1)}, u32[]{:S(2)}) copy-start(f32[8,3,32]{2,1,0:T(4,128)S(1)} %constant_dynamic-update-slice_fusion.13.refs_0_) | copy-start | bytes 9220
  126.5 13.8 %collective-permute-start.11 = (f32[8,3,32]{2,1,0:T(4,128)S(1)}, f32[8,3,32]{2,1,0:T(4,128)S(1)}, u32[]{:S(2)}, u32[]{:S(2)}) collective-permute-start(f32[8,3,32]{2,1,0:T(4,128)S(1)} %constant_dynamic-update-slice_fusion.13.refs_0_), channel_id=1, source_target_pairs={{0,8},{1,9},{2,10},{3,11},{4,12},{5,13},{6,14},{7,15},{8,0},{9,1},... | collective-permute-start | bytes 9224 | tf_op jit(solution)/shard_map/ppermute | solution.py:242
  129.5 10.9 %collective-permute-start.12 = (f32[8,3,32]{2,1,0:T(4,128)S(1)}, f32[8,3,32]{2,1,0:T(4,128)S(1)}, u32[]{:S(2)}, u32[]{:S(2)}) collective-permute-start(f32[8,3,32]{2,1,0:T(4,128)S(1)} %constant_dynamic-update-slice_fusion.13.refs_0_), channel_id=1, source_target_pairs={{0,1},{1,0},{2,3},{3,2},{4,5},{5,4},{6,7},{7,6},{8,9},{9,8},{10,11... | collective-permute-start | bytes 9224 | tf_op jit(solution)/shard_map/ppermute | solution.py:242
  134.8 5.6 %collective-permute-start.13 = (f32[8,3,32]{2,1,0:T(4,128)S(1)}, f32[8,3,32]{2,1,0:T(4,128)S(1)}, u32[]{:S(2)}, u32[]{:S(2)}) collective-permute-start(f32[8,3,32]{2,1,0:T(4,128)S(1)} %constant_dynamic-update-slice_fusion.13.refs_0_), channel_id=1, source_target_pairs={{0,9},{1,8},{2,11},{3,10},{4,13},{5,12},{6,15},{7,14},{8,1},{9,0},... | collective-permute-start | bytes 9224 | tf_op jit(solution)/shard_map/ppermute | solution.py:242
  (5 other events, 12.6 us)

commit v6 on v5

--- a/solution.py
+++ b/solution.py
@@ -22,10 +22,9 @@
 ROOMY = 58 << 20
 
 
-def pack_kernel(keeps, lengths, least, most, *refs):
-    number = (len(refs) - 5) // (2 + keeps)
-    caches, fresh, (packed, *written) = refs[:number], refs[number : 2 * number], refs[2 * number : -4]
-    held, in_sems, out_sems, send_sems = refs[-4:]
+def pack_kernel(sends, lengths, least, most, *refs):
+    caches, fresh, outs = refs[:2], refs[2:4], refs[4:-3]
+    held, in_sems, out_sems = refs[-3:]
     count, suffix, _ = caches[0].shape
     goals = least.shape[0]
     share = count // CHUNKS
@@ -33,20 +32,20 @@
     def load(chunk, n):
         rows = pl.ds(chunk * share, share)
         return pltpu.make_async_copy(
-            caches[n].at[rows], held.at[n, rows], in_sems.at[chunk * number + n]
+            caches[n].at[rows], held.at[rows, pl.ds(n * suffix, suffix)], in_sems.at[chunk * 2 + n]
         )
 
     def keep(n):
-        return pltpu.make_async_copy(held.at[n], written[n], out_sems.at[n])
+        return pltpu.make_async_copy(
+            held.at[:, pl.ds(n * suffix, suffix)], outs[n], out_sems.at[n]
+        )
 
     def low(d):
-        return pltpu.make_async_copy(
-            held.at[number - 1, least[d]], packed.at[2 * d], send_sems.at[2 * d]
-        )
+        return pltpu.make_async_copy(held.at[least[d]], outs[0].at[2 * d], out_sems.at[2 * d])
 
     def high(d):
         return pltpu.make_async_copy(
-            held.at[number - 1, most[d]], packed.at[2 * d + 1], send_sems.at[2 * d + 1]
+            held.at[most[d]], outs[0].at[2 * d + 1], out_sems.at[2 * d + 1]
         )
 
     def patch(group):
@@ -55,8 +54,8 @@
             p = group * GROUP + i
             length = lengths[p]
             base = pl.multiple_of(jnp.minimum(length // 16 * 16, suffix - WINDOW), 16)
-            for n in range(number):
-                place = (n, p, pl.ds(base, WINDOW))
+            for n in range(2):
+                place = (p, pl.ds(base + n * suffix, WINDOW))
                 block = held[place].astype(jnp.float32)
                 lines = fresh[n][p].astype(jnp.float32)
                 row = lax.broadcasted_iota(jnp.int32, block.shape, 0) + base
@@ -67,19 +66,21 @@
             held[place] = block
 
     for chunk in range(CHUNKS):
-        for n in range(number):
+        for n in range(2):
             load(chunk, n).start()
     for chunk in range(CHUNKS):
-        for n in range(number):
+        for n in range(2):
             load(chunk, n).wait()
         groups = share // GROUP
         repeat(groups, lambda g, chunk=chunk: patch(g + chunk * groups), 1)
-    repeat(goals, lambda d: (low(d).start(), high(d).start()))
-    for n in range(number * keeps):
-        keep(n).start()
-    repeat(goals, lambda d: (low(d).wait(), high(d).wait()))
-    for n in range(number * keeps):
-        keep(n).wait()
+    if sends:
+        repeat(goals, lambda d: (low(d).start(), high(d).start()), 8)
+        repeat(goals, lambda d: (low(d).wait(), high(d).wait()), 8)
+    else:
+        for n in range(2):
+            keep(n).start()
+        for n in range(2):
+            keep(n).wait()
 
 
 def repeat(count, body, unroll=4):
@@ -90,22 +91,24 @@
     lax.fori_loop(0, count, step, 0, unroll=unroll)
 
 
-def pack(caches, fresh, lengths, least, most, keeps):
-    cache, number = caches[0], len(caches)
-    count, goals = cache.shape[0], least.shape[0]
+def pack(caches, fresh, lengths, least, most, sends):
+    cache = caches[0]
+    (count, suffix, width), goals = cache.shape, least.shape[0]
     smem = pl.BlockSpec(memory_space=pltpu.SMEM)
     hbm = pl.BlockSpec(memory_space=pltpu.HBM)
     vmem = pl.BlockSpec(memory_space=pltpu.VMEM)
+    if sends:
+        shapes = [(goals * DISTINCT, 2 * suffix, width)]
+    else:
+        shapes = [cache.shape] * 2
     return pl.pallas_call(
-        functools.partial(pack_kernel, keeps),
-        out_shape=[jax.ShapeDtypeStruct((goals * DISTINCT,) + cache.shape[1:], cache.dtype)]
-        + [jax.ShapeDtypeStruct(cache.shape, cache.dtype)] * (number * keeps),
-        in_specs=[smem] * 3 + [hbm] * number + [vmem] * number,
-        out_specs=[hbm] * (1 + number * keeps),
+        functools.partial(pack_kernel, sends),
+        out_shape=[jax.ShapeDtypeStruct(shape, cache.dtype) for shape in shapes],
+        in_specs=[smem] * 3 + [hbm] * 2 + [vmem] * 2,
+        out_specs=[hbm] * len(shapes),
         scratch_shapes=[
-            pltpu.VMEM((number,) + cache.shape, cache.dtype),
-            pltpu.SemaphoreType.DMA((number * CHUNKS,)),
-            pltpu.SemaphoreType.DMA((number,)),
+            pltpu.VMEM((count, 2 * suffix, width), cache.dtype),
+            pltpu.SemaphoreType.DMA((2 * CHUNKS,)),
             pltpu.SemaphoreType.DMA((goals * DISTINCT,)),
         ],
         name="pack",
@@ -125,42 +128,45 @@
     )(array, *others)
 
 
-def unpack_kernel(slots, arrived, _, result, mark, held, in_sems, out_sems):
-    count = result.shape[0]
+def unpack_kernel(slots, arrived, _, next_keys, next_values, mark, held, in_sems, out_sems):
+    count, suffix, _ = next_keys.shape
     share = count // CHUNKS
 
     def load(p):
         return pltpu.make_async_copy(arrived.at[slots[p]], held.at[p], in_sems.at[p])
 
-    def keep(chunk):
+    def keep(chunk, half):
         rows = pl.ds(chunk * share, share)
-        return pltpu.make_async_copy(held.at[rows], result.at[rows], out_sems.at[chunk])
+        return pltpu.make_async_copy(
+            held.at[rows, pl.ds(half * suffix, suffix)],
+            (next_keys, next_values)[half].at[rows],
+            out_sems.at[chunk * 2 + half],
+        )
 
     mark[...] = jnp.zeros_like(mark)
     repeat(count, lambda p: load(p).start(), count)
     for chunk in range(CHUNKS):
         repeat(share, lambda p, chunk=chunk: load(p + chunk * share).wait(), share)
-        keep(chunk).start()
+        for half in range(2):
+            keep(chunk, half).start()
     for chunk in range(CHUNKS):
-        keep(chunk).wait()
+        for half in range(2):
+            keep(chunk, half).wait()
 
 
 def unpack(arrived, slots, other):
-    count, (_, suffix, width) = slots.shape[0], arrived.shape
+    count, (_, length, width) = slots.shape[0], arrived.shape
     hbm = pl.BlockSpec(memory_space=pltpu.HBM)
-    shape = (count, suffix, width)
+    shape = jax.ShapeDtypeStruct((count, length // 2, width), arrived.dtype)
     return pl.pallas_call(
         unpack_kernel,
-        out_shape=(
-            jax.ShapeDtypeStruct(shape, arrived.dtype),
-            jax.ShapeDtypeStruct((1, width), jnp.float32),
-        ),
+        out_shape=(shape, shape, jax.ShapeDtypeStruct((1, width), jnp.float32)),
         in_specs=[pl.BlockSpec(memory_space=pltpu.SMEM), hbm, pl.BlockSpec(memory_space=pl.ANY)],
-        out_specs=(hbm, pl.BlockSpec(memory_space=pltpu.VMEM)),
+        out_specs=(hbm, hbm, pl.BlockSpec(memory_space=pltpu.VMEM)),
         scratch_shapes=[
-            pltpu.VMEM(shape, arrived.dtype),
+            pltpu.VMEM((count, length, width), arrived.dtype),
             pltpu.SemaphoreType.DMA((count,)),
-            pltpu.SemaphoreType.DMA((CHUNKS,)),
+            pltpu.SemaphoreType.DMA((2 * CHUNKS,)),
         ],
         name="unpack",
     )(slots, arrived, other)
@@ -264,20 +270,6 @@
     sources = lax.axis_size("particle")
     device = lax.axis_index("particle")
 
-    low = -jnp.inf
-    shard = jnp.maximum(
-        jnp.pad(prompt_keys, ((0, 0), (0, HEAD_DIM)), constant_values=low),
-        jnp.pad(prompt_values, ((0, 0), (HEAD_DIM, 0)), constant_values=low),
-    )
-    column = shard
-    for bit in (1, 2):
-        swapped = lax.ppermute(column, "particle", [(i, i ^ bit * 8) for i in range(sources)])
-        column = jnp.concatenate([column, swapped], axis=0)
-    plane = jnp.concatenate(along(column, (1,)), axis=0)
-    prompt = jnp.concatenate(along(plane, (2,)), axis=0)
-    all_keys = prompt[:, :HEAD_DIM]
-    all_values = prompt[:, HEAD_DIM:]
-
     wanted = ancestors.reshape(sources, per_device)
     owner = wanted // per_device
     local = wanted % per_device
@@ -290,17 +282,28 @@
     first = jnp.min(jnp.where(same_owner, mine[None, :], sources * per_device), axis=1)
     slot = mine_owner * DISTINCT + (mine != first).astype(jnp.int32)
 
-    exchange = functools.partial(
-        lax.all_to_all, axis_name="particle", split_axis=0, concat_axis=0, tiled=True
-    )
-    places = (lengths, least, most)
-    (outgoing_keys,) = pack((key_cache,), (new_keys,), *places, False)
-    arrived_keys = exchange(after(outgoing_keys, column))
-    outgoing_values, written_keys, written_values = pack(
-        (key_cache, value_cache), (new_keys, new_values), *places, True
-    )
-    arrived_values = exchange(after(outgoing_values, arrived_keys))
-    next_keys, mark = unpack(arrived_keys, slot, column)
+    low = -jnp.inf
+    shard = jnp.maximum(
+        jnp.pad(prompt_keys, ((0, 0), (0, HEAD_DIM)), constant_values=low),
+        jnp.pad(prompt_values, ((0, 0), (HEAD_DIM, 0)), constant_values=low),
+    )
+    column = shard
+    for bit in (1, 2):
+        swapped = lax.ppermute(column, "particle", [(i, i ^ bit * 8) for i in range(sources)])
+        column = jnp.concatenate([column, swapped], axis=0)
+        if bit == 1:
+            column = column + jnp.minimum(least[0], 0).astype(column.dtype)
+    columns = along(column, (1,))
+    prompt = jnp.concatenate(along(jnp.concatenate(columns, axis=0), (2,)), axis=0)
+    all_keys = prompt[:, :HEAD_DIM]
+    all_values = prompt[:, HEAD_DIM:]
+
+    given = ((key_cache, value_cache), (new_keys, new_values), lengths, least, most)
+    (outgoing,) = pack(*given, True)
+    arrived = lax.all_to_all(
+        after(outgoing, *columns[1:]), "particle", split_axis=0, concat_axis=0, tiled=True
+    )
+    written_keys, written_values = pack(*given, False)
 
     query = queries.reshape(per_device, STEPS, groups, HEAD_DIM)
     front = (
@@ -346,12 +349,13 @@
         [
             jnp.pad(local_peak, (0, spare)),
             jnp.pad(local_sum, (0, spare), constant_values=1.0),
-            lengths.astype(jnp.float32) + mark[0, :per_device],
+            lengths.astype(jnp.float32),
         ]
     )[None]
     near = jnp.concatenate(along(shared, (2,)), axis=0)
+    near = after(near, attention)
     cross = jnp.concatenate(columns_of(near), axis=0)
-    next_values, mark = unpack(arrived_values, slot, near)
+    next_keys, next_values, mark = unpack(arrived, slot, near)
     parts = [cross] + copies_of(cross)
 
     counted = jnp.sum((rungs[:, None] == ladder[None, :]).astype(jnp.float32), axis=0)

time: 145 us -> 149 us (1.028)
  waiting for transfers between devices: 46.4 us -> 55.7 us
  starting transfers between devices: 37.4 us -> 33.1 us
  Pallas kernels: 21.8 us -> 19.8 us
    ppermute x4, waiting for transfers between devices: 6.93 us -> 52.2 us  [columns_of(): parts.append(lax.ppermute(array, ('particle', 'tensor'), pairs))]
    all_to_all x2 -> x1, waiting for transfers between devices: 36.4 us -> 0.01 us  [shards(): lax.all_to_all(after(outgoing, *columns[1:]), 'particle', split_axis=0, c...]
    all_to_all x2 -> x1, starting transfers between devices: 11.4 us -> 5.02 us  [shards(): lax.all_to_all(after(outgoing, *columns[1:]), 'particle', split_axis=0, c...]
    pallas_call x4 -> x3, Pallas kernels: 20.2 us -> 18.2 us  [the longest x2 12.6 us: pack(): pl.pallas_call(functools.partial(pack_kernel, sends), out_shape=[jax.Shap...]
    ppermute x2, waiting for transfers between devices: 1.58 us -> 3.46 us  [shards(): lax.ppermute(column, 'particle', [(i, i ^ bit * 8) for i in range(sources)])]
    ppermute x5, waiting for transfers between devices: 1.55 us -> 0.01 us  [along(): lax.ppermute(array, 'particle', pairs)]
    ppermute x3, starting transfers between devices: 8.37 us -> 9.88 us  [copies_of(): parts.append(lax.ppermute(array, ('particle', 'tensor'), pairs))]
  transfers between devices with their start and end apart: 16 -> 15, of which waited for: 6 -> 5; matrix products, arithmetic and copies ran while one was open for 13% -> 13% of each run, Pallas kernels for 14% -> 12%
where the time goes in v6:
time: 149 us; the launch traced here: 146 us
  waiting for transfers between devices  55.7 us (37%)
  starting transfers between devices  33.1 us (22%)
  Pallas kernels  19.8 us (13%)
  blocking collectives  15.2 us (10%)
  other arithmetic  8.76 us (6%)
  matrix products  8.11 us (5%)
  local copies, waits for them, and re-layouts  4.57 us (3%)
    ppermute x4, waiting for transfers between devices, columns_of(): parts.append(lax.ppermute(array, ('particle', 'tensor'), pairs))  52.2 us
    psum x1, blocking collectives, shards(): weights = prior + lax.psum(partial_reward, 'tensor')  15.2 us
    pallas_call x2, Pallas kernels, pack(): pl.pallas_call(functools.partial(pack_kernel, sends), out_shape=[jax.Shap...  12.6 us
    ppermute x3, starting transfers between devices, copies_of(): parts.append(lax.ppermute(array, ('particle', 'tensor'), pairs))  9.88 us
    ppermute x4, starting transfers between devices, columns_of(): parts.append(lax.ppermute(array, ('particle', 'tensor'), pairs))  7.22 us
    ppermute x5, starting transfers between devices, along(): lax.ppermute(array, 'particle', pairs)  6.11 us
    pallas_call x1, Pallas kernels, unpack(): pl.pallas_call(unpack_kernel, out_shape=(shape, shape, jax.ShapeDtypeStru...  5.6 us
    all_to_all x1, starting transfers between devices, shards(): lax.all_to_all(after(outgoing, *columns[1:]), 'particle', split_axis=0, c...  5.02 us
  transfers between devices with their start and end apart: 15, of which 5 were waited for; matrix products, arithmetic and copies ran while one was open for 13% of the time, Pallas kernels for 12%

profile of v6, /device:TPU:128, one launch (start us, length us, event | category | flops | bytes accessed | tf_op | source)
XLA Modules:
  0.0 146.3 jit_solution(12458543243107999721)
XLA Ops:
  1.4 1.6 %collective-permute-start = (bf16[64,256]{1,0:T(8,128)(2,1)S(1)}, bf16[64,256]{1,0:T(8,128)(2,1)S(1)}, u32[]{:S(2)}, u32[]{:S(2)}) collective-permute-start(bf16[64,256]{1,0:T(8,128)(2,1)S(1)} %pad_maximum_fusion.1), channel_id=1, source_target_pairs={{0,64},{8,72},{16,80},{24,88},{32,96},{40,104},{48,112},{56,120},{... | collective-permute-start | bytes 98312 | tf_op jit(solution)/shard_map/ppermute | solution.py:292
  5.3 3.3 %collective-permute-start.1 = (bf16[128,256]{1,0:T(8,128)(2,1)S(1)}, bf16[128,256]{1,0:T(8,128)(2,1)S(1)}, u32[]{:S(2)}, u32[]{:S(2)}) collective-permute-start(bf16[128,256]{1,0:T(8,128)(2,1)S(1)} %get-tuple-element.27), channel_id=1, source_target_pairs={{0,128},{8,136},{16,144},{24,152},{32,160},{40,168},{48,176},{56,1... | collective-permute-start | bytes 196616 | tf_op jit(solution)/shard_map/ppermute | solution.py:292
  8.6 2.6 %collective-permute-done.1 = bf16[128,256]{1,0:T(8,128)(2,1)S(1)} collective-permute-done((bf16[128,256]{1,0:T(8,128)(2,1)S(1)}, bf16[128,256]{1,0:T(8,128)(2,1)S(1)}, u32[]{:S(2)}, u32[]{:S(2)}) %collective-permute-start.1) | collective-permute-done | bytes 65568 | tf_op jit(solution)/shard_map/ppermute | solution.py:292
  11.2 1.6 %collective-permute-start.2 = (bf16[256,256]{1,0:T(8,128)(2,1)S(1)}, bf16[256,256]{1,0:T(8,128)(2,1)S(1)}, u32[]{:S(2)}, u32[]{:S(2)}) collective-permute-start(bf16[256,256]{1,0:T(8,128)(2,1)S(1)} %pad_maximum_fusion), channel_id=1, source_target_pairs={{0,16},{8,24},{16,32},{24,40},{32,48},{40,56},{48,0},{56,8},{64,80... | collective-permute-start | bytes 393224 | tf_op jit(solution)/shard_map/ppermute | solution.py:218
  12.7 2.7 %collective-permute-start.3 = (bf16[256,256]{1,0:T(8,128)(2,1)S(1)}, bf16[256,256]{1,0:T(8,128)(2,1)S(1)}, u32[]{:S(2)}, u32[]{:S(2)}) collective-permute-start(bf16[256,256]{1,0:T(8,128)(2,1)S(1)} %pad_maximum_fusion), channel_id=1, source_target_pairs={{0,32},{8,40},{16,48},{24,56},{32,0},{40,8},{48,16},{56,24},{64,96... | collective-permute-start | bytes 393224 | tf_op jit(solution)/shard_map/ppermute | solution.py:218
  15.5 1.4 collective-permute-start.4
  16.9 6.9 %pack.3.refs_0_ = bf16[64,512,128]{2,1,0:T(8,128)(2,1)} custom-call(s32[32]{0:T(128)} %lengths.3, s32[32]{0:T(128)} %copy-done.12, s32[32]{0:T(128)} %get-tuple-element.20.most, bf16[32,256,128]{2,1,0:T(8,128)(2,1)} %refs_0_.3, bf16[32,256,128]{2,1,0:T(8,128)(2,1)} %refs_1_.3, bf16[32,2,128]{2,1,0:T(2,128)(2,1)} %refs_2_.3, bf16[32,2,128]{2,1,0:T(2,128)(2,1)} %refs_3_.3), custom_call_target="tpu_custom_call" | custom-call | tf_op jit(solution)/shard_map/pack/pallas_call | solution.py:104
  25.2 5.0 %all-to-all-start = ((bf16[64,512,128]{2,1,0:T(8,128)(2,1)}), bf16[64,512,128]{2,1,0:T(8,128)(2,1)}, u32[]{:S(2)}, u32[]{:S(2)}) async-start(bf16[64,512,128]{2,1,0:T(8,128)(2,1)} %after.3), calls=%async_computation | async-start | bytes 16777216 | tf_op jit(solution)/shard_map/all_to_all | solution.py:303
  30.3 5.8 %pack.2 = (bf16[32,256,128]{2,1,0:T(8,128)(2,1)}, bf16[32,256,128]{2,1,0:T(8,128)(2,1)}) custom-call(s32[32]{0:T(128)} %lengths.3, s32[32]{0:T(128)} %copy-done.12, s32[32]{0:T(128)} %get-tuple-element.20.most, bf16[32,256,128]{2,1,0:T(8,128)(2,1)} %refs_0_.3, bf16[32,256,128]{2,1,0:T(8,128)(2,1)} %refs_1_.3, bf16[32,2,128]{2,1,0:T(2,128)(2,1)} %refs_2_.3, ...), custom_call_target="tpu_custom_call" | custom-call | tf_op jit(solution)/shard_map/pack/pallas_call | solution.py:104
  36.8 2.3 %fusion.50 = (f32[32,2,8]{2,1,0:T(2,128)S(1)}, f32[32,2,8,256]{3,2,1,0:T(8,128)S(1)}) fusion(bf16[32,2,8,128]{3,2,1,0:T(8,128)(2,1)S(1)} %reshape.73, bf16[32,256,128]{2,1,0:T(8,128)(2,1)} %get-tuple-element.13, pred[32,2,256]{2,1,0:T(4,128)(4,1)S(1)} %iota_compare_fusion), kind=kOutput, calls=%fused_computation.114 | convolution fusion | flops 33947136 | bytes 2770944 | tf_op jit(solution)/shard_map/pshd,pld->pshl/dot_general | solution.py:313
  39.3 1.3 fusion.41
  41.5 2.7 %bitcast_reduce_fusion = (f32[32,2,8]{0,2,1:T(8,128)S(1)}, f32[2048,32,2,8]{0,1,3,2:T(8,128)}) fusion(bf16[32,2,8,128]{3,2,1,0:T(8,128)(2,1)S(1)} %reshape.73, bf16[2048,256]{1,0:T(8,128)(2,1)S(1)} %constant_dynamic-update-slice_fusion.5), kind=kOutput, calls=%fused_computation.1 | convolution fusion | flops 270532096 | bytes 4851712 | tf_op jit(solution)/shard_map/pshd,nd->pshn/dot_general | solution.py:310
  44.6 3.2 %fusion.1 = f32[32,2,8]{0,2,1:T(8,128)S(1)} fusion(f32[2048,32,2,8]{0,1,3,2:T(8,128)} %get-tuple-element.41, f32[32,2,8]{0,2,1:T(8,128)S(1)} %max.11), kind=kLoop, calls=%fused_computation.3 | loop fusion | flops 3145216 | bytes 4198400 | tf_op jit(solution)/shard_map/reduce_sum | solution.py:323
  47.8 2.0 %fusion.5 = f32[32,2,8,128]{3,2,1,0:T(8,128)S(1)} fusion(bf16[32,256,128]{2,1,0:T(8,128)(2,1)} %get-tuple-element.14, f32[32,2,8,256]{3,2,1,0:T(8,128)S(1)} %get-tuple-element.43, f32[32,2,8]{2,1,0:T(2,128)S(1)} %copy.35), kind=kOutput, calls=%fused_computation.6 | convolution fusion | flops 33816576 | bytes 2885632 | tf_op jit(solution)/shard_map/pshl,pld->pshd/dot_general | solution.py:329
  50.9 15.2 %psum.7 = f32[32]{0:T(128)S(1)} all-reduce(f32[32]{0:T(128)S(1)} %get-tuple-element.28), channel_id=1, replica_groups=mesh['particle'=32,'tensor'=8] {'tensor'}, use_global_device_ids=true, to_apply=%region_7.8 | all-reduce | flops 32 | bytes 256 | tf_op jit(solution)/shard_map/psum | solution.py:339
  69.9 1.8 %collective-permute-start.8 = (f32[2,3,32]{2,1,0:T(4,128)}, f32[2,3,32]{2,1,0:T(4,128)S(1)}, u32[]{:S(2)}, u32[]{:S(2)}) collective-permute-start(f32[2,3,32]{2,1,0:T(4,128)} %after.2._), channel_id=1, source_target_pairs={{0,64},{1,97},{2,66},{3,99},{4,68},{5,101},{6,70},{7,103},{8,88},{... | collective-permute-start | bytes 2312 | tf_op jit(solution)/shard_map/ppermute | solution.py:238
  71.6 2.7 %collective-permute-start.9 = (f32[2,3,32]{2,1,0:T(4,128)}, f32[2,3,32]{2,1,0:T(4,128)S(1)}, u32[]{:S(2)}, u32[]{:S(2)}) collective-permute-start(f32[2,3,32]{2,1,0:T(4,128)} %after.2._), channel_id=1, source_target_pairs={{0,128},{1,161},{2,130},{3,163},{4,132},{5,165},{6,134},{7,167},{8... | collective-permute-start | bytes 2312 | tf_op jit(solution)/shard_map/ppermute | solution.py:238
  74.4 1.4 collective-permute-start.10
  75.8 44.4 %collective-permute-done.8 = f32[2,3,32]{2,1,0:T(4,128)S(1)} collective-permute-done((f32[2,3,32]{2,1,0:T(4,128)}, f32[2,3,32]{2,1,0:T(4,128)S(1)}, u32[]{:S(2)}, u32[]{:S(2)}) %collective-permute-start.8) | collective-permute-done | bytes 800 | tf_op jit(solution)/shard_map/ppermute | solution.py:238
  120.2 3.7 %collective-permute-done.9 = f32[2,3,32]{2,1,0:T(4,128)S(1)} collective-permute-done((f32[2,3,32]{2,1,0:T(4,128)}, f32[2,3,32]{2,1,0:T(4,128)S(1)}, u32[]{:S(2)}, u32[]{:S(2)}) %collective-permute-start.9) | collective-permute-done | bytes 800 | tf_op jit(solution)/shard_map/ppermute | solution.py:238
  123.9 4.1 %collective-permute-done.10 = f32[2,3,32]{2,1,0:T(4,128)S(1)} collective-permute-done((f32[2,3,32]{2,1,0:T(4,128)}, f32[2,3,32]{2,1,0:T(4,128)S(1)}, u32[]{:S(2)}, u32[]{:S(2)}) %collective-permute-start.10) | collective-permute-done | bytes 800 | tf_op jit(solution)/shard_map/ppermute | solution.py:238
  128.0 9.8 %collective-permute-start.12 = (f32[8,3,32]{2,1,0:T(4,128)S(1)}, f32[8,3,32]{2,1,0:T(4,128)S(1)}, u32[]{:S(2)}, u32[]{:S(2)}) collective-permute-start(f32[8,3,32]{2,1,0:T(4,128)S(1)} %constant_dynamic-update-slice_fusion.11.refs_0_), channel_id=1, source_target_pairs={{0,1},{1,0},{2,3},{3,2},{4,5},{5,4},{6,7},{7,6},{8,9},{9,8},{10,11... | collective-permute-start | bytes 9224 | tf_op jit(solution)/shard_map/ppermute | solution.py:248
  138.5 5.6 %unpack.1 = (bf16[32,256,128]{2,1,0:T(8,128)(2,1)}, bf16[32,256,128]{2,1,0:T(8,128)(2,1)}, f32[1,128]{1,0:T(1,128)}) custom-call(s32[32]{0:T(128)} %fusion.42.slots, bf16[64,512,128]{2,1,0:T(8,128)(2,1)} %all-to-all-done.arrived, f32[2,3,32]{2,1,0:T(4,128)} %after.2._), custom_call_target="tpu_custom_call" | custom-call | tf_op jit(solution)/shard_map/unpack/pallas_call | solution.py:161
  144.7 1.5 %finish.1 = (f32[1,8]{1,0:T(1,128)}, s32[1,32]{1,0:T(1,128)}) custom-call(f32[1,32]{1,0:T(1,128)} %pad_bitcast_fusion.2.counted, s32[1,32]{1,0:T(1,128)} %get-tuple-element.24.step, s32[1,32]{1,0:T(1,128)} %get-tuple-element.22.place, f32[8,3,32]{2,1,0:T(4,128)} %copy-done.8, f32[8,3,32]{2,1,0:T(4,128)} %copy-done.9, f32[8,3,32]{2,1,0:T(4,128)} %copy-done.10, ...), custom_call_target="tpu_custom_call" | custom-call | tf_op jit(solution)/shard_map/finish/pallas_call | solution.py:194
  (94 shorter events, 12.6 us)
Async XLA Ops:
  1.4 3.9 %collective-permute-start = (bf16[64,256]{1,0:T(8,128)(2,1)S(1)}, bf16[64,256]{1,0:T(8,128)(2,1)S(1)}, u32[]{:S(2)}, u32[]{:S(2)}) collective-permute-start(bf16[64,256]{1,0:T(8,128)(2,1)S(1)} %pad_maximum_fusion.1), channel_id=1, source_target_pairs={{0,64},{8,72},{16,80},{24,88},{32,96},{40,104},{48,112},{56,120},{... | collective-permute-start | bytes 98312 | tf_op jit(solution)/shard_map/ppermute | solution.py:292
  4.3 12.6 %copy-start.12 = (s32[32]{0:T(128)}, s32[32]{0:T(128)S(1)}, u32[]{:S(2)}) copy-start(s32[32]{0:T(128)S(1)} %get-tuple-element.21.least) | copy-start | bytes 388
  5.3 5.9 %collective-permute-start.1 = (bf16[128,256]{1,0:T(8,128)(2,1)S(1)}, bf16[128,256]{1,0:T(8,128)(2,1)S(1)}, u32[]{:S(2)}, u32[]{:S(2)}) collective-permute-start(bf16[128,256]{1,0:T(8,128)(2,1)S(1)} %get-tuple-element.27), channel_id=1, source_target_pairs={{0,128},{8,136},{16,144},{24,152},{32,160},{40,168},{48,176},{56,1... | collective-permute-start | bytes 196616 | tf_op jit(solution)/shard_map/ppermute | solution.py:292
  11.2 12.6 %collective-permute-start.2 = (bf16[256,256]{1,0:T(8,128)(2,1)S(1)}, bf16[256,256]{1,0:T(8,128)(2,1)S(1)}, u32[]{:S(2)}, u32[]{:S(2)}) collective-permute-start(bf16[256,256]{1,0:T(8,128)(2,1)S(1)} %pad_maximum_fusion), channel_id=1, source_target_pairs={{0,16},{8,24},{16,32},{24,40},{32,48},{40,56},{48,0},{56,8},{64,80... | collective-permute-start | bytes 393224 | tf_op jit(solution)/shard_map/ppermute | solution.py:218
  12.7 11.1 %collective-permute-start.3 = (bf16[256,256]{1,0:T(8,128)(2,1)S(1)}, bf16[256,256]{1,0:T(8,128)(2,1)S(1)}, u32[]{:S(2)}, u32[]{:S(2)}) collective-permute-start(bf16[256,256]{1,0:T(8,128)(2,1)S(1)} %pad_maximum_fusion), channel_id=1, source_target_pairs={{0,32},{8,40},{16,48},{24,56},{32,0},{40,8},{48,16},{56,24},{64,96... | collective-permute-start | bytes 393224 | tf_op jit(solution)/shard_map/ppermute | solution.py:218
  15.5 8.4 %collective-permute-start.4 = (bf16[256,256]{1,0:T(8,128)(2,1)S(1)}, bf16[256,256]{1,0:T(8,128)(2,1)S(1)}, u32[]{:S(2)}, u32[]{:S(2)}) collective-permute-start(bf16[256,256]{1,0:T(8,128)(2,1)S(1)} %pad_maximum_fusion), channel_id=1, source_target_pairs={{0,48},{8,56},{16,0},{24,8},{32,16},{40,24},{48,32},{56,40},{64,11... | collective-permute-start | bytes 393224 | tf_op jit(solution)/shard_map/ppermute | solution.py:218
  25.2 113.3 %all-to-all-start = ((bf16[64,512,128]{2,1,0:T(8,128)(2,1)}), bf16[64,512,128]{2,1,0:T(8,128)(2,1)}, u32[]{:S(2)}, u32[]{:S(2)}) async-start(bf16[64,512,128]{2,1,0:T(8,128)(2,1)} %after.3), calls=%async_computation | async-start | bytes 16777216 | tf_op jit(solution)/shard_map/all_to_all | solution.py:303
  30.2 5.9 %copy-start.14 = (s32[32]{0:T(128)S(1)}, s32[32]{0:T(128)}, u32[]{:S(2)}) copy-start(s32[32]{0:T(128)} %lengths.3) | copy-start | bytes 388
  30.2 6.2 %copy-start.6 = (bf16[256,256]{1,0:T(8,128)(2,1)S(1)}, bf16[256,256]{1,0:T(8,128)(2,1)}, u32[]{:S(2)}) copy-start(bf16[256,256]{1,0:T(8,128)(2,1)} %copy-done.5) | copy-start | bytes 393220
  30.2 6.2 %copy-start.4 = (bf16[256,256]{1,0:T(8,128)(2,1)S(1)}, bf16[256,256]{1,0:T(8,128)(2,1)}, u32[]{:S(2)}) copy-start(bf16[256,256]{1,0:T(8,128)(2,1)} %copy-done.3) | copy-start | bytes 393220
  30.2 6.2 %copy-start.2 = (bf16[256,256]{1,0:T(8,128)(2,1)S(1)}, bf16[256,256]{1,0:T(8,128)(2,1)}, u32[]{:S(2)}) copy-start(bf16[256,256]{1,0:T(8,128)(2,1)} %copy-done.1) | copy-start | bytes 393220
  30.2 9.0 %copy-start.13 = (s32[1024]{0:T(1024)S(1)}, s32[1024]{0:T(1024)}, u32[]{:S(2)}) copy-start(s32[1024]{0:T(1024)} %param.22) | copy-start | bytes 12292
  36.5 5.0 %collective-permute-start.5 = (bf16[1024,256]{1,0:T(8,128)(2,1)S(1)}, bf16[1024,256]{1,0:T(8,128)(2,1)S(1)}, u32[]{:S(2)}, u32[]{:S(2)}) collective-permute-start(bf16[1024,256]{1,0:T(8,128)(2,1)S(1)} %get-tuple-element.30), channel_id=1, source_target_pairs={{0,8},{8,0},{16,24},{24,16},{32,40},{40,32},{48,56},{56,48},{64,72... | collective-permute-start | bytes 1572872 | tf_op jit(solution)/shard_map/ppermute | solution.py:218
  47.8 18.3 %copy-start.17 = (f32[32]{0:T(128)S(1)}, f32[32]{0:T(128)}, u32[]{:S(2)}) copy-start(f32[32]{0:T(128)} %param.20) | copy-start | bytes 388
  66.1 78.0 %copy-start.15 = (f32[32]{0:T(128)}, f32[32]{0:T(128)S(1)}, u32[]{:S(2)}) copy-start(f32[32]{0:T(128)S(1)} %add.135) | copy-start | bytes 388
  66.5 1.4 collective-permute-start.6
  68.4 7.3 %collective-permute-start.7 = (f32[2,3,32]{2,1,0:T(4,128)}, f32[2,3,32]{2,1,0:T(4,128)S(1)}, u32[]{:S(2)}, u32[]{:S(2)}) collective-permute-start(f32[2,3,32]{2,1,0:T(4,128)} %after.2._), channel_id=1, source_target_pairs={{0,0},{1,33},{2,2},{3,35},{4,4},{5,37},{6,6},{7,39},{8,24},{9,57},... | collective-permute-start | bytes 2312 | tf_op jit(solution)/shard_map/ppermute | solution.py:238
  69.9 50.3 %collective-permute-start.8 = (f32[2,3,32]{2,1,0:T(4,128)}, f32[2,3,32]{2,1,0:T(4,128)S(1)}, u32[]{:S(2)}, u32[]{:S(2)}) collective-permute-start(f32[2,3,32]{2,1,0:T(4,128)} %after.2._), channel_id=1, source_target_pairs={{0,64},{1,97},{2,66},{3,99},{4,68},{5,101},{6,70},{7,103},{8,88},{... | collective-permute-start | bytes 2312 | tf_op jit(solution)/shard_map/ppermute | solution.py:238
  71.6 52.3 %collective-permute-start.9 = (f32[2,3,32]{2,1,0:T(4,128)}, f32[2,3,32]{2,1,0:T(4,128)S(1)}, u32[]{:S(2)}, u32[]{:S(2)}) collective-permute-start(f32[2,3,32]{2,1,0:T(4,128)} %after.2._), channel_id=1, source_target_pairs={{0,128},{1,161},{2,130},{3,163},{4,132},{5,165},{6,134},{7,167},{8... | collective-permute-start | bytes 2312 | tf_op jit(solution)/shard_map/ppermute | solution.py:238
  74.4 53.6 %collective-permute-start.10 = (f32[2,3,32]{2,1,0:T(4,128)}, f32[2,3,32]{2,1,0:T(4,128)S(1)}, u32[]{:S(2)}, u32[]{:S(2)}) collective-permute-start(f32[2,3,32]{2,1,0:T(4,128)} %after.2._), channel_id=1, source_target_pairs={{0,192},{1,225},{2,194},{3,227},{4,196},{5,229},{6,198},{7,231},{8... | collective-permute-start | bytes 2312 | tf_op jit(solution)/shard_map/ppermute | solution.py:238
  128.0 16.1 %copy-start.8 = (f32[8,3,32]{2,1,0:T(4,128)}, f32[8,3,32]{2,1,0:T(4,128)S(1)}, u32[]{:S(2)}) copy-start(f32[8,3,32]{2,1,0:T(4,128)S(1)} %constant_dynamic-update-slice_fusion.11.refs_0_) | copy-start | bytes 9220
  128.0 16.1 %collective-permute-start.11 = (f32[8,3,32]{2,1,0:T(4,128)S(1)}, f32[8,3,32]{2,1,0:T(4,128)S(1)}, u32[]{:S(2)}, u32[]{:S(2)}) collective-permute-start(f32[8,3,32]{2,1,0:T(4,128)S(1)} %constant_dynamic-update-slice_fusion.11.refs_0_), channel_id=1, source_target_pairs={{0,8},{1,9},{2,10},{3,11},{4,12},{5,13},{6,14},{7,15},{8,0},{9,1},... | collective-permute-start | bytes 9224 | tf_op jit(solution)/shard_map/ppermute | solution.py:248
  128.0 16.1 %collective-permute-start.12 = (f32[8,3,32]{2,1,0:T(4,128)S(1)}, f32[8,3,32]{2,1,0:T(4,128)S(1)}, u32[]{:S(2)}, u32[]{:S(2)}) collective-permute-start(f32[8,3,32]{2,1,0:T(4,128)S(1)} %constant_dynamic-update-slice_fusion.11.refs_0_), channel_id=1, source_target_pairs={{0,1},{1,0},{2,3},{3,2},{4,5},{5,4},{6,7},{7,6},{8,9},{9,8},{10,11... | collective-permute-start | bytes 9224 | tf_op jit(solution)/shard_map/ppermute | solution.py:248
  137.8 6.3 %collective-permute-start.13 = (f32[8,3,32]{2,1,0:T(4,128)S(1)}, f32[8,3,32]{2,1,0:T(4,128)S(1)}, u32[]{:S(2)}, u32[]{:S(2)}) collective-permute-start(f32[8,3,32]{2,1,0:T(4,128)S(1)} %constant_dynamic-update-slice_fusion.11.refs_0_), channel_id=1, source_target_pairs={{0,9},{1,8},{2,11},{3,10},{4,13},{5,12},{6,15},{7,14},{8,1},{9,0},... | collective-permute-start | bytes 9224 | tf_op jit(solution)/shard_map/ppermute | solution.py:248
  (9 other events, 20.5 us)

commit v7 on v5

--- a/solution.py
+++ b/solution.py
@@ -213,6 +213,19 @@
     return parts
 
 
+def half_of(array):
+    tall, wide, cores = SIDES
+    parts = []
+    for hop, step in itertools.product(range(2), range(2)):
+        pairs = []
+        for i in range(tall * wide * cores):
+            y, x, core = i // (wide * cores), i // cores % wide, i % cores
+            goal = (y ^ 2 * hop) * wide + (x + 2 * core + step) % wide
+            pairs.append((i, goal * cores + core))
+        parts.append(lax.ppermute(array, "particle", pairs))
+    return parts
+
+
 def devices():
     tall, wide, cores = SIDES
     return [
@@ -264,20 +277,6 @@
     sources = lax.axis_size("particle")
     device = lax.axis_index("particle")
 
-    low = -jnp.inf
-    shard = jnp.maximum(
-        jnp.pad(prompt_keys, ((0, 0), (0, HEAD_DIM)), constant_values=low),
-        jnp.pad(prompt_values, ((0, 0), (HEAD_DIM, 0)), constant_values=low),
-    )
-    column = shard
-    for bit in (1, 2):
-        swapped = lax.ppermute(column, "particle", [(i, i ^ bit * 8) for i in range(sources)])
-        column = jnp.concatenate([column, swapped], axis=0)
-    plane = jnp.concatenate(along(column, (1,)), axis=0)
-    prompt = jnp.concatenate(along(plane, (2,)), axis=0)
-    all_keys = prompt[:, :HEAD_DIM]
-    all_values = prompt[:, HEAD_DIM:]
-
     wanted = ancestors.reshape(sources, per_device)
     owner = wanted // per_device
     local = wanted % per_device
@@ -289,6 +288,20 @@
     same_owner = mine_owner[:, None] == mine_owner[None, :]
     first = jnp.min(jnp.where(same_owner, mine[None, :], sources * per_device), axis=1)
     slot = mine_owner * DISTINCT + (mine != first).astype(jnp.int32)
+
+    low = -jnp.inf
+    shard = jnp.maximum(
+        jnp.pad(prompt_keys, ((0, 0), (0, HEAD_DIM)), constant_values=low),
+        jnp.pad(prompt_values, ((0, 0), (HEAD_DIM, 0)), constant_values=low),
+    )
+    chip = jnp.concatenate(along(shard, (2,)), axis=0)
+    chip = chip + jnp.minimum(least[0], 0).astype(chip.dtype)
+    beside = lax.ppermute(chip, "particle", [(i, i ^ 8) for i in range(sources)])
+    column = jnp.concatenate([chip, beside], axis=0)
+    half = jnp.concatenate(half_of(column), axis=0)
+    prompt = jnp.concatenate(along(half, (2,)), axis=0)
+    all_keys = prompt[:, :HEAD_DIM]
+    all_values = prompt[:, HEAD_DIM:]
 
     exchange = functools.partial(
         lax.all_to_all, axis_name="particle", split_axis=0, concat_axis=0, tiled=True
@@ -333,7 +346,11 @@
     attention = output.astype(jnp.bfloat16)
 
     partial_reward = jnp.sum(output * reward_dir[None, None, :], axis=(1, 2))
-    weights = prior + lax.psum(partial_reward, "tensor")
+    reward = partial_reward
+    for bit in (1, 2, 4):
+        pairs = [(i, i ^ bit) for i in range(PLANES)]
+        reward = reward + lax.ppermute(reward, "tensor", pairs)
+    weights = prior + reward
     own_rungs = lax.dynamic_slice_in_dim(rungs, device * per_device, per_device)
     ladder = jnp.arange(RUNGS, dtype=jnp.int32)
     member = own_rungs[:, None] == ladder[None, :]
@@ -346,10 +363,11 @@
         [
             jnp.pad(local_peak, (0, spare)),
             jnp.pad(local_sum, (0, spare), constant_values=1.0),
-            lengths.astype(jnp.float32) + mark[0, :per_device],
+            lengths.astype(jnp.float32),
         ]
     )[None]
     near = jnp.concatenate(along(shared, (2,)), axis=0)
+    near = after(near, attention, mark)
     cross = jnp.concatenate(columns_of(near), axis=0)
     next_values, mark = unpack(arrived_values, slot, near)
     parts = [cross] + copies_of(cross)

time: 145 us -> 147 us (1.014)
  blocking collectives: 15.2 us -> 0 us
  waiting for transfers between devices: 46.4 us -> 60.4 us
  starting transfers between devices: 37.4 us -> 40.7 us
    ppermute x2 -> x8, waiting for transfers between devices: 1.58 us -> 52.4 us  [the longest x4 40.4 us: half_of(): parts.append(lax.ppermute(array, 'particle', pairs))]
    all_to_all x1, waiting for transfers between devices: 36.4 us -> 0.01 us  [shards(): arrived_keys = exchange(after(outgoing_keys, column))]
    psum x1 -> x0, blocking collectives: 15.2 us -> none  [shards(): weights = prior + lax.psum(partial_reward, 'tensor')]
    ppermute x2 -> x8, starting transfers between devices: 4.86 us -> 11.1 us  [the longest x4 6.89 us: half_of(): parts.append(lax.ppermute(array, 'particle', pairs))]
    ppermute x5 -> x3, starting transfers between devices: 6.23 us -> 1.98 us  [along(): lax.ppermute(array, 'particle', pairs)]
    all_to_all x1, starting transfers between devices: 5.44 us -> 7.29 us  [shards(): arrived_keys = exchange(after(outgoing_keys, column))]
    ppermute x5 -> x3, waiting for transfers between devices: 1.55 us -> 0.01 us  [along(): lax.ppermute(array, 'particle', pairs)]
  transfers between devices with their start and end apart: 16 -> 20, of which waited for: 6 -> 7; matrix products, arithmetic and copies ran while one was open for 13% -> 13% of each run, Pallas kernels for 14% -> 14%
where the time goes in v7:
time: 147 us; the launch traced here: 145 us
  waiting for transfers between devices  60.4 us (41%)
  starting transfers between devices  40.7 us (28%)
  Pallas kernels  21.7 us (15%)
  other arithmetic  9.39 us (6%)
  matrix products  8.11 us (6%)
  local copies, waits for them, and re-layouts  3.16 us (2%)
    ppermute x4, waiting for transfers between devices, half_of(): parts.append(lax.ppermute(array, 'particle', pairs))  40.4 us
    ppermute x3, waiting for transfers between devices, shards(): reward = reward + lax.ppermute(reward, 'tensor', pairs)  12 us
    pallas_call x2, Pallas kernels, pack(): pl.pallas_call(functools.partial(pack_kernel, keeps), out_shape=[jax.Shap...  11.8 us
    ppermute x3, starting transfers between devices, copies_of(): parts.append(lax.ppermute(array, ('particle', 'tensor'), pairs))  8.44 us
    pallas_call x2, Pallas kernels, unpack(): pl.pallas_call(unpack_kernel, out_shape=(jax.ShapeDtypeStruct(shape, arri...  8.33 us
    ppermute x4, waiting for transfers between devices, columns_of(): parts.append(lax.ppermute(array, ('particle', 'tensor'), pairs))  7.95 us
    all_to_all x1, starting transfers between devices, shards(): arrived_keys = exchange(after(outgoing_keys, column))  7.29 us
    ppermute x4, starting transfers between devices, columns_of(): parts.append(lax.ppermute(array, ('particle', 'tensor'), pairs))  6.96 us
  transfers between devices with their start and end apart: 20, of which 7 were waited for; matrix products, arithmetic and copies ran while one was open for 13% of the time, Pallas kernels for 14%

profile of v7, /device:TPU:128, one launch (start us, length us, event | category | flops | bytes accessed | tf_op | source)
XLA Modules:
  0.0 144.5 jit_solution(13762381179339235107)
XLA Ops:
  4.5 4.9 %pack.3.refs_0_ = bf16[64,256,128]{2,1,0:T(8,128)(2,1)} custom-call(s32[32]{0:T(128)} %lengths.3, s32[32]{0:T(128)} %copy-done.7, s32[32]{0:T(128)} %get-tuple-element.24.most, bf16[32,256,128]{2,1,0:T(8,128)(2,1)} %refs_0_.3, bf16[32,2,128]{2,1,0:T(2,128)(2,1)} %refs_1_.3), custom_call_target="tpu_custom_call" | custom-call | tf_op jit(solution)/shard_map/pack/pallas_call | solution.py:99
  10.1 7.3 %all-to-all-start = ((bf16[64,256,128]{2,1,0:T(8,128)(2,1)}), bf16[64,256,128]{2,1,0:T(8,128)(2,1)}, u32[]{:S(2)}, u32[]{:S(2)}) async-start(bf16[64,256,128]{2,1,0:T(8,128)(2,1)} %after.3), calls=%async_computation | async-start | bytes 8388608 | tf_op jit(solution)/shard_map/all_to_all | solution.py:311
  17.5 7.0 %pack.2 = (bf16[64,256,128]{2,1,0:T(8,128)(2,1)}, bf16[32,256,128]{2,1,0:T(8,128)(2,1)}, bf16[32,256,128]{2,1,0:T(8,128)(2,1)}) custom-call(s32[32]{0:T(128)} %lengths.3, s32[32]{0:T(128)} %copy-done.7, s32[32]{0:T(128)} %get-tuple-element.24.most, bf16[32,256,128]{2,1,0:T(8,128)(2,1)} %refs_0_.3, bf16[32,256,128]{2,1,0:T(8,128)(2,1)} %refs_1_.2, ...), custom_call_target="tpu_custom_call" | custom-call | tf_op jit(solution)/shard_map/pack/pallas_call | solution.py:99
  25.4 1.8 %collective-permute-start.3 = (bf16[256,256]{1,0:T(8,128)(2,1)S(1)}, bf16[256,256]{1,0:T(8,128)(2,1)S(1)}, u32[]{:S(2)}, u32[]{:S(2)}) collective-permute-start(bf16[256,256]{1,0:T(8,128)(2,1)S(1)} %copy-done.1), channel_id=1, source_target_pairs={{0,16},{8,56},{16,32},{24,8},{32,48},{40,24},{48,0},{56,40},{64,80... | collective-permute-start | bytes 393224 | tf_op jit(solution)/shard_map/ppermute | solution.py:225
  27.2 3.0 %collective-permute-start.4 = (bf16[256,256]{1,0:T(8,128)(2,1)S(1)}, bf16[256,256]{1,0:T(8,128)(2,1)S(1)}, u32[]{:S(2)}, u32[]{:S(2)}) collective-permute-start(bf16[256,256]{1,0:T(8,128)(2,1)S(1)} %copy-done.1), channel_id=1, source_target_pairs={{0,128},{8,168},{16,144},{24,184},{32,160},{40,136},{48,176},{56,1... | collective-permute-start | bytes 393224 | tf_op jit(solution)/shard_map/ppermute | solution.py:225
  31.6 2.3 %fusion.50 = (f32[32,2,8]{2,1,0:T(2,128)S(1)}, f32[32,2,8,256]{3,2,1,0:T(8,128)S(1)}) fusion(bf16[32,2,8,128]{3,2,1,0:T(8,128)(2,1)S(1)} %reshape.73, bf16[32,256,128]{2,1,0:T(8,128)(2,1)} %get-tuple-element.15, pred[32,2,256]{2,1,0:T(4,128)(4,1)S(1)} %iota_compare_fusion), kind=kOutput, calls=%fused_computation.110 | convolution fusion | flops 33947136 | bytes 2770944 | tf_op jit(solution)/shard_map/pshd,pld->pshl/dot_general | solution.py:323
  34.1 34.1 %collective-permute-done.3 = bf16[256,256]{1,0:T(8,128)(2,1)S(1)} collective-permute-done((bf16[256,256]{1,0:T(8,128)(2,1)S(1)}, bf16[256,256]{1,0:T(8,128)(2,1)S(1)}, u32[]{:S(2)}, u32[]{:S(2)}) %collective-permute-start.3) | collective-permute-done | bytes 131104 | tf_op jit(solution)/shard_map/ppermute | solution.py:225
  68.2 6.3 %collective-permute-done.5 = bf16[256,256]{1,0:T(8,128)(2,1)S(1)} collective-permute-done((bf16[256,256]{1,0:T(8,128)(2,1)S(1)}, bf16[256,256]{1,0:T(8,128)(2,1)S(1)}, u32[]{:S(2)}, u32[]{:S(2)}) %collective-permute-start.5) | collective-permute-done | bytes 131104 | tf_op jit(solution)/shard_map/ppermute | solution.py:225
  74.5 1.7 %collective-permute-start.6 = (bf16[1024,256]{1,0:T(8,128)(2,1)S(1)}, bf16[1024,256]{1,0:T(8,128)(2,1)S(1)}, u32[]{:S(2)}, u32[]{:S(2)}) collective-permute-start(bf16[1024,256]{1,0:T(8,128)(2,1)S(1)} %pad_maximum_fusion), channel_id=1, source_target_pairs={{0,8},{8,0},{16,24},{24,16},{32,40},{40,32},{48,56},{56,48},{64,72... | collective-permute-start | bytes 1572872 | tf_op jit(solution)/shard_map/ppermute | solution.py:212
  77.5 4.9 %all-to-all-start.1 = ((bf16[64,256,128]{2,1,0:T(8,128)(2,1)}), bf16[64,256,128]{2,1,0:T(8,128)(2,1)}, u32[]{:S(2)}, u32[]{:S(2)}) async-start(bf16[64,256,128]{2,1,0:T(8,128)(2,1)} %after.5), calls=%async_computation.1 | async-start | bytes 8388608 | tf_op jit(solution)/shard_map/all_to_all | solution.py:315
  82.5 2.6 %bitcast_reduce_fusion = (f32[32,2,8]{0,2,1:T(8,128)S(1)}, f32[2048,32,2,8]{0,1,3,2:T(8,128)}) fusion(bf16[32,2,8,128]{3,2,1,0:T(8,128)(2,1)S(1)} %reshape.73, bf16[2048,256]{1,0:T(8,128)(2,1)S(1)} %constant_dynamic-update-slice_fusion), kind=kOutput, calls=%fused_computation.1 | convolution fusion | flops 270532096 | bytes 4851712 | tf_op jit(solution)/shard_map/pshd,nd->pshn/dot_general | solution.py:320
  85.6 3.2 %fusion.1 = f32[32,2,8]{0,2,1:T(8,128)S(1)} fusion(f32[2048,32,2,8]{0,1,3,2:T(8,128)} %get-tuple-element.35, f32[32,2,8]{0,2,1:T(8,128)S(1)} %max.11), kind=kLoop, calls=%fused_computation.3 | loop fusion | flops 3145216 | bytes 4198400 | tf_op jit(solution)/shard_map/reduce_sum | solution.py:333
  88.8 2.1 %fusion.5 = f32[32,2,8,128]{3,2,1,0:T(8,128)S(1)} fusion(bf16[32,256,128]{2,1,0:T(8,128)(2,1)} %get-tuple-element.16, f32[32,2,8,256]{3,2,1,0:T(8,128)S(1)} %get-tuple-element.37, f32[32,2,8]{2,1,0:T(2,128)S(1)} %copy.36), kind=kOutput, calls=%fused_computation.6 | convolution fusion | flops 33816576 | bytes 2885632 | tf_op jit(solution)/shard_map/pshl,pld->pshd/dot_general | solution.py:339
  93.7 1.9 %collective-permute-done.7 = f32[32]{0:T(128)S(1)} collective-permute-done((f32[32]{0:T(128)S(1)}, f32[32]{0:T(128)S(1)}, u32[]{:S(2)}, u32[]{:S(2)}) %collective-permute-start.7) | collective-permute-done | bytes 160 | tf_op jit(solution)/shard_map/ppermute | solution.py:352
  97.2 2.8 %collective-permute-done.8 = f32[32]{0:T(128)S(1)} collective-permute-done((f32[32]{0:T(128)S(1)}, f32[32]{0:T(128)S(1)}, u32[]{:S(2)}, u32[]{:S(2)}) %collective-permute-start.8) | collective-permute-done | bytes 160 | tf_op jit(solution)/shard_map/ppermute | solution.py:352
  100.1 7.4 %collective-permute-done.9 = f32[32]{0:T(128)S(1)} collective-permute-done((f32[32]{0:T(128)S(1)}, f32[32]{0:T(128)S(1)}, u32[]{:S(2)}, u32[]{:S(2)}) %collective-permute-start.9) | collective-permute-done | bytes 160 | tf_op jit(solution)/shard_map/ppermute | solution.py:352
  110.0 4.2 %unpack.2 = (bf16[32,256,128]{2,1,0:T(8,128)(2,1)}, f32[1,128]{1,0:T(1,128)}) custom-call(s32[32]{0:T(128)} %fusion.42.slots, bf16[64,256,128]{2,1,0:T(8,128)(2,1)} %all-to-all-done.arrived.refs_1_, bf16[256,256]{1,0:T(8,128)(2,1)} %pad_maximum_fusion.1.refs_1_._), custom_call_target="tpu_custom_call" | custom-call | tf_op jit(solution)/shard_map/unpack/pallas_call | solution.py:152
  115.6 1.8 %collective-permute-start.12 = (f32[2,3,32]{2,1,0:T(4,128)}, f32[2,3,32]{2,1,0:T(4,128)S(1)}, u32[]{:S(2)}, u32[]{:S(2)}) collective-permute-start(f32[2,3,32]{2,1,0:T(4,128)} %after.4._), channel_id=1, source_target_pairs={{0,64},{1,97},{2,66},{3,99},{4,68},{5,101},{6,70},{7,103},{8,88},{... | collective-permute-start | bytes 2312 | tf_op jit(solution)/shard_map/ppermute | solution.py:245
  117.3 2.9 %collective-permute-start.13 = (f32[2,3,32]{2,1,0:T(4,128)}, f32[2,3,32]{2,1,0:T(4,128)S(1)}, u32[]{:S(2)}, u32[]{:S(2)}) collective-permute-start(f32[2,3,32]{2,1,0:T(4,128)} %after.4._), channel_id=1, source_target_pairs={{0,128},{1,161},{2,130},{3,163},{4,132},{5,165},{6,134},{7,167},{8... | collective-permute-start | bytes 2312 | tf_op jit(solution)/shard_map/ppermute | solution.py:245
  121.2 4.2 %collective-permute-done.12 = f32[2,3,32]{2,1,0:T(4,128)S(1)} collective-permute-done((f32[2,3,32]{2,1,0:T(4,128)}, f32[2,3,32]{2,1,0:T(4,128)S(1)}, u32[]{:S(2)}, u32[]{:S(2)}) %collective-permute-start.12) | collective-permute-done | bytes 800 | tf_op jit(solution)/shard_map/ppermute | solution.py:245
  125.4 3.8 %collective-permute-done.13 = f32[2,3,32]{2,1,0:T(4,128)S(1)} collective-permute-done((f32[2,3,32]{2,1,0:T(4,128)}, f32[2,3,32]{2,1,0:T(4,128)S(1)}, u32[]{:S(2)}, u32[]{:S(2)}) %collective-permute-start.13) | collective-permute-done | bytes 800 | tf_op jit(solution)/shard_map/ppermute | solution.py:245
  129.2 3.1 %collective-permute-start.15 = (f32[8,3,32]{2,1,0:T(4,128)S(1)}, f32[8,3,32]{2,1,0:T(4,128)S(1)}, u32[]{:S(2)}, u32[]{:S(2)}) collective-permute-start(f32[8,3,32]{2,1,0:T(4,128)S(1)} %constant_dynamic-update-slice_fusion.5.refs_0_), channel_id=1, source_target_pairs={{0,8},{1,9},{2,10},{3,11},{4,12},{5,13},{6,14},{7,15},{8,0},{9,1},... | collective-permute-start | bytes 9224 | tf_op jit(solution)/shard_map/ppermute | solution.py:255
  132.2 5.3 %collective-permute-start.16 = (f32[8,3,32]{2,1,0:T(4,128)S(1)}, f32[8,3,32]{2,1,0:T(4,128)S(1)}, u32[]{:S(2)}, u32[]{:S(2)}) collective-permute-start(f32[8,3,32]{2,1,0:T(4,128)S(1)} %constant_dynamic-update-slice_fusion.5.refs_0_), channel_id=1, source_target_pairs={{0,1},{1,0},{2,3},{3,2},{4,5},{5,4},{6,7},{7,6},{8,9},{9,8},{10,11... | collective-permute-start | bytes 9224 | tf_op jit(solution)/shard_map/ppermute | solution.py:255
  138.2 4.2 %unpack.3 = (bf16[32,256,128]{2,1,0:T(8,128)(2,1)}, f32[1,128]{1,0:T(1,128)}) custom-call(s32[32]{0:T(128)} %fusion.42.slots, bf16[64,256,128]{2,1,0:T(8,128)(2,1)} %all-to-all-done.1.arrived, f32[2,3,32]{2,1,0:T(4,128)} %after.4._), custom_call_target="tpu_custom_call" | custom-call | tf_op jit(solution)/shard_map/unpack/pallas_call | solution.py:152
  (97 shorter events, 21.0 us)
Async XLA Ops:
  1.4 1.5 %collective-permute-start = (bf16[64,256]{1,0:T(8,128)(2,1)S(1)}, bf16[64,256]{1,0:T(8,128)(2,1)S(1)}, u32[]{:S(2)}, u32[]{:S(2)}) collective-permute-start(bf16[64,256]{1,0:T(8,128)(2,1)S(1)} %pad_maximum_fusion.2), channel_id=1, source_target_pairs={{0,8},{8,0},{16,24},{24,16},{32,40},{40,32},{48,56},{56,48},{64,72... | collective-permute-start | bytes 98312 | tf_op jit(solution)/shard_map/ppermute | solution.py:212
  2.9 6.6 %collective-permute-start.1 = (bf16[128,256]{1,0:T(8,128)(2,1)S(1)}, bf16[128,256]{1,0:T(8,128)(2,1)S(1)}, u32[]{:S(2)}, u32[]{:S(2)}) collective-permute-start(bf16[128,256]{1,0:T(8,128)(2,1)S(1)} %maximum_add_fusion), channel_id=1, source_target_pairs={{0,64},{8,72},{16,80},{24,88},{32,96},{40,104},{48,112},{56,120},{... | collective-permute-start | bytes 196616 | tf_op jit(solution)/shard_map/ppermute | solution.py:299
  10.1 67.4 %all-to-all-start = ((bf16[64,256,128]{2,1,0:T(8,128)(2,1)}), bf16[64,256,128]{2,1,0:T(8,128)(2,1)}, u32[]{:S(2)}, u32[]{:S(2)}) async-start(bf16[64,256,128]{2,1,0:T(8,128)(2,1)} %after.3), calls=%async_computation | async-start | bytes 8388608 | tf_op jit(solution)/shard_map/all_to_all | solution.py:311
  24.7 9.4 %collective-permute-start.2 = (bf16[256,256]{1,0:T(8,128)(2,1)S(1)}, bf16[256,256]{1,0:T(8,128)(2,1)S(1)}, u32[]{:S(2)}, u32[]{:S(2)}) collective-permute-start(bf16[256,256]{1,0:T(8,128)(2,1)S(1)} %copy-done.1), channel_id=1, source_target_pairs={{0,0},{8,40},{16,16},{24,56},{32,32},{40,8},{48,48},{56,24},{64,64... | collective-permute-start | bytes 393224 | tf_op jit(solution)/shard_map/ppermute | solution.py:225
  25.4 42.8 %collective-permute-start.3 = (bf16[256,256]{1,0:T(8,128)(2,1)S(1)}, bf16[256,256]{1,0:T(8,128)(2,1)S(1)}, u32[]{:S(2)}, u32[]{:S(2)}) collective-permute-start(bf16[256,256]{1,0:T(8,128)(2,1)S(1)} %copy-done.1), channel_id=1, source_target_pairs={{0,16},{8,56},{16,32},{24,8},{32,48},{40,24},{48,0},{56,40},{64,80... | collective-permute-start | bytes 393224 | tf_op jit(solution)/shard_map/ppermute | solution.py:225
  27.2 41.0 %collective-permute-start.4 = (bf16[256,256]{1,0:T(8,128)(2,1)S(1)}, bf16[256,256]{1,0:T(8,128)(2,1)S(1)}, u32[]{:S(2)}, u32[]{:S(2)}) collective-permute-start(bf16[256,256]{1,0:T(8,128)(2,1)S(1)} %copy-done.1), channel_id=1, source_target_pairs={{0,128},{8,168},{16,144},{24,184},{32,160},{40,136},{48,176},{56,1... | collective-permute-start | bytes 393224 | tf_op jit(solution)/shard_map/ppermute | solution.py:225
  30.2 44.3 %collective-permute-start.5 = (bf16[256,256]{1,0:T(8,128)(2,1)S(1)}, bf16[256,256]{1,0:T(8,128)(2,1)S(1)}, u32[]{:S(2)}, u32[]{:S(2)}) collective-permute-start(bf16[256,256]{1,0:T(8,128)(2,1)S(1)} %copy-done.1), channel_id=1, source_target_pairs={{0,144},{8,184},{16,160},{24,136},{32,176},{40,152},{48,128},{56,1... | collective-permute-start | bytes 393224 | tf_op jit(solution)/shard_map/ppermute | solution.py:225
  74.5 7.9 %collective-permute-start.6 = (bf16[1024,256]{1,0:T(8,128)(2,1)S(1)}, bf16[1024,256]{1,0:T(8,128)(2,1)S(1)}, u32[]{:S(2)}, u32[]{:S(2)}) collective-permute-start(bf16[1024,256]{1,0:T(8,128)(2,1)S(1)} %pad_maximum_fusion), channel_id=1, source_target_pairs={{0,8},{8,0},{16,24},{24,16},{32,40},{40,32},{48,56},{56,48},{64,72... | collective-permute-start | bytes 1572872 | tf_op jit(solution)/shard_map/ppermute | solution.py:212
  77.5 60.6 %all-to-all-start.1 = ((bf16[64,256,128]{2,1,0:T(8,128)(2,1)}), bf16[64,256,128]{2,1,0:T(8,128)(2,1)}, u32[]{:S(2)}, u32[]{:S(2)}) async-start(bf16[64,256,128]{2,1,0:T(8,128)(2,1)} %after.5), calls=%async_computation.1 | async-start | bytes 8388608 | tf_op jit(solution)/shard_map/all_to_all | solution.py:315
  88.8 11.2 %copy-start.8 = (s32[1024]{0:T(1024)S(1)}, s32[1024]{0:T(1024)}, u32[]{:S(2)}) copy-start(s32[1024]{0:T(1024)} %param.22) | copy-start | bytes 12292
  88.8 18.7 %copy-start.11 = (f32[32]{0:T(128)S(1)}, f32[32]{0:T(128)}, u32[]{:S(2)}) copy-start(f32[32]{0:T(128)} %param.20) | copy-start | bytes 388
  92.0 3.6 %collective-permute-start.7 = (f32[32]{0:T(128)S(1)}, f32[32]{0:T(128)S(1)}, u32[]{:S(2)}, u32[]{:S(2)}) collective-permute-start(f32[32]{0:T(128)S(1)} %get-tuple-element.30), channel_id=1, source_target_pairs={{0,1},{1,0},{2,3},{3,2},{4,5},{5,4},{6,7},{7,6},{8,9},{9,8},{10,11... | collective-permute-start | bytes 392 | tf_op jit(solution)/shard_map/ppermute | solution.py:352
  95.6 4.4 %collective-permute-start.8 = (f32[32]{0:T(128)S(1)}, f32[32]{0:T(128)S(1)}, u32[]{:S(2)}, u32[]{:S(2)}) collective-permute-start(f32[32]{0:T(128)S(1)} %add.142), channel_id=1, source_target_pairs={{0,2},{1,3},{2,0},{3,1},{4,6},{5,7},{6,4},{7,5},{8,10},{9,11},{10,... | collective-permute-start | bytes 392 | tf_op jit(solution)/shard_map/ppermute | solution.py:352
  100.0 7.4 %collective-permute-start.9 = (f32[32]{0:T(128)S(1)}, f32[32]{0:T(128)S(1)}, u32[]{:S(2)}, u32[]{:S(2)}) collective-permute-start(f32[32]{0:T(128)S(1)} %add.143), channel_id=1, source_target_pairs={{0,4},{1,5},{2,6},{3,7},{4,0},{5,1},{6,2},{7,3},{8,12},{9,13},{10,... | collective-permute-start | bytes 392 | tf_op jit(solution)/shard_map/ppermute | solution.py:352
  107.5 34.9 %copy-start.10 = (f32[32]{0:T(128)}, f32[32]{0:T(128)S(1)}, u32[]{:S(2)}) copy-start(f32[32]{0:T(128)S(1)} %add_add_fusion) | copy-start | bytes 388
  107.8 1.5 %collective-permute-start.10 = (f32[1,3,32]{2,1,0:T(4,128)S(1)}, f32[1,3,32]{2,1,0:T(4,128)S(1)}, u32[]{:S(2)}, u32[]{:S(2)}) collective-permute-start(f32[1,3,32]{2,1,0:T(4,128)S(1)} %maximum_bitcast_fusion), channel_id=1, source_target_pairs={{0,8},{8,0},{16,24},{24,16},{32,40},{40,32},{48,56},{56,48},{64,72... | collective-permute-start | bytes 1160 | tf_op jit(solution)/shard_map/ppermute | solution.py:212
  114.1 7.1 %collective-permute-start.11 = (f32[2,3,32]{2,1,0:T(4,128)}, f32[2,3,32]{2,1,0:T(4,128)S(1)}, u32[]{:S(2)}, u32[]{:S(2)}) collective-permute-start(f32[2,3,32]{2,1,0:T(4,128)} %after.4._), channel_id=1, source_target_pairs={{0,0},{1,33},{2,2},{3,35},{4,4},{5,37},{6,6},{7,39},{8,24},{9,57},... | collective-permute-start | bytes 2312 | tf_op jit(solution)/shard_map/ppermute | solution.py:245
  115.6 9.8 %collective-permute-start.12 = (f32[2,3,32]{2,1,0:T(4,128)}, f32[2,3,32]{2,1,0:T(4,128)S(1)}, u32[]{:S(2)}, u32[]{:S(2)}) collective-permute-start(f32[2,3,32]{2,1,0:T(4,128)} %after.4._), channel_id=1, source_target_pairs={{0,64},{1,97},{2,66},{3,99},{4,68},{5,101},{6,70},{7,103},{8,88},{... | collective-permute-start | bytes 2312 | tf_op jit(solution)/shard_map/ppermute | solution.py:245
  117.3 11.8 %collective-permute-start.13 = (f32[2,3,32]{2,1,0:T(4,128)}, f32[2,3,32]{2,1,0:T(4,128)S(1)}, u32[]{:S(2)}, u32[]{:S(2)}) collective-permute-start(f32[2,3,32]{2,1,0:T(4,128)} %after.4._), channel_id=1, source_target_pairs={{0,128},{1,161},{2,130},{3,163},{4,132},{5,165},{6,134},{7,167},{8... | collective-permute-start | bytes 2312 | tf_op jit(solution)/shard_map/ppermute | solution.py:245
  120.2 9.0 %collective-permute-start.14 = (f32[2,3,32]{2,1,0:T(4,128)}, f32[2,3,32]{2,1,0:T(4,128)S(1)}, u32[]{:S(2)}, u32[]{:S(2)}) collective-permute-start(f32[2,3,32]{2,1,0:T(4,128)} %after.4._), channel_id=1, source_target_pairs={{0,192},{1,225},{2,194},{3,227},{4,196},{5,229},{6,198},{7,231},{8... | collective-permute-start | bytes 2312 | tf_op jit(solution)/shard_map/ppermute | solution.py:245
  129.2 13.2 %copy-start.3 = (f32[8,3,32]{2,1,0:T(4,128)}, f32[8,3,32]{2,1,0:T(4,128)S(1)}, u32[]{:S(2)}) copy-start(f32[8,3,32]{2,1,0:T(4,128)S(1)} %constant_dynamic-update-slice_fusion.5.refs_0_) | copy-start | bytes 9220
  129.2 13.2 %collective-permute-start.15 = (f32[8,3,32]{2,1,0:T(4,128)S(1)}, f32[8,3,32]{2,1,0:T(4,128)S(1)}, u32[]{:S(2)}, u32[]{:S(2)}) collective-permute-start(f32[8,3,32]{2,1,0:T(4,128)S(1)} %constant_dynamic-update-slice_fusion.5.refs_0_), channel_id=1, source_target_pairs={{0,8},{1,9},{2,10},{3,11},{4,12},{5,13},{6,14},{7,15},{8,0},{9,1},... | collective-permute-start | bytes 9224 | tf_op jit(solution)/shard_map/ppermute | solution.py:255
  132.2 10.1 %collective-permute-start.16 = (f32[8,3,32]{2,1,0:T(4,128)S(1)}, f32[8,3,32]{2,1,0:T(4,128)S(1)}, u32[]{:S(2)}, u32[]{:S(2)}) collective-permute-start(f32[8,3,32]{2,1,0:T(4,128)S(1)} %constant_dynamic-update-slice_fusion.5.refs_0_), channel_id=1, source_target_pairs={{0,1},{1,0},{2,3},{3,2},{4,5},{5,4},{6,7},{7,6},{8,9},{9,8},{10,11... | collective-permute-start | bytes 9224 | tf_op jit(solution)/shard_map/ppermute | solution.py:255
  137.6 4.8 %collective-permute-start.17 = (f32[8,3,32]{2,1,0:T(4,128)S(1)}, f32[8,3,32]{2,1,0:T(4,128)S(1)}, u32[]{:S(2)}, u32[]{:S(2)}) collective-permute-start(f32[8,3,32]{2,1,0:T(4,128)S(1)} %constant_dynamic-update-slice_fusion.5.refs_0_), channel_id=1, source_target_pairs={{0,9},{1,8},{2,11},{3,10},{4,13},{5,12},{6,15},{7,14},{8,1},{9,0},... | collective-permute-start | bytes 9224 | tf_op jit(solution)/shard_map/ppermute | solution.py:255
  (9 other events, 36.2 us)

commit v8 on v7

--- a/solution.py
+++ b/solution.py
@@ -226,36 +226,6 @@
     return parts
 
 
-def devices():
-    tall, wide, cores = SIDES
-    return [
-        (i, z, i % cores + cores * (z % 2)) for i in range(tall * wide * cores) for z in range(PLANES)
-    ]
-
-
-def columns_of(array):
-    tall, wide, cores = SIDES
-    parts = []
-    for step in range(tall):
-        pairs = []
-        for i, z, copy in devices():
-            y, x = i // (wide * cores), i // cores % wide
-            goal = (((y + step) % tall) * wide + (x + copy) % wide) * cores + i % cores
-            pairs.append((i * PLANES + z, goal * PLANES + z))
-        parts.append(lax.ppermute(array, ("particle", "tensor"), pairs))
-    return parts
-
-
-def copies_of(array):
-    parts = []
-    for other in range(1, 4):
-        pairs = [
-            (i * PLANES + z, (i ^ other % 2) * PLANES + (z ^ other // 2)) for i, z, _ in devices()
-        ]
-        parts.append(lax.ppermute(array, ("particle", "tensor"), pairs))
-    return parts
-
-
 def shards(
     queries,
     new_keys,
@@ -298,10 +268,7 @@
     chip = chip + jnp.minimum(least[0], 0).astype(chip.dtype)
     beside = lax.ppermute(chip, "particle", [(i, i ^ 8) for i in range(sources)])
     column = jnp.concatenate([chip, beside], axis=0)
-    half = jnp.concatenate(half_of(column), axis=0)
-    prompt = jnp.concatenate(along(half, (2,)), axis=0)
-    all_keys = prompt[:, :HEAD_DIM]
-    all_values = prompt[:, HEAD_DIM:]
+    halves = half_of(column)
 
     exchange = functools.partial(
         lax.all_to_all, axis_name="particle", split_axis=0, concat_axis=0, tiled=True
@@ -314,6 +281,12 @@
     )
     arrived_values = exchange(after(outgoing_values, arrived_keys))
     next_keys, mark = unpack(arrived_keys, slot, column)
+
+    none = jnp.minimum(jnp.abs(arrived_keys[0, 0, 0]), 0)
+    half = jnp.concatenate(halves, axis=0) + none
+    prompt = jnp.concatenate(along(half, (2,)), axis=0)
+    all_keys = prompt[:, :HEAD_DIM]
+    all_values = prompt[:, HEAD_DIM:]
 
     query = queries.reshape(per_device, STEPS, groups, HEAD_DIM)
     front = (
@@ -367,19 +340,17 @@
         ]
     )[None]
     near = jnp.concatenate(along(shared, (2,)), axis=0)
-    near = after(near, attention, mark)
-    cross = jnp.concatenate(columns_of(near), axis=0)
+    near = after(near, attention)
+    near = jnp.concatenate(along(near, (0,)), axis=0) + mark[0, :per_device]
+    parts = along(near, (1,))
     next_values, mark = unpack(arrived_values, slot, near)
-    parts = [cross] + copies_of(cross)
 
     counted = jnp.sum((rungs[:, None] == ladder[None, :]).astype(jnp.float32), axis=0)
     tall, wide, cores = SIDES
     up = (device // (wide * cores) - mine_owner // (wide * cores)) % tall
     right = (device // cores % wide - mine_owner // cores % wide) % wide
     across = (device % cores - mine_owner % cores) % cores
-    copy = device % cores + cores * (lax.axis_index("tensor") % 2)
-    part = right ^ copy
-    step = (part * tall + up) * cores + (across ^ part % cores)
+    step = (right * tall + up) * cores + across
     rung_means, next_lengths = finish(
         parts,
         jnp.pad(counted, (0, spare), constant_values=1.0)[None],

time: 147 us -> 143 us (0.973); the launches traced: 145 us -> 142 us
  starting transfers between devices: 40.7 us -> 36.4 us
  local copies, waits for them, and re-layouts: 3.16 us -> 4.98 us
    all_to_all x1, waiting for transfers between devices: 0.01 us -> 41.2 us  [shards(): arrived_keys = exchange(after(outgoing_keys, column))]
    ppermute x4, waiting for transfers between devices: 40.4 us -> 0.01 us  [half_of(): parts.append(lax.ppermute(array, 'particle', pairs))]
    ppermute x7 -> x0, starting transfers between devices: 15.4 us -> none  [the longest x3 8.44 us: copies_of(): parts.append(lax.ppermute(array, ('particle', 'tensor'), pairs))]
    ppermute x3 -> x9, starting transfers between devices: 1.98 us -> 13 us  [along(): lax.ppermute(array, 'particle', pairs)]
    ppermute x7 -> x0, waiting for transfers between devices: 7.96 us -> none  [the longest x4 7.95 us: columns_of(): parts.append(lax.ppermute(array, ('particle', 'tensor'), pairs))]
    ppermute x3 -> x9, waiting for transfers between devices: 0.01 us -> 7.13 us  [along(): lax.ppermute(array, 'particle', pairs)]
    dot_general x1, matrix products: 2.06 us -> 0.45 us  [shards(): jnp.einsum('pshl,pld->pshd', back.astype(jnp.bfloat16), written_values, p...]
    dot_general x1, matrix products: 2.34 us -> 0.75 us  [shards(): jnp.einsum('pshd,pld->pshl', query, written_keys, preferred_element_type=...]
  transfers between devices with their start and end apart: 20 -> 19, of which waited for: 7 -> 7; matrix products, arithmetic and copies ran while one was open for 13% -> 14% of each run, Pallas kernels for 14% -> 14%
where the time goes in v8:
time: 143 us; the launch traced here: 142 us
  waiting for transfers between devices  60.5 us (42%)
  starting transfers between devices  36.4 us (25%)
  Pallas kernels  21.7 us (15%)
  other arithmetic  10.1 us (7%)
  matrix products  6.95 us (5%)
  local copies, waits for them, and re-layouts  4.98 us (3%)
  between operations  1.73 us (1%)
    all_to_all x1, waiting for transfers between devices, shards(): arrived_keys = exchange(after(outgoing_keys, column))  41.2 us
    ppermute x9, starting transfers between devices, along(): lax.ppermute(array, 'particle', pairs)  13 us
    ppermute x3, waiting for transfers between devices, shards(): reward = reward + lax.ppermute(reward, 'tensor', pairs)  12.2 us
    pallas_call x2, Pallas kernels, pack(): pl.pallas_call(functools.partial(pack_kernel, keeps), out_shape=[jax.Shap...  11.9 us
    pallas_call x2, Pallas kernels, unpack(): pl.pallas_call(unpack_kernel, out_shape=(jax.ShapeDtypeStruct(shape, arri...  8.31 us
    all_to_all x1, starting transfers between devices, shards(): arrived_keys = exchange(after(outgoing_keys, column))  7.29 us
    ppermute x9, waiting for transfers between devices, along(): lax.ppermute(array, 'particle', pairs)  7.13 us
    ppermute x4, starting transfers between devices, half_of(): parts.append(lax.ppermute(array, 'particle', pairs))  6.83 us
  transfers between devices with their start and end apart: 19, of which 7 were waited for; matrix products, arithmetic and copies ran while one was open for 14% of the time, Pallas kernels for 14%

profile of v8, /device:TPU:128, one launch (start us, length us, event | category | flops | bytes accessed | tf_op | source)
XLA Modules:
  0.0 142.3 jit_solution(7618575613781751975)
XLA Ops:
  2.9 1.7 %collective-permute-start.1 = (bf16[128,256]{1,0:T(8,128)(2,1)S(1)}, bf16[128,256]{1,0:T(8,128)(2,1)S(1)}, u32[]{:S(2)}, u32[]{:S(2)}) collective-permute-start(bf16[128,256]{1,0:T(8,128)(2,1)S(1)} %maximum_add_fusion.1), channel_id=1, source_target_pairs={{0,64},{8,72},{16,80},{24,88},{32,96},{40,104},{48,112},{56,120},{... | collective-permute-start | bytes 196616 | tf_op jit(solution)/shard_map/ppermute | solution.py:269
  4.5 4.9 %pack.2.refs_0_ = bf16[64,256,128]{2,1,0:T(8,128)(2,1)} custom-call(s32[32]{0:T(128)} %lengths.3, s32[32]{0:T(128)} %copy-done.8, s32[32]{0:T(128)} %get-tuple-element.24.most, bf16[32,256,128]{2,1,0:T(8,128)(2,1)} %refs_0_.3, bf16[32,2,128]{2,1,0:T(2,128)(2,1)} %refs_2_.1), custom_call_target="tpu_custom_call" | custom-call | tf_op jit(solution)/shard_map/pack/pallas_call | solution.py:99
  10.1 7.3 %all-to-all-start = ((bf16[64,256,128]{2,1,0:T(8,128)(2,1)}), bf16[64,256,128]{2,1,0:T(8,128)(2,1)}, u32[]{:S(2)}, u32[]{:S(2)}) async-start(bf16[64,256,128]{2,1,0:T(8,128)(2,1)} %after.3), calls=%async_computation | async-start | bytes 8388608 | tf_op jit(solution)/shard_map/all_to_all | solution.py:278
  17.6 7.0 %pack.3 = (bf16[64,256,128]{2,1,0:T(8,128)(2,1)}, bf16[32,256,128]{2,1,0:T(8,128)(2,1)}, bf16[32,256,128]{2,1,0:T(8,128)(2,1)}) custom-call(s32[32]{0:T(128)} %lengths.3, s32[32]{0:T(128)} %copy-done.8, s32[32]{0:T(128)} %get-tuple-element.24.most, bf16[32,256,128]{2,1,0:T(8,128)(2,1)} %refs_0_.3, bf16[32,256,128]{2,1,0:T(8,128)(2,1)} %refs_1_.3, ...), custom_call_target="tpu_custom_call" | custom-call | tf_op jit(solution)/shard_map/pack/pallas_call | solution.py:99
  24.6 4.2 %collective-permute-start.5 = (bf16[256,256]{1,0:T(8,128)(2,1)S(1)}, bf16[256,256]{1,0:T(8,128)(2,1)S(1)}, u32[]{:S(2)}, u32[]{:S(2)}) collective-permute-start(bf16[256,256]{1,0:T(8,128)(2,1)S(1)} %copy-done.2), channel_id=1, source_target_pairs={{0,144},{8,184},{16,160},{24,136},{32,176},{40,152},{48,128},{56,1... | collective-permute-start | bytes 393224 | tf_op jit(solution)/shard_map/ppermute | solution.py:225
  29.3 1.5 %collective-permute-start.3 = (bf16[256,256]{1,0:T(8,128)(2,1)S(1)}, bf16[256,256]{1,0:T(8,128)(2,1)S(1)}, u32[]{:S(2)}, u32[]{:S(2)}) collective-permute-start(bf16[256,256]{1,0:T(8,128)(2,1)S(1)} %copy-done.2), channel_id=1, source_target_pairs={{0,16},{8,56},{16,32},{24,8},{32,48},{40,24},{48,0},{56,40},{64,80... | collective-permute-start | bytes 393224 | tf_op jit(solution)/shard_map/ppermute | solution.py:225
  31.6 41.2 %all-to-all-done.arrived.refs_1_ = bf16[64,256,128]{2,1,0:T(8,128)(2,1)} async-done(((bf16[64,256,128]{2,1,0:T(8,128)(2,1)}), bf16[64,256,128]{2,1,0:T(8,128)(2,1)}, u32[]{:S(2)}, u32[]{:S(2)}) %all-to-all-start) | async-done | bytes 4194336 | tf_op jit(solution)/shard_map/all_to_all | solution.py:278
  72.7 1.2 slice.20
  74.6 5.0 %all-to-all-start.1 = ((bf16[64,256,128]{2,1,0:T(8,128)(2,1)}), bf16[64,256,128]{2,1,0:T(8,128)(2,1)}, u32[]{:S(2)}, u32[]{:S(2)}) async-start(bf16[64,256,128]{2,1,0:T(8,128)(2,1)} %after.5), calls=%async_computation.1 | async-start | bytes 8388608 | tf_op jit(solution)/shard_map/all_to_all | solution.py:282
  80.8 1.3 fusion.46
  82.7 3.7 %bitcast_reduce_fusion = (f32[32,2,8]{0,2,1:T(8,128)S(1)}, f32[2048,32,2,8]{0,1,3,2:T(8,128)}) fusion(bf16[32,2,8,128]{3,2,1,0:T(8,128)(2,1)S(1)} %reshape.77, bf16[1024,256]{1,0:T(8,128)(2,1)S(1)} %maximum_add_fusion, bf16[1024,256]{1,0:T(8,128)(2,1)} %collective-permute-done.6), kind=kOutput, calls=%fused_computation.1 | convolution fusion | flops 271580672 | bytes 5376000 | tf_op jit(solution)/shard_map/pshd,nd->pshn/dot_general | solution.py:293
  86.8 3.2 %fusion.1 = f32[32,2,8]{0,2,1:T(8,128)S(1)} fusion(f32[2048,32,2,8]{0,1,3,2:T(8,128)} %get-tuple-element.35, f32[32,2,8]{0,2,1:T(8,128)S(1)} %max.11), kind=kLoop, calls=%fused_computation.3 | loop fusion | flops 3145216 | bytes 4198400 | tf_op jit(solution)/shard_map/reduce_sum | solution.py:306
  90.5 2.0 %multiply_reduce_fusion = (f32[32]{0:T(128)S(1)}, bf16[32,2,8,128]{3,0,2,1:T(8,128)(2,1)S(1)}) fusion(f32[8,128]{1,0:T(8,128)S(1)} %bitcast.78, f32[32,2,8]{0,2,1:T(8,128)S(1)} %add.148, f32[32,2,8,128]{3,2,1,0:T(8,128)S(1)} %fusion.5, bf16[1024,256]{1,0:T(8,128)(2,1)} %collective-permute-done.6, bf16[1024,256]{1,0:T(8,128)(2,1)S(1)} %maximum_add_fusion, ...), kind=kOutput, calls=%fused_computation.29 | convolution fusion | flops 272957408 | bytes 5644416 | tf_op jit(solution)/shard_map/pshn,nd->pshd/dot_general | solution.py:307
  93.8 2.3 %collective-permute-done.7 = f32[32]{0:T(128)S(1)} collective-permute-done((f32[32]{0:T(128)S(1)}, f32[32]{0:T(128)S(1)}, u32[]{:S(2)}, u32[]{:S(2)}) %collective-permute-start.7) | collective-permute-done | bytes 160 | tf_op jit(solution)/shard_map/ppermute | solution.py:325
  96.2 1.5 %collective-permute-start.8 = (f32[32]{0:T(128)S(1)}, f32[32]{0:T(128)S(1)}, u32[]{:S(2)}, u32[]{:S(2)}) collective-permute-start(f32[32]{0:T(128)S(1)} %add.149), channel_id=1, source_target_pairs={{0,2},{1,3},{2,0},{3,1},{4,6},{5,7},{6,4},{7,5},{8,10},{9,11},{10,... | collective-permute-start | bytes 392 | tf_op jit(solution)/shard_map/ppermute | solution.py:325
  98.2 2.5 %collective-permute-done.8 = f32[32]{0:T(128)S(1)} collective-permute-done((f32[32]{0:T(128)S(1)}, f32[32]{0:T(128)S(1)}, u32[]{:S(2)}, u32[]{:S(2)}) %collective-permute-start.8) | collective-permute-done | bytes 160 | tf_op jit(solution)/shard_map/ppermute | solution.py:325
  100.7 7.4 %collective-permute-done.9 = f32[32]{0:T(128)S(1)} collective-permute-done((f32[32]{0:T(128)S(1)}, f32[32]{0:T(128)S(1)}, u32[]{:S(2)}, u32[]{:S(2)}) %collective-permute-start.9) | collective-permute-done | bytes 160 | tf_op jit(solution)/shard_map/ppermute | solution.py:325
  108.8 4.1 %unpack.2 = (bf16[32,256,128]{2,1,0:T(8,128)(2,1)}, f32[1,128]{1,0:T(1,128)}) custom-call(s32[32]{0:T(128)} %fusion.47.slots, bf16[64,256,128]{2,1,0:T(8,128)(2,1)} %all-to-all-done.arrived.refs_1_, bf16[256,256]{1,0:T(8,128)(2,1)} %pad_maximum_fusion.1.refs_1_._), custom_call_target="tpu_custom_call" | custom-call | tf_op jit(solution)/shard_map/unpack/pallas_call | solution.py:152
  114.3 3.1 %collective-permute-start.13 = (f32[2,3,32]{2,1,0:T(4,128)}, f32[2,3,32]{2,1,0:T(4,128)S(1)}, u32[]{:S(2)}, u32[]{:S(2)}) collective-permute-start(f32[2,3,32]{2,1,0:T(4,128)} %after.4), channel_id=1, source_target_pairs={{0,192},{8,200},{16,208},{24,216},{32,224},{40,232},{48,240},{56,2... | collective-permute-start | bytes 2312 | tf_op jit(solution)/shard_map/ppermute | solution.py:212
  119.8 6.3 %collective-permute-done.13 = f32[2,3,32]{2,1,0:T(4,128)S(1)} collective-permute-done((f32[2,3,32]{2,1,0:T(4,128)}, f32[2,3,32]{2,1,0:T(4,128)S(1)}, u32[]{:S(2)}, u32[]{:S(2)}) %collective-permute-start.13) | collective-permute-done | bytes 800 | tf_op jit(solution)/shard_map/ppermute | solution.py:212
  128.6 4.2 %collective-permute-start.15 = (f32[8,3,32]{2,1,0:T(4,128)S(1)}, f32[8,3,32]{2,1,0:T(4,128)S(1)}, u32[]{:S(2)}, u32[]{:S(2)}) collective-permute-start(f32[8,3,32]{2,1,0:T(4,128)S(1)} %maximum_add_fusion.2._.refs_0_), channel_id=1, source_target_pairs={{0,32},{8,40},{16,48},{24,56},{32,0},{40,8},{48,16},{56,24},{64,96... | collective-permute-start | bytes 9224 | tf_op jit(solution)/shard_map/ppermute | solution.py:212
  132.8 2.5 %collective-permute-start.16 = (f32[8,3,32]{2,1,0:T(4,128)S(1)}, f32[8,3,32]{2,1,0:T(4,128)S(1)}, u32[]{:S(2)}, u32[]{:S(2)}) collective-permute-start(f32[8,3,32]{2,1,0:T(4,128)S(1)} %maximum_add_fusion.2._.refs_0_), channel_id=1, source_target_pairs={{0,48},{8,56},{16,0},{24,8},{32,16},{40,24},{48,32},{56,40},{64,11... | collective-permute-start | bytes 9224 | tf_op jit(solution)/shard_map/ppermute | solution.py:212
  135.9 4.2 %unpack.3 = (bf16[32,256,128]{2,1,0:T(8,128)(2,1)}, f32[1,128]{1,0:T(1,128)}) custom-call(s32[32]{0:T(128)} %fusion.47.slots, bf16[64,256,128]{2,1,0:T(8,128)(2,1)} %all-to-all-done.1.arrived, f32[8,3,32]{2,1,0:T(4,128)} %copy-done.3), custom_call_target="tpu_custom_call" | custom-call | tf_op jit(solution)/shard_map/unpack/pallas_call | solution.py:152
  140.8 1.5 %finish.1 = (f32[1,8]{1,0:T(1,128)}, s32[1,32]{1,0:T(1,128)}) custom-call(f32[1,32]{1,0:T(1,128)} %pad_bitcast_fusion.2.counted, s32[1,32]{1,0:T(1,128)} %get-tuple-element.28.step, s32[1,32]{1,0:T(1,128)} %get-tuple-element.26.place, f32[8,3,32]{2,1,0:T(4,128)} %copy-done.3, f32[8,3,32]{2,1,0:T(4,128)} %copy-done.5, f32[8,3,32]{2,1,0:T(4,128)} %copy-done.6, ...), custom_call_target="tpu_custom_call" | custom-call | tf_op jit(solution)/shard_map/finish/pallas_call | solution.py:188
  (93 shorter events, 17.0 us)
Async XLA Ops:
  1.4 1.5 %collective-permute-start = (bf16[64,256]{1,0:T(8,128)(2,1)S(1)}, bf16[64,256]{1,0:T(8,128)(2,1)S(1)}, u32[]{:S(2)}, u32[]{:S(2)}) collective-permute-start(bf16[64,256]{1,0:T(8,128)(2,1)S(1)} %pad_maximum_fusion.2), channel_id=1, source_target_pairs={{0,8},{8,0},{16,24},{24,16},{32,40},{40,32},{48,56},{56,48},{64,72... | collective-permute-start | bytes 98312 | tf_op jit(solution)/shard_map/ppermute | solution.py:212
  2.9 6.6 %collective-permute-start.1 = (bf16[128,256]{1,0:T(8,128)(2,1)S(1)}, bf16[128,256]{1,0:T(8,128)(2,1)S(1)}, u32[]{:S(2)}, u32[]{:S(2)}) collective-permute-start(bf16[128,256]{1,0:T(8,128)(2,1)S(1)} %maximum_add_fusion.1), channel_id=1, source_target_pairs={{0,64},{8,72},{16,80},{24,88},{32,96},{40,104},{48,112},{56,120},{... | collective-permute-start | bytes 196616 | tf_op jit(solution)/shard_map/ppermute | solution.py:269
  10.1 62.6 %all-to-all-start = ((bf16[64,256,128]{2,1,0:T(8,128)(2,1)}), bf16[64,256,128]{2,1,0:T(8,128)(2,1)}, u32[]{:S(2)}, u32[]{:S(2)}) async-start(bf16[64,256,128]{2,1,0:T(8,128)(2,1)} %after.3), calls=%async_computation | async-start | bytes 8388608 | tf_op jit(solution)/shard_map/all_to_all | solution.py:278
  24.6 55.0 %collective-permute-start.5 = (bf16[256,256]{1,0:T(8,128)(2,1)S(1)}, bf16[256,256]{1,0:T(8,128)(2,1)S(1)}, u32[]{:S(2)}, u32[]{:S(2)}) collective-permute-start(bf16[256,256]{1,0:T(8,128)(2,1)S(1)} %copy-done.2), channel_id=1, source_target_pairs={{0,144},{8,184},{16,160},{24,136},{32,176},{40,152},{48,128},{56,1... | collective-permute-start | bytes 393224 | tf_op jit(solution)/shard_map/ppermute | solution.py:225
  28.8 50.9 %collective-permute-start.4 = (bf16[256,256]{1,0:T(8,128)(2,1)S(1)}, bf16[256,256]{1,0:T(8,128)(2,1)S(1)}, u32[]{:S(2)}, u32[]{:S(2)}) collective-permute-start(bf16[256,256]{1,0:T(8,128)(2,1)S(1)} %copy-done.2), channel_id=1, source_target_pairs={{0,128},{8,168},{16,144},{24,184},{32,160},{40,136},{48,176},{56,1... | collective-permute-start | bytes 393224 | tf_op jit(solution)/shard_map/ppermute | solution.py:225
  29.3 50.3 %collective-permute-start.3 = (bf16[256,256]{1,0:T(8,128)(2,1)S(1)}, bf16[256,256]{1,0:T(8,128)(2,1)S(1)}, u32[]{:S(2)}, u32[]{:S(2)}) collective-permute-start(bf16[256,256]{1,0:T(8,128)(2,1)S(1)} %copy-done.2), channel_id=1, source_target_pairs={{0,16},{8,56},{16,32},{24,8},{32,48},{40,24},{48,0},{56,40},{64,80... | collective-permute-start | bytes 393224 | tf_op jit(solution)/shard_map/ppermute | solution.py:225
  30.8 48.9 %collective-permute-start.2 = (bf16[256,256]{1,0:T(8,128)(2,1)S(1)}, bf16[256,256]{1,0:T(8,128)(2,1)S(1)}, u32[]{:S(2)}, u32[]{:S(2)}) collective-permute-start(bf16[256,256]{1,0:T(8,128)(2,1)S(1)} %copy-done.2), channel_id=1, source_target_pairs={{0,0},{8,40},{16,16},{24,56},{32,32},{40,8},{48,48},{56,24},{64,64... | collective-permute-start | bytes 393224 | tf_op jit(solution)/shard_map/ppermute | solution.py:225
  74.6 61.3 %all-to-all-start.1 = ((bf16[64,256,128]{2,1,0:T(8,128)(2,1)}), bf16[64,256,128]{2,1,0:T(8,128)(2,1)}, u32[]{:S(2)}, u32[]{:S(2)}) async-start(bf16[64,256,128]{2,1,0:T(8,128)(2,1)} %after.5), calls=%async_computation.1 | async-start | bytes 8388608 | tf_op jit(solution)/shard_map/all_to_all | solution.py:282
  79.8 2.9 %collective-permute-start.6 = (bf16[1024,256]{1,0:T(8,128)(2,1)S(1)}, bf16[1024,256]{1,0:T(8,128)(2,1)}, u32[]{:S(2)}, u32[]{:S(2)}) collective-permute-start(bf16[1024,256]{1,0:T(8,128)(2,1)S(1)} %maximum_add_fusion), channel_id=1, source_target_pairs={{0,8},{8,0},{16,24},{24,16},{32,40},{40,32},{48,56},{56,48},{64,72... | collective-permute-start | bytes 1572872 | tf_op jit(solution)/shard_map/ppermute | solution.py:212
  82.7 7.4 %copy-start.13 = (bf16[32,256,128]{2,1,0:T(8,128)(2,1)S(1)}, bf16[32,256,128]{2,1,0:T(8,128)(2,1)}, u32[]{:S(2)}) copy-start(bf16[32,256,128]{2,1,0:T(8,128)(2,1)} %get-tuple-element.16) | copy-start | bytes 6291460
  90.0 10.6 %copy-start.9 = (s32[1024]{0:T(1024)S(1)}, s32[1024]{0:T(1024)}, u32[]{:S(2)}) copy-start(s32[1024]{0:T(1024)} %param.22) | copy-start | bytes 12292
  90.0 18.0 %copy-start.12 = (f32[32]{0:T(128)S(1)}, f32[32]{0:T(128)}, u32[]{:S(2)}) copy-start(f32[32]{0:T(128)} %param.20) | copy-start | bytes 388
  92.5 3.6 %collective-permute-start.7 = (f32[32]{0:T(128)S(1)}, f32[32]{0:T(128)S(1)}, u32[]{:S(2)}, u32[]{:S(2)}) collective-permute-start(f32[32]{0:T(128)S(1)} %get-tuple-element.30), channel_id=1, source_target_pairs={{0,1},{1,0},{2,3},{3,2},{4,5},{5,4},{6,7},{7,6},{8,9},{9,8},{10,11... | collective-permute-start | bytes 392 | tf_op jit(solution)/shard_map/ppermute | solution.py:325
  96.2 4.4 %collective-permute-start.8 = (f32[32]{0:T(128)S(1)}, f32[32]{0:T(128)S(1)}, u32[]{:S(2)}, u32[]{:S(2)}) collective-permute-start(f32[32]{0:T(128)S(1)} %add.149), channel_id=1, source_target_pairs={{0,2},{1,3},{2,0},{3,1},{4,6},{5,7},{6,4},{7,5},{8,10},{9,11},{10,... | collective-permute-start | bytes 392 | tf_op jit(solution)/shard_map/ppermute | solution.py:325
  100.6 7.4 %collective-permute-start.9 = (f32[32]{0:T(128)S(1)}, f32[32]{0:T(128)S(1)}, u32[]{:S(2)}, u32[]{:S(2)}) collective-permute-start(f32[32]{0:T(128)S(1)} %add.150), channel_id=1, source_target_pairs={{0,4},{1,5},{2,6},{3,7},{4,0},{5,1},{6,2},{7,3},{8,12},{9,13},{10,... | collective-permute-start | bytes 392 | tf_op jit(solution)/shard_map/ppermute | solution.py:325
  108.1 32.1 %copy-start.11 = (f32[32]{0:T(128)}, f32[32]{0:T(128)S(1)}, u32[]{:S(2)}) copy-start(f32[32]{0:T(128)S(1)} %add_add_fusion) | copy-start | bytes 388
  108.4 5.3 %collective-permute-start.10 = (f32[1,3,32]{2,1,0:T(4,128)S(1)}, f32[1,3,32]{2,1,0:T(4,128)S(1)}, u32[]{:S(2)}, u32[]{:S(2)}) collective-permute-start(f32[1,3,32]{2,1,0:T(4,128)S(1)} %maximum_bitcast_fusion), channel_id=1, source_target_pairs={{0,8},{8,0},{16,24},{24,16},{32,40},{40,32},{48,56},{56,48},{64,72... | collective-permute-start | bytes 1160 | tf_op jit(solution)/shard_map/ppermute | solution.py:212
  114.3 11.8 %collective-permute-start.13 = (f32[2,3,32]{2,1,0:T(4,128)}, f32[2,3,32]{2,1,0:T(4,128)S(1)}, u32[]{:S(2)}, u32[]{:S(2)}) collective-permute-start(f32[2,3,32]{2,1,0:T(4,128)} %after.4), channel_id=1, source_target_pairs={{0,192},{8,200},{16,208},{24,216},{32,224},{40,232},{48,240},{56,2... | collective-permute-start | bytes 2312 | tf_op jit(solution)/shard_map/ppermute | solution.py:212
  117.4 9.2 %collective-permute-start.12 = (f32[2,3,32]{2,1,0:T(4,128)}, f32[2,3,32]{2,1,0:T(4,128)S(1)}, u32[]{:S(2)}, u32[]{:S(2)}) collective-permute-start(f32[2,3,32]{2,1,0:T(4,128)} %after.4), channel_id=1, source_target_pairs={{0,128},{8,136},{16,144},{24,152},{32,160},{40,168},{48,176},{56,1... | collective-permute-start | bytes 2312 | tf_op jit(solution)/shard_map/ppermute | solution.py:212
  118.1 8.8 %collective-permute-start.11 = (f32[2,3,32]{2,1,0:T(4,128)}, f32[2,3,32]{2,1,0:T(4,128)S(1)}, u32[]{:S(2)}, u32[]{:S(2)}) collective-permute-start(f32[2,3,32]{2,1,0:T(4,128)} %after.4), channel_id=1, source_target_pairs={{0,64},{8,72},{16,80},{24,88},{32,96},{40,104},{48,112},{56,120},{... | collective-permute-start | bytes 2312 | tf_op jit(solution)/shard_map/ppermute | solution.py:212
  127.6 8.3 %copy-start.3 = (f32[8,3,32]{2,1,0:T(4,128)}, f32[8,3,32]{2,1,0:T(4,128)S(1)}, u32[]{:S(2)}) copy-start(f32[8,3,32]{2,1,0:T(4,128)S(1)} %maximum_add_fusion.2._.refs_0_) | copy-start | bytes 9220
  127.6 12.5 %collective-permute-start.14 = (f32[8,3,32]{2,1,0:T(4,128)S(1)}, f32[8,3,32]{2,1,0:T(4,128)S(1)}, u32[]{:S(2)}, u32[]{:S(2)}) collective-permute-start(f32[8,3,32]{2,1,0:T(4,128)S(1)} %maximum_add_fusion.2._.refs_0_), channel_id=1, source_target_pairs={{0,16},{8,24},{16,32},{24,40},{32,48},{40,56},{48,0},{56,8},{64,80... | collective-permute-start | bytes 9224 | tf_op jit(solution)/shard_map/ppermute | solution.py:212
  128.6 11.6 %collective-permute-start.15 = (f32[8,3,32]{2,1,0:T(4,128)S(1)}, f32[8,3,32]{2,1,0:T(4,128)S(1)}, u32[]{:S(2)}, u32[]{:S(2)}) collective-permute-start(f32[8,3,32]{2,1,0:T(4,128)S(1)} %maximum_add_fusion.2._.refs_0_), channel_id=1, source_target_pairs={{0,32},{8,40},{16,48},{24,56},{32,0},{40,8},{48,16},{56,24},{64,96... | collective-permute-start | bytes 9224 | tf_op jit(solution)/shard_map/ppermute | solution.py:212
  132.8 7.4 %collective-permute-start.16 = (f32[8,3,32]{2,1,0:T(4,128)S(1)}, f32[8,3,32]{2,1,0:T(4,128)S(1)}, u32[]{:S(2)}, u32[]{:S(2)}) collective-permute-start(f32[8,3,32]{2,1,0:T(4,128)S(1)} %maximum_add_fusion.2._.refs_0_), channel_id=1, source_target_pairs={{0,48},{8,56},{16,0},{24,8},{32,16},{40,24},{48,32},{56,40},{64,11... | collective-permute-start | bytes 9224 | tf_op jit(solution)/shard_map/ppermute | solution.py:212
  (10 other events, 38.4 us)

commit v9 on v8

--- a/solution.py
+++ b/solution.py
@@ -48,6 +48,10 @@
         return pltpu.make_async_copy(
             held.at[number - 1, most[d]], packed.at[2 * d + 1], send_sems.at[2 * d + 1]
         )
+
+    def each(d, act):
+        pl.when(least[d] <= most[d])(lambda: act(low(d)))
+        pl.when(least[d] < most[d])(lambda: act(high(d)))
 
     def patch(group):
         found = []
@@ -74,10 +78,10 @@
             load(chunk, n).wait()
         groups = share // GROUP
         repeat(groups, lambda g, chunk=chunk: patch(g + chunk * groups), 1)
-    repeat(goals, lambda d: (low(d).start(), high(d).start()))
+    repeat(goals, lambda d: each(d, lambda copy: copy.start()))
     for n in range(number * keeps):
         keep(n).start()
-    repeat(goals, lambda d: (low(d).wait(), high(d).wait()))
+    repeat(goals, lambda d: each(d, lambda copy: copy.wait()))
     for n in range(number * keeps):
         keep(n).wait()
 
@@ -125,6 +129,20 @@
     )(array, *others)
 
 
+def zero_kernel(_, zero):
+    zero[...] = jnp.zeros_like(zero)
+
+
+def zero_after(array):
+    return pl.pallas_call(
+        zero_kernel,
+        out_shape=jax.ShapeDtypeStruct((1, HEAD_DIM), jnp.float32),
+        in_specs=[pl.BlockSpec(memory_space=pltpu.HBM)],
+        out_specs=pl.BlockSpec(memory_space=pltpu.VMEM),
+        name="zero",
+    )(array)
+
+
 def unpack_kernel(slots, arrived, _, result, mark, held, in_sems, out_sems):
     count = result.shape[0]
     share = count // CHUNKS
@@ -282,8 +300,7 @@
     arrived_values = exchange(after(outgoing_values, arrived_keys))
     next_keys, mark = unpack(arrived_keys, slot, column)
 
-    none = jnp.minimum(jnp.abs(arrived_keys[0, 0, 0]), 0)
-    half = jnp.concatenate(halves, axis=0) + none
+    half = jnp.concatenate(halves, axis=0) + zero_after(arrived_keys)[0, 0].astype(shard.dtype)
     prompt = jnp.concatenate(along(half, (2,)), axis=0)
     all_keys = prompt[:, :HEAD_DIM]
     all_values = prompt[:, HEAD_DIM:]
@@ -340,8 +357,8 @@
         ]
     )[None]
     near = jnp.concatenate(along(shared, (2,)), axis=0)
-    near = after(near, attention)
-    near = jnp.concatenate(along(near, (0,)), axis=0) + mark[0, :per_device]
+    near = after(near, attention, mark)
+    near = jnp.concatenate(along(near, (0,)), axis=0)
     parts = along(near, (1,))
     next_values, mark = unpack(arrived_values, slot, near)
 

time: 143 us -> 141 us (0.986)
  local copies, waits for them, and re-layouts: 4.98 us -> 3.15 us
  transfers between devices with their start and end apart: 19 -> 19, of which waited for: 7 -> 7; matrix products, arithmetic and copies ran while one was open for 14% -> 13% of each run, Pallas kernels for 14% -> 14%
where the time goes in v9:
time: 141 us; the launch traced here: 140 us
  waiting for transfers between devices  60.7 us (43%)
  starting transfers between devices  35.9 us (25%)
  Pallas kernels  21.2 us (15%)
  other arithmetic  10.8 us (8%)
  matrix products  6.94 us (5%)
  local copies, waits for them, and re-layouts  3.15 us (2%)
    all_to_all x1, waiting for transfers between devices, shards(): arrived_keys = exchange(after(outgoing_keys, column))  42.2 us
    ppermute x9, starting transfers between devices, along(): lax.ppermute(array, 'particle', pairs)  12.9 us
    ppermute x3, waiting for transfers between devices, shards(): reward = reward + lax.ppermute(reward, 'tensor', pairs)  12 us
    pallas_call x2, Pallas kernels, pack(): pl.pallas_call(functools.partial(pack_kernel, keeps), out_shape=[jax.Shap...  10.6 us
    pallas_call x2, Pallas kernels, unpack(): pl.pallas_call(unpack_kernel, out_shape=(jax.ShapeDtypeStruct(shape, arri...  8.54 us
    all_to_all x1, starting transfers between devices, shards(): arrived_keys = exchange(after(outgoing_keys, column))  7.09 us
    ppermute x4, starting transfers between devices, half_of(): parts.append(lax.ppermute(array, 'particle', pairs))  6.72 us
    ppermute x9, waiting for transfers between devices, along(): lax.ppermute(array, 'particle', pairs)  6.43 us
  transfers between devices with their start and end apart: 19, of which 7 were waited for; matrix products, arithmetic and copies ran while one was open for 13% of the time, Pallas kernels for 14%

profile of v9, /device:TPU:128, one launch (start us, length us, event | category | flops | bytes accessed | tf_op | source)
XLA Modules:
  0.0 139.6 jit_solution(9926233069497214008)
XLA Ops:
  2.9 1.7 %collective-permute-start.1 = (bf16[128,256]{1,0:T(8,128)(2,1)S(1)}, bf16[128,256]{1,0:T(8,128)(2,1)S(1)}, u32[]{:S(2)}, u32[]{:S(2)}) collective-permute-start(bf16[128,256]{1,0:T(8,128)(2,1)S(1)} %maximum_add_fusion.1), channel_id=1, source_target_pairs={{0,64},{8,72},{16,80},{24,88},{32,96},{40,104},{48,112},{56,120},{... | collective-permute-start | bytes 196616 | tf_op jit(solution)/shard_map/ppermute | solution.py:287
  4.5 4.2 %pack.2.refs_0_ = bf16[64,256,128]{2,1,0:T(8,128)(2,1)} custom-call(s32[32]{0:T(128)} %lengths.3, s32[32]{0:T(128)} %copy-done.8, s32[32]{0:T(128)} %get-tuple-element.24.most, bf16[32,256,128]{2,1,0:T(8,128)(2,1)} %refs_0_.3, bf16[32,2,128]{2,1,0:T(2,128)(2,1)} %refs_2_.1), custom_call_target="tpu_custom_call" | custom-call | tf_op jit(solution)/shard_map/pack/pallas_call | solution.py:103
  9.4 7.1 %all-to-all-start = ((bf16[64,256,128]{2,1,0:T(8,128)(2,1)}), bf16[64,256,128]{2,1,0:T(8,128)(2,1)}, u32[]{:S(2)}, u32[]{:S(2)}) async-start(bf16[64,256,128]{2,1,0:T(8,128)(2,1)} %after.3), calls=%async_computation | async-start | bytes 8388608 | tf_op jit(solution)/shard_map/all_to_all | solution.py:296
  16.6 6.3 %pack.3 = (bf16[64,256,128]{2,1,0:T(8,128)(2,1)}, bf16[32,256,128]{2,1,0:T(8,128)(2,1)}, bf16[32,256,128]{2,1,0:T(8,128)(2,1)}) custom-call(s32[32]{0:T(128)} %lengths.3, s32[32]{0:T(128)} %copy-done.8, s32[32]{0:T(128)} %get-tuple-element.24.most, bf16[32,256,128]{2,1,0:T(8,128)(2,1)} %refs_0_.3, bf16[32,256,128]{2,1,0:T(8,128)(2,1)} %refs_1_.3, ...), custom_call_target="tpu_custom_call" | custom-call | tf_op jit(solution)/shard_map/pack/pallas_call | solution.py:103
  22.9 4.4 %collective-permute-start.5 = (bf16[256,256]{1,0:T(8,128)(2,1)S(1)}, bf16[256,256]{1,0:T(8,128)(2,1)S(1)}, u32[]{:S(2)}, u32[]{:S(2)}) collective-permute-start(bf16[256,256]{1,0:T(8,128)(2,1)S(1)} %copy-done.2), channel_id=1, source_target_pairs={{0,144},{8,184},{16,160},{24,136},{32,176},{40,152},{48,128},{56,1... | collective-permute-start | bytes 393224 | tf_op jit(solution)/shard_map/ppermute | solution.py:243
  27.6 1.4 %collective-permute-start.3 = (bf16[256,256]{1,0:T(8,128)(2,1)S(1)}, bf16[256,256]{1,0:T(8,128)(2,1)S(1)}, u32[]{:S(2)}, u32[]{:S(2)}) collective-permute-start(bf16[256,256]{1,0:T(8,128)(2,1)S(1)} %copy-done.2), channel_id=1, source_target_pairs={{0,16},{8,56},{16,32},{24,8},{32,48},{40,24},{48,0},{56,40},{64,80... | collective-permute-start | bytes 393224 | tf_op jit(solution)/shard_map/ppermute | solution.py:243
  29.7 42.2 %all-to-all-done._.arrived.refs_1_ = bf16[64,256,128]{2,1,0:T(8,128)(2,1)} async-done(((bf16[64,256,128]{2,1,0:T(8,128)(2,1)}), bf16[64,256,128]{2,1,0:T(8,128)(2,1)}, u32[]{:S(2)}, u32[]{:S(2)}) %all-to-all-start) | async-done | bytes 4194336 | tf_op jit(solution)/shard_map/all_to_all | solution.py:296
  71.9 5.0 %all-to-all-start.1 = ((bf16[64,256,128]{2,1,0:T(8,128)(2,1)}), bf16[64,256,128]{2,1,0:T(8,128)(2,1)}, u32[]{:S(2)}, u32[]{:S(2)}) async-start(bf16[64,256,128]{2,1,0:T(8,128)(2,1)} %after.5), calls=%async_computation.1 | async-start | bytes 8388608 | tf_op jit(solution)/shard_map/all_to_all | solution.py:300
  79.5 1.3 fusion.46
  80.8 3.7 %bitcast_reduce_fusion = (f32[32,2,8]{0,2,1:T(8,128)S(1)}, f32[2048,32,2,8]{0,1,3,2:T(8,128)}) fusion(bf16[32,2,8,128]{3,2,1,0:T(8,128)(2,1)S(1)} %reshape.74, bf16[1024,256]{1,0:T(8,128)(2,1)S(1)} %maximum_add_fusion, bf16[1024,256]{1,0:T(8,128)(2,1)} %collective-permute-done.6), kind=kOutput, calls=%fused_computation.1 | convolution fusion | flops 271580672 | bytes 5376000 | tf_op jit(solution)/shard_map/pshd,nd->pshn/dot_general | solution.py:310
  85.0 3.2 %fusion.1 = f32[32,2,8]{0,2,1:T(8,128)S(1)} fusion(f32[2048,32,2,8]{0,1,3,2:T(8,128)} %get-tuple-element.35, f32[32,2,8]{0,2,1:T(8,128)S(1)} %max.11), kind=kLoop, calls=%fused_computation.3 | loop fusion | flops 3145216 | bytes 4198400 | tf_op jit(solution)/shard_map/reduce_sum | solution.py:323
  88.6 2.0 %multiply_reduce_fusion = (f32[32]{0:T(128)S(1)}, bf16[32,2,8,128]{3,0,2,1:T(8,128)(2,1)S(1)}) fusion(f32[8,128]{1,0:T(8,128)S(1)} %bitcast.78, f32[32,2,8]{0,2,1:T(8,128)S(1)} %add.138, f32[32,2,8,128]{3,2,1,0:T(8,128)S(1)} %fusion.5, bf16[1024,256]{1,0:T(8,128)(2,1)} %collective-permute-done.6, bf16[1024,256]{1,0:T(8,128)(2,1)S(1)} %maximum_add_fusion, ...), kind=kOutput, calls=%fused_computation.29 | convolution fusion | flops 272957408 | bytes 5644416 | tf_op jit(solution)/shard_map/pshn,nd->pshd/dot_general | solution.py:324
  92.4 1.9 %collective-permute-done.7 = f32[32]{0:T(128)S(1)} collective-permute-done((f32[32]{0:T(128)S(1)}, f32[32]{0:T(128)S(1)}, u32[]{:S(2)}, u32[]{:S(2)}) %collective-permute-start.7) | collective-permute-done | bytes 160 | tf_op jit(solution)/shard_map/ppermute | solution.py:342
  94.3 1.5 %collective-permute-start.8 = (f32[32]{0:T(128)S(1)}, f32[32]{0:T(128)S(1)}, u32[]{:S(2)}, u32[]{:S(2)}) collective-permute-start(f32[32]{0:T(128)S(1)} %add.139), channel_id=1, source_target_pairs={{0,2},{1,3},{2,0},{3,1},{4,6},{5,7},{6,4},{7,5},{8,10},{9,11},{10,... | collective-permute-start | bytes 392 | tf_op jit(solution)/shard_map/ppermute | solution.py:342
  95.9 2.8 %collective-permute-done.8 = f32[32]{0:T(128)S(1)} collective-permute-done((f32[32]{0:T(128)S(1)}, f32[32]{0:T(128)S(1)}, u32[]{:S(2)}, u32[]{:S(2)}) %collective-permute-start.8) | collective-permute-done | bytes 160 | tf_op jit(solution)/shard_map/ppermute | solution.py:342
  98.8 7.4 %collective-permute-done.9 = f32[32]{0:T(128)S(1)} collective-permute-done((f32[32]{0:T(128)S(1)}, f32[32]{0:T(128)S(1)}, u32[]{:S(2)}, u32[]{:S(2)}) %collective-permute-start.9) | collective-permute-done | bytes 160 | tf_op jit(solution)/shard_map/ppermute | solution.py:342
  107.3 4.3 %unpack.2 = (bf16[32,256,128]{2,1,0:T(8,128)(2,1)}, f32[1,128]{1,0:T(1,128)}) custom-call(s32[32]{0:T(128)} %fusion.47.slots, bf16[64,256,128]{2,1,0:T(8,128)(2,1)} %all-to-all-done._.arrived.refs_1_, bf16[256,256]{1,0:T(8,128)(2,1)} %pad_maximum_fusion.1.refs_1_._), custom_call_target="tpu_custom_call" | custom-call | tf_op jit(solution)/shard_map/unpack/pallas_call | solution.py:170
  113.0 2.8 %collective-permute-start.13 = (f32[2,3,32]{2,1,0:T(4,128)}, f32[2,3,32]{2,1,0:T(4,128)S(1)}, u32[]{:S(2)}, u32[]{:S(2)}) collective-permute-start(f32[2,3,32]{2,1,0:T(4,128)} %after.4), channel_id=1, source_target_pairs={{0,192},{8,200},{16,208},{24,216},{32,224},{40,232},{48,240},{56,2... | collective-permute-start | bytes 2312 | tf_op jit(solution)/shard_map/ppermute | solution.py:230
  117.7 5.6 %collective-permute-done.13 = f32[2,3,32]{2,1,0:T(4,128)S(1)} collective-permute-done((f32[2,3,32]{2,1,0:T(4,128)}, f32[2,3,32]{2,1,0:T(4,128)S(1)}, u32[]{:S(2)}, u32[]{:S(2)}) %collective-permute-start.13) | collective-permute-done | bytes 800 | tf_op jit(solution)/shard_map/ppermute | solution.py:230
  124.9 3.0 %collective-permute-start.14 = (f32[8,3,32]{2,1,0:T(4,128)S(1)}, f32[8,3,32]{2,1,0:T(4,128)S(1)}, u32[]{:S(2)}, u32[]{:S(2)}) collective-permute-start(f32[8,3,32]{2,1,0:T(4,128)S(1)} %pad_maximum_fusion.3._.refs_0_), channel_id=1, source_target_pairs={{0,16},{8,24},{16,32},{24,40},{32,48},{40,56},{48,0},{56,8},{64,80... | collective-permute-start | bytes 9224 | tf_op jit(solution)/shard_map/ppermute | solution.py:230
  127.9 2.2 %collective-permute-start.15 = (f32[8,3,32]{2,1,0:T(4,128)S(1)}, f32[8,3,32]{2,1,0:T(4,128)S(1)}, u32[]{:S(2)}, u32[]{:S(2)}) collective-permute-start(f32[8,3,32]{2,1,0:T(4,128)S(1)} %pad_maximum_fusion.3._.refs_0_), channel_id=1, source_target_pairs={{0,32},{8,40},{16,48},{24,56},{32,0},{40,8},{48,16},{56,24},{64,96... | collective-permute-start | bytes 9224 | tf_op jit(solution)/shard_map/ppermute | solution.py:230
  130.1 2.5 %collective-permute-start.16 = (f32[8,3,32]{2,1,0:T(4,128)S(1)}, f32[8,3,32]{2,1,0:T(4,128)S(1)}, u32[]{:S(2)}, u32[]{:S(2)}) collective-permute-start(f32[8,3,32]{2,1,0:T(4,128)S(1)} %pad_maximum_fusion.3._.refs_0_), channel_id=1, source_target_pairs={{0,48},{8,56},{16,0},{24,8},{32,16},{40,24},{48,32},{56,40},{64,11... | collective-permute-start | bytes 9224 | tf_op jit(solution)/shard_map/ppermute | solution.py:230
  133.2 4.2 %unpack.3 = (bf16[32,256,128]{2,1,0:T(8,128)(2,1)}, f32[1,128]{1,0:T(1,128)}) custom-call(s32[32]{0:T(128)} %fusion.47.slots, bf16[64,256,128]{2,1,0:T(8,128)(2,1)} %all-to-all-done.1.arrived, f32[8,3,32]{2,1,0:T(4,128)} %copy-done.3), custom_call_target="tpu_custom_call" | custom-call | tf_op jit(solution)/shard_map/unpack/pallas_call | solution.py:170
  138.1 1.5 %finish.1 = (f32[1,8]{1,0:T(1,128)}, s32[1,32]{1,0:T(1,128)}) custom-call(f32[1,32]{1,0:T(1,128)} %pad_bitcast_fusion.2.counted, s32[1,32]{1,0:T(1,128)} %get-tuple-element.28.step, s32[1,32]{1,0:T(1,128)} %get-tuple-element.26.place, f32[8,3,32]{2,1,0:T(4,128)} %copy-done.3, f32[8,3,32]{2,1,0:T(4,128)} %copy-done.5, f32[8,3,32]{2,1,0:T(4,128)} %copy-done.6, ...), custom_call_target="tpu_custom_call" | custom-call | tf_op jit(solution)/shard_map/finish/pallas_call | solution.py:206
  (93 shorter events, 16.4 us)
Async XLA Ops:
  1.4 1.5 %collective-permute-start = (bf16[64,256]{1,0:T(8,128)(2,1)S(1)}, bf16[64,256]{1,0:T(8,128)(2,1)S(1)}, u32[]{:S(2)}, u32[]{:S(2)}) collective-permute-start(bf16[64,256]{1,0:T(8,128)(2,1)S(1)} %pad_maximum_fusion.2), channel_id=1, source_target_pairs={{0,8},{8,0},{16,24},{24,16},{32,40},{40,32},{48,56},{56,48},{64,72... | collective-permute-start | bytes 98312 | tf_op jit(solution)/shard_map/ppermute | solution.py:230
  2.9 5.9 %collective-permute-start.1 = (bf16[128,256]{1,0:T(8,128)(2,1)S(1)}, bf16[128,256]{1,0:T(8,128)(2,1)S(1)}, u32[]{:S(2)}, u32[]{:S(2)}) collective-permute-start(bf16[128,256]{1,0:T(8,128)(2,1)S(1)} %maximum_add_fusion.1), channel_id=1, source_target_pairs={{0,64},{8,72},{16,80},{24,88},{32,96},{40,104},{48,112},{56,120},{... | collective-permute-start | bytes 196616 | tf_op jit(solution)/shard_map/ppermute | solution.py:287
  9.4 62.4 %all-to-all-start = ((bf16[64,256,128]{2,1,0:T(8,128)(2,1)}), bf16[64,256,128]{2,1,0:T(8,128)(2,1)}, u32[]{:S(2)}, u32[]{:S(2)}) async-start(bf16[64,256,128]{2,1,0:T(8,128)(2,1)} %after.3), calls=%async_computation | async-start | bytes 8388608 | tf_op jit(solution)/shard_map/all_to_all | solution.py:296
  22.9 55.3 %collective-permute-start.5 = (bf16[256,256]{1,0:T(8,128)(2,1)S(1)}, bf16[256,256]{1,0:T(8,128)(2,1)S(1)}, u32[]{:S(2)}, u32[]{:S(2)}) collective-permute-start(bf16[256,256]{1,0:T(8,128)(2,1)S(1)} %copy-done.2), channel_id=1, source_target_pairs={{0,144},{8,184},{16,160},{24,136},{32,176},{40,152},{48,128},{56,1... | collective-permute-start | bytes 393224 | tf_op jit(solution)/shard_map/ppermute | solution.py:243
  27.4 50.9 %collective-permute-start.4 = (bf16[256,256]{1,0:T(8,128)(2,1)S(1)}, bf16[256,256]{1,0:T(8,128)(2,1)S(1)}, u32[]{:S(2)}, u32[]{:S(2)}) collective-permute-start(bf16[256,256]{1,0:T(8,128)(2,1)S(1)} %copy-done.2), channel_id=1, source_target_pairs={{0,128},{8,168},{16,144},{24,184},{32,160},{40,136},{48,176},{56,1... | collective-permute-start | bytes 393224 | tf_op jit(solution)/shard_map/ppermute | solution.py:243
  27.6 50.6 %collective-permute-start.3 = (bf16[256,256]{1,0:T(8,128)(2,1)S(1)}, bf16[256,256]{1,0:T(8,128)(2,1)S(1)}, u32[]{:S(2)}, u32[]{:S(2)}) collective-permute-start(bf16[256,256]{1,0:T(8,128)(2,1)S(1)} %copy-done.2), channel_id=1, source_target_pairs={{0,16},{8,56},{16,32},{24,8},{32,48},{40,24},{48,0},{56,40},{64,80... | collective-permute-start | bytes 393224 | tf_op jit(solution)/shard_map/ppermute | solution.py:243
  29.0 49.2 %collective-permute-start.2 = (bf16[256,256]{1,0:T(8,128)(2,1)S(1)}, bf16[256,256]{1,0:T(8,128)(2,1)S(1)}, u32[]{:S(2)}, u32[]{:S(2)}) collective-permute-start(bf16[256,256]{1,0:T(8,128)(2,1)S(1)} %copy-done.2), channel_id=1, source_target_pairs={{0,0},{8,40},{16,16},{24,56},{32,32},{40,8},{48,48},{56,24},{64,64... | collective-permute-start | bytes 393224 | tf_op jit(solution)/shard_map/ppermute | solution.py:243
  71.9 61.4 %all-to-all-start.1 = ((bf16[64,256,128]{2,1,0:T(8,128)(2,1)}), bf16[64,256,128]{2,1,0:T(8,128)(2,1)}, u32[]{:S(2)}, u32[]{:S(2)}) async-start(bf16[64,256,128]{2,1,0:T(8,128)(2,1)} %after.5), calls=%async_computation.1 | async-start | bytes 8388608 | tf_op jit(solution)/shard_map/all_to_all | solution.py:300
  78.4 2.4 %collective-permute-start.6 = (bf16[1024,256]{1,0:T(8,128)(2,1)S(1)}, bf16[1024,256]{1,0:T(8,128)(2,1)}, u32[]{:S(2)}, u32[]{:S(2)}) collective-permute-start(bf16[1024,256]{1,0:T(8,128)(2,1)S(1)} %maximum_add_fusion), channel_id=1, source_target_pairs={{0,8},{8,0},{16,24},{24,16},{32,40},{40,32},{48,56},{56,48},{64,72... | collective-permute-start | bytes 1572872 | tf_op jit(solution)/shard_map/ppermute | solution.py:230
  80.8 7.4 %copy-start.13 = (bf16[32,256,128]{2,1,0:T(8,128)(2,1)S(1)}, bf16[32,256,128]{2,1,0:T(8,128)(2,1)}, u32[]{:S(2)}) copy-start(bf16[32,256,128]{2,1,0:T(8,128)(2,1)} %get-tuple-element.16) | copy-start | bytes 6291460
  88.1 10.6 %copy-start.9 = (s32[1024]{0:T(1024)S(1)}, s32[1024]{0:T(1024)}, u32[]{:S(2)}) copy-start(s32[1024]{0:T(1024)} %param.22) | copy-start | bytes 12292
  88.2 18.0 %copy-start.12 = (f32[32]{0:T(128)S(1)}, f32[32]{0:T(128)}, u32[]{:S(2)}) copy-start(f32[32]{0:T(128)} %param.20) | copy-start | bytes 388
  90.6 3.6 %collective-permute-start.7 = (f32[32]{0:T(128)S(1)}, f32[32]{0:T(128)S(1)}, u32[]{:S(2)}, u32[]{:S(2)}) collective-permute-start(f32[32]{0:T(128)S(1)} %get-tuple-element.30), channel_id=1, source_target_pairs={{0,1},{1,0},{2,3},{3,2},{4,5},{5,4},{6,7},{7,6},{8,9},{9,8},{10,11... | collective-permute-start | bytes 392 | tf_op jit(solution)/shard_map/ppermute | solution.py:342
  94.3 4.4 %collective-permute-start.8 = (f32[32]{0:T(128)S(1)}, f32[32]{0:T(128)S(1)}, u32[]{:S(2)}, u32[]{:S(2)}) collective-permute-start(f32[32]{0:T(128)S(1)} %add.139), channel_id=1, source_target_pairs={{0,2},{1,3},{2,0},{3,1},{4,6},{5,7},{6,4},{7,5},{8,10},{9,11},{10,... | collective-permute-start | bytes 392 | tf_op jit(solution)/shard_map/ppermute | solution.py:342
  98.7 7.4 %collective-permute-start.9 = (f32[32]{0:T(128)S(1)}, f32[32]{0:T(128)S(1)}, u32[]{:S(2)}, u32[]{:S(2)}) collective-permute-start(f32[32]{0:T(128)S(1)} %add.140), channel_id=1, source_target_pairs={{0,4},{1,5},{2,6},{3,7},{4,0},{5,1},{6,2},{7,3},{8,12},{9,13},{10,... | collective-permute-start | bytes 392 | tf_op jit(solution)/shard_map/ppermute | solution.py:342
  106.2 31.3 %copy-start.11 = (f32[32]{0:T(128)}, f32[32]{0:T(128)S(1)}, u32[]{:S(2)}) copy-start(f32[32]{0:T(128)S(1)} %add_add_fusion) | copy-start | bytes 388
  106.5 5.9 %collective-permute-start.10 = (f32[1,3,32]{2,1,0:T(4,128)S(1)}, f32[1,3,32]{2,1,0:T(4,128)S(1)}, u32[]{:S(2)}, u32[]{:S(2)}) collective-permute-start(f32[1,3,32]{2,1,0:T(4,128)S(1)} %maximum_bitcast_fusion), channel_id=1, source_target_pairs={{0,8},{8,0},{16,24},{24,16},{32,40},{40,32},{48,56},{56,48},{64,72... | collective-permute-start | bytes 1160 | tf_op jit(solution)/shard_map/ppermute | solution.py:230
  113.0 10.4 %collective-permute-start.13 = (f32[2,3,32]{2,1,0:T(4,128)}, f32[2,3,32]{2,1,0:T(4,128)S(1)}, u32[]{:S(2)}, u32[]{:S(2)}) collective-permute-start(f32[2,3,32]{2,1,0:T(4,128)} %after.4), channel_id=1, source_target_pairs={{0,192},{8,200},{16,208},{24,216},{32,224},{40,232},{48,240},{56,2... | collective-permute-start | bytes 2312 | tf_op jit(solution)/shard_map/ppermute | solution.py:230
  115.8 8.0 %collective-permute-start.12 = (f32[2,3,32]{2,1,0:T(4,128)}, f32[2,3,32]{2,1,0:T(4,128)S(1)}, u32[]{:S(2)}, u32[]{:S(2)}) collective-permute-start(f32[2,3,32]{2,1,0:T(4,128)} %after.4), channel_id=1, source_target_pairs={{0,128},{8,136},{16,144},{24,152},{32,160},{40,168},{48,176},{56,1... | collective-permute-start | bytes 2312 | tf_op jit(solution)/shard_map/ppermute | solution.py:230
  116.7 7.5 %collective-permute-start.11 = (f32[2,3,32]{2,1,0:T(4,128)}, f32[2,3,32]{2,1,0:T(4,128)S(1)}, u32[]{:S(2)}, u32[]{:S(2)}) collective-permute-start(f32[2,3,32]{2,1,0:T(4,128)} %after.4), channel_id=1, source_target_pairs={{0,64},{8,72},{16,80},{24,88},{32,96},{40,104},{48,112},{56,120},{... | collective-permute-start | bytes 2312 | tf_op jit(solution)/shard_map/ppermute | solution.py:230
  124.8 8.4 %copy-start.3 = (f32[8,3,32]{2,1,0:T(4,128)}, f32[8,3,32]{2,1,0:T(4,128)S(1)}, u32[]{:S(2)}) copy-start(f32[8,3,32]{2,1,0:T(4,128)S(1)} %pad_maximum_fusion.3._.refs_0_) | copy-start | bytes 9220
  124.9 12.6 %collective-permute-start.14 = (f32[8,3,32]{2,1,0:T(4,128)S(1)}, f32[8,3,32]{2,1,0:T(4,128)S(1)}, u32[]{:S(2)}, u32[]{:S(2)}) collective-permute-start(f32[8,3,32]{2,1,0:T(4,128)S(1)} %pad_maximum_fusion.3._.refs_0_), channel_id=1, source_target_pairs={{0,16},{8,24},{16,32},{24,40},{32,48},{40,56},{48,0},{56,8},{64,80... | collective-permute-start | bytes 9224 | tf_op jit(solution)/shard_map/ppermute | solution.py:230
  127.9 9.6 %collective-permute-start.15 = (f32[8,3,32]{2,1,0:T(4,128)S(1)}, f32[8,3,32]{2,1,0:T(4,128)S(1)}, u32[]{:S(2)}, u32[]{:S(2)}) collective-permute-start(f32[8,3,32]{2,1,0:T(4,128)S(1)} %pad_maximum_fusion.3._.refs_0_), channel_id=1, source_target_pairs={{0,32},{8,40},{16,48},{24,56},{32,0},{40,8},{48,16},{56,24},{64,96... | collective-permute-start | bytes 9224 | tf_op jit(solution)/shard_map/ppermute | solution.py:230
  130.1 7.4 %collective-permute-start.16 = (f32[8,3,32]{2,1,0:T(4,128)S(1)}, f32[8,3,32]{2,1,0:T(4,128)S(1)}, u32[]{:S(2)}, u32[]{:S(2)}) collective-permute-start(f32[8,3,32]{2,1,0:T(4,128)S(1)} %pad_maximum_fusion.3._.refs_0_), channel_id=1, source_target_pairs={{0,48},{8,56},{16,0},{24,8},{32,16},{40,24},{48,32},{56,40},{64,11... | collective-permute-start | bytes 9224 | tf_op jit(solution)/shard_map/ppermute | solution.py:230
  (10 other events, 31.0 us)

commit v10 on v9

--- a/solution.py
+++ b/solution.py
@@ -19,7 +19,6 @@
 WINDOW = 32
 CHUNKS = 4
 GROUP = 2
-ROOMY = 58 << 20
 
 
 def pack_kernel(keeps, lengths, least, most, *refs):
@@ -124,7 +123,6 @@
         in_specs=[hbm] + [pl.BlockSpec(memory_space=pl.ANY)] * len(others),
         out_specs=hbm,
         input_output_aliases={0: 0},
-        compiler_params=pltpu.CompilerParams(vmem_limit_bytes=ROOMY),
         name="after",
     )(array, *others)
 
@@ -143,7 +141,7 @@
     )(array)
 
 
-def unpack_kernel(slots, arrived, _, result, mark, held, in_sems, out_sems):
+def move_rows(slots, arrived, result, held, in_sems, out_sems, meanwhile):
     count = result.shape[0]
     share = count // CHUNKS
 
@@ -154,13 +152,20 @@
         rows = pl.ds(chunk * share, share)
         return pltpu.make_async_copy(held.at[rows], result.at[rows], out_sems.at[chunk])
 
-    mark[...] = jnp.zeros_like(mark)
     repeat(count, lambda p: load(p).start(), count)
+    meanwhile()
     for chunk in range(CHUNKS):
         repeat(share, lambda p, chunk=chunk: load(p + chunk * share).wait(), share)
         keep(chunk).start()
     for chunk in range(CHUNKS):
         keep(chunk).wait()
+
+
+def unpack_kernel(slots, arrived, _, result, mark, held, in_sems, out_sems):
+    def clear():
+        mark[...] = jnp.zeros_like(mark)
+
+    move_rows(slots, arrived, result, held, in_sems, out_sems, clear)
 
 
 def unpack(arrived, slots, other):
@@ -184,36 +189,48 @@
     )(slots, arrived, other)
 
 
-def finish_kernel(counted, step, place, *refs):
-    *parts, _, rung_means, next_lengths = refs
-    shared = jnp.concatenate([part[...] for part in parts], axis=0)
-    peaks, sums, filled = shared[:, 0], shared[:, 1], shared[:, 2]
-    top = jnp.max(peaks, axis=0, keepdims=True)
-    summed = jnp.sum(sums * jnp.exp(peaks - top), axis=0, keepdims=True)
-    rung_means[...] = (top + jnp.log(summed) - jnp.log(counted[...]))[:, :RUNGS]
-    order = lax.broadcasted_iota(jnp.int32, filled.shape, 0)
-    owner = (order == step[...]).astype(jnp.float32)
-    found = lax.dot_general(
-        filled, owner, (((0,), (0,)), ((), ())), preferred_element_type=jnp.float32
-    )
-    order = lax.broadcasted_iota(jnp.int32, found.shape, 0)
-    length = jnp.sum(jnp.where(order == place[...], found, 0.0), axis=0, keepdims=True)
-    next_lengths[...] = length.astype(jnp.int32) + STEPS
-
-
-def finish(parts, counted, step, place, other):
+def finish_kernel(slots, arrived, counted, step, place, *refs):
+    *parts, result, rung_means, next_lengths, held, in_sems, out_sems = refs
+
+    def sums():
+        shared = jnp.concatenate([part[...] for part in parts], axis=0)
+        peaks, sums, filled = shared[:, 0], shared[:, 1], shared[:, 2]
+        top = jnp.max(peaks, axis=0, keepdims=True)
+        summed = jnp.sum(sums * jnp.exp(peaks - top), axis=0, keepdims=True)
+        rung_means[...] = (top + jnp.log(summed) - jnp.log(counted[...]))[:, :RUNGS]
+        order = lax.broadcasted_iota(jnp.int32, filled.shape, 0)
+        owner = (order == step[...]).astype(jnp.float32)
+        found = lax.dot_general(
+            filled, owner, (((0,), (0,)), ((), ())), preferred_element_type=jnp.float32
+        )
+        order = lax.broadcasted_iota(jnp.int32, found.shape, 0)
+        length = jnp.sum(jnp.where(order == place[...], found, 0.0), axis=0, keepdims=True)
+        next_lengths[...] = length.astype(jnp.int32) + STEPS
+
+    move_rows(slots, arrived, result, held, in_sems, out_sems, sums)
+
+
+def finish(arrived, slots, parts, counted, step, place):
+    count, (_, suffix, width) = slots.shape[0], arrived.shape
+    hbm = pl.BlockSpec(memory_space=pltpu.HBM)
     vmem = pl.BlockSpec(memory_space=pltpu.VMEM)
+    shape = (count, suffix, width)
     return pl.pallas_call(
         finish_kernel,
         out_shape=(
+            jax.ShapeDtypeStruct(shape, arrived.dtype),
             jax.ShapeDtypeStruct((1, RUNGS), jnp.float32),
             jax.ShapeDtypeStruct(step.shape, jnp.int32),
         ),
-        in_specs=[vmem] * (3 + len(parts)) + [pl.BlockSpec(memory_space=pl.ANY)],
-        out_specs=(vmem, vmem),
-        compiler_params=pltpu.CompilerParams(vmem_limit_bytes=ROOMY),
+        in_specs=[pl.BlockSpec(memory_space=pltpu.SMEM), hbm] + [vmem] * (3 + len(parts)),
+        out_specs=(hbm, vmem, vmem),
+        scratch_shapes=[
+            pltpu.VMEM(shape, arrived.dtype),
+            pltpu.SemaphoreType.DMA((count,)),
+            pltpu.SemaphoreType.DMA((CHUNKS,)),
+        ],
         name="finish",
-    )(counted, step, place, *parts, other)
+    )(slots, arrived, counted, step, place, *parts)
 
 
 def along(array, axes):
@@ -238,7 +255,7 @@
         pairs = []
         for i in range(tall * wide * cores):
             y, x, core = i // (wide * cores), i // cores % wide, i % cores
-            goal = (y ^ 2 * hop) * wide + (x + 2 * core + step) % wide
+            goal = (y ^ hop) * wide + (x + 2 * core + step) % wide
             pairs.append((i, goal * cores + core))
         parts.append(lax.ppermute(array, "particle", pairs))
     return parts
@@ -284,7 +301,7 @@
     )
     chip = jnp.concatenate(along(shard, (2,)), axis=0)
     chip = chip + jnp.minimum(least[0], 0).astype(chip.dtype)
-    beside = lax.ppermute(chip, "particle", [(i, i ^ 8) for i in range(sources)])
+    beside = lax.ppermute(chip, "particle", [(i, i ^ 16) for i in range(sources)])
     column = jnp.concatenate([chip, beside], axis=0)
     halves = half_of(column)
 
@@ -360,7 +377,6 @@
     near = after(near, attention, mark)
     near = jnp.concatenate(along(near, (0,)), axis=0)
     parts = along(near, (1,))
-    next_values, mark = unpack(arrived_values, slot, near)
 
     counted = jnp.sum((rungs[:, None] == ladder[None, :]).astype(jnp.float32), axis=0)
     tall, wide, cores = SIDES
@@ -368,12 +384,13 @@
     right = (device // cores % wide - mine_owner // cores % wide) % wide
     across = (device % cores - mine_owner % cores) % cores
     step = (right * tall + up) * cores + across
-    rung_means, next_lengths = finish(
+    next_values, rung_means, next_lengths = finish(
+        arrived_values,
+        slot,
         parts,
         jnp.pad(counted, (0, spare), constant_values=1.0)[None],
         step[None],
         (mine % per_device)[None],
-        mark,
     )
     rung_means = rung_means[0]
     next_lengths = next_lengths[0]

time: 141 us -> 140 us (level)
  Pallas kernels: 21.2 us -> 19.1 us
    pallas_call x2 -> x1, Pallas kernels: 8.54 us -> 4.2 us  [unpack(): pl.pallas_call(unpack_kernel, out_shape=(jax.ShapeDtypeStruct(shape, arri...]
    pallas_call x1, Pallas kernels: 1.52 us -> 4.31 us  [finish(): pl.pallas_call(finish_kernel, out_shape=(jax.ShapeDtypeStruct(shape, arri...]
    ppermute x1, starting transfers between devices: 1.66 us -> 3.28 us  [shards(): lax.ppermute(chip, 'particle', [(i, i ^ 16) for i in range(sources)])]
  transfers between devices with their start and end apart: 19 -> 19, of which waited for: 7 -> 8; matrix products, arithmetic and copies ran while one was open for 13% -> 14% of each run, Pallas kernels for 14% -> 11%
where the time goes in v10:
time: 140 us; the launch traced here: 138 us
  waiting for transfers between devices  61.2 us (44%)
  starting transfers between devices  35.7 us (26%)
  Pallas kernels  19.1 us (14%)
  other arithmetic  10.9 us (8%)
  matrix products  6.94 us (5%)
  local copies, waits for them, and re-layouts  3.07 us (2%)
    all_to_all x1, waiting for transfers between devices, shards(): arrived_keys = exchange(after(outgoing_keys, column))  42 us
    ppermute x9, starting transfers between devices, along(): lax.ppermute(array, 'particle', pairs)  13 us
    ppermute x3, waiting for transfers between devices, shards(): reward = reward + lax.ppermute(reward, 'tensor', pairs)  12.1 us
    pallas_call x2, Pallas kernels, pack(): pl.pallas_call(functools.partial(pack_kernel, keeps), out_shape=[jax.Shap...  10.1 us
    ppermute x9, waiting for transfers between devices, along(): lax.ppermute(array, 'particle', pairs)  7.1 us
    all_to_all x1, starting transfers between devices, shards(): arrived_keys = exchange(after(outgoing_keys, column))  6.28 us
    ppermute x4, starting transfers between devices, half_of(): parts.append(lax.ppermute(array, 'particle', pairs))  5.52 us
    all_to_all x1, starting transfers between devices, shards(): arrived_values = exchange(after(outgoing_values, arrived_keys))  4.99 us
  transfers between devices with their start and end apart: 19, of which 8 were waited for; matrix products, arithmetic and copies ran while one was open for 14% of the time, Pallas kernels for 11%

profile of v10, /device:TPU:128, one launch (start us, length us, event | category | flops | bytes accessed | tf_op | source)
XLA Modules:
  0.0 138.1 jit_solution(512979605550165164)
XLA Ops:
  2.9 3.3 %collective-permute-start.1 = (bf16[128,256]{1,0:T(8,128)(2,1)S(1)}, bf16[128,256]{1,0:T(8,128)(2,1)S(1)}, u32[]{:S(2)}, u32[]{:S(2)}) collective-permute-start(bf16[128,256]{1,0:T(8,128)(2,1)S(1)} %maximum_add_fusion.1), channel_id=1, source_target_pairs={{0,128},{8,136},{16,144},{24,152},{32,160},{40,168},{48,176},{56,1... | collective-permute-start | bytes 196616 | tf_op jit(solution)/shard_map/ppermute | solution.py:304
  6.1 4.0 %pack.2.refs_0_ = bf16[64,256,128]{2,1,0:T(8,128)(2,1)} custom-call(s32[32]{0:T(128)} %lengths.3, s32[32]{0:T(128)} %copy-done.8, s32[32]{0:T(128)} %get-tuple-element.22.most, bf16[32,256,128]{2,1,0:T(8,128)(2,1)} %refs_0_.3, bf16[32,2,128]{2,1,0:T(2,128)(2,1)} %refs_2_.1), custom_call_target="tpu_custom_call" | custom-call | tf_op jit(solution)/shard_map/pack/pallas_call | solution.py:102
  10.8 6.3 %all-to-all-start = ((bf16[64,256,128]{2,1,0:T(8,128)(2,1)}), bf16[64,256,128]{2,1,0:T(8,128)(2,1)}, u32[]{:S(2)}, u32[]{:S(2)}) async-start(bf16[64,256,128]{2,1,0:T(8,128)(2,1)} %after.3), calls=%async_computation | async-start | bytes 8388608 | tf_op jit(solution)/shard_map/all_to_all | solution.py:313
  17.1 6.1 %pack.3 = (bf16[64,256,128]{2,1,0:T(8,128)(2,1)}, bf16[32,256,128]{2,1,0:T(8,128)(2,1)}, bf16[32,256,128]{2,1,0:T(8,128)(2,1)}) custom-call(s32[32]{0:T(128)} %lengths.3, s32[32]{0:T(128)} %copy-done.8, s32[32]{0:T(128)} %get-tuple-element.22.most, bf16[32,256,128]{2,1,0:T(8,128)(2,1)} %refs_0_.3, bf16[32,256,128]{2,1,0:T(8,128)(2,1)} %refs_1_.3, ...), custom_call_target="tpu_custom_call" | custom-call | tf_op jit(solution)/shard_map/pack/pallas_call | solution.py:102
  23.2 3.1 %collective-permute-start.5 = (bf16[256,256]{1,0:T(8,128)(2,1)S(1)}, bf16[256,256]{1,0:T(8,128)(2,1)S(1)}, u32[]{:S(2)}, u32[]{:S(2)}) collective-permute-start(bf16[256,256]{1,0:T(8,128)(2,1)S(1)} %copy-done.2), channel_id=1, source_target_pairs={{0,80},{8,120},{16,96},{24,72},{32,112},{40,88},{48,64},{56,104},{... | collective-permute-start | bytes 393224 | tf_op jit(solution)/shard_map/ppermute | solution.py:260
  26.6 1.5 %collective-permute-start.3 = (bf16[256,256]{1,0:T(8,128)(2,1)S(1)}, bf16[256,256]{1,0:T(8,128)(2,1)S(1)}, u32[]{:S(2)}, u32[]{:S(2)}) collective-permute-start(bf16[256,256]{1,0:T(8,128)(2,1)S(1)} %copy-done.2), channel_id=1, source_target_pairs={{0,16},{8,56},{16,32},{24,8},{32,48},{40,24},{48,0},{56,40},{64,80... | collective-permute-start | bytes 393224 | tf_op jit(solution)/shard_map/ppermute | solution.py:260
  28.8 42.0 %all-to-all-done._.refs_1_.arrived = bf16[64,256,128]{2,1,0:T(8,128)(2,1)} async-done(((bf16[64,256,128]{2,1,0:T(8,128)(2,1)}), bf16[64,256,128]{2,1,0:T(8,128)(2,1)}, u32[]{:S(2)}, u32[]{:S(2)}) %all-to-all-start) | async-done | bytes 4194336 | tf_op jit(solution)/shard_map/all_to_all | solution.py:313
  70.8 5.0 %all-to-all-start.1 = ((bf16[64,256,128]{2,1,0:T(8,128)(2,1)}), bf16[64,256,128]{2,1,0:T(8,128)(2,1)}, u32[]{:S(2)}, u32[]{:S(2)}) async-start(bf16[64,256,128]{2,1,0:T(8,128)(2,1)} %after.4), calls=%async_computation.1 | async-start | bytes 8388608 | tf_op jit(solution)/shard_map/all_to_all | solution.py:317
  78.4 1.3 fusion.47
  79.8 3.7 %bitcast_reduce_fusion = (f32[32,2,8]{0,2,1:T(8,128)S(1)}, f32[2048,32,2,8]{0,1,3,2:T(8,128)}) fusion(bf16[32,2,8,128]{3,2,1,0:T(8,128)(2,1)S(1)} %reshape.74, bf16[1024,256]{1,0:T(8,128)(2,1)S(1)} %maximum_add_fusion, bf16[1024,256]{1,0:T(8,128)(2,1)} %collective-permute-done.6), kind=kOutput, calls=%fused_computation.1 | convolution fusion | flops 271580672 | bytes 5376000 | tf_op jit(solution)/shard_map/pshd,nd->pshn/dot_general | solution.py:327
  84.0 3.2 %fusion.1 = f32[32,2,8]{0,2,1:T(8,128)S(1)} fusion(f32[2048,32,2,8]{0,1,3,2:T(8,128)} %get-tuple-element.33, f32[32,2,8]{0,2,1:T(8,128)S(1)} %max.11), kind=kLoop, calls=%fused_computation.3 | loop fusion | flops 3145216 | bytes 4198400 | tf_op jit(solution)/shard_map/reduce_sum | solution.py:340
  87.7 2.0 %multiply_reduce_fusion = (f32[32]{0:T(128)S(1)}, bf16[32,2,8,128]{3,0,2,1:T(8,128)(2,1)S(1)}) fusion(f32[8,128]{1,0:T(8,128)S(1)} %bitcast.78, f32[32,2,8]{0,2,1:T(8,128)S(1)} %add.138, f32[32,2,8,128]{3,2,1,0:T(8,128)S(1)} %fusion.5, bf16[1024,256]{1,0:T(8,128)(2,1)} %collective-permute-done.6, bf16[1024,256]{1,0:T(8,128)(2,1)S(1)} %maximum_add_fusion, ...), kind=kOutput, calls=%fused_computation.29 | convolution fusion | flops 272957408 | bytes 5644416 | tf_op jit(solution)/shard_map/pshn,nd->pshd/dot_general | solution.py:341
  89.7 1.1 collective-permute-start.7
  91.4 1.9 %collective-permute-done.7 = f32[32]{0:T(128)S(1)} collective-permute-done((f32[32]{0:T(128)S(1)}, f32[32]{0:T(128)S(1)}, u32[]{:S(2)}, u32[]{:S(2)}) %collective-permute-start.7) | collective-permute-done | bytes 160 | tf_op jit(solution)/shard_map/ppermute | solution.py:359
  93.3 1.5 %collective-permute-start.8 = (f32[32]{0:T(128)S(1)}, f32[32]{0:T(128)S(1)}, u32[]{:S(2)}, u32[]{:S(2)}) collective-permute-start(f32[32]{0:T(128)S(1)} %add.139), channel_id=1, source_target_pairs={{0,2},{1,3},{2,0},{3,1},{4,6},{5,7},{6,4},{7,5},{8,10},{9,11},{10,... | collective-permute-start | bytes 392 | tf_op jit(solution)/shard_map/ppermute | solution.py:359
  95.0 2.8 %collective-permute-done.8 = f32[32]{0:T(128)S(1)} collective-permute-done((f32[32]{0:T(128)S(1)}, f32[32]{0:T(128)S(1)}, u32[]{:S(2)}, u32[]{:S(2)}) %collective-permute-start.8) | collective-permute-done | bytes 160 | tf_op jit(solution)/shard_map/ppermute | solution.py:359
  97.8 7.4 %collective-permute-done.9 = f32[32]{0:T(128)S(1)} collective-permute-done((f32[32]{0:T(128)S(1)}, f32[32]{0:T(128)S(1)}, u32[]{:S(2)}, u32[]{:S(2)}) %collective-permute-start.9) | collective-permute-done | bytes 160 | tf_op jit(solution)/shard_map/ppermute | solution.py:359
  106.4 4.2 %unpack.1 = (bf16[32,256,128]{2,1,0:T(8,128)(2,1)}, f32[1,128]{1,0:T(1,128)}) custom-call(s32[32]{0:T(128)} %fusion.43.slots, bf16[64,256,128]{2,1,0:T(8,128)(2,1)} %all-to-all-done._.refs_1_.arrived, bf16[256,256]{1,0:T(8,128)(2,1)} %pad_maximum_fusion.1.refs_1_._), custom_call_target="tpu_custom_call" | custom-call | tf_op jit(solution)/shard_map/unpack/pallas_call | solution.py:175
  112.0 3.0 %collective-permute-start.13 = (f32[2,3,32]{2,1,0:T(4,128)}, f32[2,3,32]{2,1,0:T(4,128)S(1)}, u32[]{:S(2)}, u32[]{:S(2)}) collective-permute-start(f32[2,3,32]{2,1,0:T(4,128)} %after.5), channel_id=1, source_target_pairs={{0,192},{8,200},{16,208},{24,216},{32,224},{40,232},{48,240},{56,2... | collective-permute-start | bytes 2312 | tf_op jit(solution)/shard_map/ppermute | solution.py:247
  116.9 5.4 %collective-permute-done.13 = f32[2,3,32]{2,1,0:T(4,128)S(1)} collective-permute-done((f32[2,3,32]{2,1,0:T(4,128)}, f32[2,3,32]{2,1,0:T(4,128)S(1)}, u32[]{:S(2)}, u32[]{:S(2)}) %collective-permute-start.13) | collective-permute-done | bytes 800 | tf_op jit(solution)/shard_map/ppermute | solution.py:247
  123.8 3.0 %collective-permute-start.14 = (f32[8,3,32]{2,1,0:T(4,128)S(1)}, f32[8,3,32]{2,1,0:T(4,128)S(1)}, u32[]{:S(2)}, u32[]{:S(2)}) collective-permute-start(f32[8,3,32]{2,1,0:T(4,128)S(1)} %pad_maximum_fusion.3.refs_0_), channel_id=1, source_target_pairs={{0,16},{8,24},{16,32},{24,40},{32,48},{40,56},{48,0},{56,8},{64,80... | collective-permute-start | bytes 9224 | tf_op jit(solution)/shard_map/ppermute | solution.py:247
  126.8 2.2 %collective-permute-start.15 = (f32[8,3,32]{2,1,0:T(4,128)S(1)}, f32[8,3,32]{2,1,0:T(4,128)S(1)}, u32[]{:S(2)}, u32[]{:S(2)}) collective-permute-start(f32[8,3,32]{2,1,0:T(4,128)S(1)} %pad_maximum_fusion.3.refs_0_), channel_id=1, source_target_pairs={{0,32},{8,40},{16,48},{24,56},{32,0},{40,8},{48,16},{56,24},{64,96... | collective-permute-start | bytes 9224 | tf_op jit(solution)/shard_map/ppermute | solution.py:247
  129.0 2.5 %collective-permute-start.16 = (f32[8,3,32]{2,1,0:T(4,128)S(1)}, f32[8,3,32]{2,1,0:T(4,128)S(1)}, u32[]{:S(2)}, u32[]{:S(2)}) collective-permute-start(f32[8,3,32]{2,1,0:T(4,128)S(1)} %pad_maximum_fusion.3.refs_0_), channel_id=1, source_target_pairs={{0,48},{8,56},{16,0},{24,8},{32,16},{40,24},{48,32},{56,40},{64,11... | collective-permute-start | bytes 9224 | tf_op jit(solution)/shard_map/ppermute | solution.py:247
  133.6 4.3 %finish.1 = (bf16[32,256,128]{2,1,0:T(8,128)(2,1)}, f32[1,8]{1,0:T(1,128)}, s32[1,32]{1,0:T(1,128)}) custom-call(s32[32]{0:T(128)} %fusion.43.slots, bf16[64,256,128]{2,1,0:T(8,128)(2,1)} %all-to-all-done.1.arrived, f32[1,32]{1,0:T(1,128)} %pad_bitcast_fusion.2.counted, s32[1,32]{1,0:T(1,128)} %get-tuple-element.26.step, s32[1,32]{1,0:T(1,128)} %get-tuple-element.24.place, ...), custom_call_target="tpu_custom_call" | custom-call | tf_op jit(solution)/shard_map/finish/pallas_call | solution.py:218
  (92 shorter events, 16.1 us)
Async XLA Ops:
  1.4 1.5 %collective-permute-start = (bf16[64,256]{1,0:T(8,128)(2,1)S(1)}, bf16[64,256]{1,0:T(8,128)(2,1)S(1)}, u32[]{:S(2)}, u32[]{:S(2)}) collective-permute-start(bf16[64,256]{1,0:T(8,128)(2,1)S(1)} %pad_maximum_fusion.2), channel_id=1, source_target_pairs={{0,8},{8,0},{16,24},{24,16},{32,40},{40,32},{48,56},{56,48},{64,72... | collective-permute-start | bytes 98312 | tf_op jit(solution)/shard_map/ppermute | solution.py:247
  2.9 7.3 %collective-permute-start.1 = (bf16[128,256]{1,0:T(8,128)(2,1)S(1)}, bf16[128,256]{1,0:T(8,128)(2,1)S(1)}, u32[]{:S(2)}, u32[]{:S(2)}) collective-permute-start(bf16[128,256]{1,0:T(8,128)(2,1)S(1)} %maximum_add_fusion.1), channel_id=1, source_target_pairs={{0,128},{8,136},{16,144},{24,152},{32,160},{40,168},{48,176},{56,1... | collective-permute-start | bytes 196616 | tf_op jit(solution)/shard_map/ppermute | solution.py:304
  10.8 60.0 %all-to-all-start = ((bf16[64,256,128]{2,1,0:T(8,128)(2,1)}), bf16[64,256,128]{2,1,0:T(8,128)(2,1)}, u32[]{:S(2)}, u32[]{:S(2)}) async-start(bf16[64,256,128]{2,1,0:T(8,128)(2,1)} %after.3), calls=%async_computation | async-start | bytes 8388608 | tf_op jit(solution)/shard_map/all_to_all | solution.py:313
  23.2 53.9 %collective-permute-start.5 = (bf16[256,256]{1,0:T(8,128)(2,1)S(1)}, bf16[256,256]{1,0:T(8,128)(2,1)S(1)}, u32[]{:S(2)}, u32[]{:S(2)}) collective-permute-start(bf16[256,256]{1,0:T(8,128)(2,1)S(1)} %copy-done.2), channel_id=1, source_target_pairs={{0,80},{8,120},{16,96},{24,72},{32,112},{40,88},{48,64},{56,104},{... | collective-permute-start | bytes 393224 | tf_op jit(solution)/shard_map/ppermute | solution.py:260
  26.3 50.9 %collective-permute-start.4 = (bf16[256,256]{1,0:T(8,128)(2,1)S(1)}, bf16[256,256]{1,0:T(8,128)(2,1)S(1)}, u32[]{:S(2)}, u32[]{:S(2)}) collective-permute-start(bf16[256,256]{1,0:T(8,128)(2,1)S(1)} %copy-done.2), channel_id=1, source_target_pairs={{0,64},{8,104},{16,80},{24,120},{32,96},{40,72},{48,112},{56,88},{... | collective-permute-start | bytes 393224 | tf_op jit(solution)/shard_map/ppermute | solution.py:260
  26.6 50.5 %collective-permute-start.3 = (bf16[256,256]{1,0:T(8,128)(2,1)S(1)}, bf16[256,256]{1,0:T(8,128)(2,1)S(1)}, u32[]{:S(2)}, u32[]{:S(2)}) collective-permute-start(bf16[256,256]{1,0:T(8,128)(2,1)S(1)} %copy-done.2), channel_id=1, source_target_pairs={{0,16},{8,56},{16,32},{24,8},{32,48},{40,24},{48,0},{56,40},{64,80... | collective-permute-start | bytes 393224 | tf_op jit(solution)/shard_map/ppermute | solution.py:260
  28.1 49.1 %collective-permute-start.2 = (bf16[256,256]{1,0:T(8,128)(2,1)S(1)}, bf16[256,256]{1,0:T(8,128)(2,1)S(1)}, u32[]{:S(2)}, u32[]{:S(2)}) collective-permute-start(bf16[256,256]{1,0:T(8,128)(2,1)S(1)} %copy-done.2), channel_id=1, source_target_pairs={{0,0},{8,40},{16,16},{24,56},{32,32},{40,8},{48,48},{56,24},{64,64... | collective-permute-start | bytes 393224 | tf_op jit(solution)/shard_map/ppermute | solution.py:260
  70.8 62.2 %all-to-all-start.1 = ((bf16[64,256,128]{2,1,0:T(8,128)(2,1)}), bf16[64,256,128]{2,1,0:T(8,128)(2,1)}, u32[]{:S(2)}, u32[]{:S(2)}) async-start(bf16[64,256,128]{2,1,0:T(8,128)(2,1)} %after.4), calls=%async_computation.1 | async-start | bytes 8388608 | tf_op jit(solution)/shard_map/all_to_all | solution.py:317
  77.3 2.5 %collective-permute-start.6 = (bf16[1024,256]{1,0:T(8,128)(2,1)S(1)}, bf16[1024,256]{1,0:T(8,128)(2,1)}, u32[]{:S(2)}, u32[]{:S(2)}) collective-permute-start(bf16[1024,256]{1,0:T(8,128)(2,1)S(1)} %maximum_add_fusion), channel_id=1, source_target_pairs={{0,8},{8,0},{16,24},{24,16},{32,40},{40,32},{48,56},{56,48},{64,72... | collective-permute-start | bytes 1572872 | tf_op jit(solution)/shard_map/ppermute | solution.py:247
  79.8 7.4 %copy-start.13 = (bf16[32,256,128]{2,1,0:T(8,128)(2,1)S(1)}, bf16[32,256,128]{2,1,0:T(8,128)(2,1)}, u32[]{:S(2)}) copy-start(bf16[32,256,128]{2,1,0:T(8,128)(2,1)} %get-tuple-element.15) | copy-start | bytes 6291460
  87.2 10.6 %copy-start.9 = (s32[1024]{0:T(1024)S(1)}, s32[1024]{0:T(1024)}, u32[]{:S(2)}) copy-start(s32[1024]{0:T(1024)} %param.22) | copy-start | bytes 12292
  87.2 18.0 %copy-start.12 = (f32[32]{0:T(128)S(1)}, f32[32]{0:T(128)}, u32[]{:S(2)}) copy-start(f32[32]{0:T(128)} %param.20) | copy-start | bytes 388
  89.7 3.6 %collective-permute-start.7 = (f32[32]{0:T(128)S(1)}, f32[32]{0:T(128)S(1)}, u32[]{:S(2)}, u32[]{:S(2)}) collective-permute-start(f32[32]{0:T(128)S(1)} %get-tuple-element.28), channel_id=1, source_target_pairs={{0,1},{1,0},{2,3},{3,2},{4,5},{5,4},{6,7},{7,6},{8,9},{9,8},{10,11... | collective-permute-start | bytes 392 | tf_op jit(solution)/shard_map/ppermute | solution.py:359
  93.3 4.4 %collective-permute-start.8 = (f32[32]{0:T(128)S(1)}, f32[32]{0:T(128)S(1)}, u32[]{:S(2)}, u32[]{:S(2)}) collective-permute-start(f32[32]{0:T(128)S(1)} %add.139), channel_id=1, source_target_pairs={{0,2},{1,3},{2,0},{3,1},{4,6},{5,7},{6,4},{7,5},{8,10},{9,11},{10,... | collective-permute-start | bytes 392 | tf_op jit(solution)/shard_map/ppermute | solution.py:359
  97.7 7.4 %collective-permute-start.9 = (f32[32]{0:T(128)S(1)}, f32[32]{0:T(128)S(1)}, u32[]{:S(2)}, u32[]{:S(2)}) collective-permute-start(f32[32]{0:T(128)S(1)} %add.140), channel_id=1, source_target_pairs={{0,4},{1,5},{2,6},{3,7},{4,0},{5,1},{6,2},{7,3},{8,12},{9,13},{10,... | collective-permute-start | bytes 392 | tf_op jit(solution)/shard_map/ppermute | solution.py:359
  105.2 32.7 %copy-start.11 = (f32[32]{0:T(128)}, f32[32]{0:T(128)S(1)}, u32[]{:S(2)}) copy-start(f32[32]{0:T(128)S(1)} %add_add_fusion) | copy-start | bytes 388
  105.5 5.8 %collective-permute-start.10 = (f32[1,3,32]{2,1,0:T(4,128)S(1)}, f32[1,3,32]{2,1,0:T(4,128)S(1)}, u32[]{:S(2)}, u32[]{:S(2)}) collective-permute-start(f32[1,3,32]{2,1,0:T(4,128)S(1)} %maximum_bitcast_fusion), channel_id=1, source_target_pairs={{0,8},{8,0},{16,24},{24,16},{32,40},{40,32},{48,56},{56,48},{64,72... | collective-permute-start | bytes 1160 | tf_op jit(solution)/shard_map/ppermute | solution.py:247
  112.0 10.3 %collective-permute-start.13 = (f32[2,3,32]{2,1,0:T(4,128)}, f32[2,3,32]{2,1,0:T(4,128)S(1)}, u32[]{:S(2)}, u32[]{:S(2)}) collective-permute-start(f32[2,3,32]{2,1,0:T(4,128)} %after.5), channel_id=1, source_target_pairs={{0,192},{8,200},{16,208},{24,216},{32,224},{40,232},{48,240},{56,2... | collective-permute-start | bytes 2312 | tf_op jit(solution)/shard_map/ppermute | solution.py:247
  115.0 7.7 %collective-permute-start.12 = (f32[2,3,32]{2,1,0:T(4,128)}, f32[2,3,32]{2,1,0:T(4,128)S(1)}, u32[]{:S(2)}, u32[]{:S(2)}) collective-permute-start(f32[2,3,32]{2,1,0:T(4,128)} %after.5), channel_id=1, source_target_pairs={{0,128},{8,136},{16,144},{24,152},{32,160},{40,168},{48,176},{56,1... | collective-permute-start | bytes 2312 | tf_op jit(solution)/shard_map/ppermute | solution.py:247
  115.8 7.3 %collective-permute-start.11 = (f32[2,3,32]{2,1,0:T(4,128)}, f32[2,3,32]{2,1,0:T(4,128)S(1)}, u32[]{:S(2)}, u32[]{:S(2)}) collective-permute-start(f32[2,3,32]{2,1,0:T(4,128)} %after.5), channel_id=1, source_target_pairs={{0,64},{8,72},{16,80},{24,88},{32,96},{40,104},{48,112},{56,120},{... | collective-permute-start | bytes 2312 | tf_op jit(solution)/shard_map/ppermute | solution.py:247
  123.8 9.3 %copy-start.4 = (f32[8,3,32]{2,1,0:T(4,128)}, f32[8,3,32]{2,1,0:T(4,128)S(1)}, u32[]{:S(2)}) copy-start(f32[8,3,32]{2,1,0:T(4,128)S(1)} %pad_maximum_fusion.3.refs_0_) | copy-start | bytes 9220
  123.8 8.3 %collective-permute-start.14 = (f32[8,3,32]{2,1,0:T(4,128)S(1)}, f32[8,3,32]{2,1,0:T(4,128)S(1)}, u32[]{:S(2)}, u32[]{:S(2)}) collective-permute-start(f32[8,3,32]{2,1,0:T(4,128)S(1)} %pad_maximum_fusion.3.refs_0_), channel_id=1, source_target_pairs={{0,16},{8,24},{16,32},{24,40},{32,48},{40,56},{48,0},{56,8},{64,80... | collective-permute-start | bytes 9224 | tf_op jit(solution)/shard_map/ppermute | solution.py:247
  126.8 5.3 %collective-permute-start.15 = (f32[8,3,32]{2,1,0:T(4,128)S(1)}, f32[8,3,32]{2,1,0:T(4,128)S(1)}, u32[]{:S(2)}, u32[]{:S(2)}) collective-permute-start(f32[8,3,32]{2,1,0:T(4,128)S(1)} %pad_maximum_fusion.3.refs_0_), channel_id=1, source_target_pairs={{0,32},{8,40},{16,48},{24,56},{32,0},{40,8},{48,16},{56,24},{64,96... | collective-permute-start | bytes 9224 | tf_op jit(solution)/shard_map/ppermute | solution.py:247
  129.0 4.0 %collective-permute-start.16 = (f32[8,3,32]{2,1,0:T(4,128)S(1)}, f32[8,3,32]{2,1,0:T(4,128)S(1)}, u32[]{:S(2)}, u32[]{:S(2)}) collective-permute-start(f32[8,3,32]{2,1,0:T(4,128)S(1)} %pad_maximum_fusion.3.refs_0_), channel_id=1, source_target_pairs={{0,48},{8,56},{16,0},{24,8},{32,16},{40,24},{48,32},{56,40},{64,11... | collective-permute-start | bytes 9224 | tf_op jit(solution)/shard_map/ppermute | solution.py:247
  (10 other events, 32.7 us)

commit v11 on v10

--- a/solution.py
+++ b/solution.py
@@ -242,7 +242,7 @@
         for i in range(total):
             goal = [i // (sides[1] * sides[2]), i // sides[2] % sides[1], i % sides[2]]
             for axis, step in zip(axes, steps):
-                goal[axis] = (goal[axis] + step) % sides[axis]
+                goal[axis] ^= step
             pairs.append((i, (goal[0] * sides[1] + goal[1]) * sides[2] + goal[2]))
         parts.append(lax.ppermute(array, "particle", pairs) if any(steps) else array)
     return parts
@@ -255,7 +255,7 @@
         pairs = []
         for i in range(tall * wide * cores):
             y, x, core = i // (wide * cores), i // cores % wide, i % cores
-            goal = (y ^ hop) * wide + (x + 2 * core + step) % wide
+            goal = (y ^ hop) * wide + (x ^ (2 * core + step))
             pairs.append((i, goal * cores + core))
         parts.append(lax.ppermute(array, "particle", pairs))
     return parts
@@ -310,7 +310,7 @@
     )
     places = (lengths, least, most)
     (outgoing_keys,) = pack((key_cache,), (new_keys,), *places, False)
-    arrived_keys = exchange(after(outgoing_keys, column))
+    arrived_keys = exchange(after(outgoing_keys, beside))
     outgoing_values, written_keys, written_values = pack(
         (key_cache, value_cache), (new_keys, new_values), *places, True
     )
@@ -380,9 +380,9 @@
 
     counted = jnp.sum((rungs[:, None] == ladder[None, :]).astype(jnp.float32), axis=0)
     tall, wide, cores = SIDES
-    up = (device // (wide * cores) - mine_owner // (wide * cores)) % tall
-    right = (device // cores % wide - mine_owner // cores % wide) % wide
-    across = (device % cores - mine_owner % cores) % cores
+    up = (device // (wide * cores)) ^ (mine_owner // (wide * cores))
+    right = (device // cores % wide) ^ (mine_owner // cores % wide)
+    across = (device % cores) ^ (mine_owner % cores)
     step = (right * tall + up) * cores + across
     next_values, rung_means, next_lengths = finish(
         arrived_values,

time: 140 us -> 140 us (level)
  waiting for transfers between devices: 61.2 us -> 65.4 us
  starting transfers between devices: 35.7 us -> 31.8 us
    ppermute x9, waiting for transfers between devices: 7.1 us -> 10.3 us  [along(): lax.ppermute(array, 'particle', pairs)]
    ppermute x9, starting transfers between devices: 13 us -> 10.7 us  [along(): lax.ppermute(array, 'particle', pairs)]
  transfers between devices with their start and end apart: 19 -> 19, of which waited for: 8 -> 7; matrix products, arithmetic and copies ran while one was open for 14% -> 14% of each run, Pallas kernels for 11% -> 11%
where the time goes in v11:
time: 140 us; the launch traced here: 139 us
  waiting for transfers between devices  65.4 us (47%)
  starting transfers between devices  31.8 us (23%)
  Pallas kernels  19.6 us (14%)
  other arithmetic  10.3 us (7%)
  matrix products  6.95 us (5%)
  local copies, waits for them, and re-layouts  3.75 us (3%)
    all_to_all x1, waiting for transfers between devices, shards(): arrived_keys = exchange(after(outgoing_keys, beside))  43 us
    ppermute x3, waiting for transfers between devices, shards(): reward = reward + lax.ppermute(reward, 'tensor', pairs)  12.1 us
    pallas_call x2, Pallas kernels, pack(): pl.pallas_call(functools.partial(pack_kernel, keeps), out_shape=[jax.Shap...  10.7 us
    ppermute x9, starting transfers between devices, along(): lax.ppermute(array, 'particle', pairs)  10.7 us
    ppermute x9, waiting for transfers between devices, along(): lax.ppermute(array, 'particle', pairs)  10.3 us
    all_to_all x1, starting transfers between devices, shards(): arrived_keys = exchange(after(outgoing_keys, beside))  5.97 us
    all_to_all x1, starting transfers between devices, shards(): arrived_values = exchange(after(outgoing_values, arrived_keys))  5 us
    ppermute x4, starting transfers between devices, half_of(): parts.append(lax.ppermute(array, 'particle', pairs))  4.23 us
  transfers between devices with their start and end apart: 19, of which 7 were waited for; matrix products, arithmetic and copies ran while one was open for 14% of the time, Pallas kernels for 11%

profile of v11, /device:TPU:128, one launch (start us, length us, event | category | flops | bytes accessed | tf_op | source)
XLA Modules:
  0.0 138.9 jit_solution(1018097584959910568)
XLA Ops:
  2.9 3.3 %collective-permute-start.1 = (bf16[128,256]{1,0:T(8,128)(2,1)S(1)}, bf16[128,256]{1,0:T(8,128)(2,1)S(1)}, u32[]{:S(2)}, u32[]{:S(2)}) collective-permute-start(bf16[128,256]{1,0:T(8,128)(2,1)S(1)} %maximum_add_fusion.1), channel_id=1, source_target_pairs={{0,128},{8,136},{16,144},{24,152},{32,160},{40,168},{48,176},{56,1... | collective-permute-start | bytes 196616 | tf_op jit(solution)/shard_map/ppermute | solution.py:304
  6.1 4.3 %pack.2.refs_0_ = bf16[64,256,128]{2,1,0:T(8,128)(2,1)} custom-call(s32[32]{0:T(128)} %lengths.3, s32[32]{0:T(128)} %copy-done.10, s32[32]{0:T(128)} %get-tuple-element.22.most, bf16[32,256,128]{2,1,0:T(8,128)(2,1)} %refs_0_.3, bf16[32,2,128]{2,1,0:T(2,128)(2,1)} %refs_2_.1), custom_call_target="tpu_custom_call" | custom-call | tf_op jit(solution)/shard_map/pack/pallas_call | solution.py:102
  11.1 6.0 %all-to-all-start = ((bf16[64,256,128]{2,1,0:T(8,128)(2,1)}), bf16[64,256,128]{2,1,0:T(8,128)(2,1)}, u32[]{:S(2)}, u32[]{:S(2)}) async-start(bf16[64,256,128]{2,1,0:T(8,128)(2,1)} %after.3), calls=%async_computation | async-start | bytes 8388608 | tf_op jit(solution)/shard_map/all_to_all | solution.py:313
  17.1 6.4 %pack.3 = (bf16[64,256,128]{2,1,0:T(8,128)(2,1)}, bf16[32,256,128]{2,1,0:T(8,128)(2,1)}, bf16[32,256,128]{2,1,0:T(8,128)(2,1)}) custom-call(s32[32]{0:T(128)} %lengths.3, s32[32]{0:T(128)} %copy-done.10, s32[32]{0:T(128)} %get-tuple-element.22.most, bf16[32,256,128]{2,1,0:T(8,128)(2,1)} %refs_0_.3, bf16[32,256,128]{2,1,0:T(8,128)(2,1)} %refs_1_.3, ...), custom_call_target="tpu_custom_call" | custom-call | tf_op jit(solution)/shard_map/pack/pallas_call | solution.py:102
  23.6 2.6 %collective-permute-start.5 = (bf16[256,256]{1,0:T(8,128)(2,1)S(1)}, bf16[256,256]{1,0:T(8,128)(2,1)S(1)}, u32[]{:S(2)}, u32[]{:S(2)}) collective-permute-start(bf16[256,256]{1,0:T(8,128)(2,1)S(1)} %pad_maximum_fusion.1._), channel_id=1, source_target_pairs={{0,80},{8,120},{16,64},{24,104},{32,112},{40,88},{48,96},{56,72},{... | collective-permute-start | bytes 393224 | tf_op jit(solution)/shard_map/ppermute | solution.py:260
  27.8 43.0 %all-to-all-done._.refs_1_.arrived = bf16[64,256,128]{2,1,0:T(8,128)(2,1)} async-done(((bf16[64,256,128]{2,1,0:T(8,128)(2,1)}), bf16[64,256,128]{2,1,0:T(8,128)(2,1)}, u32[]{:S(2)}, u32[]{:S(2)}) %all-to-all-start) | async-done | bytes 4194336 | tf_op jit(solution)/shard_map/all_to_all | solution.py:313
  70.8 5.0 %all-to-all-start.1 = ((bf16[64,256,128]{2,1,0:T(8,128)(2,1)}), bf16[64,256,128]{2,1,0:T(8,128)(2,1)}, u32[]{:S(2)}, u32[]{:S(2)}) async-start(bf16[64,256,128]{2,1,0:T(8,128)(2,1)} %after.4), calls=%async_computation.1 | async-start | bytes 8388608 | tf_op jit(solution)/shard_map/all_to_all | solution.py:317
  78.4 1.4 fusion.47
  79.8 3.7 %bitcast_reduce_fusion = (f32[32,2,8]{0,2,1:T(8,128)S(1)}, f32[2048,32,2,8]{0,1,3,2:T(8,128)}) fusion(bf16[32,2,8,128]{3,2,1,0:T(8,128)(2,1)S(1)} %reshape.74, bf16[1024,256]{1,0:T(8,128)(2,1)S(1)} %maximum_add_fusion, bf16[1024,256]{1,0:T(8,128)(2,1)} %collective-permute-done.6), kind=kOutput, calls=%fused_computation.1 | convolution fusion | flops 271580672 | bytes 5376000 | tf_op jit(solution)/shard_map/pshd,nd->pshn/dot_general | solution.py:327
  84.0 3.2 %fusion.1 = f32[32,2,8]{0,2,1:T(8,128)S(1)} fusion(f32[2048,32,2,8]{0,1,3,2:T(8,128)} %get-tuple-element.33, f32[32,2,8]{0,2,1:T(8,128)S(1)} %max.11), kind=kLoop, calls=%fused_computation.3 | loop fusion | flops 3145216 | bytes 4198400 | tf_op jit(solution)/shard_map/reduce_sum | solution.py:340
  87.7 2.0 %multiply_reduce_fusion = (f32[32]{0:T(128)S(1)}, bf16[32,2,8,128]{3,0,2,1:T(8,128)(2,1)S(1)}) fusion(f32[8,128]{1,0:T(8,128)S(1)} %bitcast.78, f32[32,2,8]{0,2,1:T(8,128)S(1)} %add.126, f32[32,2,8,128]{3,2,1,0:T(8,128)S(1)} %fusion.5, bf16[1024,256]{1,0:T(8,128)(2,1)} %collective-permute-done.6, bf16[1024,256]{1,0:T(8,128)(2,1)S(1)} %maximum_add_fusion, ...), kind=kOutput, calls=%fused_computation.29 | convolution fusion | flops 272957408 | bytes 5644416 | tf_op jit(solution)/shard_map/pshn,nd->pshd/dot_general | solution.py:341
  89.7 1.1 collective-permute-start.7
  91.4 1.9 %collective-permute-done.7 = f32[32]{0:T(128)S(1)} collective-permute-done((f32[32]{0:T(128)S(1)}, f32[32]{0:T(128)S(1)}, u32[]{:S(2)}, u32[]{:S(2)}) %collective-permute-start.7) | collective-permute-done | bytes 160 | tf_op jit(solution)/shard_map/ppermute | solution.py:359
  93.3 1.5 %collective-permute-start.8 = (f32[32]{0:T(128)S(1)}, f32[32]{0:T(128)S(1)}, u32[]{:S(2)}, u32[]{:S(2)}) collective-permute-start(f32[32]{0:T(128)S(1)} %add.127), channel_id=1, source_target_pairs={{0,2},{1,3},{2,0},{3,1},{4,6},{5,7},{6,4},{7,5},{8,10},{9,11},{10,... | collective-permute-start | bytes 392 | tf_op jit(solution)/shard_map/ppermute | solution.py:359
  95.0 2.8 %collective-permute-done.8 = f32[32]{0:T(128)S(1)} collective-permute-done((f32[32]{0:T(128)S(1)}, f32[32]{0:T(128)S(1)}, u32[]{:S(2)}, u32[]{:S(2)}) %collective-permute-start.8) | collective-permute-done | bytes 160 | tf_op jit(solution)/shard_map/ppermute | solution.py:359
  97.9 7.4 %collective-permute-done.9 = f32[32]{0:T(128)S(1)} collective-permute-done((f32[32]{0:T(128)S(1)}, f32[32]{0:T(128)S(1)}, u32[]{:S(2)}, u32[]{:S(2)}) %collective-permute-start.9) | collective-permute-done | bytes 160 | tf_op jit(solution)/shard_map/ppermute | solution.py:359
  106.4 4.2 %unpack.1 = (bf16[32,256,128]{2,1,0:T(8,128)(2,1)}, f32[1,128]{1,0:T(1,128)}) custom-call(s32[32]{0:T(128)} %fusion.41.slots, bf16[64,256,128]{2,1,0:T(8,128)(2,1)} %all-to-all-done._.refs_1_.arrived, bf16[256,256]{1,0:T(8,128)(2,1)} %copy-done.2), custom_call_target="tpu_custom_call" | custom-call | tf_op jit(solution)/shard_map/unpack/pallas_call | solution.py:175
  112.0 3.3 %collective-permute-start.13 = (f32[2,3,32]{2,1,0:T(4,128)}, f32[2,3,32]{2,1,0:T(4,128)S(1)}, u32[]{:S(2)}, u32[]{:S(2)}) collective-permute-start(f32[2,3,32]{2,1,0:T(4,128)} %after.5), channel_id=1, source_target_pairs={{0,192},{8,200},{16,208},{24,216},{32,224},{40,232},{48,240},{56,2... | collective-permute-start | bytes 2312 | tf_op jit(solution)/shard_map/ppermute | solution.py:247
  116.2 6.9 %collective-permute-done.13 = f32[2,3,32]{2,1,0:T(4,128)S(1)} collective-permute-done((f32[2,3,32]{2,1,0:T(4,128)}, f32[2,3,32]{2,1,0:T(4,128)S(1)}, u32[]{:S(2)}, u32[]{:S(2)}) %collective-permute-start.13) | collective-permute-done | bytes 800 | tf_op jit(solution)/shard_map/ppermute | solution.py:247
  123.8 3.4 %collective-permute-start.14 = (f32[8,3,32]{2,1,0:T(4,128)S(1)}, f32[8,3,32]{2,1,0:T(4,128)S(1)}, u32[]{:S(2)}, u32[]{:S(2)}) collective-permute-start(f32[8,3,32]{2,1,0:T(4,128)S(1)} %pad_maximum_fusion.3.refs_0_), channel_id=1, source_target_pairs={{0,16},{8,24},{16,0},{24,8},{32,48},{40,56},{48,32},{56,40},{64,80... | collective-permute-start | bytes 9224 | tf_op jit(solution)/shard_map/ppermute | solution.py:247
  127.1 1.9 %collective-permute-start.15 = (f32[8,3,32]{2,1,0:T(4,128)S(1)}, f32[8,3,32]{2,1,0:T(4,128)S(1)}, u32[]{:S(2)}, u32[]{:S(2)}) collective-permute-start(f32[8,3,32]{2,1,0:T(4,128)S(1)} %pad_maximum_fusion.3.refs_0_), channel_id=1, source_target_pairs={{0,32},{8,40},{16,48},{24,56},{32,0},{40,8},{48,16},{56,24},{64,96... | collective-permute-start | bytes 9224 | tf_op jit(solution)/shard_map/ppermute | solution.py:247
  130.5 1.9 %collective-permute-done.15.refs_2_ = f32[8,3,32]{2,1,0:T(4,128)S(1)} collective-permute-done((f32[8,3,32]{2,1,0:T(4,128)S(1)}, f32[8,3,32]{2,1,0:T(4,128)S(1)}, u32[]{:S(2)}, u32[]{:S(2)}) %collective-permute-start.15) | collective-permute-done | bytes 3104 | tf_op jit(solution)/shard_map/ppermute | solution.py:247
  132.4 1.6 %collective-permute-done.16.refs_3_ = f32[8,3,32]{2,1,0:T(4,128)S(1)} collective-permute-done((f32[8,3,32]{2,1,0:T(4,128)S(1)}, f32[8,3,32]{2,1,0:T(4,128)S(1)}, u32[]{:S(2)}, u32[]{:S(2)}) %collective-permute-start.16) | collective-permute-done | bytes 3104 | tf_op jit(solution)/shard_map/ppermute | solution.py:247
  134.6 4.2 %finish.1 = (bf16[32,256,128]{2,1,0:T(8,128)(2,1)}, f32[1,8]{1,0:T(1,128)}, s32[1,32]{1,0:T(1,128)}) custom-call(s32[32]{0:T(128)} %fusion.41.slots, bf16[64,256,128]{2,1,0:T(8,128)(2,1)} %all-to-all-done.1.arrived, f32[1,32]{1,0:T(1,128)} %pad_bitcast_fusion.2.counted, s32[1,32]{1,0:T(1,128)} %get-tuple-element.26.step, s32[1,32]{1,0:T(1,128)} %get-tuple-element.24.place, ...), custom_call_target="tpu_custom_call" | custom-call | tf_op jit(solution)/shard_map/finish/pallas_call | solution.py:218
  (96 shorter events, 15.2 us)
Async XLA Ops:
  1.4 1.5 %collective-permute-start = (bf16[64,256]{1,0:T(8,128)(2,1)S(1)}, bf16[64,256]{1,0:T(8,128)(2,1)S(1)}, u32[]{:S(2)}, u32[]{:S(2)}) collective-permute-start(bf16[64,256]{1,0:T(8,128)(2,1)S(1)} %pad_maximum_fusion.2), channel_id=1, source_target_pairs={{0,8},{8,0},{16,24},{24,16},{32,40},{40,32},{48,56},{56,48},{64,72... | collective-permute-start | bytes 98312 | tf_op jit(solution)/shard_map/ppermute | solution.py:247
  2.9 7.6 %collective-permute-start.1 = (bf16[128,256]{1,0:T(8,128)(2,1)S(1)}, bf16[128,256]{1,0:T(8,128)(2,1)S(1)}, u32[]{:S(2)}, u32[]{:S(2)}) collective-permute-start(bf16[128,256]{1,0:T(8,128)(2,1)S(1)} %maximum_add_fusion.1), channel_id=1, source_target_pairs={{0,128},{8,136},{16,144},{24,152},{32,160},{40,168},{48,176},{56,1... | collective-permute-start | bytes 196616 | tf_op jit(solution)/shard_map/ppermute | solution.py:304
  11.1 59.7 %all-to-all-start = ((bf16[64,256,128]{2,1,0:T(8,128)(2,1)}), bf16[64,256,128]{2,1,0:T(8,128)(2,1)}, u32[]{:S(2)}, u32[]{:S(2)}) async-start(bf16[64,256,128]{2,1,0:T(8,128)(2,1)} %after.3), calls=%async_computation | async-start | bytes 8388608 | tf_op jit(solution)/shard_map/all_to_all | solution.py:313
  23.6 47.2 %copy-start.2 = (bf16[256,256]{1,0:T(8,128)(2,1)}, bf16[256,256]{1,0:T(8,128)(2,1)S(1)}, u32[]{:S(2)}) copy-start(bf16[256,256]{1,0:T(8,128)(2,1)S(1)} %pad_maximum_fusion.1._) | copy-start | bytes 393220
  23.6 53.6 %collective-permute-start.5 = (bf16[256,256]{1,0:T(8,128)(2,1)S(1)}, bf16[256,256]{1,0:T(8,128)(2,1)S(1)}, u32[]{:S(2)}, u32[]{:S(2)}) collective-permute-start(bf16[256,256]{1,0:T(8,128)(2,1)S(1)} %pad_maximum_fusion.1._), channel_id=1, source_target_pairs={{0,80},{8,120},{16,64},{24,104},{32,112},{40,88},{48,96},{56,72},{... | collective-permute-start | bytes 393224 | tf_op jit(solution)/shard_map/ppermute | solution.py:260
  26.1 51.0 %collective-permute-start.4 = (bf16[256,256]{1,0:T(8,128)(2,1)S(1)}, bf16[256,256]{1,0:T(8,128)(2,1)S(1)}, u32[]{:S(2)}, u32[]{:S(2)}) collective-permute-start(bf16[256,256]{1,0:T(8,128)(2,1)S(1)} %pad_maximum_fusion.1._), channel_id=1, source_target_pairs={{0,64},{8,104},{16,80},{24,120},{32,96},{40,72},{48,112},{56,88},{... | collective-permute-start | bytes 393224 | tf_op jit(solution)/shard_map/ppermute | solution.py:260
  26.8 50.4 %collective-permute-start.3 = (bf16[256,256]{1,0:T(8,128)(2,1)S(1)}, bf16[256,256]{1,0:T(8,128)(2,1)S(1)}, u32[]{:S(2)}, u32[]{:S(2)}) collective-permute-start(bf16[256,256]{1,0:T(8,128)(2,1)S(1)} %pad_maximum_fusion.1._), channel_id=1, source_target_pairs={{0,16},{8,56},{16,0},{24,40},{32,48},{40,24},{48,32},{56,8},{64,80... | collective-permute-start | bytes 393224 | tf_op jit(solution)/shard_map/ppermute | solution.py:260
  27.1 50.0 %collective-permute-start.2 = (bf16[256,256]{1,0:T(8,128)(2,1)S(1)}, bf16[256,256]{1,0:T(8,128)(2,1)S(1)}, u32[]{:S(2)}, u32[]{:S(2)}) collective-permute-start(bf16[256,256]{1,0:T(8,128)(2,1)S(1)} %pad_maximum_fusion.1._), channel_id=1, source_target_pairs={{0,0},{8,40},{16,16},{24,56},{32,32},{40,8},{48,48},{56,24},{64,64... | collective-permute-start | bytes 393224 | tf_op jit(solution)/shard_map/ppermute | solution.py:260
  70.8 63.2 %all-to-all-start.1 = ((bf16[64,256,128]{2,1,0:T(8,128)(2,1)}), bf16[64,256,128]{2,1,0:T(8,128)(2,1)}, u32[]{:S(2)}, u32[]{:S(2)}) async-start(bf16[64,256,128]{2,1,0:T(8,128)(2,1)} %after.4), calls=%async_computation.1 | async-start | bytes 8388608 | tf_op jit(solution)/shard_map/all_to_all | solution.py:317
  77.3 2.5 %collective-permute-start.6 = (bf16[1024,256]{1,0:T(8,128)(2,1)S(1)}, bf16[1024,256]{1,0:T(8,128)(2,1)}, u32[]{:S(2)}, u32[]{:S(2)}) collective-permute-start(bf16[1024,256]{1,0:T(8,128)(2,1)S(1)} %maximum_add_fusion), channel_id=1, source_target_pairs={{0,8},{8,0},{16,24},{24,16},{32,40},{40,32},{48,56},{56,48},{64,72... | collective-permute-start | bytes 1572872 | tf_op jit(solution)/shard_map/ppermute | solution.py:247
  87.2 10.6 %copy-start.11 = (s32[1024]{0:T(1024)S(1)}, s32[1024]{0:T(1024)}, u32[]{:S(2)}) copy-start(s32[1024]{0:T(1024)} %param.22) | copy-start | bytes 12292
  87.2 18.0 %copy-start.14 = (f32[32]{0:T(128)S(1)}, f32[32]{0:T(128)}, u32[]{:S(2)}) copy-start(f32[32]{0:T(128)} %param.20) | copy-start | bytes 388
  89.7 3.6 %collective-permute-start.7 = (f32[32]{0:T(128)S(1)}, f32[32]{0:T(128)S(1)}, u32[]{:S(2)}, u32[]{:S(2)}) collective-permute-start(f32[32]{0:T(128)S(1)} %get-tuple-element.28), channel_id=1, source_target_pairs={{0,1},{1,0},{2,3},{3,2},{4,5},{5,4},{6,7},{7,6},{8,9},{9,8},{10,11... | collective-permute-start | bytes 392 | tf_op jit(solution)/shard_map/ppermute | solution.py:359
  93.3 4.4 %collective-permute-start.8 = (f32[32]{0:T(128)S(1)}, f32[32]{0:T(128)S(1)}, u32[]{:S(2)}, u32[]{:S(2)}) collective-permute-start(f32[32]{0:T(128)S(1)} %add.127), channel_id=1, source_target_pairs={{0,2},{1,3},{2,0},{3,1},{4,6},{5,7},{6,4},{7,5},{8,10},{9,11},{10,... | collective-permute-start | bytes 392 | tf_op jit(solution)/shard_map/ppermute | solution.py:359
  97.8 7.4 %collective-permute-start.9 = (f32[32]{0:T(128)S(1)}, f32[32]{0:T(128)S(1)}, u32[]{:S(2)}, u32[]{:S(2)}) collective-permute-start(f32[32]{0:T(128)S(1)} %add.128), channel_id=1, source_target_pairs={{0,4},{1,5},{2,6},{3,7},{4,0},{5,1},{6,2},{7,3},{8,12},{9,13},{10,... | collective-permute-start | bytes 392 | tf_op jit(solution)/shard_map/ppermute | solution.py:359
  105.2 33.6 %copy-start.13 = (f32[32]{0:T(128)}, f32[32]{0:T(128)S(1)}, u32[]{:S(2)}) copy-start(f32[32]{0:T(128)S(1)} %add_add_fusion) | copy-start | bytes 388
  105.6 5.8 %collective-permute-start.10 = (f32[1,3,32]{2,1,0:T(4,128)S(1)}, f32[1,3,32]{2,1,0:T(4,128)S(1)}, u32[]{:S(2)}, u32[]{:S(2)}) collective-permute-start(f32[1,3,32]{2,1,0:T(4,128)S(1)} %maximum_bitcast_fusion), channel_id=1, source_target_pairs={{0,8},{8,0},{16,24},{24,16},{32,40},{40,32},{48,56},{56,48},{64,72... | collective-permute-start | bytes 1160 | tf_op jit(solution)/shard_map/ppermute | solution.py:247
  112.0 11.1 %collective-permute-start.13 = (f32[2,3,32]{2,1,0:T(4,128)}, f32[2,3,32]{2,1,0:T(4,128)S(1)}, u32[]{:S(2)}, u32[]{:S(2)}) collective-permute-start(f32[2,3,32]{2,1,0:T(4,128)} %after.5), channel_id=1, source_target_pairs={{0,192},{8,200},{16,208},{24,216},{32,224},{40,232},{48,240},{56,2... | collective-permute-start | bytes 2312 | tf_op jit(solution)/shard_map/ppermute | solution.py:247
  115.2 7.8 %collective-permute-start.12 = (f32[2,3,32]{2,1,0:T(4,128)}, f32[2,3,32]{2,1,0:T(4,128)S(1)}, u32[]{:S(2)}, u32[]{:S(2)}) collective-permute-start(f32[2,3,32]{2,1,0:T(4,128)} %after.5), channel_id=1, source_target_pairs={{0,128},{8,136},{16,144},{24,152},{32,160},{40,168},{48,176},{56,1... | collective-permute-start | bytes 2312 | tf_op jit(solution)/shard_map/ppermute | solution.py:247
  115.9 7.2 %collective-permute-start.11 = (f32[2,3,32]{2,1,0:T(4,128)}, f32[2,3,32]{2,1,0:T(4,128)S(1)}, u32[]{:S(2)}, u32[]{:S(2)}) collective-permute-start(f32[2,3,32]{2,1,0:T(4,128)} %after.5), channel_id=1, source_target_pairs={{0,64},{8,72},{16,80},{24,88},{32,96},{40,104},{48,112},{56,120},{... | collective-permute-start | bytes 2312 | tf_op jit(solution)/shard_map/ppermute | solution.py:247
  123.8 10.2 %copy-start.6 = (f32[8,3,32]{2,1,0:T(4,128)}, f32[8,3,32]{2,1,0:T(4,128)S(1)}, u32[]{:S(2)}) copy-start(f32[8,3,32]{2,1,0:T(4,128)S(1)} %pad_maximum_fusion.3.refs_0_) | copy-start | bytes 9220
  123.8 6.7 %collective-permute-start.14 = (f32[8,3,32]{2,1,0:T(4,128)S(1)}, f32[8,3,32]{2,1,0:T(4,128)S(1)}, u32[]{:S(2)}, u32[]{:S(2)}) collective-permute-start(f32[8,3,32]{2,1,0:T(4,128)S(1)} %pad_maximum_fusion.3.refs_0_), channel_id=1, source_target_pairs={{0,16},{8,24},{16,0},{24,8},{32,48},{40,56},{48,32},{56,40},{64,80... | collective-permute-start | bytes 9224 | tf_op jit(solution)/shard_map/ppermute | solution.py:247
  127.1 5.2 %collective-permute-start.15 = (f32[8,3,32]{2,1,0:T(4,128)S(1)}, f32[8,3,32]{2,1,0:T(4,128)S(1)}, u32[]{:S(2)}, u32[]{:S(2)}) collective-permute-start(f32[8,3,32]{2,1,0:T(4,128)S(1)} %pad_maximum_fusion.3.refs_0_), channel_id=1, source_target_pairs={{0,32},{8,40},{16,48},{24,56},{32,0},{40,8},{48,16},{56,24},{64,96... | collective-permute-start | bytes 9224 | tf_op jit(solution)/shard_map/ppermute | solution.py:247
  129.0 4.9 %collective-permute-start.16 = (f32[8,3,32]{2,1,0:T(4,128)S(1)}, f32[8,3,32]{2,1,0:T(4,128)S(1)}, u32[]{:S(2)}, u32[]{:S(2)}) collective-permute-start(f32[8,3,32]{2,1,0:T(4,128)S(1)} %pad_maximum_fusion.3.refs_0_), channel_id=1, source_target_pairs={{0,48},{8,56},{16,32},{24,40},{32,16},{40,24},{48,0},{56,8},{64,11... | collective-permute-start | bytes 9224 | tf_op jit(solution)/shard_map/ppermute | solution.py:247
  (12 other events, 44.7 us)

commit v12 on v10

--- a/solution.py
+++ b/solution.py
@@ -18,6 +18,7 @@
 PLANES = 8
 WINDOW = 32
 CHUNKS = 4
+SHARE = 8
 GROUP = 2
 
 
@@ -141,9 +142,8 @@
     )(array)
 
 
-def move_rows(slots, arrived, result, held, in_sems, out_sems, meanwhile):
-    count = result.shape[0]
-    share = count // CHUNKS
+def move_rows(slots, arrived, result, held, in_sems, out_sems, meanwhile, first, last):
+    share = SHARE
 
     def load(p):
         return pltpu.make_async_copy(arrived.at[slots[p]], held.at[p], in_sems.at[p])
@@ -152,28 +152,29 @@
         rows = pl.ds(chunk * share, share)
         return pltpu.make_async_copy(held.at[rows], result.at[rows], out_sems.at[chunk])
 
-    repeat(count, lambda p: load(p).start(), count)
+    chunks = range(first // share, last // share)
+    repeat(last - first, lambda p: load(p + first).start(), last - first)
     meanwhile()
-    for chunk in range(CHUNKS):
+    for chunk in chunks:
         repeat(share, lambda p, chunk=chunk: load(p + chunk * share).wait(), share)
         keep(chunk).start()
-    for chunk in range(CHUNKS):
+    for chunk in chunks:
         keep(chunk).wait()
 
 
-def unpack_kernel(slots, arrived, _, result, mark, held, in_sems, out_sems):
+def unpack_kernel(last, slots, arrived, _, result, mark, held, in_sems, out_sems):
     def clear():
         mark[...] = jnp.zeros_like(mark)
 
-    move_rows(slots, arrived, result, held, in_sems, out_sems, clear)
-
-
-def unpack(arrived, slots, other):
+    move_rows(slots, arrived, result, held, in_sems, out_sems, clear, 0, last)
+
+
+def unpack(arrived, slots, other, last):
     count, (_, suffix, width) = slots.shape[0], arrived.shape
     hbm = pl.BlockSpec(memory_space=pltpu.HBM)
     shape = (count, suffix, width)
     return pl.pallas_call(
-        unpack_kernel,
+        functools.partial(unpack_kernel, last),
         out_shape=(
             jax.ShapeDtypeStruct(shape, arrived.dtype),
             jax.ShapeDtypeStruct((1, width), jnp.float32),
@@ -189,7 +190,7 @@
     )(slots, arrived, other)
 
 
-def finish_kernel(slots, arrived, counted, step, place, *refs):
+def finish_kernel(first, slots, arrived, _, counted, step, place, *refs):
     *parts, result, rung_means, next_lengths, held, in_sems, out_sems = refs
 
     def sums():
@@ -207,30 +208,32 @@
         length = jnp.sum(jnp.where(order == place[...], found, 0.0), axis=0, keepdims=True)
         next_lengths[...] = length.astype(jnp.int32) + STEPS
 
-    move_rows(slots, arrived, result, held, in_sems, out_sems, sums)
-
-
-def finish(arrived, slots, parts, counted, step, place):
+    last = result.shape[0]
+    move_rows(slots, arrived, result, held, in_sems, out_sems, sums, first, last)
+
+
+def finish(arrived, slots, begun, first, parts, counted, step, place):
     count, (_, suffix, width) = slots.shape[0], arrived.shape
     hbm = pl.BlockSpec(memory_space=pltpu.HBM)
     vmem = pl.BlockSpec(memory_space=pltpu.VMEM)
     shape = (count, suffix, width)
     return pl.pallas_call(
-        finish_kernel,
+        functools.partial(finish_kernel, first),
         out_shape=(
             jax.ShapeDtypeStruct(shape, arrived.dtype),
             jax.ShapeDtypeStruct((1, RUNGS), jnp.float32),
             jax.ShapeDtypeStruct(step.shape, jnp.int32),
         ),
-        in_specs=[pl.BlockSpec(memory_space=pltpu.SMEM), hbm] + [vmem] * (3 + len(parts)),
+        in_specs=[pl.BlockSpec(memory_space=pltpu.SMEM), hbm, hbm] + [vmem] * (3 + len(parts)),
         out_specs=(hbm, vmem, vmem),
         scratch_shapes=[
             pltpu.VMEM(shape, arrived.dtype),
             pltpu.SemaphoreType.DMA((count,)),
             pltpu.SemaphoreType.DMA((CHUNKS,)),
         ],
+        input_output_aliases={2: 0},
         name="finish",
-    )(slots, arrived, counted, step, place, *parts)
+    )(slots, arrived, begun, counted, step, place, *parts)
 
 
 def along(array, axes):
@@ -315,7 +318,7 @@
         (key_cache, value_cache), (new_keys, new_values), *places, True
     )
     arrived_values = exchange(after(outgoing_values, arrived_keys))
-    next_keys, mark = unpack(arrived_keys, slot, column)
+    next_keys, mark = unpack(arrived_keys, slot, column, per_device)
 
     half = jnp.concatenate(halves, axis=0) + zero_after(arrived_keys)[0, 0].astype(shard.dtype)
     prompt = jnp.concatenate(along(half, (2,)), axis=0)
@@ -384,9 +387,12 @@
     right = (device // cores % wide - mine_owner // cores % wide) % wide
     across = (device % cores - mine_owner % cores) % cores
     step = (right * tall + up) * cores + across
+    begun, _ = unpack(arrived_values, slot, near, per_device // 2)
     next_values, rung_means, next_lengths = finish(
         arrived_values,
         slot,
+        begun,
+        per_device // 2,
         parts,
         jnp.pad(counted, (0, spare), constant_values=1.0)[None],
         step[None],

time: 140 us -> 141 us (level)
  Pallas kernels: 19.1 us -> 22 us
    pallas_call x2 -> x3, Pallas kernels: 8.52 us -> 11.1 us  [the longest x2 7.39 us: unpack(): pl.pallas_call(functools.partial(unpack_kernel, last), out_shape=(jax.Sha...]
  transfers between devices with their start and end apart: 19 -> 19, of which waited for: 8 -> 7; matrix products, arithmetic and copies ran while one was open for 14% -> 13% of each run, Pallas kernels for 11% -> 13%
where the time goes in v12:
time: 141 us; the launch traced here: 140 us
  waiting for transfers between devices  60.4 us (43%)
  starting transfers between devices  35.7 us (25%)
  Pallas kernels  22 us (16%)
  other arithmetic  10.9 us (8%)
  matrix products  6.94 us (5%)
  local copies, waits for them, and re-layouts  3.1 us (2%)
    all_to_all x1, waiting for transfers between devices, shards(): arrived_keys = exchange(after(outgoing_keys, column))  41.8 us
    ppermute x9, starting transfers between devices, along(): lax.ppermute(array, 'particle', pairs)  13.2 us
    ppermute x3, waiting for transfers between devices, shards(): reward = reward + lax.ppermute(reward, 'tensor', pairs)  12 us
    pallas_call x2, Pallas kernels, pack(): pl.pallas_call(functools.partial(pack_kernel, keeps), out_shape=[jax.Shap...  10.4 us
    pallas_call x2, Pallas kernels, unpack(): pl.pallas_call(functools.partial(unpack_kernel, last), out_shape=(jax.Sha...  7.39 us
    ppermute x9, waiting for transfers between devices, along(): lax.ppermute(array, 'particle', pairs)  6.52 us
    all_to_all x1, starting transfers between devices, shards(): arrived_keys = exchange(after(outgoing_keys, column))  6.12 us
    ppermute x4, starting transfers between devices, half_of(): parts.append(lax.ppermute(array, 'particle', pairs))  5.58 us
  transfers between devices with their start and end apart: 19, of which 7 were waited for; matrix products, arithmetic and copies ran while one was open for 13% of the time, Pallas kernels for 13%

profile of v12, /device:TPU:128, one launch (start us, length us, event | category | flops | bytes accessed | tf_op | source)
XLA Modules:
  0.0 140.2 jit_solution(2926746164233085050)
XLA Ops:
  2.9 3.3 %collective-permute-start.1 = (bf16[128,256]{1,0:T(8,128)(2,1)S(1)}, bf16[128,256]{1,0:T(8,128)(2,1)S(1)}, u32[]{:S(2)}, u32[]{:S(2)}) collective-permute-start(bf16[128,256]{1,0:T(8,128)(2,1)S(1)} %maximum_add_fusion.1), channel_id=1, source_target_pairs={{0,128},{8,136},{16,144},{24,152},{32,160},{40,168},{48,176},{56,1... | collective-permute-start | bytes 196616 | tf_op jit(solution)/shard_map/ppermute | solution.py:307
  6.1 4.1 %pack.2.refs_0_ = bf16[64,256,128]{2,1,0:T(8,128)(2,1)} custom-call(s32[32]{0:T(128)} %lengths.3, s32[32]{0:T(128)} %copy-done.8, s32[32]{0:T(128)} %get-tuple-element.24.most, bf16[32,256,128]{2,1,0:T(8,128)(2,1)} %refs_0_.3, bf16[32,2,128]{2,1,0:T(2,128)(2,1)} %refs_2_.1), custom_call_target="tpu_custom_call" | custom-call | tf_op jit(solution)/shard_map/pack/pallas_call | solution.py:103
  11.0 6.1 %all-to-all-start = ((bf16[64,256,128]{2,1,0:T(8,128)(2,1)}), bf16[64,256,128]{2,1,0:T(8,128)(2,1)}, u32[]{:S(2)}, u32[]{:S(2)}) async-start(bf16[64,256,128]{2,1,0:T(8,128)(2,1)} %after.3), calls=%async_computation | async-start | bytes 8388608 | tf_op jit(solution)/shard_map/all_to_all | solution.py:316
  17.1 6.3 %pack.3 = (bf16[64,256,128]{2,1,0:T(8,128)(2,1)}, bf16[32,256,128]{2,1,0:T(8,128)(2,1)}, bf16[32,256,128]{2,1,0:T(8,128)(2,1)}) custom-call(s32[32]{0:T(128)} %lengths.3, s32[32]{0:T(128)} %copy-done.8, s32[32]{0:T(128)} %get-tuple-element.24.most, bf16[32,256,128]{2,1,0:T(8,128)(2,1)} %refs_0_.3, bf16[32,256,128]{2,1,0:T(8,128)(2,1)} %refs_1_.3, ...), custom_call_target="tpu_custom_call" | custom-call | tf_op jit(solution)/shard_map/pack/pallas_call | solution.py:103
  23.4 2.8 %collective-permute-start.5 = (bf16[256,256]{1,0:T(8,128)(2,1)S(1)}, bf16[256,256]{1,0:T(8,128)(2,1)S(1)}, u32[]{:S(2)}, u32[]{:S(2)}) collective-permute-start(bf16[256,256]{1,0:T(8,128)(2,1)S(1)} %copy-done.2), channel_id=1, source_target_pairs={{0,80},{8,120},{16,96},{24,72},{32,112},{40,88},{48,64},{56,104},{... | collective-permute-start | bytes 393224 | tf_op jit(solution)/shard_map/ppermute | solution.py:263
  26.7 1.7 %collective-permute-start.3 = (bf16[256,256]{1,0:T(8,128)(2,1)S(1)}, bf16[256,256]{1,0:T(8,128)(2,1)S(1)}, u32[]{:S(2)}, u32[]{:S(2)}) collective-permute-start(bf16[256,256]{1,0:T(8,128)(2,1)S(1)} %copy-done.2), channel_id=1, source_target_pairs={{0,16},{8,56},{16,32},{24,8},{32,48},{40,24},{48,0},{56,40},{64,80... | collective-permute-start | bytes 393224 | tf_op jit(solution)/shard_map/ppermute | solution.py:263
  29.0 41.8 %all-to-all-done._.refs_1_.arrived = bf16[64,256,128]{2,1,0:T(8,128)(2,1)} async-done(((bf16[64,256,128]{2,1,0:T(8,128)(2,1)}), bf16[64,256,128]{2,1,0:T(8,128)(2,1)}, u32[]{:S(2)}, u32[]{:S(2)}) %all-to-all-start) | async-done | bytes 4194336 | tf_op jit(solution)/shard_map/all_to_all | solution.py:316
  70.8 5.0 %all-to-all-start.1 = ((bf16[64,256,128]{2,1,0:T(8,128)(2,1)}), bf16[64,256,128]{2,1,0:T(8,128)(2,1)}, u32[]{:S(2)}, u32[]{:S(2)}) async-start(bf16[64,256,128]{2,1,0:T(8,128)(2,1)} %after.4), calls=%async_computation.1 | async-start | bytes 8388608 | tf_op jit(solution)/shard_map/all_to_all | solution.py:320
  78.5 1.3 fusion.47
  79.7 3.7 %bitcast_reduce_fusion = (f32[32,2,8]{0,2,1:T(8,128)S(1)}, f32[2048,32,2,8]{0,1,3,2:T(8,128)}) fusion(bf16[32,2,8,128]{3,2,1,0:T(8,128)(2,1)S(1)} %reshape.74, bf16[1024,256]{1,0:T(8,128)(2,1)S(1)} %maximum_add_fusion, bf16[1024,256]{1,0:T(8,128)(2,1)} %collective-permute-done.6), kind=kOutput, calls=%fused_computation.1 | convolution fusion | flops 271580672 | bytes 5376000 | tf_op jit(solution)/shard_map/pshd,nd->pshn/dot_general | solution.py:330
  83.9 3.2 %fusion.1 = f32[32,2,8]{0,2,1:T(8,128)S(1)} fusion(f32[2048,32,2,8]{0,1,3,2:T(8,128)} %get-tuple-element.35, f32[32,2,8]{0,2,1:T(8,128)S(1)} %max.11), kind=kLoop, calls=%fused_computation.3 | loop fusion | flops 3145216 | bytes 4198400 | tf_op jit(solution)/shard_map/reduce_sum | solution.py:343
  87.6 2.0 %multiply_reduce_fusion = (f32[32]{0:T(128)S(1)}, bf16[32,2,8,128]{3,0,2,1:T(8,128)(2,1)S(1)}) fusion(f32[8,128]{1,0:T(8,128)S(1)} %bitcast.78, f32[32,2,8]{0,2,1:T(8,128)S(1)} %add.138, f32[32,2,8,128]{3,2,1,0:T(8,128)S(1)} %fusion.5, bf16[1024,256]{1,0:T(8,128)(2,1)} %collective-permute-done.6, bf16[1024,256]{1,0:T(8,128)(2,1)S(1)} %maximum_add_fusion, ...), kind=kOutput, calls=%fused_computation.29 | convolution fusion | flops 272957408 | bytes 5644416 | tf_op jit(solution)/shard_map/pshn,nd->pshd/dot_general | solution.py:344
  91.3 1.9 %collective-permute-done.7 = f32[32]{0:T(128)S(1)} collective-permute-done((f32[32]{0:T(128)S(1)}, f32[32]{0:T(128)S(1)}, u32[]{:S(2)}, u32[]{:S(2)}) %collective-permute-start.7) | collective-permute-done | bytes 160 | tf_op jit(solution)/shard_map/ppermute | solution.py:362
  93.2 1.5 %collective-permute-start.8 = (f32[32]{0:T(128)S(1)}, f32[32]{0:T(128)S(1)}, u32[]{:S(2)}, u32[]{:S(2)}) collective-permute-start(f32[32]{0:T(128)S(1)} %add.139), channel_id=1, source_target_pairs={{0,2},{1,3},{2,0},{3,1},{4,6},{5,7},{6,4},{7,5},{8,10},{9,11},{10,... | collective-permute-start | bytes 392 | tf_op jit(solution)/shard_map/ppermute | solution.py:362
  94.9 2.8 %collective-permute-done.8 = f32[32]{0:T(128)S(1)} collective-permute-done((f32[32]{0:T(128)S(1)}, f32[32]{0:T(128)S(1)}, u32[]{:S(2)}, u32[]{:S(2)}) %collective-permute-start.8) | collective-permute-done | bytes 160 | tf_op jit(solution)/shard_map/ppermute | solution.py:362
  97.8 7.4 %collective-permute-done.9 = f32[32]{0:T(128)S(1)} collective-permute-done((f32[32]{0:T(128)S(1)}, f32[32]{0:T(128)S(1)}, u32[]{:S(2)}, u32[]{:S(2)}) %collective-permute-start.9) | collective-permute-done | bytes 160 | tf_op jit(solution)/shard_map/ppermute | solution.py:362
  106.3 3.9 %unpack.2 = (bf16[32,256,128]{2,1,0:T(8,128)(2,1)}, f32[1,128]{1,0:T(1,128)}) custom-call(s32[32]{0:T(128)} %fusion.43.slots, bf16[64,256,128]{2,1,0:T(8,128)(2,1)} %all-to-all-done._.refs_1_.arrived, bf16[256,256]{1,0:T(8,128)(2,1)} %pad_maximum_fusion.1.refs_1_._), custom_call_target="tpu_custom_call" | custom-call | tf_op jit(solution)/shard_map/unpack/pallas_call | solution.py:176
  111.5 3.4 %collective-permute-start.13 = (f32[2,3,32]{2,1,0:T(4,128)}, f32[2,3,32]{2,1,0:T(4,128)S(1)}, u32[]{:S(2)}, u32[]{:S(2)}) collective-permute-start(f32[2,3,32]{2,1,0:T(4,128)} %after.5), channel_id=1, source_target_pairs={{0,192},{8,200},{16,208},{24,216},{32,224},{40,232},{48,240},{56,2... | collective-permute-start | bytes 2312 | tf_op jit(solution)/shard_map/ppermute | solution.py:250
  116.6 5.7 %collective-permute-done.13 = f32[2,3,32]{2,1,0:T(4,128)S(1)} collective-permute-done((f32[2,3,32]{2,1,0:T(4,128)}, f32[2,3,32]{2,1,0:T(4,128)S(1)}, u32[]{:S(2)}, u32[]{:S(2)}) %collective-permute-start.13) | collective-permute-done | bytes 800 | tf_op jit(solution)/shard_map/ppermute | solution.py:250
  123.8 3.0 %collective-permute-start.14 = (f32[8,3,32]{2,1,0:T(4,128)S(1)}, f32[8,3,32]{2,1,0:T(4,128)S(1)}, u32[]{:S(2)}, u32[]{:S(2)}) collective-permute-start(f32[8,3,32]{2,1,0:T(4,128)S(1)} %pad_maximum_fusion.3._.refs_0_), channel_id=1, source_target_pairs={{0,16},{8,24},{16,32},{24,40},{32,48},{40,56},{48,0},{56,8},{64,80... | collective-permute-start | bytes 9224 | tf_op jit(solution)/shard_map/ppermute | solution.py:250
  126.8 2.2 %collective-permute-start.15 = (f32[8,3,32]{2,1,0:T(4,128)S(1)}, f32[8,3,32]{2,1,0:T(4,128)S(1)}, u32[]{:S(2)}, u32[]{:S(2)}) collective-permute-start(f32[8,3,32]{2,1,0:T(4,128)S(1)} %pad_maximum_fusion.3._.refs_0_), channel_id=1, source_target_pairs={{0,32},{8,40},{16,48},{24,56},{32,0},{40,8},{48,16},{56,24},{64,96... | collective-permute-start | bytes 9224 | tf_op jit(solution)/shard_map/ppermute | solution.py:250
  129.1 2.5 %collective-permute-start.16 = (f32[8,3,32]{2,1,0:T(4,128)S(1)}, f32[8,3,32]{2,1,0:T(4,128)S(1)}, u32[]{:S(2)}, u32[]{:S(2)}) collective-permute-start(f32[8,3,32]{2,1,0:T(4,128)S(1)} %pad_maximum_fusion.3._.refs_0_), channel_id=1, source_target_pairs={{0,48},{8,56},{16,0},{24,8},{32,16},{40,24},{48,32},{56,40},{64,11... | collective-permute-start | bytes 9224 | tf_op jit(solution)/shard_map/ppermute | solution.py:250
  132.1 3.5 %unpack.3 = (bf16[32,256,128]{2,1,0:T(8,128)(2,1)}, f32[1,128]{1,0:T(1,128)}) custom-call(s32[32]{0:T(128)} %fusion.43.slots, bf16[64,256,128]{2,1,0:T(8,128)(2,1)} %all-to-all-done.1.arrived, f32[8,3,32]{2,1,0:T(4,128)} %copy-done.3), custom_call_target="tpu_custom_call" | custom-call | tf_op jit(solution)/shard_map/unpack/pallas_call | solution.py:176
  136.3 3.7 %finish.1 = (bf16[32,256,128]{2,1,0:T(8,128)(2,1)}, f32[1,8]{1,0:T(1,128)}, s32[1,32]{1,0:T(1,128)}) custom-call(s32[32]{0:T(128)} %fusion.43.slots, bf16[64,256,128]{2,1,0:T(8,128)(2,1)} %all-to-all-done.1.arrived, bf16[32,256,128]{2,1,0:T(8,128)(2,1)} %get-tuple-element.19._, f32[1,32]{1,0:T(1,128)} %pad_bitcast_fusion.counted, ...), custom_call_target="tpu_custom_call", output_to_operand_aliasing={{0}: (2, {})} | custom-call | tf_op jit(solution)/shard_map/finish/pallas_call | solution.py:220
  (93 shorter events, 16.2 us)
Async XLA Ops:
  1.4 1.5 %collective-permute-start = (bf16[64,256]{1,0:T(8,128)(2,1)S(1)}, bf16[64,256]{1,0:T(8,128)(2,1)S(1)}, u32[]{:S(2)}, u32[]{:S(2)}) collective-permute-start(bf16[64,256]{1,0:T(8,128)(2,1)S(1)} %pad_maximum_fusion.2), channel_id=1, source_target_pairs={{0,8},{8,0},{16,24},{24,16},{32,40},{40,32},{48,56},{56,48},{64,72... | collective-permute-start | bytes 98312 | tf_op jit(solution)/shard_map/ppermute | solution.py:250
  2.9 7.4 %collective-permute-start.1 = (bf16[128,256]{1,0:T(8,128)(2,1)S(1)}, bf16[128,256]{1,0:T(8,128)(2,1)S(1)}, u32[]{:S(2)}, u32[]{:S(2)}) collective-permute-start(bf16[128,256]{1,0:T(8,128)(2,1)S(1)} %maximum_add_fusion.1), channel_id=1, source_target_pairs={{0,128},{8,136},{16,144},{24,152},{32,160},{40,168},{48,176},{56,1... | collective-permute-start | bytes 196616 | tf_op jit(solution)/shard_map/ppermute | solution.py:307
  11.0 59.8 %all-to-all-start = ((bf16[64,256,128]{2,1,0:T(8,128)(2,1)}), bf16[64,256,128]{2,1,0:T(8,128)(2,1)}, u32[]{:S(2)}, u32[]{:S(2)}) async-start(bf16[64,256,128]{2,1,0:T(8,128)(2,1)} %after.3), calls=%async_computation | async-start | bytes 8388608 | tf_op jit(solution)/shard_map/all_to_all | solution.py:316
  23.4 53.8 %collective-permute-start.5 = (bf16[256,256]{1,0:T(8,128)(2,1)S(1)}, bf16[256,256]{1,0:T(8,128)(2,1)S(1)}, u32[]{:S(2)}, u32[]{:S(2)}) collective-permute-start(bf16[256,256]{1,0:T(8,128)(2,1)S(1)} %copy-done.2), channel_id=1, source_target_pairs={{0,80},{8,120},{16,96},{24,72},{32,112},{40,88},{48,64},{56,104},{... | collective-permute-start | bytes 393224 | tf_op jit(solution)/shard_map/ppermute | solution.py:263
  26.3 50.9 %collective-permute-start.4 = (bf16[256,256]{1,0:T(8,128)(2,1)S(1)}, bf16[256,256]{1,0:T(8,128)(2,1)S(1)}, u32[]{:S(2)}, u32[]{:S(2)}) collective-permute-start(bf16[256,256]{1,0:T(8,128)(2,1)S(1)} %copy-done.2), channel_id=1, source_target_pairs={{0,64},{8,104},{16,80},{24,120},{32,96},{40,72},{48,112},{56,88},{... | collective-permute-start | bytes 393224 | tf_op jit(solution)/shard_map/ppermute | solution.py:263
  26.7 50.5 %collective-permute-start.3 = (bf16[256,256]{1,0:T(8,128)(2,1)S(1)}, bf16[256,256]{1,0:T(8,128)(2,1)S(1)}, u32[]{:S(2)}, u32[]{:S(2)}) collective-permute-start(bf16[256,256]{1,0:T(8,128)(2,1)S(1)} %copy-done.2), channel_id=1, source_target_pairs={{0,16},{8,56},{16,32},{24,8},{32,48},{40,24},{48,0},{56,40},{64,80... | collective-permute-start | bytes 393224 | tf_op jit(solution)/shard_map/ppermute | solution.py:263
  28.3 48.9 %collective-permute-start.2 = (bf16[256,256]{1,0:T(8,128)(2,1)S(1)}, bf16[256,256]{1,0:T(8,128)(2,1)S(1)}, u32[]{:S(2)}, u32[]{:S(2)}) collective-permute-start(bf16[256,256]{1,0:T(8,128)(2,1)S(1)} %copy-done.2), channel_id=1, source_target_pairs={{0,0},{8,40},{16,16},{24,56},{32,32},{40,8},{48,48},{56,24},{64,64... | collective-permute-start | bytes 393224 | tf_op jit(solution)/shard_map/ppermute | solution.py:263
  70.8 61.3 %all-to-all-start.1 = ((bf16[64,256,128]{2,1,0:T(8,128)(2,1)}), bf16[64,256,128]{2,1,0:T(8,128)(2,1)}, u32[]{:S(2)}, u32[]{:S(2)}) async-start(bf16[64,256,128]{2,1,0:T(8,128)(2,1)} %after.4), calls=%async_computation.1 | async-start | bytes 8388608 | tf_op jit(solution)/shard_map/all_to_all | solution.py:320
  77.3 2.4 %collective-permute-start.6 = (bf16[1024,256]{1,0:T(8,128)(2,1)S(1)}, bf16[1024,256]{1,0:T(8,128)(2,1)}, u32[]{:S(2)}, u32[]{:S(2)}) collective-permute-start(bf16[1024,256]{1,0:T(8,128)(2,1)S(1)} %maximum_add_fusion), channel_id=1, source_target_pairs={{0,8},{8,0},{16,24},{24,16},{32,40},{40,32},{48,56},{56,48},{64,72... | collective-permute-start | bytes 1572872 | tf_op jit(solution)/shard_map/ppermute | solution.py:250
  79.7 7.4 %copy-start.13 = (bf16[32,256,128]{2,1,0:T(8,128)(2,1)S(1)}, bf16[32,256,128]{2,1,0:T(8,128)(2,1)}, u32[]{:S(2)}) copy-start(bf16[32,256,128]{2,1,0:T(8,128)(2,1)} %get-tuple-element.16) | copy-start | bytes 6291460
  87.1 10.6 %copy-start.9 = (s32[1024]{0:T(1024)S(1)}, s32[1024]{0:T(1024)}, u32[]{:S(2)}) copy-start(s32[1024]{0:T(1024)} %param.22) | copy-start | bytes 12292
  87.1 18.0 %copy-start.12 = (f32[32]{0:T(128)S(1)}, f32[32]{0:T(128)}, u32[]{:S(2)}) copy-start(f32[32]{0:T(128)} %param.20) | copy-start | bytes 388
  89.6 3.6 %collective-permute-start.7 = (f32[32]{0:T(128)S(1)}, f32[32]{0:T(128)S(1)}, u32[]{:S(2)}, u32[]{:S(2)}) collective-permute-start(f32[32]{0:T(128)S(1)} %get-tuple-element.30), channel_id=1, source_target_pairs={{0,1},{1,0},{2,3},{3,2},{4,5},{5,4},{6,7},{7,6},{8,9},{9,8},{10,11... | collective-permute-start | bytes 392 | tf_op jit(solution)/shard_map/ppermute | solution.py:362
  93.2 4.4 %collective-permute-start.8 = (f32[32]{0:T(128)S(1)}, f32[32]{0:T(128)S(1)}, u32[]{:S(2)}, u32[]{:S(2)}) collective-permute-start(f32[32]{0:T(128)S(1)} %add.139), channel_id=1, source_target_pairs={{0,2},{1,3},{2,0},{3,1},{4,6},{5,7},{6,4},{7,5},{8,10},{9,11},{10,... | collective-permute-start | bytes 392 | tf_op jit(solution)/shard_map/ppermute | solution.py:362
  97.7 7.4 %collective-permute-start.9 = (f32[32]{0:T(128)S(1)}, f32[32]{0:T(128)S(1)}, u32[]{:S(2)}, u32[]{:S(2)}) collective-permute-start(f32[32]{0:T(128)S(1)} %add.140), channel_id=1, source_target_pairs={{0,4},{1,5},{2,6},{3,7},{4,0},{5,1},{6,2},{7,3},{8,12},{9,13},{10,... | collective-permute-start | bytes 392 | tf_op jit(solution)/shard_map/ppermute | solution.py:362
  105.1 30.5 %copy-start.11 = (f32[32]{0:T(128)}, f32[32]{0:T(128)S(1)}, u32[]{:S(2)}) copy-start(f32[32]{0:T(128)S(1)} %add_add_fusion) | copy-start | bytes 388
  105.5 5.5 %collective-permute-start.10 = (f32[1,3,32]{2,1,0:T(4,128)S(1)}, f32[1,3,32]{2,1,0:T(4,128)S(1)}, u32[]{:S(2)}, u32[]{:S(2)}) collective-permute-start(f32[1,3,32]{2,1,0:T(4,128)S(1)} %maximum_bitcast_fusion), channel_id=1, source_target_pairs={{0,8},{8,0},{16,24},{24,16},{32,40},{40,32},{48,56},{56,48},{64,72... | collective-permute-start | bytes 1160 | tf_op jit(solution)/shard_map/ppermute | solution.py:250
  111.5 10.8 %collective-permute-start.13 = (f32[2,3,32]{2,1,0:T(4,128)}, f32[2,3,32]{2,1,0:T(4,128)S(1)}, u32[]{:S(2)}, u32[]{:S(2)}) collective-permute-start(f32[2,3,32]{2,1,0:T(4,128)} %after.5), channel_id=1, source_target_pairs={{0,192},{8,200},{16,208},{24,216},{32,224},{40,232},{48,240},{56,2... | collective-permute-start | bytes 2312 | tf_op jit(solution)/shard_map/ppermute | solution.py:250
  114.9 7.8 %collective-permute-start.12 = (f32[2,3,32]{2,1,0:T(4,128)}, f32[2,3,32]{2,1,0:T(4,128)S(1)}, u32[]{:S(2)}, u32[]{:S(2)}) collective-permute-start(f32[2,3,32]{2,1,0:T(4,128)} %after.5), channel_id=1, source_target_pairs={{0,128},{8,136},{16,144},{24,152},{32,160},{40,168},{48,176},{56,1... | collective-permute-start | bytes 2312 | tf_op jit(solution)/shard_map/ppermute | solution.py:250
  115.6 7.5 %collective-permute-start.11 = (f32[2,3,32]{2,1,0:T(4,128)}, f32[2,3,32]{2,1,0:T(4,128)S(1)}, u32[]{:S(2)}, u32[]{:S(2)}) collective-permute-start(f32[2,3,32]{2,1,0:T(4,128)} %after.5), channel_id=1, source_target_pairs={{0,64},{8,72},{16,80},{24,88},{32,96},{40,104},{48,112},{56,120},{... | collective-permute-start | bytes 2312 | tf_op jit(solution)/shard_map/ppermute | solution.py:250
  123.8 8.3 %copy-start.3 = (f32[8,3,32]{2,1,0:T(4,128)}, f32[8,3,32]{2,1,0:T(4,128)S(1)}, u32[]{:S(2)}) copy-start(f32[8,3,32]{2,1,0:T(4,128)S(1)} %pad_maximum_fusion.3._.refs_0_) | copy-start | bytes 9220
  123.8 11.9 %collective-permute-start.14 = (f32[8,3,32]{2,1,0:T(4,128)S(1)}, f32[8,3,32]{2,1,0:T(4,128)S(1)}, u32[]{:S(2)}, u32[]{:S(2)}) collective-permute-start(f32[8,3,32]{2,1,0:T(4,128)S(1)} %pad_maximum_fusion.3._.refs_0_), channel_id=1, source_target_pairs={{0,16},{8,24},{16,32},{24,40},{32,48},{40,56},{48,0},{56,8},{64,80... | collective-permute-start | bytes 9224 | tf_op jit(solution)/shard_map/ppermute | solution.py:250
  126.8 8.9 %collective-permute-start.15 = (f32[8,3,32]{2,1,0:T(4,128)S(1)}, f32[8,3,32]{2,1,0:T(4,128)S(1)}, u32[]{:S(2)}, u32[]{:S(2)}) collective-permute-start(f32[8,3,32]{2,1,0:T(4,128)S(1)} %pad_maximum_fusion.3._.refs_0_), channel_id=1, source_target_pairs={{0,32},{8,40},{16,48},{24,56},{32,0},{40,8},{48,16},{56,24},{64,96... | collective-permute-start | bytes 9224 | tf_op jit(solution)/shard_map/ppermute | solution.py:250
  129.1 6.7 %collective-permute-start.16 = (f32[8,3,32]{2,1,0:T(4,128)S(1)}, f32[8,3,32]{2,1,0:T(4,128)S(1)}, u32[]{:S(2)}, u32[]{:S(2)}) collective-permute-start(f32[8,3,32]{2,1,0:T(4,128)S(1)} %pad_maximum_fusion.3._.refs_0_), channel_id=1, source_target_pairs={{0,48},{8,56},{16,0},{24,8},{32,16},{40,24},{48,32},{56,40},{64,11... | collective-permute-start | bytes 9224 | tf_op jit(solution)/shard_map/ppermute | solution.py:250
  (10 other events, 32.4 us)
